TPU v7x, 32 devices: a whole 2x2x4 slice. The times are simulated.
32 devices in a mesh: shard: 8 (over z, y), rep: 4 (over x, core).
Axes of the slice: x: 2, y: 2, z: 4, core: 2. Of those that a mesh axis runs over, the one named last changes fastest.
Arguments:
- memory: bfloat16 [8192, 512], P('shard'), may hold values from -4 to 4
- touch_owner: int32 [8192, 1], P(('shard', 'rep')), may hold values from 0 to 7; in each aligned block of 256 rows (0 to 255, 256 to 511, ...) at most 66 rows name the same one
- touch_row: int32 [8192], P(('shard', 'rep')), may hold values from 0 to 1023
- touch_time: int32 [8192], P(('shard', 'rep')), may hold values from 0 to 999
- src_slot: int32 [12288], P(('shard', 'rep')), may hold values from 0 to 255
- dst_slot: int32 [12288], P(('shard', 'rep')), may hold values from 0 to 255
- event_time: int32 [12288], P(('shard', 'rep')), may hold values from 1000 to 1999
- neighbour_blocks: int32 [96, 2], P(('shard', 'rep')), may hold values from 0 to 2
- time_freq: float32 [128], replicated, may hold values from 0.001 to 1
- time_phase: float32 [128], replicated, may hold values from -3.140625 to 3.140625
- w_input: bfloat16 [512, 1536], P(None, 'rep'), may hold values from -0.25 to 0.25
- w_time: bfloat16 [128, 1536], P(None, 'rep'), may hold values from -0.5 to 0.5
- w_hidden: bfloat16 [512, 1536], P(None, 'rep'), may hold values from -0.25 to 0.25
- w_query: bfloat16 [512, 512], P(None, 'rep'), may hold values from -0.25 to 0.25
- w_keyval: bfloat16 [512, 1024], P(None, 'rep'), may hold values from -0.25 to 0.25
Outputs:
- event_embed: bfloat16 [12288, 512], P(('shard', 'rep'))
- new_memory: bfloat16 [8192, 512], P('shard')
Inputs may be any that keep to these rules, and one draw needn't show every extreme that they name: `touch_owner`: in each batch of 256 touched entries at most 66 have the same owner, and some owner has exactly 66 in every draw.
All inputs are finite; a program needn't handle non-finite values.
Results may differ from a plain program's by a relative error of at most 0.0054.
Values may be sent and summed in bfloat16 or wider, within the bound.
No kernel may reach another device: no remote copies, remote signals or barrier semaphores. Data moves between devices by JAX's collectives and lax.ppermute only.
A program may use at most 64 MiB of HBM per device.

v0:
```python
import math

import jax
import jax.numpy as jnp
from jax import lax
from jax.sharding import PartitionSpec as P

H = 4
BLK = 128
NB = 2


def event_update(
    fetched,
    tick,
    source,
    target,
    stamp,
    listed,
    time_freq,
    time_phase,
    w_input,
    w_time,
    w_hidden,
    w_query,
    w_keyval,
):
    width = fetched.shape[1]
    count = stamp.shape[0]
    hsrc = fetched[source]
    hdst = fetched[target]
    spans = (stamp - tick[source]).astype(jnp.float32)
    encode = jnp.cos(spans[:, None] * time_freq[None, :] + time_phase[None, :]).astype(jnp.bfloat16)
    gin = jnp.dot(hdst, w_input, preferred_element_type=jnp.float32) + jnp.dot(
        encode, w_time, preferred_element_type=jnp.float32
    )
    ghid = jnp.dot(hsrc, w_hidden, preferred_element_type=jnp.float32)
    reset = jax.nn.sigmoid(gin[:, :width] + ghid[:, :width])
    update = jax.nn.sigmoid(gin[:, width : 2 * width] + ghid[:, width : 2 * width])
    fresh = jnp.tanh(gin[:, 2 * width :] + reset * ghid[:, 2 * width :])
    hold = hsrc.astype(jnp.float32)
    hnew = (1.0 - update) * fresh + update * hold
    entries = fetched.shape[0]
    counts = jax.ops.segment_sum(jnp.ones((count,), jnp.float32), source, entries)
    delta = jax.ops.segment_sum(hnew - hold, source, entries) / jnp.maximum(counts, 1.0)[:, None]
    hround = hnew.astype(jnp.bfloat16)
    query = jnp.dot(hround, w_query, preferred_element_type=jnp.float32).astype(jnp.bfloat16)
    keyval = jnp.dot(hdst, w_keyval, preferred_element_type=jnp.float32).astype(jnp.bfloat16)
    blocks = count // BLK
    headsz = width // H
    query4 = query.reshape(blocks, BLK, H, headsz)
    keys = (
        keyval[:, :width]
        .reshape(blocks, BLK, H, headsz)[listed]
        .reshape(blocks, NB * BLK, H, headsz)
    )
    values = (
        keyval[:, width:]
        .reshape(blocks, BLK, H, headsz)[listed]
        .reshape(blocks, NB * BLK, H, headsz)
    )
    scores = jnp.einsum(
        "qihd,qjhd->qhij", query4, keys, preferred_element_type=jnp.float32
    ) / math.sqrt(headsz)
    prob = jax.nn.softmax(scores, axis=-1).astype(jnp.bfloat16)
    attend = jnp.einsum(
        "qhij,qjhd->qihd", prob, values, preferred_element_type=jnp.float32
    ).reshape(count, width)
    embed = (hnew + attend).astype(jnp.bfloat16)
    return (embed, delta)


def shards(
    memory,
    touch_owner,
    touch_row,
    touch_time,
    src_slot,
    dst_slot,
    event_time,
    neighbour_blocks,
    time_freq,
    time_phase,
    w_input,
    w_time,
    w_hidden,
    w_query,
    w_keyval,
):
    owners = lax.axis_size("shard")
    entries = touch_row.shape[0]
    stored = memory.shape[0]
    width = memory.shape[1]
    capacity = 2 * entries // owners + 2
    owner = touch_owner[:, 0]
    hits = (owner[:, None] == jnp.arange(owners, dtype=jnp.int32)[None, :]).astype(jnp.int32)
    before = jnp.cumsum(hits, axis=0) - hits
    place = jnp.sum(before * hits, axis=1)
    request = jnp.full((owners, capacity), -1, jnp.int32).at[owner, place].set(touch_row)
    asked = lax.all_to_all(request, "shard", split_axis=0, concat_axis=0, tiled=True)
    valid = asked >= 0
    safe = jnp.clip(asked, 0, stored - 1)
    served = jnp.where(valid[:, :, None], memory[safe], jnp.zeros((), jnp.bfloat16))
    returned = lax.all_to_all(served, "shard", split_axis=0, concat_axis=0, tiled=True)
    fetched = returned[owner, place]
    full_input, full_time, full_hidden, full_query, full_keyval = (
        lax.all_gather(w_input, "rep", axis=1, tiled=True),
        lax.all_gather(w_time, "rep", axis=1, tiled=True),
        lax.all_gather(w_hidden, "rep", axis=1, tiled=True),
        lax.all_gather(w_query, "rep", axis=1, tiled=True),
        lax.all_gather(w_keyval, "rep", axis=1, tiled=True),
    )
    embed, delta = event_update(
        fetched,
        touch_time,
        src_slot,
        dst_slot,
        event_time,
        neighbour_blocks,
        time_freq,
        time_phase,
        full_input,
        full_time,
        full_hidden,
        full_query,
        full_keyval,
    )
    outgoing = jnp.zeros((owners, capacity, width), jnp.float32).at[owner, place].set(delta)
    landed = lax.all_to_all(outgoing, "shard", split_axis=0, concat_axis=0, tiled=True)
    targets = jnp.where(valid, asked, stored).reshape(-1)
    owner_part = jax.ops.segment_sum(landed.reshape(-1, width), targets, stored + 1)[:stored]
    total = lax.psum(owner_part, "rep")
    new_memory = (memory.astype(jnp.float32) + total).astype(jnp.bfloat16)
    return (embed, new_memory)


def solution(mesh):
    placed = (
        P("shard", None),
        P(("shard", "rep"), None),
        P(("shard", "rep")),
        P(("shard", "rep")),
        P(("shard", "rep")),
        P(("shard", "rep")),
        P(("shard", "rep")),
        P(("shard", "rep"), None),
        P(),
        P(),
        P(None, "rep"),
        P(None, "rep"),
        P(None, "rep"),
        P(None, "rep"),
        P(None, "rep"),
    )
    return jax.shard_map(
        shards,
        mesh=mesh,
        in_specs=placed,
        out_specs=(P(("shard", "rep"), None), P("shard", None)),
        check_vma=False,
    )
```

profile of v0, /device:TPU:0, one launch (start us, length us, event | category | flops | bytes accessed | tf_op | source)
XLA Modules:
  0.0 228.6 jit_solution(12938545822512952120)
XLA Ops:
  12.2 38.7 %scatter_fusion = s32[8,66]{1,0:T(8,128)} fusion(s32[8,66]{1,0:T(8,128)} %broadcast_in_dim.33, s32[256]{0:T(256)S(1)} %bitcast.43, s32[256]{0:T(256)} %param.17), kind=kCustom, calls=%fused_computation.7 | custom fusion | bytes 5120 | tf_op jit(solution)/shard_map/scatter | solution.py:99
  50.9 7.4 %all-to-all-start = ((s32[8,1,66]{2,1,0:T(1,128)}), s32[8,1,66]{2,1,0:T(1,128)S(1)}, u32[]{:S(2)}, u32[]{:S(2)}) async-start(s32[8,1,66]{2,1,0:T(1,128)} %bitcast.7), calls=%async_computation | async-start | bytes 8192 | tf_op jit(solution)/shard_map/all_to_all | solution.py:100
  59.1 2.8 %gather_fusion.3 = s32[384]{0:T(512)S(1)} fusion(s32[256]{0:T(256)S(1)} %copy-done, s32[1024]{0:T(1024)S(1)} %pad_clamp_fusion.1), kind=kCustom, calls=%fused_computation.3 | custom fusion | bytes 4608 | tf_op jit(solution)/shard_map/gather | solution.py:32
  62.0 3.9 %scatter_custom_fusion.2 = f32[256]{0:T(256)S(1)} fusion(s32[384]{0:T(512)S(1)} %copy-done.14, f32[384]{0:T(512)S(1)} %broadcast.178, f32[]{:T(128)} %constant.25.clone.1), kind=kCustom, calls=%fused_computation.82 | custom fusion | flops 384 | bytes 1028 | tf_op jit(solution)/shard_map/scatter-add | solution.py:44
  66.0 2.7 %gather_fusion = bf16[528,512]{1,0:T(8,128)(2,1)S(1)} fusion(bf16[1024,512]{1,0:T(8,128)(2,1)S(1)} %copy-done.1, s32[1024]{0:T(1024)S(1)} %pad_clamp_fusion.3), kind=kCustom, calls=%fused_computation | custom fusion | bytes 1083456 | tf_op jit(solution)/shard_map/gather | solution.py:103
  69.9 6.0 %all-to-all-start.1 = ((bf16[8,66,512]{2,1,0:T(8,128)(2,1)}), bf16[8,66,512]{2,1,0:T(8,128)(2,1)S(1)}, u32[]{:S(2)}, u32[]{:S(2)}) async-start(bf16[8,66,512]{2,1,0:T(8,128)(2,1)} %broadcast_select_fusion), calls=%async_computation.1 | async-start | bytes 1179648 | tf_op jit(solution)/shard_map/all_to_all | solution.py:104
  75.9 6.6 %all_gather.16 = bf16[128,1536]{1,0:T(8,128)(2,1)S(1)} all-gather(bf16[128,384]{1,0:T(8,128)(2,1)S(1)} %copy-done.11), channel_id=1, replica_groups=mesh['shard'=8,'rep'=4] {'rep'}, dimensions={1}, use_global_device_ids=true | all-gather | bytes 491520 | tf_op jit(solution)/shard_map/all_gather | solution.py:108
  82.6 2.5 %fusion.24 = f32[384,1536]{1,0:T(8,128)} fusion(bf16[128,1536]{1,0:T(8,128)(2,1)S(1)} %all_gather.16, f32[128]{0:T(128)S(1)} %copy-done.16, f32[128]{0:T(128)S(1)} %copy-done.17, f32[384]{0:T(512)S(1)} %subtract_convert_fusion), kind=kOutput, calls=%fused_computation.52 | convolution fusion | flops 151142400 | bytes 2755072 | tf_op jit(solution)/shard_map/dot_general | solution.py:34
  85.0 6.2 %all-to-all-done.1 = bf16[8,66,512]{2,1,0:T(8,128)(2,1)S(1)} async-done(((bf16[8,66,512]{2,1,0:T(8,128)(2,1)}), bf16[8,66,512]{2,1,0:T(8,128)(2,1)S(1)}, u32[]{:S(2)}, u32[]{:S(2)}) %all-to-all-start.1) | async-done | bytes 540704 | tf_op jit(solution)/shard_map/all_to_all | solution.py:104
  91.4 2.0 gather_fusion.1
  93.4 2.6 %gather_fusion.4 = bf16[384,512]{1,0:T(8,128)(2,1)} fusion(bf16[256,512]{1,0:T(8,128)(2,1)S(1)} %gather_fusion.1, s32[1024]{0:T(1024)S(1)} %pad_clamp_fusion.1), kind=kCustom, calls=%fused_computation.4 | custom fusion | bytes 787968 | tf_op jit(solution)/shard_map/gather | solution.py:30
  96.0 2.6 %gather_fusion.2 = bf16[384,512]{1,0:T(8,128)(2,1)} fusion(bf16[256,512]{1,0:T(8,128)(2,1)S(1)} %gather_fusion.1, s32[1024]{0:T(1024)S(1)} %pad_clamp_fusion.2), kind=kCustom, calls=%fused_computation.2 | custom fusion | bytes 787968 | tf_op jit(solution)/shard_map/gather | solution.py:31
  98.6 3.9 %fusion.48 = f32[384,1536]{1,0:T(8,128)} fusion(bf16[384,512]{1,0:T(8,128)(2,1)} %gather_fusion.4, bf16[512,1536]{1,0:T(8,128)(2,1)} %all-gather.6.cloned.1.call-done), kind=kOutput, calls=%fused_computation.88 | convolution fusion | flops 603979776 | bytes 4325376 | tf_op jit(solution)/shard_map/dot_general | solution.py:37
  102.5 2.5 %convolution_add_fusion = f32[384,1536]{1,0:T(8,128)S(1)} fusion(f32[384,1536]{1,0:T(8,128)S(1)} %copy-done.3, bf16[384,512]{1,0:T(8,128)(2,1)} %gather_fusion.2, bf16[512,1536]{1,0:T(8,128)(2,1)} %all-gather.4.cloned.1.call-done), kind=kOutput, calls=%fused_computation.13 | convolution fusion | flops 604569600 | bytes 6684672 | tf_op jit(solution)/shard_map/dot_general | solution.py:34
  105.9 3.0 %scatter_custom_fusion.1 = f32[256,512]{1,0:T(8,128)S(1)} fusion(s32[384]{0:T(512)S(1)} %copy-done.14, f32[384,512]{1,0:T(8,128)S(1)} %fusion.5, bf16[384,512]{1,0:T(8,128)(2,1)S(1)} %copy-done.5, f32[]{:T(128)} %constant.25.clone.1), kind=kCustom, calls=%fused_computation.27 | custom fusion | flops 589824 | bytes 1703940 | tf_op jit(solution)/shard_map/scatter-add | solution.py:45
  109.2 12.3 %scatter_fusion.1 = f32[8,66,512]{2,0,1:T(8,128)S(1)} fusion(f32[8,66,512]{2,0,1:T(8,128)S(1)} %broadcast_in_dim.69, s32[256]{0:T(256)S(1)} %bitcast.44, f32[256,512]{1,0:T(8,128)S(1)} %broadcast_divide_fusion), kind=kCustom, calls=%fused_computation.10 | custom fusion | bytes 1574912 | tf_op jit(solution)/shard_map/scatter | solution.py:128
  121.5 1.6 copy.67
  123.2 3.7 %all-to-all-start.2 = ((f32[8,66,512]{2,1,0:T(8,128)}), f32[8,66,512]{2,1,0:T(8,128)S(1)}, u32[]{:S(2)}, u32[]{:S(2)}) async-start(f32[8,66,512]{2,1,0:T(8,128)} %copy.67), calls=%async_computation.2 | async-start | bytes 2359296 | tf_op jit(solution)/shard_map/all_to_all | solution.py:129
  127.2 7.9 %all_gather.19 = bf16[512,512]{1,0:T(8,128)(2,1)} all-gather(bf16[512,128]{1,0:T(8,128)(2,1)S(1)} %copy-done.10), channel_id=1, replica_groups=mesh['shard'=8,'rep'=4] {'rep'}, dimensions={1}, use_global_device_ids=true | all-gather | bytes 655360 | tf_op jit(solution)/shard_map/all_gather | solution.py:110
  136.4 1.8 convolution_convert_fusion
  140.9 1.6 gather_fusion.6
  142.5 2.2 copy.62
  146.5 1.6 gather_fusion.5
  148.1 2.1 copy.60
  150.2 5.2 %all-to-all-done.2 = f32[8,66,512]{2,1,0:T(8,128)S(1)} async-done(((f32[8,66,512]{2,1,0:T(8,128)}), f32[8,66,512]{2,1,0:T(8,128)S(1)}, u32[]{:S(2)}, u32[]{:S(2)}) %all-to-all-start.2) | async-done | bytes 1081376 | tf_op jit(solution)/shard_map/all_to_all | solution.py:129
  155.4 1.1 reshape.204
  156.5 8.8 %scatter_custom_fusion.4 = f32[1025,512]{1,0:T(8,128)} fusion(s32[528]{0:T(1024)S(1)} %fusion.35, f32[528,512]{1,0:T(8,128)} %reshape.204, f32[]{:T(128)} %constant.25.clone.1), kind=kCustom, calls=%fused_computation.22 | custom fusion | flops 270336 | bytes 2099712 | tf_op jit(solution)/shard_map/scatter-add | solution.py:131
  165.3 3.1 %slice.71 = f32[1024,512]{1,0:T(8,128)} slice(f32[1025,512]{1,0:T(8,128)} %scatter_custom_fusion.4), slice={[0:1024], [0:512]} | slice | bytes 4194304 | tf_op jit(solution)/shard_map/slice | solution.py:131
  171.4 1.5 convolution_multiply_fusion
  172.9 5.2 %convolution_bitcast_fusion = f32[3,128,4,128]{1,3,2,0:T(8,128)S(1)} fusion(bf16[3,256,4,128]{3,1,0,2:T(8,128)(2,1)} %bitcast.49, f32[3,4,128]{2,1,0:T(4,128)S(1)} %fusion.43, f32[3,4,128,256]{3,2,1,0:T(8,128)} %convolution_multiply_fusion), kind=kOutput, calls=%fused_computation.20 | convolution fusion | flops 101844736 | bytes 3151872 | tf_op jit(solution)/shard_map/qhij,qjhd->qihd/dot_general | solution.py:66
  179.4 39.7 %all-reduce.2.cloned.1.call-done = f32[1024,512]{1,0:T(8,128)} async-done(((f32[1024,512]{1,0:T(8,128)}), f32[1024,512]{1,0:T(8,128)}) %all-reduce.2.cloned.1.call-update) | async-done | bytes 2097168 | tf_op jit(solution)/shard_map/psum | solution.py:132
  219.1 3.0 %add_convert_fusion = bf16[1024,512]{1,0:T(8,128)(2,1)} fusion(f32[1024,512]{1,0:T(8,128)} %all-reduce.2.cloned.1.call-done, bf16[1024,512]{1,0:T(8,128)(2,1)S(1)} %copy-done.1), kind=kLoop, calls=%fused_computation.14 | loop fusion | flops 1572864 | bytes 4194304 | tf_op jit(solution)/shard_map/convert_element_type | solution.py:133
  (91 shorter events, 18.7 us)
Async XLA Ops:
  7.2 52.0 %copy-start = (s32[256]{0:T(256)S(1)}, s32[256]{0:T(256)}, u32[]{:S(2)}) copy-start(s32[256]{0:T(256)} %param.18) | copy-start | bytes 3076
  7.2 91.4 %all-gather.6.cloned.1.call-start = ((), (), s32[]{:S(2)}) async-start(), calls=%async_computation.4 | async-start | bytes 1966080 | tf_op jit(solution)/shard_map/all_gather | solution.py:109
  7.9 51.2 %copy-start.14 = (s32[384]{0:T(512)S(1)}, s32[384]{0:T(512)}, u32[]{:S(2)}) copy-start(s32[384]{0:T(512)} %param.19) | copy-start | bytes 4612
  7.9 51.2 %copy-start.13 = (s32[384]{0:T(512)S(1)}, s32[384]{0:T(512)}, u32[]{:S(2)}) copy-start(s32[384]{0:T(512)} %param.20) | copy-start | bytes 4612
  7.9 94.5 %all-gather.4.cloned.1.call-start = ((), (), s32[]{:S(2)}) async-start(), calls=%async_computation.3 | async-start | bytes 1966080 | tf_op jit(solution)/shard_map/all_gather | solution.py:107
  50.9 15.1 %copy-start.1 = (bf16[1024,512]{1,0:T(8,128)(2,1)S(1)}, bf16[1024,512]{1,0:T(8,128)(2,1)}, u32[]{:S(2)}) copy-start(bf16[1024,512]{1,0:T(8,128)(2,1)} %param.15) | copy-start | bytes 3145732
  50.9 14.9 %all-to-all-start = ((s32[8,1,66]{2,1,0:T(1,128)}), s32[8,1,66]{2,1,0:T(1,128)S(1)}, u32[]{:S(2)}, u32[]{:S(2)}) async-start(s32[8,1,66]{2,1,0:T(1,128)} %bitcast.7), calls=%async_computation | async-start | bytes 8192 | tf_op jit(solution)/shard_map/all_to_all | solution.py:100
  58.3 78.1 %all-gather.8.cloned.1.call-start = ((), (), s32[]{:S(2)}) async-start(), calls=%async_computation.5 | async-start | bytes 1310720 | tf_op jit(solution)/shard_map/all_gather | solution.py:111
  68.7 7.2 %copy-start.11 = (bf16[128,384]{1,0:T(8,128)(2,1)S(1)}, bf16[128,384]{1,0:T(8,128)(2,1)}, u32[]{:S(2)}) copy-start(bf16[128,384]{1,0:T(8,128)(2,1)} %param.26) | copy-start | bytes 294916
  68.9 13.7 %copy-start.12 = (s32[384]{0:T(512)S(1)}, s32[384]{0:T(512)}, u32[]{:S(2)}) copy-start(s32[384]{0:T(512)} %param.21) | copy-start | bytes 4612
  68.9 13.6 %copy-start.16 = (f32[128]{0:T(128)S(1)}, f32[128]{0:T(128)}, u32[]{:S(2)}) copy-start(f32[128]{0:T(128)} %param.24) | copy-start | bytes 1540
  68.9 13.6 %copy-start.17 = (f32[128]{0:T(128)S(1)}, f32[128]{0:T(128)}, u32[]{:S(2)}) copy-start(f32[128]{0:T(128)} %param.23) | copy-start | bytes 1540
  69.9 21.4 %all-to-all-start.1 = ((bf16[8,66,512]{2,1,0:T(8,128)(2,1)}), bf16[8,66,512]{2,1,0:T(8,128)(2,1)S(1)}, u32[]{:S(2)}, u32[]{:S(2)}) async-start(bf16[8,66,512]{2,1,0:T(8,128)(2,1)} %broadcast_select_fusion), calls=%async_computation.1 | async-start | bytes 1179648 | tf_op jit(solution)/shard_map/all_to_all | solution.py:104
  98.6 3.9 %copy-start.3 = (f32[384,1536]{1,0:T(8,128)S(1)}, f32[384,1536]{1,0:T(8,128)}, u32[]{:S(2)}) copy-start(f32[384,1536]{1,0:T(8,128)} %fusion.24) | copy-start | bytes 7077892
  102.4 2.5 %copy-start.2 = (f32[384,1536]{1,0:T(8,128)S(1)}, f32[384,1536]{1,0:T(8,128)}, u32[]{:S(2)}) copy-start(f32[384,1536]{1,0:T(8,128)} %fusion.48) | copy-start | bytes 7077892
  102.4 2.5 %copy-start.4 = (bf16[384,512]{1,0:T(8,128)(2,1)S(1)}, bf16[384,512]{1,0:T(8,128)(2,1)}, u32[]{:S(2)}) copy-start(bf16[384,512]{1,0:T(8,128)(2,1)} %gather_fusion.4) | copy-start | bytes 1179652
  104.9 1.0 copy-start.5
  123.2 3.8 %copy-start.15 = (s32[3,2]{0,1:T(2,128)S(1)}, s32[3,2]{0,1:T(2,128)}, u32[]{:S(2)}) copy-start(s32[3,2]{0,1:T(2,128)} %param.22) | copy-start | bytes 76
  123.2 4.0 %copy-start.10 = (bf16[512,128]{1,0:T(8,128)(2,1)S(1)}, bf16[512,128]{1,0:T(8,128)(2,1)}, u32[]{:S(2)}) copy-start(bf16[512,128]{1,0:T(8,128)(2,1)} %param.28) | copy-start | bytes 393220
  123.2 13.2 %copy-start.8 = (bf16[384,512]{1,0:T(8,128)(2,1)S(1)}, bf16[384,512]{1,0:T(8,128)(2,1)}, u32[]{:S(2)}) copy-start(bf16[384,512]{1,0:T(8,128)(2,1)} %gather_fusion.2) | copy-start | bytes 1179652
  123.2 32.2 %all-to-all-start.2 = ((f32[8,66,512]{2,1,0:T(8,128)}), f32[8,66,512]{2,1,0:T(8,128)S(1)}, u32[]{:S(2)}, u32[]{:S(2)}) async-start(f32[8,66,512]{2,1,0:T(8,128)} %copy.67), calls=%async_computation.2 | async-start | bytes 2359296 | tf_op jit(solution)/shard_map/all_to_all | solution.py:129
  126.9 92.2 %all-reduce.2.cloned.1.call-start = ((), (), s32[]{:S(2)}) async-start(), calls=%async_computation.6 | async-start | bytes 4194304 | tf_op jit(solution)/shard_map/psum | solution.py:132
  142.5 2.2 copy-start.9
  168.4 1.0 copy-start.7
  169.4 1.1 copy-start.6
Sparse Core Ops, SparseCore 0:
  9.6 22.3 all-gather.5
  33.5 19.6 all-gather.3
  60.7 18.2 all-gather.7
  168.5 50.5 all-reduce.1
where the time goes:
time: 230 us; the launch traced here: 229 us
  local copies, waits for them, and re-layouts  86.1 us (37%)
  waiting for transfers between devices  53.2 us (23%)
  other arithmetic  24.7 us (11%)
  matrix products  18.6 us (8%)
  starting transfers between devices  17.3 us (8%)
  blocking collectives  14.5 us (6%)
  between operations  14.2 us (6%)
    psum x1, waiting for transfers between devices, shards(): total = lax.psum(owner_part, 'rep')  39.7 us
    scatter x1, local copies, waits for them, and re-layouts, shards(): jnp.full((owners, capacity), -1, jnp.int32).at[owner, place].set(touch_row)  38.7 us
    scatter x2, local copies, waits for them, and re-layouts, shards(): jnp.zeros((owners, capacity, width), jnp.float32).at[owner, place]  14 us
    scatter-add x1, other arithmetic, shards(): jax.ops.segment_sum(landed.reshape(-1, width), targets, stored + 1)[:stored]  8.78 us
    all_gather x1, blocking collectives, shards(): lax.all_gather(w_query, 'rep', axis=1, tiled=True)  7.9 us
    all_to_all x1, starting transfers between devices, shards(): lax.all_to_all(request, 'shard', split_axis=0, concat_axis=0, tiled=True)  7.41 us
    all_gather x1, blocking collectives, shards(): lax.all_gather(w_time, 'rep', axis=1, tiled=True)  6.64 us
    all_to_all x1, waiting for transfers between devices, shards(): lax.all_to_all(served, 'shard', split_axis=0, concat_axis=0, tiled=True)  6.19 us
  transfers between devices with their start and end apart: 7, of which 3 were waited for; matrix products, arithmetic and copies ran while one was open for 49% of the time, Pallas kernels for 0%

commit v1 on v0

v1 whole, which is shorter than its diff:
```python
import functools
import math

import jax
import jax.numpy as jnp
from jax import lax
from jax.experimental import pallas as pl
from jax.experimental.pallas import tpu as pltpu
from jax.sharding import PartitionSpec as P

H = 4
BLK = 128
NB = 2
LANES = 128
F32 = jnp.float32
BF16 = jnp.bfloat16
I32 = jnp.int32
VMEM = pl.BlockSpec(memory_space=pltpu.VMEM)
SMEM = pl.BlockSpec(memory_space=pltpu.SMEM)


def iota(shape, dim):
    return lax.broadcasted_iota(I32, shape, dim)


def dot(a, b):
    return jnp.dot(a, b, preferred_element_type=F32)


def call(body, outs, specs, flops, bytes_, name, scratch=(), limit=32):
    return pl.pallas_call(
        body,
        out_shape=outs,
        in_specs=specs,
        out_specs=[VMEM] * len(outs),
        scratch_shapes=list(scratch),
        compiler_params=pltpu.CompilerParams(vmem_limit_bytes=limit << 20),
        cost_estimate=pl.CostEstimate(flops=flops, bytes_accessed=bytes_, transcendentals=0),
        name=name,
    )


class Plan:
    def __init__(self, owners, reps, entries):
        self.owners = owners
        self.reps = reps
        self.entries = entries
        self.cap = 2 * entries // owners + 2
        self.tail = self.cap % 16 if self.cap % 16 * 4 == 8 else 0
        self.main = self.cap - self.tail if self.tail else -(-self.cap // 16) * 16
        self.rows = self.owners * (self.main + self.tail)
        self.pad = -(-self.cap // 8) * 8


def rank_of(own_col, own_row, entries):
    earlier = (own_col == own_row) & (iota((entries, entries), 0) < iota((entries, entries), 1))
    later = (own_col == own_row) & (iota((entries, entries), 1) < iota((entries, entries), 0))
    place_row = jnp.sum(jnp.where(earlier, 1, 0), axis=0, keepdims=True)
    place_col = jnp.sum(jnp.where(later, 1, 0), axis=1, keepdims=True)
    return place_row, place_col


def to_col(row, size):
    eye = iota((size, size), 0) == iota((size, size), 1)
    return jnp.sum(jnp.where(eye, row, 0), axis=1, keepdims=True)


def request_kernel(plan, owner_ref, row_ref, out_ref):
    own_row = owner_ref[...]
    own_col = to_col(own_row, plan.entries)
    _, place_col = rank_of(own_col, own_row, plan.entries)
    row = row_ref[...]
    mine = iota((plan.owners, plan.entries), 0) == own_row
    spot = jnp.where(place_col == iota((plan.entries, LANES), 1), 1.0, 0.0).astype(BF16)
    high = jnp.where(mine, row >> 5, 0).astype(F32).astype(BF16)
    low = jnp.where(mine, row & 31, 0).astype(F32).astype(BF16)
    out_ref[...] = (dot(high, spot) * 32.0 + dot(low, spot)).astype(I32)


def index_kernel(plan, owner_ref, tick_ref, src_ref, dst_ref, stamp_ref, freq_ref, phase_ref, enc_ref, col_ref, row_ref):
    events = src_ref.shape[1]
    own_row = owner_ref[...]
    own_col = to_col(own_row, plan.entries)
    _, place = rank_of(own_col, own_row, plan.entries)
    tick = to_col(tick_ref[...], plan.entries)
    spot = own_col * plan.main + place
    if plan.tail:
        spare = plan.owners * plan.main + (place - plan.main) * plan.owners + own_col
        spot = jnp.where(place < plan.main, spot, spare)
    back = own_col * plan.pad + place
    isrc = iota((plan.entries, events), 0) == src_ref[...]
    idst = iota((plan.entries, events), 0) == dst_ref[...]

    def pick(mask, values):
        return jnp.sum(jnp.where(mask, values, 0), axis=0, keepdims=True)

    src_spot = pick(isrc, spot)
    dst_spot = pick(idst, spot)
    src_back = pick(isrc, back)
    span = stamp_ref[...] - pick(isrc, tick)
    zero = jnp.zeros((8 - 3, events), I32)
    rows = jnp.concatenate([src_spot, dst_spot, span, zero], axis=0)
    row_ref[...] = jnp.concatenate([src_back, jnp.zeros((7, events), I32)], axis=0)
    cols = rows.astype(F32).T
    col_ref[...] = cols
    enc_ref[...] = jnp.cos(cols[:, 2:3] * freq_ref[...] + phase_ref[...]).astype(BF16)


def tail_order(plan, forward):
    count = 4 * plan.tail * plan.owners
    across = 0 if forward else 1
    there = iota((count, count), across)
    here = iota((count, count), 1 - across)
    part = 4 * plan.tail
    owner, inner = there // part, there % part
    return jnp.where((inner * plan.owners + owner) == here, 1.0, 0.0).astype(BF16)


def serve_kernel(plan, asked_ref, memory_ref, out_ref):
    stored, width = memory_ref.shape
    piece = width // 4
    asked = asked_ref[...].astype(F32)
    turned = asked.T
    blocks = [
        jnp.where(turned[: plan.main, s : s + 1].astype(I32) == iota((plan.main, stored), 1), 1.0, 0.0)
        for s in range(plan.owners)
    ]
    for i in range(plan.tail):
        spare = asked_ref[:, plan.main + i : plan.main + i + 1]
        blocks.append(jnp.where(spare == iota((plan.owners, stored), 1), 1.0, 0.0))
    hot = jnp.concatenate(blocks, axis=0).astype(BF16)
    rows = dot(hot, memory_ref[...])
    main = plan.main
    for s in range(plan.owners):
        for c in range(4):
            out_ref[s, c * main : (c + 1) * main, :] = rows[
                s * main : (s + 1) * main, c * piece : (c + 1) * piece
            ].astype(BF16)
    if plan.tail:
        spare = rows[plan.owners * main :]
        stack = jnp.concatenate([spare[:, c * piece : (c + 1) * piece] for c in range(4)], axis=0)
        ordered = dot(tail_order(plan, True), stack.astype(BF16))
        for s in range(plan.owners):
            out_ref[s, 4 * main : 4 * (main + plan.tail), :] = ordered[
                s * 4 * plan.tail : (s + 1) * 4 * plan.tail
            ].astype(BF16)


def table_of(plan, ret_ref):
    main = plan.main
    pieces = [
        jnp.concatenate([ret_ref[s, c * main : (c + 1) * main, :] for s in range(plan.owners)], axis=0)
        for c in range(4)
    ]
    table = jnp.concatenate(pieces, axis=1)
    if plan.tail:
        stack = jnp.concatenate(
            [ret_ref[s, 4 * main : 4 * (main + plan.tail), :].astype(F32) for s in range(plan.owners)], axis=0
        )
        ordered = dot(tail_order(plan, False), stack.astype(BF16))
        count = plan.tail * plan.owners
        spare = jnp.concatenate([ordered[c * count : (c + 1) * count] for c in range(4)], axis=1)
        table = jnp.concatenate([table, spare.astype(BF16)], axis=0)
    return table


def gru_kernel(plan, ret_ref, enc_ref, col_ref, row_ref, *refs):
    reps = plan.reps
    w_in, w_time, w_hid = refs[:reps], refs[reps : 2 * reps], refs[2 * reps : 3 * reps]
    out_ref, hnew_ref, hdst_ref, gin, ghid, delta = refs[3 * reps :]
    me = lax.axis_index("rep")
    events, width = hnew_ref.shape
    piece = width // reps
    cols = col_ref[...].astype(I32)
    spots = iota((events, plan.rows), 1)
    table = table_of(plan, ret_ref)
    hsrc = dot(jnp.where(cols[:, 0:1] == spots, 1.0, 0.0).astype(BF16), table)
    source = hsrc.astype(BF16)
    target = dot(jnp.where(cols[:, 1:2] == spots, 1.0, 0.0).astype(BF16), table).astype(BF16)
    hdst_ref[...] = target
    enc = enc_ref[...]
    part = w_in[0].shape[1]
    for k in range(reps):
        at = pl.ds(pl.multiple_of((me ^ k) * part, LANES), part)
        gin[:, at] = dot(target, w_in[k][...]) + dot(enc, w_time[k][...])
        ghid[:, at] = dot(source, w_hid[k][...])
    step = 64
    for i in range(0, events, step):
        at = slice(i, i + step)
        reset = 0.5 * jnp.tanh(0.5 * (gin[at, :width] + ghid[at, :width])) + 0.5
        update = 0.5 * jnp.tanh(0.5 * (gin[at, width : 2 * width] + ghid[at, width : 2 * width])) + 0.5
        fresh = jnp.tanh(gin[at, 2 * width :] + reset * ghid[at, 2 * width :])
        hold = hsrc[at]
        new = (1.0 - update) * fresh + update * hold
        hnew_ref[at, :] = new
        delta[at, :] = new - hold
    change = delta[...]
    high = change.astype(BF16)
    low = (change - high.astype(F32)).astype(BF16)
    slots = plan.owners * plan.pad
    hits = jnp.where(row_ref[0:1, :] == iota((slots, events), 0), 1.0, 0.0)
    counts = jnp.maximum(jnp.sum(hits, axis=1, keepdims=True), 1.0)
    hits = hits.astype(BF16)
    mean = (dot(hits, high) + dot(hits, low)) / counts
    for o in range(plan.owners):
        for q in range(reps):
            out_ref[o * reps + q] = mean[o * plan.pad : (o + 1) * plan.pad, q * piece : (q + 1) * piece].astype(BF16)


def attend_kernel(plan, listed_ref, hnew_ref, hdst_ref, *refs):
    reps = plan.reps
    w_query, w_keyval = refs[:reps], refs[reps : 2 * reps]
    out_ref, query, keyval = refs[2 * reps :]
    me = lax.axis_index("rep")
    events, width = hnew_ref.shape
    head = width // H
    hround = hnew_ref[...].astype(BF16)
    target = hdst_ref[...]
    for k in range(reps):
        part = w_query[k].shape[1]
        query[:, pl.ds(pl.multiple_of((me ^ k) * part, LANES), part)] = dot(hround, w_query[k][...]).astype(BF16)
        part = w_keyval[k].shape[1]
        keyval[:, pl.ds(pl.multiple_of((me ^ k) * part, LANES), part)] = dot(target, w_keyval[k][...]).astype(BF16)
    for i in range(events // BLK):
        spans = [pl.ds(pl.multiple_of(listed_ref[i, j] * BLK, BLK), BLK) for j in range(NB)]
        at = slice(i * BLK, (i + 1) * BLK)
        for h in range(H):
            lane = slice(h * head, (h + 1) * head)
            keys = jnp.concatenate([keyval[s, lane] for s in spans], axis=0)
            values = jnp.concatenate([keyval[s, width + h * head : width + (h + 1) * head] for s in spans], axis=0)
            scores = lax.dot_general(
                query[at, lane], keys, (((1,), (1,)), ((), ())), preferred_element_type=F32
            ) * (1.0 / math.sqrt(head))
            peak = jnp.max(scores, axis=1, keepdims=True)
            power = jnp.exp(scores - peak)
            prob = (power / jnp.sum(power, axis=1, keepdims=True)).astype(BF16)
            out_ref[at, lane] = (hnew_ref[at, lane] + dot(prob, values)).astype(BF16)


def apply_kernel(plan, ids_ref, landed_ref, memory_ref, out_ref):
    stored = memory_ref.shape[0]
    piece = out_ref.shape[1]
    count = landed_ref.shape[0]
    me = lax.axis_index("rep")
    landed = landed_ref[...]
    lane = pl.ds(pl.multiple_of(me * piece, LANES), piece)
    step = min(256, stored)
    ids = ids_ref[...]
    for i in range(0, stored, step):
        hot = jnp.where(iota((step, count), 0) + i == ids, 1.0, 0.0).astype(BF16)
        total = dot(hot, landed)
        out_ref[i : i + step, :] = (memory_ref[i : i + step, lane].astype(F32) + total).astype(BF16)


def join_kernel(plan, *refs):
    me = lax.axis_index("rep")
    out_ref = refs[-1]
    for k in range(plan.reps):
        piece = refs[k].shape[1]
        out_ref[:, pl.ds(pl.multiple_of((me ^ k) * piece, LANES), piece)] = refs[k][...]


def swap(x, bit, reps):
    return lax.ppermute(x, "rep", [(i, i ^ bit) for i in range(reps)])


def spread(arrays, reps):
    held = [{0: x} for x in arrays]
    bit = reps // 2
    while bit:
        for parts in held:
            for k in list(parts):
                parts[k ^ bit] = swap(parts[k], bit, reps)
        bit //= 2
    return [[parts[k] for k in range(reps)] for parts in held]


def shards(
    memory,
    touch_owner,
    touch_row,
    touch_time,
    src_slot,
    dst_slot,
    event_time,
    neighbour_blocks,
    time_freq,
    time_phase,
    w_input,
    w_time,
    w_hidden,
    w_query,
    w_keyval,
):
    owners = lax.axis_size("shard")
    reps = lax.axis_size("rep")
    entries = touch_row.shape[0]
    events = event_time.shape[0]
    stored, width = memory.shape
    plan = Plan(owners, reps, entries)
    piece = width // reps
    run = functools.partial
    sds = jax.ShapeDtypeStruct

    owner = touch_owner.reshape(1, entries)
    request = call(
        run(request_kernel, plan), [sds((owners, LANES), I32)], [VMEM] * 2, 1 << 20, 1 << 14, "request", limit=8
    )(owner, touch_row.reshape(1, entries))[0]

    full_hidden, full_input, full_time, full_keyval, full_query = spread(
        [w_hidden, w_input, w_time, w_keyval, w_query], reps
    )

    asked = lax.all_to_all(request, "shard", split_axis=0, concat_axis=0, tiled=True)
    encode, cols, rows = call(
        run(index_kernel, plan),
        [sds((events, time_freq.shape[0]), BF16), sds((events, 8), F32), sds((8, events), I32)],
        [VMEM] * 7,
        1 << 22,
        1 << 18,
        "index",
        limit=8,
    )(
        owner,
        touch_time.reshape(1, entries),
        src_slot.reshape(1, events),
        dst_slot.reshape(1, events),
        event_time.reshape(1, events),
        time_freq.reshape(1, -1),
        time_phase.reshape(1, -1),
    )
    everyone = [x for x in spread([asked], reps)[0]]

    chunk = 4 * (plan.main + plan.tail)
    served = call(
        run(serve_kernel, plan),
        [sds((owners, chunk, width // 4), BF16)],
        [VMEM] * 2,
        2 * plan.rows * stored * width,
        2 * stored * width + 2 * plan.rows * width,
        "serve",
        limit=24,
    )(asked, memory)[0]
    returned = lax.all_to_all(served, "shard", split_axis=0, concat_axis=0, tiled=True)

    outgoing, hnew, hdst = call(
        run(gru_kernel, plan),
        [sds((owners * reps, plan.pad, piece), BF16), sds((events, width), F32), sds((events, width), BF16)],
        [VMEM] * (4 + 3 * reps),
        2 * events * width * 3 * width * 2,
        8 << 20,
        "gru",
        scratch=[
            pltpu.VMEM((events, 3 * width), F32),
            pltpu.VMEM((events, 3 * width), F32),
            pltpu.VMEM((events, width), F32),
        ],
        limit=40,
    )(returned, encode, cols, rows, *full_input, *full_time, *full_hidden)
    landed = lax.all_to_all(outgoing, ("shard", "rep"), split_axis=0, concat_axis=0, tiled=True)

    embed = call(
        run(attend_kernel, plan),
        [sds((events, width), BF16)],
        [SMEM] + [VMEM] * (2 + 2 * reps),
        2 * events * width * 3 * width,
        4 << 20,
        "attend",
        scratch=[pltpu.VMEM((events, width), BF16), pltpu.VMEM((events, 2 * width), BF16)],
        limit=24,
    )(neighbour_blocks, hnew, hdst, *full_query, *full_keyval)[0]

    me = lax.axis_index("rep")
    stack = jnp.stack([x[:, : plan.pad] for x in everyone])
    order = me ^ jnp.arange(reps, dtype=I32)
    ids = jnp.swapaxes(stack[order], 0, 1).reshape(1, owners * reps * plan.pad)
    quarter = call(
        run(apply_kernel, plan),
        [sds((stored, piece), BF16)],
        [VMEM] * 3,
        2 * stored * owners * reps * plan.pad * piece * 2,
        4 << 20,
        "apply",
        limit=32,
    )(ids, landed.reshape(owners * reps * plan.pad, piece), memory)[0]
    new_memory = call(
        run(join_kernel, plan), [sds((stored, width), BF16)], [VMEM] * reps, 1 << 20, 2 << 20, "join", limit=8
    )(*spread([quarter], reps)[0])[0]
    return (embed, new_memory)


def solution(mesh):
    placed = (
        P("shard", None),
        P(("shard", "rep"), None),
        P(("shard", "rep")),
        P(("shard", "rep")),
        P(("shard", "rep")),
        P(("shard", "rep")),
        P(("shard", "rep")),
        P(("shard", "rep"), None),
        P(),
        P(),
        P(None, "rep"),
        P(None, "rep"),
        P(None, "rep"),
        P(None, "rep"),
        P(None, "rep"),
    )
    return jax.shard_map(
        shards,
        mesh=mesh,
        in_specs=placed,
        out_specs=(P(("shard", "rep"), None), P("shard", None)),
        check_vma=False,
    )
```

time: 230 us -> 116 us (0.50)
  local copies, waits for them, and re-layouts: 86.1 us -> 21.3 us
  other arithmetic: 24.7 us -> 0.02 us
  matrix products: 18.6 us -> 0 us
  Pallas kernels: 0 us -> 15.9 us
  between operations: 14.2 us -> 0.83 us
  waiting for transfers between devices: 53.2 us -> 44.7 us
    scatter x3 -> x0, local copies, waits for them, and re-layouts: 52.6 us -> none  [the longest x1 38.7 us: shards(): jnp.full((owners, capacity), -1, jnp.int32).at[owner, place].set(touch_row)]
    psum x1 -> x0, waiting for transfers between devices: 39.7 us -> none  [shards(): total = lax.psum(owner_part, 'rep')]
    ppermute x0 -> x21, waiting for transfers between devices: none -> 34.7 us  [swap(): return lax.ppermute(x, 'rep', [(i, i ^ bit) for i in range(reps)])]
    gather x10 -> x1, local copies, waits for them, and re-layouts: 20.2 us -> 0.55 us  [shards(): ids = jnp.swapaxes(stack[order], 0, 1).reshape(1, owners * reps * plan.pad)]
    unnamed x36 -> x71, local copies, waits for them, and re-layouts: 2.11 us -> 20.6 us
    dot_general x7 -> x0, matrix products: 17.8 us -> none  [the longest x1 5.25 us: event_update(): jnp.einsum('qhij,qjhd->qihd', prob, values, preferred_element_type=jnp.fl...]
    pallas_call x0 -> x7, Pallas kernels: none -> 15.9 us  [the longest x1 6.04 us: shards(): call(run(gru_kernel, plan), [sds((owners * reps, plan.pad, piece), BF16),...]
    scatter-add x3 -> x0, other arithmetic: 15.7 us -> none  [the longest x1 8.78 us: shards(): jax.ops.segment_sum(landed.reshape(-1, width), targets, stored + 1)[:stored]]
  transfers between devices with their start and end apart: 7 -> 23, of which waited for: 3 -> 9; matrix products, arithmetic and copies ran while one was open for 49% -> 1% of each run, Pallas kernels for 0% -> 11%
where the time goes in v1:
time: 116 us; the launch traced here: 115 us
  waiting for transfers between devices  44.7 us (39%)
  local copies, waits for them, and re-layouts  21.3 us (18%)
  starting transfers between devices  19 us (16%)
  Pallas kernels  15.9 us (14%)
  blocking collectives  13.5 us (12%)
    ppermute x21, waiting for transfers between devices, swap(): return lax.ppermute(x, 'rep', [(i, i ^ bit) for i in range(reps)])  34.7 us
    unnamed x71, local copies, waits for them, and re-layouts  20.6 us
    all_to_all x1, blocking collectives, shards(): lax.all_to_all(request, 'shard', split_axis=0, concat_axis=0, tiled=True)  13.5 us
    ppermute x21, starting transfers between devices, swap(): return lax.ppermute(x, 'rep', [(i, i ^ bit) for i in range(reps)])  10.7 us
    all_to_all x1, waiting for transfers between devices, shards(): lax.all_to_all(outgoing, ('shard', 'rep'), split_axis=0, concat_axis=0, t...  9.96 us
    pallas_call x1, Pallas kernels, shards(): call(run(gru_kernel, plan), [sds((owners * reps, plan.pad, piece), BF16),...  6.04 us
    all_to_all x1, starting transfers between devices, shards(): lax.all_to_all(outgoing, ('shard', 'rep'), split_axis=0, concat_axis=0, t...  4.67 us
    pallas_call x1, Pallas kernels, shards(): call(run(attend_kernel, plan), [sds((events, width), BF16)], [SMEM] + [VM...  3.86 us
  transfers between devices with their start and end apart: 23, of which 9 were waited for; matrix products, arithmetic and copies ran while one was open for 1% of the time, Pallas kernels for 11%

profile of v1, /device:TPU:0, one launch (start us, length us, event | category | flops | bytes accessed | tf_op | source)
XLA Modules:
  0.0 115.3 jit_solution(3778620717392605080)
XLA Ops:
  1.7 13.5 %all_to_all.21 = s32[8,1,128]{2,1,0:T(1,128)S(1)} all-to-all(s32[8,1,128]{2,1,0:T(1,128)S(1)} %bitcast.26), channel_id=1, replica_groups=mesh['shard'=8,'rep'=4] {'shard'}, dimensions={0} | all-to-all | bytes 8192 | tf_op jit(solution)/shard_map/all_to_all | solution.py:314
  15.2 1.2 %copy-done.6 = bf16[1024,512]{1,0:T(8,128)(2,1)S(1)} copy-done((bf16[1024,512]{1,0:T(8,128)(2,1)S(1)}, bf16[1024,512]{1,0:T(8,128)(2,1)}, u32[]{:S(2)}) %copy-start.6) | copy-done | bytes 1048600
  16.5 1.9 %serve.1 = bf16[8,264,128]{2,1,0:T(8,128)(2,1)} custom-call(s32[8,128]{1,0:T(8,128)S(1)} %bitcast.22, bf16[1024,512]{1,0:T(8,128)(2,1)S(1)} %copy-done.6), custom_call_target="tpu_custom_call" | custom-call | flops 553648128 | bytes 1589248 | tf_op jit(solution)/shard_map/serve/pallas_call | solution.py:335
  18.3 3.7 %all-to-all-start.1 = ((bf16[8,264,128]{2,1,0:T(8,128)(2,1)}), bf16[8,264,128]{2,1,0:T(8,128)(2,1)S(1)}, u32[]{:S(2)}, u32[]{:S(2)}) async-start(bf16[8,264,128]{2,1,0:T(8,128)(2,1)} %serve.1), calls=%async_computation.1 | async-start | bytes 1081344 | tf_op jit(solution)/shard_map/all_to_all | solution.py:344
  22.0 1.5 %collective-permute-start.1 = (bf16[512,384]{1,0:T(8,128)(2,1)S(1)}, bf16[512,384]{1,0:T(8,128)(2,1)S(1)}, u32[]{:S(2)}, u32[]{:S(2)}) collective-permute-start(bf16[512,384]{1,0:T(8,128)(2,1)S(1)} %copy-done.8), channel_id=1, source_target_pairs={{0,2},{1,3},{2,0},{3,1},{4,6},{5,7},{6,4},{7,5},{8,10},{9,11},{10,... | collective-permute-start | bytes 1179656 | tf_op jit(solution)/shard_map/ppermute | solution.py:264
  24.6 9.5 %collective-permute-done.1.refs_2_ = bf16[512,384]{1,0:T(8,128)(2,1)S(1)} collective-permute-done((bf16[512,384]{1,0:T(8,128)(2,1)S(1)}, bf16[512,384]{1,0:T(8,128)(2,1)S(1)}, u32[]{:S(2)}, u32[]{:S(2)}) %collective-permute-start.1) | collective-permute-done | bytes 393248 | tf_op jit(solution)/shard_map/ppermute | solution.py:264
  34.1 5.8 %collective-permute-done.7.refs_10_ = bf16[512,384]{1,0:T(8,128)(2,1)S(1)} collective-permute-done((bf16[512,384]{1,0:T(8,128)(2,1)S(1)}, bf16[512,384]{1,0:T(8,128)(2,1)S(1)}, u32[]{:S(2)}, u32[]{:S(2)}) %collective-permute-start.7) | collective-permute-done | bytes 393248 | tf_op jit(solution)/shard_map/ppermute | solution.py:264
  40.7 1.5 %collective-permute-start.4 = (bf16[128,384]{1,0:T(8,128)(2,1)S(1)}, bf16[128,384]{1,0:T(8,128)(2,1)S(1)}, u32[]{:S(2)}, u32[]{:S(2)}) collective-permute-start(bf16[128,384]{1,0:T(8,128)(2,1)S(1)} %copy-done.16), channel_id=1, source_target_pairs={{0,2},{1,3},{2,0},{3,1},{4,6},{5,7},{6,4},{7,5},{8,10},{9,11},{10,... | collective-permute-start | bytes 294920 | tf_op jit(solution)/shard_map/ppermute | solution.py:264
  42.2 3.7 %collective-permute-done.4.refs_6_ = bf16[128,384]{1,0:T(8,128)(2,1)S(1)} collective-permute-done((bf16[128,384]{1,0:T(8,128)(2,1)S(1)}, bf16[128,384]{1,0:T(8,128)(2,1)S(1)}, u32[]{:S(2)}, u32[]{:S(2)}) %collective-permute-start.4) | collective-permute-done | bytes 98336 | tf_op jit(solution)/shard_map/ppermute | solution.py:264
  45.9 1.3 %collective-permute-done.3.refs_5_ = bf16[128,384]{1,0:T(8,128)(2,1)S(1)} collective-permute-done((bf16[128,384]{1,0:T(8,128)(2,1)S(1)}, bf16[128,384]{1,0:T(8,128)(2,1)S(1)}, u32[]{:S(2)}, u32[]{:S(2)}) %collective-permute-start.3) | collective-permute-done | bytes 98336 | tf_op jit(solution)/shard_map/ppermute | solution.py:264
  50.7 1.2 %index.1 = (bf16[384,128]{1,0:T(8,128)(2,1)S(1)}, f32[384,8]{1,0:T(8,128)S(1)}, s32[8,384]{1,0:T(8,128)S(1)}) custom-call(s32[1,256]{1,0:T(1,128)S(1)} %bitcast.29, s32[1,256]{1,0:T(1,128)S(1)} %bitcast.30, s32[1,384]{1,0:T(1,128)S(1)} %reshape.55.src_ref, s32[1,384]{1,0:T(1,128)S(1)} %reshape.56.dst_ref, s32[1,384]{1,0:T(1,128)S(1)} %reshape.57.stamp_ref, ...), custom_call_target="tpu_custom_call" | custom-call | flops 4194304 | bytes 262144 | tf_op jit(solution)/shard_map/index/pallas_call | solution.py:315
  53.9 1.5 %collective-permute-start.13 = (bf16[512,256]{1,0:T(8,128)(2,1)S(1)}, bf16[512,256]{1,0:T(8,128)(2,1)S(1)}, u32[]{:S(2)}, u32[]{:S(2)}) collective-permute-start(bf16[512,256]{1,0:T(8,128)(2,1)S(1)} %copy-done), channel_id=1, source_target_pairs={{0,2},{1,3},{2,0},{3,1},{4,6},{5,7},{6,4},{7,5},{8,10},{9,11},{10,... | collective-permute-start | bytes 786440 | tf_op jit(solution)/shard_map/ppermute | solution.py:264
  56.9 1.0 copy-done.11
  57.9 1.0 copy-done.13
  58.9 1.0 copy-done.15
  59.8 0.9 copy-done.17
  60.7 0.9 copy-done.19
  63.4 0.9 copy-done.28
  65.2 6.0 %gru.1 = (bf16[32,72,128]{2,1,0:T(8,128)(2,1)}, f32[384,512]{1,0:T(8,128)S(1)}, bf16[384,512]{1,0:T(8,128)(2,1)S(1)}) custom-call(bf16[8,264,128]{2,1,0:T(8,128)(2,1)S(1)} %all-to-all-done.1.ret_ref, bf16[384,128]{1,0:T(8,128)(2,1)S(1)} %copy-done.30, f32[384,8]{1,0:T(8,128)S(1)} %copy-done.28, s32[8,384]{1,0:T(8,128)S(1)} %get-tuple-element.10.row_ref, ...), custom_call_target="tpu_custom_call" | custom-call | flops 1207959552 | bytes 8388608 | tf_op jit(solution)/shard_map/gru/pallas_call | solution.py:346
  71.3 4.7 %all-to-all-start.2 = ((bf16[32,72,128]{2,1,0:T(8,128)(2,1)}), bf16[32,72,128]{2,1,0:T(8,128)(2,1)S(1)}, u32[]{:S(2)}, u32[]{:S(2)}) async-start(bf16[32,72,128]{2,1,0:T(8,128)(2,1)} %get-tuple-element.13), calls=%async_computation.2 | async-start | bytes 1179648 | tf_op jit(solution)/shard_map/all_to_all | solution.py:360
  76.0 1.8 %collective-permute-start.16 = (s32[8,128]{1,0:T(8,128)S(1)}, s32[8,128]{1,0:T(8,128)S(1)}, u32[]{:S(2)}, u32[]{:S(2)}) collective-permute-start(s32[8,128]{1,0:T(8,128)S(1)} %bitcast.23), channel_id=1, source_target_pairs={{0,2},{1,3},{2,0},{3,1},{4,6},{5,7},{6,4},{7,5},{8,10},{9,11},{10,... | collective-permute-start | bytes 12296 | tf_op jit(solution)/shard_map/ppermute | solution.py:264
  77.8 3.1 %collective-permute-done.16 = s32[8,128]{1,0:T(8,128)S(1)} collective-permute-done((s32[8,128]{1,0:T(8,128)S(1)}, s32[8,128]{1,0:T(8,128)S(1)}, u32[]{:S(2)}, u32[]{:S(2)}) %collective-permute-start.16) | collective-permute-done | bytes 4128 | tf_op jit(solution)/shard_map/ppermute | solution.py:264
  80.9 1.1 collective-permute-done.17
  82.7 10.0 %all-to-all-done.2 = bf16[32,72,128]{2,1,0:T(8,128)(2,1)S(1)} async-done(((bf16[32,72,128]{2,1,0:T(8,128)(2,1)}), bf16[32,72,128]{2,1,0:T(8,128)(2,1)S(1)}, u32[]{:S(2)}, u32[]{:S(2)}) %all-to-all-start.2) | async-done | bytes 589856 | tf_op jit(solution)/shard_map/all_to_all | solution.py:360
  92.7 1.2 %copy-done.7 = bf16[1024,512]{1,0:T(8,128)(2,1)S(1)} copy-done((bf16[1024,512]{1,0:T(8,128)(2,1)S(1)}, bf16[1024,512]{1,0:T(8,128)(2,1)}, u32[]{:S(2)}) %copy-start.7) | copy-done | bytes 1048600
  93.9 1.4 %apply.1.refs_0_ = bf16[1024,128]{1,0:T(8,128)(2,1)S(1)} custom-call(s32[1,2304]{1,0:T(1,128)S(1)} %reshape.60.ids_ref, bf16[2304,128]{1,0:T(8,128)(2,1)S(1)} %bitcast.21, bf16[1024,512]{1,0:T(8,128)(2,1)S(1)} %copy-done.7), custom_call_target="tpu_custom_call" | custom-call | flops 1207959552 | bytes 4194304 | tf_op jit(solution)/shard_map/apply/pallas_call | solution.py:377
  95.3 1.2 %collective-permute-start.19 = (bf16[1024,128]{1,0:T(8,128)(2,1)S(1)}, bf16[1024,128]{1,0:T(8,128)(2,1)S(1)}, u32[]{:S(2)}, u32[]{:S(2)}) collective-permute-start(bf16[1024,128]{1,0:T(8,128)(2,1)S(1)} %apply.1.refs_0_), channel_id=1, source_target_pairs={{0,2},{1,3},{2,0},{3,1},{4,6},{5,7},{6,4},{7,5},{8,10},{9,11},{10,... | collective-permute-start | bytes 786440 | tf_op jit(solution)/shard_map/ppermute | solution.py:264
  97.9 8.6 %collective-permute-done.10.refs_2_ = bf16[512,128]{1,0:T(8,128)(2,1)} collective-permute-done((bf16[512,128]{1,0:T(8,128)(2,1)S(1)}, bf16[512,128]{1,0:T(8,128)(2,1)}, u32[]{:S(2)}, u32[]{:S(2)}) %collective-permute-start.10) | collective-permute-done | bytes 131104 | tf_op jit(solution)/shard_map/ppermute | solution.py:264
  107.8 1.6 %collective-permute-done.11.refs_3_ = bf16[512,128]{1,0:T(8,128)(2,1)} collective-permute-done((bf16[512,128]{1,0:T(8,128)(2,1)}, bf16[512,128]{1,0:T(8,128)(2,1)}, u32[]{:S(2)}, u32[]{:S(2)}) %collective-permute-start.11) | collective-permute-done | bytes 131104 | tf_op jit(solution)/shard_map/ppermute | solution.py:264
  109.4 0.9 copy-done.3
  110.3 3.9 %attend.1 = bf16[384,512]{1,0:T(8,128)(2,1)} custom-call(s32[3,2]{1,0:T(4,128)S(1)} %copy.20.listed_ref, f32[384,512]{1,0:T(8,128)S(1)} %get-tuple-element.11.hnew_ref, bf16[384,512]{1,0:T(8,128)(2,1)S(1)} %get-tuple-element.12.hdst_ref, bf16[512,128]{1,0:T(8,128)(2,1)S(1)} %copy-done.1, bf16[512,128]{1,0:T(8,128)(2,1)S(1)} %copy-done.3, ...), custom_call_target="tpu_custom_call" | custom-call | flops 603979776 | bytes 4194304 | tf_op jit(solution)/shard_map/attend/pallas_call | solution.py:362
  114.1 1.2 %join.1 = bf16[1024,512]{1,0:T(8,128)(2,1)} custom-call(bf16[1024,128]{1,0:T(8,128)(2,1)S(1)} %apply.1.refs_0_, bf16[1024,128]{1,0:T(8,128)(2,1)S(1)} %collective-permute-done.18.refs_1_, bf16[1024,128]{1,0:T(8,128)(2,1)S(1)} %collective-permute-done.19.refs_2_, bf16[1024,128]{1,0:T(8,128)(2,1)S(1)} %collective-permute-done.20.refs_3_), custom_call_target="tpu_custom_call" | custom-call | flops 1048576 | bytes 2097152 | tf_op jit(solution)/shard_map/join/pallas_call | solution.py:386
  (106 shorter events, 15.8 us)
Async XLA Ops:
  15.2 1.2 %copy-start.6 = (bf16[1024,512]{1,0:T(8,128)(2,1)S(1)}, bf16[1024,512]{1,0:T(8,128)(2,1)}, u32[]{:S(2)}) copy-start(bf16[1024,512]{1,0:T(8,128)(2,1)} %memory_ref.3) | copy-start | bytes 3145732
  16.5 24.2 %copy-start.16 = (bf16[128,384]{1,0:T(8,128)(2,1)S(1)}, bf16[128,384]{1,0:T(8,128)(2,1)}, u32[]{:S(2)}) copy-start(bf16[128,384]{1,0:T(8,128)(2,1)} %refs_4_.2) | copy-start | bytes 294916
  18.3 3.7 %copy-start.8 = (bf16[512,384]{1,0:T(8,128)(2,1)S(1)}, bf16[512,384]{1,0:T(8,128)(2,1)}, u32[]{:S(2)}) copy-start(bf16[512,384]{1,0:T(8,128)(2,1)} %refs_0_.2) | copy-start | bytes 1179652
  18.3 5.3 %copy-start.9 = (bf16[512,384]{1,0:T(8,128)(2,1)S(1)}, bf16[512,384]{1,0:T(8,128)(2,1)}, u32[]{:S(2)}) copy-start(bf16[512,384]{1,0:T(8,128)(2,1)} %refs_8_.1) | copy-start | bytes 1179652
  18.3 30.3 %copy-start.31 = (s32[384]{0:T(512)S(1)}, s32[384]{0:T(512)}, u32[]{:S(2)}) copy-start(s32[384]{0:T(512)} %param.19) | copy-start | bytes 4612
  18.3 31.7 %copy-start.26 = (f32[128]{0:T(128)S(1)}, f32[128]{0:T(128)}, u32[]{:S(2)}) copy-start(f32[128]{0:T(128)} %param.24) | copy-start | bytes 1540
  18.3 35.5 %copy-start = (bf16[512,256]{1,0:T(8,128)(2,1)S(1)}, bf16[512,256]{1,0:T(8,128)(2,1)}, u32[]{:S(2)}) copy-start(bf16[512,256]{1,0:T(8,128)(2,1)} %refs_4_.3) | copy-start | bytes 786436
  18.3 38.5 %all-to-all-start.1 = ((bf16[8,264,128]{2,1,0:T(8,128)(2,1)}), bf16[8,264,128]{2,1,0:T(8,128)(2,1)S(1)}, u32[]{:S(2)}, u32[]{:S(2)}) async-start(bf16[8,264,128]{2,1,0:T(8,128)(2,1)} %serve.1), calls=%async_computation.1 | async-start | bytes 1081344 | tf_op jit(solution)/shard_map/all_to_all | solution.py:344
  22.0 12.1 %collective-permute-start.1 = (bf16[512,384]{1,0:T(8,128)(2,1)S(1)}, bf16[512,384]{1,0:T(8,128)(2,1)S(1)}, u32[]{:S(2)}, u32[]{:S(2)}) collective-permute-start(bf16[512,384]{1,0:T(8,128)(2,1)S(1)} %copy-done.8), channel_id=1, source_target_pairs={{0,2},{1,3},{2,0},{3,1},{4,6},{5,7},{6,4},{7,5},{8,10},{9,11},{10,... | collective-permute-start | bytes 1179656 | tf_op jit(solution)/shard_map/ppermute | solution.py:264
  23.6 16.4 %collective-permute-start.7 = (bf16[512,384]{1,0:T(8,128)(2,1)S(1)}, bf16[512,384]{1,0:T(8,128)(2,1)S(1)}, u32[]{:S(2)}, u32[]{:S(2)}) collective-permute-start(bf16[512,384]{1,0:T(8,128)(2,1)S(1)} %copy-done.9), channel_id=1, source_target_pairs={{0,2},{1,3},{2,0},{3,1},{4,6},{5,7},{6,4},{7,5},{8,10},{9,11},{10,... | collective-permute-start | bytes 1179656 | tf_op jit(solution)/shard_map/ppermute | solution.py:264
  24.1 31.2 %collective-permute-start = (bf16[512,384]{1,0:T(8,128)(2,1)S(1)}, bf16[512,384]{1,0:T(8,128)(2,1)S(1)}, u32[]{:S(2)}, u32[]{:S(2)}) collective-permute-start(bf16[512,384]{1,0:T(8,128)(2,1)S(1)} %copy-done.8), channel_id=1, source_target_pairs={{0,1},{1,0},{2,3},{3,2},{4,5},{5,4},{6,7},{7,6},{8,9},{9,8},{10,11... | collective-permute-start | bytes 1179656 | tf_op jit(solution)/shard_map/ppermute | solution.py:264
  24.1 32.0 %collective-permute-start.6 = (bf16[512,384]{1,0:T(8,128)(2,1)S(1)}, bf16[512,384]{1,0:T(8,128)(2,1)S(1)}, u32[]{:S(2)}, u32[]{:S(2)}) collective-permute-start(bf16[512,384]{1,0:T(8,128)(2,1)S(1)} %copy-done.9), channel_id=1, source_target_pairs={{0,1},{1,0},{2,3},{3,2},{4,5},{5,4},{6,7},{7,6},{8,9},{9,8},{10,11... | collective-permute-start | bytes 1179656 | tf_op jit(solution)/shard_map/ppermute | solution.py:264
  34.1 22.7 %collective-permute-start.2 = (bf16[512,384]{1,0:T(8,128)(2,1)S(1)}, bf16[512,384]{1,0:T(8,128)(2,1)}, u32[]{:S(2)}, u32[]{:S(2)}) collective-permute-start(bf16[512,384]{1,0:T(8,128)(2,1)S(1)} %collective-permute-done.1.refs_2_), channel_id=1, source_target_pairs={{0,1},{1,0},{2,3},{3,2},{4,5},{5,4},{6,7},{7,6},{8,9},{9,8},{10,11... | collective-permute-start | bytes 1179656 | tf_op jit(solution)/shard_map/ppermute | solution.py:264
  39.9 16.9 %collective-permute-start.8 = (bf16[512,384]{1,0:T(8,128)(2,1)S(1)}, bf16[512,384]{1,0:T(8,128)(2,1)}, u32[]{:S(2)}, u32[]{:S(2)}) collective-permute-start(bf16[512,384]{1,0:T(8,128)(2,1)S(1)} %collective-permute-done.7.refs_10_), channel_id=1, source_target_pairs={{0,1},{1,0},{2,3},{3,2},{4,5},{5,4},{6,7},{7,6},{8,9},{9,8},{10,11... | collective-permute-start | bytes 1179656 | tf_op jit(solution)/shard_map/ppermute | solution.py:264
  40.7 5.2 %collective-permute-start.4 = (bf16[128,384]{1,0:T(8,128)(2,1)S(1)}, bf16[128,384]{1,0:T(8,128)(2,1)S(1)}, u32[]{:S(2)}, u32[]{:S(2)}) collective-permute-start(bf16[128,384]{1,0:T(8,128)(2,1)S(1)} %copy-done.16), channel_id=1, source_target_pairs={{0,2},{1,3},{2,0},{3,1},{4,6},{5,7},{6,4},{7,5},{8,10},{9,11},{10,... | collective-permute-start | bytes 294920 | tf_op jit(solution)/shard_map/ppermute | solution.py:264
  45.9 1.3 %collective-permute-start.3 = (bf16[128,384]{1,0:T(8,128)(2,1)S(1)}, bf16[128,384]{1,0:T(8,128)(2,1)S(1)}, u32[]{:S(2)}, u32[]{:S(2)}) collective-permute-start(bf16[128,384]{1,0:T(8,128)(2,1)S(1)} %copy-done.16), channel_id=1, source_target_pairs={{0,1},{1,0},{2,3},{3,2},{4,5},{5,4},{6,7},{7,6},{8,9},{9,8},{10,11... | collective-permute-start | bytes 294920 | tf_op jit(solution)/shard_map/ppermute | solution.py:264
  47.8 5.4 %collective-permute-start.5 = (bf16[128,384]{1,0:T(8,128)(2,1)S(1)}, bf16[128,384]{1,0:T(8,128)(2,1)S(1)}, u32[]{:S(2)}, u32[]{:S(2)}) collective-permute-start(bf16[128,384]{1,0:T(8,128)(2,1)S(1)} %collective-permute-done.4.refs_6_), channel_id=1, source_target_pairs={{0,1},{1,0},{2,3},{3,2},{4,5},{5,4},{6,7},{7,6},{8,9},{9,8},{10,11... | collective-permute-start | bytes 294920 | tf_op jit(solution)/shard_map/ppermute | solution.py:264
  53.9 44.1 %collective-permute-start.13 = (bf16[512,256]{1,0:T(8,128)(2,1)S(1)}, bf16[512,256]{1,0:T(8,128)(2,1)S(1)}, u32[]{:S(2)}, u32[]{:S(2)}) collective-permute-start(bf16[512,256]{1,0:T(8,128)(2,1)S(1)} %copy-done), channel_id=1, source_target_pairs={{0,2},{1,3},{2,0},{3,1},{4,6},{5,7},{6,4},{7,5},{8,10},{9,11},{10,... | collective-permute-start | bytes 786440 | tf_op jit(solution)/shard_map/ppermute | solution.py:264
  71.3 21.4 %all-to-all-start.2 = ((bf16[32,72,128]{2,1,0:T(8,128)(2,1)}), bf16[32,72,128]{2,1,0:T(8,128)(2,1)S(1)}, u32[]{:S(2)}, u32[]{:S(2)}) async-start(bf16[32,72,128]{2,1,0:T(8,128)(2,1)} %get-tuple-element.13), calls=%async_computation.2 | async-start | bytes 1179648 | tf_op jit(solution)/shard_map/all_to_all | solution.py:360
  76.0 4.9 %collective-permute-start.16 = (s32[8,128]{1,0:T(8,128)S(1)}, s32[8,128]{1,0:T(8,128)S(1)}, u32[]{:S(2)}, u32[]{:S(2)}) collective-permute-start(s32[8,128]{1,0:T(8,128)S(1)} %bitcast.23), channel_id=1, source_target_pairs={{0,2},{1,3},{2,0},{3,1},{4,6},{5,7},{6,4},{7,5},{8,10},{9,11},{10,... | collective-permute-start | bytes 12296 | tf_op jit(solution)/shard_map/ppermute | solution.py:264
  77.8 3.1 %collective-permute-start.15 = (s32[8,128]{1,0:T(8,128)S(1)}, s32[8,128]{1,0:T(8,128)S(1)}, u32[]{:S(2)}, u32[]{:S(2)}) collective-permute-start(s32[8,128]{1,0:T(8,128)S(1)} %bitcast.24), channel_id=1, source_target_pairs={{0,1},{1,0},{2,3},{3,2},{4,5},{5,4},{6,7},{7,6},{8,9},{9,8},{10,11... | collective-permute-start | bytes 12296 | tf_op jit(solution)/shard_map/ppermute | solution.py:264
  80.9 1.2 %collective-permute-start.17 = (s32[8,128]{1,0:T(8,128)S(1)}, s32[8,128]{1,0:T(8,128)S(1)}, u32[]{:S(2)}, u32[]{:S(2)}) collective-permute-start(s32[8,128]{1,0:T(8,128)S(1)} %collective-permute-done.16), channel_id=1, source_target_pairs={{0,1},{1,0},{2,3},{3,2},{4,5},{5,4},{6,7},{7,6},{8,9},{9,8},{10,11... | collective-permute-start | bytes 12296 | tf_op jit(solution)/shard_map/ppermute | solution.py:264
  93.9 2.6 %copy-start.1 = (bf16[512,128]{1,0:T(8,128)(2,1)S(1)}, bf16[512,128]{1,0:T(8,128)(2,1)}, u32[]{:S(2)}) copy-start(bf16[512,128]{1,0:T(8,128)(2,1)} %refs_0_.3) | copy-start | bytes 393220
  93.9 13.8 %copy-start.34 = (s32[3,2]{0,1:T(2,128)S(1)}, s32[3,2]{0,1:T(2,128)}, u32[]{:S(2)}) copy-start(s32[3,2]{0,1:T(2,128)} %param.22) | copy-start | bytes 76
  95.3 11.2 %collective-permute-start.19 = (bf16[1024,128]{1,0:T(8,128)(2,1)S(1)}, bf16[1024,128]{1,0:T(8,128)(2,1)S(1)}, u32[]{:S(2)}, u32[]{:S(2)}) collective-permute-start(bf16[1024,128]{1,0:T(8,128)(2,1)S(1)} %apply.1.refs_0_), channel_id=1, source_target_pairs={{0,2},{1,3},{2,0},{3,1},{4,6},{5,7},{6,4},{7,5},{8,10},{9,11},{10,... | collective-permute-start | bytes 786440 | tf_op jit(solution)/shard_map/ppermute | solution.py:264
  96.5 10.0 %collective-permute-start.10 = (bf16[512,128]{1,0:T(8,128)(2,1)S(1)}, bf16[512,128]{1,0:T(8,128)(2,1)}, u32[]{:S(2)}, u32[]{:S(2)}) collective-permute-start(bf16[512,128]{1,0:T(8,128)(2,1)S(1)} %copy-done.1), channel_id=1, source_target_pairs={{0,2},{1,3},{2,0},{3,1},{4,6},{5,7},{6,4},{7,5},{8,10},{9,11},{10,... | collective-permute-start | bytes 393224 | tf_op jit(solution)/shard_map/ppermute | solution.py:264
  97.4 9.6 %collective-permute-start.9 = (bf16[512,128]{1,0:T(8,128)(2,1)S(1)}, bf16[512,128]{1,0:T(8,128)(2,1)S(1)}, u32[]{:S(2)}, u32[]{:S(2)}) collective-permute-start(bf16[512,128]{1,0:T(8,128)(2,1)S(1)} %copy-done.1), channel_id=1, source_target_pairs={{0,1},{1,0},{2,3},{3,2},{4,5},{5,4},{6,7},{7,6},{8,9},{9,8},{10,11... | collective-permute-start | bytes 393224 | tf_op jit(solution)/shard_map/ppermute | solution.py:264
  97.4 12.0 %collective-permute-start.12 = (bf16[512,256]{1,0:T(8,128)(2,1)S(1)}, bf16[512,256]{1,0:T(8,128)(2,1)S(1)}, u32[]{:S(2)}, u32[]{:S(2)}) collective-permute-start(bf16[512,256]{1,0:T(8,128)(2,1)S(1)} %copy-done), channel_id=1, source_target_pairs={{0,1},{1,0},{2,3},{3,2},{4,5},{5,4},{6,7},{7,6},{8,9},{9,8},{10,11... | collective-permute-start | bytes 786440 | tf_op jit(solution)/shard_map/ppermute | solution.py:264
  97.9 11.4 %collective-permute-start.14 = (bf16[512,256]{1,0:T(8,128)(2,1)S(1)}, bf16[512,256]{1,0:T(8,128)(2,1)S(1)}, u32[]{:S(2)}, u32[]{:S(2)}) collective-permute-start(bf16[512,256]{1,0:T(8,128)(2,1)S(1)} %collective-permute-done.13.refs_6_), channel_id=1, source_target_pairs={{0,1},{1,0},{2,3},{3,2},{4,5},{5,4},{6,7},{7,6},{8,9},{9,8},{10,11... | collective-permute-start | bytes 786440 | tf_op jit(solution)/shard_map/ppermute | solution.py:264
  106.5 7.6 %collective-permute-start.18 = (bf16[1024,128]{1,0:T(8,128)(2,1)S(1)}, bf16[1024,128]{1,0:T(8,128)(2,1)S(1)}, u32[]{:S(2)}, u32[]{:S(2)}) collective-permute-start(bf16[1024,128]{1,0:T(8,128)(2,1)S(1)} %apply.1.refs_0_), channel_id=1, source_target_pairs={{0,1},{1,0},{2,3},{3,2},{4,5},{5,4},{6,7},{7,6},{8,9},{9,8},{10,11... | collective-permute-start | bytes 786440 | tf_op jit(solution)/shard_map/ppermute | solution.py:264
  106.5 7.6 %collective-permute-start.20 = (bf16[1024,128]{1,0:T(8,128)(2,1)S(1)}, bf16[1024,128]{1,0:T(8,128)(2,1)S(1)}, u32[]{:S(2)}, u32[]{:S(2)}) collective-permute-start(bf16[1024,128]{1,0:T(8,128)(2,1)S(1)} %collective-permute-done.19.refs_2_), channel_id=1, source_target_pairs={{0,1},{1,0},{2,3},{3,2},{4,5},{5,4},{6,7},{7,6},{8,9},{9,8},{10,11... | collective-permute-start | bytes 786440 | tf_op jit(solution)/shard_map/ppermute | solution.py:264
  107.7 1.7 %collective-permute-start.11 = (bf16[512,128]{1,0:T(8,128)(2,1)}, bf16[512,128]{1,0:T(8,128)(2,1)}, u32[]{:S(2)}, u32[]{:S(2)}) collective-permute-start(bf16[512,128]{1,0:T(8,128)(2,1)} %collective-permute-done.10.refs_2_), channel_id=1, source_target_pairs={{0,1},{1,0},{2,3},{3,2},{4,5},{5,4},{6,7},{7,6},{8,9},{9,8},{10,11... | collective-permute-start | bytes 393224 | tf_op jit(solution)/shard_map/ppermute | solution.py:264
  (26 other events, 20.7 us)

commit v2 on v1

--- a/solution.py
+++ b/solution.py
@@ -17,6 +17,7 @@
 I32 = jnp.int32
 VMEM = pl.BlockSpec(memory_space=pltpu.VMEM)
 SMEM = pl.BlockSpec(memory_space=pltpu.SMEM)
+ANY = pl.BlockSpec(memory_space=pl.ANY)
 
 
 def iota(shape, dim):
@@ -116,7 +117,8 @@
     return jnp.where((inner * plan.owners + owner) == here, 1.0, 0.0).astype(BF16)
 
 
-def serve_kernel(plan, asked_ref, memory_ref, out_ref):
+def serve_kernel(plan, asked_ref, memory_ref, *refs):
+    out_ref = refs[-1]
     stored, width = memory_ref.shape
     piece = width // 4
     asked = asked_ref[...].astype(F32)
@@ -164,10 +166,21 @@
     return table
 
 
+def fetch(groups, sems):
+    copies = []
+    for g, (parts, buffer) in enumerate(groups):
+        row = [pltpu.make_async_copy(part, buffer.at[k], sems.at[g, k]) for k, part in enumerate(parts)]
+        for copy in row:
+            copy.start()
+        copies.append(row)
+    return copies
+
+
 def gru_kernel(plan, ret_ref, enc_ref, col_ref, row_ref, *refs):
     reps = plan.reps
-    w_in, w_time, w_hid = refs[:reps], refs[reps : 2 * reps], refs[2 * reps : 3 * reps]
-    out_ref, hnew_ref, hdst_ref, gin, ghid, delta = refs[3 * reps :]
+    parts_in, parts_time, parts_hid = refs[:reps], refs[reps : 2 * reps], refs[2 * reps : 3 * reps]
+    out_ref, hnew_ref, hdst_ref, gin, ghid, delta, w_in, w_time, w_hid, sems = refs[3 * reps :]
+    copies = fetch([(parts_in, w_in), (parts_time, w_time), (parts_hid, w_hid)], sems)
     me = lax.axis_index("rep")
     events, width = hnew_ref.shape
     piece = width // reps
@@ -179,11 +192,13 @@
     target = dot(jnp.where(cols[:, 1:2] == spots, 1.0, 0.0).astype(BF16), table).astype(BF16)
     hdst_ref[...] = target
     enc = enc_ref[...]
-    part = w_in[0].shape[1]
+    part = w_in.shape[2]
     for k in range(reps):
+        for row in copies:
+            row[k].wait()
         at = pl.ds(pl.multiple_of((me ^ k) * part, LANES), part)
-        gin[:, at] = dot(target, w_in[k][...]) + dot(enc, w_time[k][...])
-        ghid[:, at] = dot(source, w_hid[k][...])
+        gin[:, at] = dot(target, w_in[k]) + dot(enc, w_time[k])
+        ghid[:, at] = dot(source, w_hid[k])
     step = 64
     for i in range(0, events, step):
         at = slice(i, i + step)
@@ -209,18 +224,21 @@
 
 def attend_kernel(plan, listed_ref, hnew_ref, hdst_ref, *refs):
     reps = plan.reps
-    w_query, w_keyval = refs[:reps], refs[reps : 2 * reps]
-    out_ref, query, keyval = refs[2 * reps :]
+    parts_query, parts_keyval = refs[:reps], refs[reps : 2 * reps]
+    out_ref, query, keyval, w_query, w_keyval, sems = refs[2 * reps :]
+    copies = fetch([(parts_query, w_query), (parts_keyval, w_keyval)], sems)
     me = lax.axis_index("rep")
     events, width = hnew_ref.shape
     head = width // H
     hround = hnew_ref[...].astype(BF16)
     target = hdst_ref[...]
     for k in range(reps):
-        part = w_query[k].shape[1]
-        query[:, pl.ds(pl.multiple_of((me ^ k) * part, LANES), part)] = dot(hround, w_query[k][...]).astype(BF16)
-        part = w_keyval[k].shape[1]
-        keyval[:, pl.ds(pl.multiple_of((me ^ k) * part, LANES), part)] = dot(target, w_keyval[k][...]).astype(BF16)
+        for row in copies:
+            row[k].wait()
+        part = w_query.shape[2]
+        query[:, pl.ds(pl.multiple_of((me ^ k) * part, LANES), part)] = dot(hround, w_query[k]).astype(BF16)
+        part = w_keyval.shape[2]
+        keyval[:, pl.ds(pl.multiple_of((me ^ k) * part, LANES), part)] = dot(target, w_keyval[k]).astype(BF16)
     for i in range(events // BLK):
         spans = [pl.ds(pl.multiple_of(listed_ref[i, j] * BLK, BLK), BLK) for j in range(NB)]
         at = slice(i * BLK, (i + 1) * BLK)
@@ -237,7 +255,7 @@
             out_ref[at, lane] = (hnew_ref[at, lane] + dot(prob, values)).astype(BF16)
 
 
-def apply_kernel(plan, ids_ref, landed_ref, memory_ref, out_ref):
+def apply_kernel(plan, ids_ref, landed_ref, memory_ref, after_ref, out_ref):
     stored = memory_ref.shape[0]
     piece = out_ref.shape[1]
     count = landed_ref.shape[0]
@@ -335,18 +353,18 @@
     served = call(
         run(serve_kernel, plan),
         [sds((owners, chunk, width // 4), BF16)],
-        [VMEM] * 2,
+        [VMEM] * 2 + [ANY] * (2 * reps),
         2 * plan.rows * stored * width,
         2 * stored * width + 2 * plan.rows * width,
         "serve",
         limit=24,
-    )(asked, memory)[0]
+    )(asked, memory, *full_hidden, *full_time)[0]
     returned = lax.all_to_all(served, "shard", split_axis=0, concat_axis=0, tiled=True)
 
     outgoing, hnew, hdst = call(
         run(gru_kernel, plan),
         [sds((owners * reps, plan.pad, piece), BF16), sds((events, width), F32), sds((events, width), BF16)],
-        [VMEM] * (4 + 3 * reps),
+        [VMEM] * 4 + [ANY] * (3 * reps),
         2 * events * width * 3 * width * 2,
         8 << 20,
         "gru",
@@ -354,20 +372,24 @@
             pltpu.VMEM((events, 3 * width), F32),
             pltpu.VMEM((events, 3 * width), F32),
             pltpu.VMEM((events, width), F32),
-        ],
-        limit=40,
+        ]
+        + [pltpu.VMEM((reps,) + x.shape, BF16) for x in (w_input, w_time, w_hidden)]
+        + [pltpu.SemaphoreType.DMA((3, reps))],
+        limit=48,
     )(returned, encode, cols, rows, *full_input, *full_time, *full_hidden)
     landed = lax.all_to_all(outgoing, ("shard", "rep"), split_axis=0, concat_axis=0, tiled=True)
 
     embed = call(
         run(attend_kernel, plan),
         [sds((events, width), BF16)],
-        [SMEM] + [VMEM] * (2 + 2 * reps),
+        [SMEM] + [VMEM] * 2 + [ANY] * (2 * reps),
         2 * events * width * 3 * width,
         4 << 20,
         "attend",
-        scratch=[pltpu.VMEM((events, width), BF16), pltpu.VMEM((events, 2 * width), BF16)],
-        limit=24,
+        scratch=[pltpu.VMEM((events, width), BF16), pltpu.VMEM((events, 2 * width), BF16)]
+        + [pltpu.VMEM((reps,) + x.shape, BF16) for x in (w_query, w_keyval)]
+        + [pltpu.SemaphoreType.DMA((2, reps))],
+        limit=48,
     )(neighbour_blocks, hnew, hdst, *full_query, *full_keyval)[0]
 
     me = lax.axis_index("rep")
@@ -377,12 +399,12 @@
     quarter = call(
         run(apply_kernel, plan),
         [sds((stored, piece), BF16)],
-        [VMEM] * 3,
+        [VMEM] * 3 + [ANY],
         2 * stored * owners * reps * plan.pad * piece * 2,
         4 << 20,
         "apply",
         limit=32,
-    )(ids, landed.reshape(owners * reps * plan.pad, piece), memory)[0]
+    )(ids, landed.reshape(owners * reps * plan.pad, piece), memory, embed)[0]
     new_memory = call(
         run(join_kernel, plan), [sds((stored, width), BF16)], [VMEM] * reps, 1 << 20, 2 << 20, "join", limit=8
     )(*spread([quarter], reps)[0])[0]

time: 116 us -> 112 us (0.966)
  waiting for transfers between devices: 44.7 us -> 38 us
  starting transfers between devices: 19 us -> 22 us
  Pallas kernels: 15.9 us -> 18.7 us
  local copies, waits for them, and re-layouts: 21.3 us -> 18.7 us
  blocking collectives: 13.5 us -> 12.3 us
    all_to_all x1, waiting for transfers between devices: 9.96 us -> 3.01 us  [shards(): lax.all_to_all(outgoing, ('shard', 'rep'), split_axis=0, concat_axis=0, t...]
    unnamed x71 -> x65, local copies, waits for them, and re-layouts: 20.6 us -> 18.1 us
    ppermute x21, starting transfers between devices: 10.7 us -> 12.4 us  [swap(): return lax.ppermute(x, 'rep', [(i, i ^ bit) for i in range(reps)])]
    pallas_call x1, Pallas kernels: 3.86 us -> 5.35 us  [shards(): call(run(attend_kernel, plan), [sds((events, width), BF16)], [SMEM] + [VM...]
    pallas_call x1, Pallas kernels: 6.04 us -> 7.38 us  [shards(): call(run(gru_kernel, plan), [sds((owners * reps, plan.pad, piece), BF16),...]
    all_to_all x1, starting transfers between devices: 4.67 us -> 5.89 us  [shards(): lax.all_to_all(outgoing, ('shard', 'rep'), split_axis=0, concat_axis=0, t...]
    all_to_all x1, blocking collectives: 13.5 us -> 12.3 us  [shards(): lax.all_to_all(request, 'shard', split_axis=0, concat_axis=0, tiled=True)]
  transfers between devices with their start and end apart: 23 -> 23, of which waited for: 9 -> 10; matrix products, arithmetic and copies ran while one was open for 1% -> 1% of each run, Pallas kernels for 11% -> 13%
where the time goes in v2:
time: 112 us; the launch traced here: 111 us
  waiting for transfers between devices  38 us (34%)
  starting transfers between devices  22 us (20%)
  local copies, waits for them, and re-layouts  18.7 us (17%)
  Pallas kernels  18.7 us (17%)
  blocking collectives  12.3 us (11%)
    ppermute x21, waiting for transfers between devices, swap(): return lax.ppermute(x, 'rep', [(i, i ^ bit) for i in range(reps)])  35 us
    unnamed x65, local copies, waits for them, and re-layouts  18.1 us
    ppermute x21, starting transfers between devices, swap(): return lax.ppermute(x, 'rep', [(i, i ^ bit) for i in range(reps)])  12.4 us
    all_to_all x1, blocking collectives, shards(): lax.all_to_all(request, 'shard', split_axis=0, concat_axis=0, tiled=True)  12.3 us
    pallas_call x1, Pallas kernels, shards(): call(run(gru_kernel, plan), [sds((owners * reps, plan.pad, piece), BF16),...  7.38 us
    all_to_all x1, starting transfers between devices, shards(): lax.all_to_all(outgoing, ('shard', 'rep'), split_axis=0, concat_axis=0, t...  5.89 us
    pallas_call x1, Pallas kernels, shards(): call(run(attend_kernel, plan), [sds((events, width), BF16)], [SMEM] + [VM...  5.35 us
    all_to_all x1, starting transfers between devices, shards(): lax.all_to_all(served, 'shard', split_axis=0, concat_axis=0, tiled=True)  3.68 us
  transfers between devices with their start and end apart: 23, of which 10 were waited for; matrix products, arithmetic and copies ran while one was open for 1% of the time, Pallas kernels for 13%

profile of v2, /device:TPU:0, one launch (start us, length us, event | category | flops | bytes accessed | tf_op | source)
XLA Modules:
  0.0 111.3 jit_solution(6534448041733736161)
XLA Ops:
  0.6 3.0 %collective-permute-start.1 = (bf16[512,384]{1,0:T(8,128)(2,1)}, bf16[512,384]{1,0:T(8,128)(2,1)S(1)}, u32[]{:S(2)}, u32[]{:S(2)}) collective-permute-start(bf16[512,384]{1,0:T(8,128)(2,1)} %refs_8_.1), channel_id=1, source_target_pairs={{0,2},{1,3},{2,0},{3,1},{4,6},{5,7},{6,4},{7,5},{8,10},{9,11},{10,... | collective-permute-start | bytes 1179656 | tf_op jit(solution)/shard_map/ppermute | solution.py:282
  3.6 9.3 %collective-permute-done.1.refs_2_.refs_10_ = bf16[512,384]{1,0:T(8,128)(2,1)S(1)} collective-permute-done((bf16[512,384]{1,0:T(8,128)(2,1)}, bf16[512,384]{1,0:T(8,128)(2,1)S(1)}, u32[]{:S(2)}, u32[]{:S(2)}) %collective-permute-start.1) | collective-permute-done | bytes 393248 | tf_op jit(solution)/shard_map/ppermute | solution.py:282
  13.0 1.7 %collective-permute-start.4 = (bf16[128,384]{1,0:T(8,128)(2,1)}, bf16[128,384]{1,0:T(8,128)(2,1)S(1)}, u32[]{:S(2)}, u32[]{:S(2)}) collective-permute-start(bf16[128,384]{1,0:T(8,128)(2,1)} %refs_4_.4), channel_id=1, source_target_pairs={{0,2},{1,3},{2,0},{3,1},{4,6},{5,7},{6,4},{7,5},{8,10},{9,11},{10,... | collective-permute-start | bytes 294920 | tf_op jit(solution)/shard_map/ppermute | solution.py:282
  14.9 3.5 %collective-permute-done.4.refs_6_ = bf16[128,384]{1,0:T(8,128)(2,1)S(1)} collective-permute-done((bf16[128,384]{1,0:T(8,128)(2,1)}, bf16[128,384]{1,0:T(8,128)(2,1)S(1)}, u32[]{:S(2)}, u32[]{:S(2)}) %collective-permute-start.4) | collective-permute-done | bytes 98336 | tf_op jit(solution)/shard_map/ppermute | solution.py:282
  19.4 12.3 %all_to_all.21 = s32[8,1,128]{2,1,0:T(1,128)S(1)} all-to-all(s32[8,1,128]{2,1,0:T(1,128)S(1)} %bitcast.26), channel_id=1, replica_groups=mesh['shard'=8,'rep'=4] {'shard'}, dimensions={0} | all-to-all | bytes 8192 | tf_op jit(solution)/shard_map/all_to_all | solution.py:332
  31.8 1.2 %copy-done = bf16[1024,512]{1,0:T(8,128)(2,1)S(1)} copy-done((bf16[1024,512]{1,0:T(8,128)(2,1)S(1)}, bf16[1024,512]{1,0:T(8,128)(2,1)}, u32[]{:S(2)}) %copy-start) | copy-done | bytes 1048600
  33.0 1.0 copy-done.2
  34.0 0.9 copy-done.6
  34.9 1.8 %serve.1 = bf16[8,264,128]{2,1,0:T(8,128)(2,1)} custom-call(s32[8,128]{1,0:T(8,128)S(1)} %bitcast.22, bf16[1024,512]{1,0:T(8,128)(2,1)S(1)} %copy-done, bf16[512,384]{1,0:T(8,128)(2,1)S(1)} %copy-done.2, bf16[512,384]{1,0:T(8,128)(2,1)S(1)} %collective-permute-done.refs_1_.refs_9_, bf16[512,384]{1,0:T(8,128)(2,1)S(1)} %collective-permute-done.1.refs_2_.refs_10_, ...), custom_call_target="tpu_custom_call" | custom-call | flops 553648128 | bytes 1589248 | tf_op jit(solution)/shard_map/serve/pallas_call | solution.py:353
  38.7 3.7 %all-to-all-start.1 = ((bf16[8,264,128]{2,1,0:T(8,128)(2,1)}), bf16[8,264,128]{2,1,0:T(8,128)(2,1)S(1)}, u32[]{:S(2)}, u32[]{:S(2)}) async-start(bf16[8,264,128]{2,1,0:T(8,128)(2,1)} %serve.1), calls=%async_computation.1 | async-start | bytes 1081344 | tf_op jit(solution)/shard_map/all_to_all | solution.py:362
  42.4 1.6 %collective-permute-start.7 = (bf16[512,384]{1,0:T(8,128)(2,1)S(1)}, bf16[512,384]{1,0:T(8,128)(2,1)S(1)}, u32[]{:S(2)}, u32[]{:S(2)}) collective-permute-start(bf16[512,384]{1,0:T(8,128)(2,1)S(1)} %copy-done.16), channel_id=1, source_target_pairs={{0,2},{1,3},{2,0},{3,1},{4,6},{5,7},{6,4},{7,5},{8,10},{9,11},{10,... | collective-permute-start | bytes 1179656 | tf_op jit(solution)/shard_map/ppermute | solution.py:282
  44.0 8.6 %collective-permute-done.7.refs_2_ = bf16[512,384]{1,0:T(8,128)(2,1)S(1)} collective-permute-done((bf16[512,384]{1,0:T(8,128)(2,1)S(1)}, bf16[512,384]{1,0:T(8,128)(2,1)S(1)}, u32[]{:S(2)}, u32[]{:S(2)}) %collective-permute-start.7) | collective-permute-done | bytes 393248 | tf_op jit(solution)/shard_map/ppermute | solution.py:282
  53.3 1.5 %collective-permute-start.13 = (bf16[512,256]{1,0:T(8,128)(2,1)}, bf16[512,256]{1,0:T(8,128)(2,1)}, u32[]{:S(2)}, u32[]{:S(2)}) collective-permute-start(bf16[512,256]{1,0:T(8,128)(2,1)} %refs_4_.5), channel_id=1, source_target_pairs={{0,2},{1,3},{2,0},{3,1},{4,6},{5,7},{6,4},{7,5},{8,10},{9,11},{10,... | collective-permute-start | bytes 786440 | tf_op jit(solution)/shard_map/ppermute | solution.py:282
  58.4 1.2 %index.1 = (bf16[384,128]{1,0:T(8,128)(2,1)S(1)}, f32[384,8]{1,0:T(8,128)S(1)}, s32[8,384]{1,0:T(8,128)S(1)}) custom-call(s32[1,256]{1,0:T(1,128)S(1)} %bitcast.29, s32[1,256]{1,0:T(1,128)S(1)} %bitcast.30, s32[1,384]{1,0:T(1,128)S(1)} %reshape.55.src_ref, s32[1,384]{1,0:T(1,128)S(1)} %reshape.56.dst_ref, s32[1,384]{1,0:T(1,128)S(1)} %reshape.57.stamp_ref, ...), custom_call_target="tpu_custom_call" | custom-call | flops 4194304 | bytes 262144 | tf_op jit(solution)/shard_map/index/pallas_call | solution.py:333
  62.5 0.9 copy-done.11
  63.4 0.9 copy-done.13
  64.3 1.0 copy-done.17
  65.3 1.0 copy-done.19
  66.3 0.9 copy-done.24
  68.1 7.4 %gru.1 = (bf16[32,72,128]{2,1,0:T(8,128)(2,1)}, f32[384,512]{1,0:T(8,128)S(1)}, bf16[384,512]{1,0:T(8,128)(2,1)S(1)}) custom-call(bf16[8,264,128]{2,1,0:T(8,128)(2,1)S(1)} %all-to-all-done.1.ret_ref, bf16[384,128]{1,0:T(8,128)(2,1)S(1)} %copy-done.26, f32[384,8]{1,0:T(8,128)S(1)} %copy-done.24, s32[8,384]{1,0:T(8,128)S(1)} %get-tuple-element.10.row_ref, ...), custom_call_target="tpu_custom_call" | custom-call | flops 1207959552 | bytes 8388608 | tf_op jit(solution)/shard_map/gru/pallas_call | solution.py:364
  75.5 5.9 %all-to-all-start.2 = ((bf16[32,72,128]{2,1,0:T(8,128)(2,1)}), bf16[32,72,128]{2,1,0:T(8,128)(2,1)S(1)}, u32[]{:S(2)}, u32[]{:S(2)}) async-start(bf16[32,72,128]{2,1,0:T(8,128)(2,1)} %get-tuple-element.13), calls=%async_computation.2 | async-start | bytes 1179648 | tf_op jit(solution)/shard_map/all_to_all | solution.py:380
  81.4 1.7 %collective-permute-start.16 = (s32[8,128]{1,0:T(8,128)S(1)}, s32[8,128]{1,0:T(8,128)S(1)}, u32[]{:S(2)}, u32[]{:S(2)}) collective-permute-start(s32[8,128]{1,0:T(8,128)S(1)} %bitcast.23), channel_id=1, source_target_pairs={{0,2},{1,3},{2,0},{3,1},{4,6},{5,7},{6,4},{7,5},{8,10},{9,11},{10,... | collective-permute-start | bytes 12296 | tf_op jit(solution)/shard_map/ppermute | solution.py:282
  83.1 3.1 %collective-permute-done.16 = s32[8,128]{1,0:T(8,128)S(1)} collective-permute-done((s32[8,128]{1,0:T(8,128)S(1)}, s32[8,128]{1,0:T(8,128)S(1)}, u32[]{:S(2)}, u32[]{:S(2)}) %collective-permute-start.16) | collective-permute-done | bytes 4128 | tf_op jit(solution)/shard_map/ppermute | solution.py:282
  86.1 1.2 %collective-permute-done.15 = s32[8,128]{1,0:T(8,128)S(1)} collective-permute-done((s32[8,128]{1,0:T(8,128)S(1)}, s32[8,128]{1,0:T(8,128)S(1)}, u32[]{:S(2)}, u32[]{:S(2)}) %collective-permute-start.15) | collective-permute-done | bytes 4128 | tf_op jit(solution)/shard_map/ppermute | solution.py:282
  89.6 5.3 %attend.1.after_ref = bf16[384,512]{1,0:T(8,128)(2,1)} custom-call(s32[3,2]{1,0:T(4,128)S(1)} %copy.20.listed_ref, f32[384,512]{1,0:T(8,128)S(1)} %get-tuple-element.11.hnew_ref, bf16[384,512]{1,0:T(8,128)(2,1)S(1)} %get-tuple-element.12.hdst_ref, bf16[512,128]{1,0:T(8,128)(2,1)S(1)} %copy-done.5, bf16[512,128]{1,0:T(8,128)(2,1)} %collective-permute-done.9.refs_1_, ...), custom_call_target="tpu_custom_call" | custom-call | flops 603979776 | bytes 4194304 | tf_op jit(solution)/shard_map/attend/pallas_call | solution.py:382
  94.9 3.0 %all-to-all-done.2 = bf16[32,72,128]{2,1,0:T(8,128)(2,1)S(1)} async-done(((bf16[32,72,128]{2,1,0:T(8,128)(2,1)}), bf16[32,72,128]{2,1,0:T(8,128)(2,1)S(1)}, u32[]{:S(2)}, u32[]{:S(2)}) %all-to-all-start.2) | async-done | bytes 589856 | tf_op jit(solution)/shard_map/all_to_all | solution.py:380
  97.9 1.0 copy-done.4
  98.9 1.4 %apply.1.refs_0_ = bf16[1024,128]{1,0:T(8,128)(2,1)S(1)} custom-call(s32[1,2304]{1,0:T(1,128)S(1)} %reshape.60.ids_ref, bf16[2304,128]{1,0:T(8,128)(2,1)S(1)} %bitcast.21, bf16[1024,512]{1,0:T(8,128)(2,1)S(1)} %copy-done.1, bf16[384,512]{1,0:T(8,128)(2,1)S(1)} %copy-done.4), custom_call_target="tpu_custom_call" | custom-call | flops 1207959552 | bytes 4194304 | tf_op jit(solution)/shard_map/apply/pallas_call | solution.py:399
  100.3 1.2 %collective-permute-start.19 = (bf16[1024,128]{1,0:T(8,128)(2,1)S(1)}, bf16[1024,128]{1,0:T(8,128)(2,1)S(1)}, u32[]{:S(2)}, u32[]{:S(2)}) collective-permute-start(bf16[1024,128]{1,0:T(8,128)(2,1)S(1)} %apply.1.refs_0_), channel_id=1, source_target_pairs={{0,2},{1,3},{2,0},{3,1},{4,6},{5,7},{6,4},{7,5},{8,10},{9,11},{10,... | collective-permute-start | bytes 786440 | tf_op jit(solution)/shard_map/ppermute | solution.py:282
  101.6 7.0 %collective-permute-done.19.refs_2_ = bf16[1024,128]{1,0:T(8,128)(2,1)S(1)} collective-permute-done((bf16[1024,128]{1,0:T(8,128)(2,1)S(1)}, bf16[1024,128]{1,0:T(8,128)(2,1)S(1)}, u32[]{:S(2)}, u32[]{:S(2)}) %collective-permute-start.19) | collective-permute-done | bytes 262176 | tf_op jit(solution)/shard_map/ppermute | solution.py:282
  108.6 1.5 %collective-permute-done.20.refs_3_ = bf16[1024,128]{1,0:T(8,128)(2,1)S(1)} collective-permute-done((bf16[1024,128]{1,0:T(8,128)(2,1)S(1)}, bf16[1024,128]{1,0:T(8,128)(2,1)S(1)}, u32[]{:S(2)}, u32[]{:S(2)}) %collective-permute-start.20) | collective-permute-done | bytes 262176 | tf_op jit(solution)/shard_map/ppermute | solution.py:282
  110.1 1.2 %join.1 = bf16[1024,512]{1,0:T(8,128)(2,1)} custom-call(bf16[1024,128]{1,0:T(8,128)(2,1)S(1)} %apply.1.refs_0_, bf16[1024,128]{1,0:T(8,128)(2,1)S(1)} %collective-permute-done.18.refs_1_, bf16[1024,128]{1,0:T(8,128)(2,1)S(1)} %collective-permute-done.19.refs_2_, bf16[1024,128]{1,0:T(8,128)(2,1)S(1)} %collective-permute-done.20.refs_3_), custom_call_target="tpu_custom_call" | custom-call | flops 1048576 | bytes 2097152 | tf_op jit(solution)/shard_map/join/pallas_call | solution.py:408
  (100 shorter events, 13.6 us)
Async XLA Ops:
  0.6 12.3 %collective-permute-start.1 = (bf16[512,384]{1,0:T(8,128)(2,1)}, bf16[512,384]{1,0:T(8,128)(2,1)S(1)}, u32[]{:S(2)}, u32[]{:S(2)}) collective-permute-start(bf16[512,384]{1,0:T(8,128)(2,1)} %refs_8_.1), channel_id=1, source_target_pairs={{0,2},{1,3},{2,0},{3,1},{4,6},{5,7},{6,4},{7,5},{8,10},{9,11},{10,... | collective-permute-start | bytes 1179656 | tf_op jit(solution)/shard_map/ppermute | solution.py:282
  3.6 28.2 %collective-permute-start = (bf16[512,384]{1,0:T(8,128)(2,1)}, bf16[512,384]{1,0:T(8,128)(2,1)S(1)}, u32[]{:S(2)}, u32[]{:S(2)}) collective-permute-start(bf16[512,384]{1,0:T(8,128)(2,1)} %refs_8_.1), channel_id=1, source_target_pairs={{0,1},{1,0},{2,3},{3,2},{4,5},{5,4},{6,7},{7,6},{8,9},{9,8},{10,11... | collective-permute-start | bytes 1179656 | tf_op jit(solution)/shard_map/ppermute | solution.py:282
  13.0 18.8 %collective-permute-start.2 = (bf16[512,384]{1,0:T(8,128)(2,1)S(1)}, bf16[512,384]{1,0:T(8,128)(2,1)S(1)}, u32[]{:S(2)}, u32[]{:S(2)}) collective-permute-start(bf16[512,384]{1,0:T(8,128)(2,1)S(1)} %collective-permute-done.1.refs_2_.refs_10_), channel_id=1, source_target_pairs={{0,1},{1,0},{2,3},{3,2},{4,5},{5,4},{6,7},{7,6},{8,9},{9,8},{10,11... | collective-permute-start | bytes 1179656 | tf_op jit(solution)/shard_map/ppermute | solution.py:282
  13.0 5.4 %collective-permute-start.4 = (bf16[128,384]{1,0:T(8,128)(2,1)}, bf16[128,384]{1,0:T(8,128)(2,1)S(1)}, u32[]{:S(2)}, u32[]{:S(2)}) collective-permute-start(bf16[128,384]{1,0:T(8,128)(2,1)} %refs_4_.4), channel_id=1, source_target_pairs={{0,2},{1,3},{2,0},{3,1},{4,6},{5,7},{6,4},{7,5},{8,10},{9,11},{10,... | collective-permute-start | bytes 294920 | tf_op jit(solution)/shard_map/ppermute | solution.py:282
  14.7 17.1 %collective-permute-start.3 = (bf16[128,384]{1,0:T(8,128)(2,1)}, bf16[128,384]{1,0:T(8,128)(2,1)S(1)}, u32[]{:S(2)}, u32[]{:S(2)}) collective-permute-start(bf16[128,384]{1,0:T(8,128)(2,1)} %refs_4_.4), channel_id=1, source_target_pairs={{0,1},{1,0},{2,3},{3,2},{4,5},{5,4},{6,7},{7,6},{8,9},{9,8},{10,11... | collective-permute-start | bytes 294920 | tf_op jit(solution)/shard_map/ppermute | solution.py:282
  18.4 13.4 %collective-permute-start.5 = (bf16[128,384]{1,0:T(8,128)(2,1)S(1)}, bf16[128,384]{1,0:T(8,128)(2,1)S(1)}, u32[]{:S(2)}, u32[]{:S(2)}) collective-permute-start(bf16[128,384]{1,0:T(8,128)(2,1)S(1)} %collective-permute-done.4.refs_6_), channel_id=1, source_target_pairs={{0,1},{1,0},{2,3},{3,2},{4,5},{5,4},{6,7},{7,6},{8,9},{9,8},{10,11... | collective-permute-start | bytes 294920 | tf_op jit(solution)/shard_map/ppermute | solution.py:282
  31.8 1.2 %copy-start = (bf16[1024,512]{1,0:T(8,128)(2,1)S(1)}, bf16[1024,512]{1,0:T(8,128)(2,1)}, u32[]{:S(2)}) copy-start(bf16[1024,512]{1,0:T(8,128)(2,1)} %memory_ref.3) | copy-start | bytes 3145732
  38.7 3.7 %copy-start.16 = (bf16[512,384]{1,0:T(8,128)(2,1)S(1)}, bf16[512,384]{1,0:T(8,128)(2,1)}, u32[]{:S(2)}) copy-start(bf16[512,384]{1,0:T(8,128)(2,1)} %refs_0_.4) | copy-start | bytes 1179652
  38.7 16.4 %copy-start.5 = (bf16[512,128]{1,0:T(8,128)(2,1)S(1)}, bf16[512,128]{1,0:T(8,128)(2,1)}, u32[]{:S(2)}) copy-start(bf16[512,128]{1,0:T(8,128)(2,1)} %refs_0_.5) | copy-start | bytes 393220
  38.7 16.9 %copy-start.27 = (s32[384]{0:T(512)S(1)}, s32[384]{0:T(512)}, u32[]{:S(2)}) copy-start(s32[384]{0:T(512)} %param.19) | copy-start | bytes 4612
  38.7 19.0 %copy-start.22 = (f32[128]{0:T(128)S(1)}, f32[128]{0:T(128)}, u32[]{:S(2)}) copy-start(f32[128]{0:T(128)} %param.24) | copy-start | bytes 1540
  38.7 22.9 %copy-start.3 = (bf16[512,384]{1,0:T(8,128)(2,1)S(1)}, bf16[512,384]{1,0:T(8,128)(2,1)}, u32[]{:S(2)}) copy-start(bf16[512,384]{1,0:T(8,128)(2,1)} %refs_8_.1) | copy-start | bytes 1179652
  38.7 22.9 %copy-start.7 = (bf16[128,384]{1,0:T(8,128)(2,1)S(1)}, bf16[128,384]{1,0:T(8,128)(2,1)}, u32[]{:S(2)}) copy-start(bf16[128,384]{1,0:T(8,128)(2,1)} %refs_4_.4) | copy-start | bytes 294916
  38.7 22.9 %all-to-all-start.1 = ((bf16[8,264,128]{2,1,0:T(8,128)(2,1)}), bf16[8,264,128]{2,1,0:T(8,128)(2,1)S(1)}, u32[]{:S(2)}, u32[]{:S(2)}) async-start(bf16[8,264,128]{2,1,0:T(8,128)(2,1)} %serve.1), calls=%async_computation.1 | async-start | bytes 1081344 | tf_op jit(solution)/shard_map/all_to_all | solution.py:362
  42.4 10.2 %collective-permute-start.7 = (bf16[512,384]{1,0:T(8,128)(2,1)S(1)}, bf16[512,384]{1,0:T(8,128)(2,1)S(1)}, u32[]{:S(2)}, u32[]{:S(2)}) collective-permute-start(bf16[512,384]{1,0:T(8,128)(2,1)S(1)} %copy-done.16), channel_id=1, source_target_pairs={{0,2},{1,3},{2,0},{3,1},{4,6},{5,7},{6,4},{7,5},{8,10},{9,11},{10,... | collective-permute-start | bytes 1179656 | tf_op jit(solution)/shard_map/ppermute | solution.py:282
  44.0 17.6 %collective-permute-start.6 = (bf16[512,384]{1,0:T(8,128)(2,1)S(1)}, bf16[512,384]{1,0:T(8,128)(2,1)}, u32[]{:S(2)}, u32[]{:S(2)}) collective-permute-start(bf16[512,384]{1,0:T(8,128)(2,1)S(1)} %copy-done.16), channel_id=1, source_target_pairs={{0,1},{1,0},{2,3},{3,2},{4,5},{5,4},{6,7},{7,6},{8,9},{9,8},{10,11... | collective-permute-start | bytes 1179656 | tf_op jit(solution)/shard_map/ppermute | solution.py:282
  52.6 9.0 %collective-permute-start.8 = (bf16[512,384]{1,0:T(8,128)(2,1)S(1)}, bf16[512,384]{1,0:T(8,128)(2,1)}, u32[]{:S(2)}, u32[]{:S(2)}) collective-permute-start(bf16[512,384]{1,0:T(8,128)(2,1)S(1)} %collective-permute-done.7.refs_2_), channel_id=1, source_target_pairs={{0,1},{1,0},{2,3},{3,2},{4,5},{5,4},{6,7},{7,6},{8,9},{9,8},{10,11... | collective-permute-start | bytes 1179656 | tf_op jit(solution)/shard_map/ppermute | solution.py:282
  53.3 34.5 %collective-permute-start.13 = (bf16[512,256]{1,0:T(8,128)(2,1)}, bf16[512,256]{1,0:T(8,128)(2,1)}, u32[]{:S(2)}, u32[]{:S(2)}) collective-permute-start(bf16[512,256]{1,0:T(8,128)(2,1)} %refs_4_.5), channel_id=1, source_target_pairs={{0,2},{1,3},{2,0},{3,1},{4,6},{5,7},{6,4},{7,5},{8,10},{9,11},{10,... | collective-permute-start | bytes 786440 | tf_op jit(solution)/shard_map/ppermute | solution.py:282
  54.8 34.3 %collective-permute-start.12 = (bf16[512,256]{1,0:T(8,128)(2,1)}, bf16[512,256]{1,0:T(8,128)(2,1)}, u32[]{:S(2)}, u32[]{:S(2)}) collective-permute-start(bf16[512,256]{1,0:T(8,128)(2,1)} %refs_4_.5), channel_id=1, source_target_pairs={{0,1},{1,0},{2,3},{3,2},{4,5},{5,4},{6,7},{7,6},{8,9},{9,8},{10,11... | collective-permute-start | bytes 786440 | tf_op jit(solution)/shard_map/ppermute | solution.py:282
  55.1 32.4 %collective-permute-start.10 = (bf16[512,128]{1,0:T(8,128)(2,1)S(1)}, bf16[512,128]{1,0:T(8,128)(2,1)}, u32[]{:S(2)}, u32[]{:S(2)}) collective-permute-start(bf16[512,128]{1,0:T(8,128)(2,1)S(1)} %copy-done.5), channel_id=1, source_target_pairs={{0,2},{1,3},{2,0},{3,1},{4,6},{5,7},{6,4},{7,5},{8,10},{9,11},{10,... | collective-permute-start | bytes 393224 | tf_op jit(solution)/shard_map/ppermute | solution.py:282
  61.6 27.6 %collective-permute-start.9 = (bf16[512,128]{1,0:T(8,128)(2,1)S(1)}, bf16[512,128]{1,0:T(8,128)(2,1)}, u32[]{:S(2)}, u32[]{:S(2)}) collective-permute-start(bf16[512,128]{1,0:T(8,128)(2,1)S(1)} %copy-done.5), channel_id=1, source_target_pairs={{0,1},{1,0},{2,3},{3,2},{4,5},{5,4},{6,7},{7,6},{8,9},{9,8},{10,11... | collective-permute-start | bytes 393224 | tf_op jit(solution)/shard_map/ppermute | solution.py:282
  75.5 5.9 %copy-start.31 = (s32[4]{0:T(128)S(1)}, s32[4]{0:T(128)}, u32[]{:S(2)}) copy-start(s32[4]{0:T(128)} %fusion) | copy-start | bytes 52
  75.5 22.4 %all-to-all-start.2 = ((bf16[32,72,128]{2,1,0:T(8,128)(2,1)}), bf16[32,72,128]{2,1,0:T(8,128)(2,1)S(1)}, u32[]{:S(2)}, u32[]{:S(2)}) async-start(bf16[32,72,128]{2,1,0:T(8,128)(2,1)} %get-tuple-element.13), calls=%async_computation.2 | async-start | bytes 1179648 | tf_op jit(solution)/shard_map/all_to_all | solution.py:380
  81.4 4.7 %collective-permute-start.16 = (s32[8,128]{1,0:T(8,128)S(1)}, s32[8,128]{1,0:T(8,128)S(1)}, u32[]{:S(2)}, u32[]{:S(2)}) collective-permute-start(s32[8,128]{1,0:T(8,128)S(1)} %bitcast.23), channel_id=1, source_target_pairs={{0,2},{1,3},{2,0},{3,1},{4,6},{5,7},{6,4},{7,5},{8,10},{9,11},{10,... | collective-permute-start | bytes 12296 | tf_op jit(solution)/shard_map/ppermute | solution.py:282
  86.1 1.2 %collective-permute-start.15 = (s32[8,128]{1,0:T(8,128)S(1)}, s32[8,128]{1,0:T(8,128)S(1)}, u32[]{:S(2)}, u32[]{:S(2)}) collective-permute-start(s32[8,128]{1,0:T(8,128)S(1)} %bitcast.25), channel_id=1, source_target_pairs={{0,1},{1,0},{2,3},{3,2},{4,5},{5,4},{6,7},{7,6},{8,9},{9,8},{10,11... | collective-permute-start | bytes 12296 | tf_op jit(solution)/shard_map/ppermute | solution.py:282
  87.3 1.2 %collective-permute-start.17 = (s32[8,128]{1,0:T(8,128)S(1)}, s32[8,128]{1,0:T(8,128)S(1)}, u32[]{:S(2)}, u32[]{:S(2)}) collective-permute-start(s32[8,128]{1,0:T(8,128)S(1)} %collective-permute-done.16), channel_id=1, source_target_pairs={{0,1},{1,0},{2,3},{3,2},{4,5},{5,4},{6,7},{7,6},{8,9},{9,8},{10,11... | collective-permute-start | bytes 12296 | tf_op jit(solution)/shard_map/ppermute | solution.py:282
  87.5 1.7 %collective-permute-start.11 = (bf16[512,128]{1,0:T(8,128)(2,1)}, bf16[512,128]{1,0:T(8,128)(2,1)S(1)}, u32[]{:S(2)}, u32[]{:S(2)}) collective-permute-start(bf16[512,128]{1,0:T(8,128)(2,1)} %collective-permute-done.10.refs_2_), channel_id=1, source_target_pairs={{0,1},{1,0},{2,3},{3,2},{4,5},{5,4},{6,7},{7,6},{8,9},{9,8},{10,11... | collective-permute-start | bytes 393224 | tf_op jit(solution)/shard_map/ppermute | solution.py:282
  87.8 1.7 %collective-permute-start.14 = (bf16[512,256]{1,0:T(8,128)(2,1)}, bf16[512,256]{1,0:T(8,128)(2,1)S(1)}, u32[]{:S(2)}, u32[]{:S(2)}) collective-permute-start(bf16[512,256]{1,0:T(8,128)(2,1)} %collective-permute-done.13.refs_6_), channel_id=1, source_target_pairs={{0,1},{1,0},{2,3},{3,2},{4,5},{5,4},{6,7},{7,6},{8,9},{9,8},{10,11... | collective-permute-start | bytes 786440 | tf_op jit(solution)/shard_map/ppermute | solution.py:282
  89.6 8.4 %copy-start.1 = (bf16[1024,512]{1,0:T(8,128)(2,1)S(1)}, bf16[1024,512]{1,0:T(8,128)(2,1)}, u32[]{:S(2)}) copy-start(bf16[1024,512]{1,0:T(8,128)(2,1)} %memory_ref.3) | copy-start | bytes 3145732
  100.3 8.3 %collective-permute-start.19 = (bf16[1024,128]{1,0:T(8,128)(2,1)S(1)}, bf16[1024,128]{1,0:T(8,128)(2,1)S(1)}, u32[]{:S(2)}, u32[]{:S(2)}) collective-permute-start(bf16[1024,128]{1,0:T(8,128)(2,1)S(1)} %apply.1.refs_0_), channel_id=1, source_target_pairs={{0,2},{1,3},{2,0},{3,1},{4,6},{5,7},{6,4},{7,5},{8,10},{9,11},{10,... | collective-permute-start | bytes 786440 | tf_op jit(solution)/shard_map/ppermute | solution.py:282
  101.5 7.1 %collective-permute-start.18 = (bf16[1024,128]{1,0:T(8,128)(2,1)S(1)}, bf16[1024,128]{1,0:T(8,128)(2,1)S(1)}, u32[]{:S(2)}, u32[]{:S(2)}) collective-permute-start(bf16[1024,128]{1,0:T(8,128)(2,1)S(1)} %apply.1.refs_0_), channel_id=1, source_target_pairs={{0,1},{1,0},{2,3},{3,2},{4,5},{5,4},{6,7},{7,6},{8,9},{9,8},{10,11... | collective-permute-start | bytes 786440 | tf_op jit(solution)/shard_map/ppermute | solution.py:282
  108.6 1.5 %collective-permute-start.20 = (bf16[1024,128]{1,0:T(8,128)(2,1)S(1)}, bf16[1024,128]{1,0:T(8,128)(2,1)S(1)}, u32[]{:S(2)}, u32[]{:S(2)}) collective-permute-start(bf16[1024,128]{1,0:T(8,128)(2,1)S(1)} %collective-permute-done.19.refs_2_), channel_id=1, source_target_pairs={{0,1},{1,0},{2,3},{3,2},{4,5},{5,4},{6,7},{7,6},{8,9},{9,8},{10,11... | collective-permute-start | bytes 786440 | tf_op jit(solution)/shard_map/ppermute | solution.py:282
  (23 other events, 18.1 us)

commit v3 on v2

--- a/solution.py
+++ b/solution.py
@@ -28,7 +28,7 @@
     return jnp.dot(a, b, preferred_element_type=F32)
 
 
-def call(body, outs, specs, flops, bytes_, name, scratch=(), limit=32):
+def call(body, outs, specs, flops, bytes_, name, scratch=(), limit=60):
     return pl.pallas_call(
         body,
         out_shape=outs,
@@ -118,7 +118,9 @@
 
 
 def serve_kernel(plan, asked_ref, memory_ref, *refs):
-    out_ref = refs[-1]
+    out_ref, held, sem = refs[-3:]
+    copy = pltpu.make_async_copy(memory_ref, held, sem)
+    copy.start()
     stored, width = memory_ref.shape
     piece = width // 4
     asked = asked_ref[...].astype(F32)
@@ -131,7 +133,8 @@
         spare = asked_ref[:, plan.main + i : plan.main + i + 1]
         blocks.append(jnp.where(spare == iota((plan.owners, stored), 1), 1.0, 0.0))
     hot = jnp.concatenate(blocks, axis=0).astype(BF16)
-    rows = dot(hot, memory_ref[...])
+    copy.wait()
+    rows = dot(hot, held[...])
     main = plan.main
     for s in range(plan.owners):
         for c in range(4):
@@ -255,19 +258,23 @@
             out_ref[at, lane] = (hnew_ref[at, lane] + dot(prob, values)).astype(BF16)
 
 
-def apply_kernel(plan, ids_ref, landed_ref, memory_ref, after_ref, out_ref):
+def apply_kernel(plan, ids_ref, landed_ref, memory_ref, after_ref, out_ref, held, sem):
     stored = memory_ref.shape[0]
     piece = out_ref.shape[1]
     count = landed_ref.shape[0]
     me = lax.axis_index("rep")
+    lane = pl.ds(pl.multiple_of(me * piece, LANES), piece)
+    copy = pltpu.make_async_copy(memory_ref.at[:, lane], held, sem)
+    copy.start()
     landed = landed_ref[...]
-    lane = pl.ds(pl.multiple_of(me * piece, LANES), piece)
     step = min(256, stored)
     ids = ids_ref[...]
     for i in range(0, stored, step):
         hot = jnp.where(iota((step, count), 0) + i == ids, 1.0, 0.0).astype(BF16)
         total = dot(hot, landed)
-        out_ref[i : i + step, :] = (memory_ref[i : i + step, lane].astype(F32) + total).astype(BF16)
+        if i == 0:
+            copy.wait()
+        out_ref[i : i + step, :] = (held[i : i + step, :].astype(F32) + total).astype(BF16)
 
 
 def join_kernel(plan, *refs):
@@ -353,12 +360,12 @@
     served = call(
         run(serve_kernel, plan),
         [sds((owners, chunk, width // 4), BF16)],
-        [VMEM] * 2 + [ANY] * (2 * reps),
+        [VMEM] + [ANY] * 3,
         2 * plan.rows * stored * width,
         2 * stored * width + 2 * plan.rows * width,
         "serve",
-        limit=24,
-    )(asked, memory, *full_hidden, *full_time)[0]
+        scratch=[pltpu.VMEM(memory.shape, BF16), pltpu.SemaphoreType.DMA],
+    )(asked, memory, full_hidden[reps // 2], full_time[reps // 2])[0]
     returned = lax.all_to_all(served, "shard", split_axis=0, concat_axis=0, tiled=True)
 
     outgoing, hnew, hdst = call(
@@ -375,7 +382,6 @@
         ]
         + [pltpu.VMEM((reps,) + x.shape, BF16) for x in (w_input, w_time, w_hidden)]
         + [pltpu.SemaphoreType.DMA((3, reps))],
-        limit=48,
     )(returned, encode, cols, rows, *full_input, *full_time, *full_hidden)
     landed = lax.all_to_all(outgoing, ("shard", "rep"), split_axis=0, concat_axis=0, tiled=True)
 
@@ -389,7 +395,6 @@
         scratch=[pltpu.VMEM((events, width), BF16), pltpu.VMEM((events, 2 * width), BF16)]
         + [pltpu.VMEM((reps,) + x.shape, BF16) for x in (w_query, w_keyval)]
         + [pltpu.SemaphoreType.DMA((2, reps))],
-        limit=48,
     )(neighbour_blocks, hnew, hdst, *full_query, *full_keyval)[0]
 
     me = lax.axis_index("rep")
@@ -399,11 +404,11 @@
     quarter = call(
         run(apply_kernel, plan),
         [sds((stored, piece), BF16)],
-        [VMEM] * 3 + [ANY],
+        [VMEM] * 2 + [ANY] * 2,
         2 * stored * owners * reps * plan.pad * piece * 2,
         4 << 20,
         "apply",
-        limit=32,
+        scratch=[pltpu.VMEM((stored, piece), BF16), pltpu.SemaphoreType.DMA],
     )(ids, landed.reshape(owners * reps * plan.pad, piece), memory, embed)[0]
     new_memory = call(
         run(join_kernel, plan), [sds((stored, width), BF16)], [VMEM] * reps, 1 << 20, 2 << 20, "join", limit=8

time: 112 us -> 94.8 us (0.85)
  waiting for transfers between devices: 38 us -> 23.1 us
  local copies, waits for them, and re-layouts: 18.7 us -> 12.1 us
  Pallas kernels: 18.7 us -> 23.8 us
    ppermute x21, waiting for transfers between devices: 35 us -> 21.7 us  [swap(): return lax.ppermute(x, 'rep', [(i, i ^ bit) for i in range(reps)])]
    unnamed x65 -> x69, local copies, waits for them, and re-layouts: 18.1 us -> 10.8 us
    pallas_call x1, Pallas kernels: 1.38 us -> 3.87 us  [shards(): call(run(apply_kernel, plan), [sds((stored, piece), BF16)], [VMEM] * 2 +...]
    pallas_call x1, Pallas kernels: 1.85 us -> 3.63 us  [shards(): call(run(serve_kernel, plan), [sds((owners, chunk, width // 4), BF16)], [...]
    all_to_all x1, waiting for transfers between devices: 3.01 us -> 1.38 us  [shards(): lax.all_to_all(outgoing, ('shard', 'rep'), split_axis=0, concat_axis=0, t...]
  transfers between devices with their start and end apart: 23 -> 23, of which waited for: 10 -> 8; matrix products, arithmetic and copies ran while one was open for 1% -> 2% of each run, Pallas kernels for 13% -> 16%
where the time goes in v3:
time: 94.8 us; the launch traced here: 94.1 us
  Pallas kernels  23.8 us (25%)
  waiting for transfers between devices  23.1 us (24%)
  starting transfers between devices  21.6 us (23%)
  blocking collectives  12.5 us (13%)
  local copies, waits for them, and re-layouts  12.1 us (13%)
    ppermute x21, waiting for transfers between devices, swap(): return lax.ppermute(x, 'rep', [(i, i ^ bit) for i in range(reps)])  21.7 us
    all_to_all x1, blocking collectives, shards(): lax.all_to_all(request, 'shard', split_axis=0, concat_axis=0, tiled=True)  12.5 us
    ppermute x21, starting transfers between devices, swap(): return lax.ppermute(x, 'rep', [(i, i ^ bit) for i in range(reps)])  11.7 us
    unnamed x69, local copies, waits for them, and re-layouts  10.8 us
    pallas_call x1, Pallas kernels, shards(): call(run(gru_kernel, plan), [sds((owners * reps, plan.pad, piece), BF16),...  7.66 us
    pallas_call x1, Pallas kernels, shards(): call(run(attend_kernel, plan), [sds((events, width), BF16)], [SMEM] + [VM...  5.89 us
    all_to_all x1, starting transfers between devices, shards(): lax.all_to_all(outgoing, ('shard', 'rep'), split_axis=0, concat_axis=0, t...  5.86 us
    all_to_all x1, starting transfers between devices, shards(): lax.all_to_all(served, 'shard', split_axis=0, concat_axis=0, tiled=True)  4.02 us
  transfers between devices with their start and end apart: 23, of which 8 were waited for; matrix products, arithmetic and copies ran while one was open for 2% of the time, Pallas kernels for 16%

profile of v3, /device:TPU:0, one launch (start us, length us, event | category | flops | bytes accessed | tf_op | source)
XLA Modules:
  0.0 94.1 jit_solution(15764710805717284889)
XLA Ops:
  0.6 3.0 %collective-permute-start = (bf16[512,384]{1,0:T(8,128)(2,1)}, bf16[512,384]{1,0:T(8,128)(2,1)S(1)}, u32[]{:S(2)}, u32[]{:S(2)}) collective-permute-start(bf16[512,384]{1,0:T(8,128)(2,1)} %refs_8_.1), channel_id=1, source_target_pairs={{0,2},{1,3},{2,0},{3,1},{4,6},{5,7},{6,4},{7,5},{8,10},{9,11},{10,... | collective-permute-start | bytes 1179656 | tf_op jit(solution)/shard_map/ppermute | solution.py:289
  3.7 0.7 copy-done.2
  4.8 12.5 %all_to_all.21 = s32[8,1,128]{2,1,0:T(1,128)} all-to-all(s32[8,1,128]{2,1,0:T(1,128)S(1)} %bitcast.21), channel_id=1, replica_groups=mesh['shard'=8,'rep'=4] {'shard'}, dimensions={0} | all-to-all | bytes 8192 | tf_op jit(solution)/shard_map/all_to_all | solution.py:339
  18.1 3.6 %serve.1 = bf16[8,264,128]{2,1,0:T(8,128)(2,1)} custom-call(s32[8,128]{1,0:T(8,128)} %bitcast.30, bf16[1024,512]{1,0:T(8,128)(2,1)} %memory_ref.3, bf16[512,384]{1,0:T(8,128)(2,1)} %copy-done.11, bf16[128,384]{1,0:T(8,128)(2,1)} %copy-done.21), custom_call_target="tpu_custom_call" | custom-call | flops 553648128 | bytes 1589248 | tf_op jit(solution)/shard_map/serve/pallas_call | solution.py:360
  21.8 4.0 %all-to-all-start.1 = ((bf16[8,264,128]{2,1,0:T(8,128)(2,1)}), bf16[8,264,128]{2,1,0:T(8,128)(2,1)S(1)}, u32[]{:S(2)}, u32[]{:S(2)}) async-start(bf16[8,264,128]{2,1,0:T(8,128)(2,1)} %serve.1), calls=%async_computation.1 | async-start | bytes 1081344 | tf_op jit(solution)/shard_map/all_to_all | solution.py:369
  25.8 1.6 %collective-permute-start.3 = (bf16[512,384]{1,0:T(8,128)(2,1)S(1)}, bf16[512,384]{1,0:T(8,128)(2,1)S(1)}, u32[]{:S(2)}, u32[]{:S(2)}) collective-permute-start(bf16[512,384]{1,0:T(8,128)(2,1)S(1)} %copy-done.29), channel_id=1, source_target_pairs={{0,2},{1,3},{2,0},{3,1},{4,6},{5,7},{6,4},{7,5},{8,10},{9,11},{10,... | collective-permute-start | bytes 1179656 | tf_op jit(solution)/shard_map/ppermute | solution.py:289
  27.9 7.6 %collective-permute-done.3.refs_2_ = bf16[512,384]{1,0:T(8,128)(2,1)S(1)} collective-permute-done((bf16[512,384]{1,0:T(8,128)(2,1)S(1)}, bf16[512,384]{1,0:T(8,128)(2,1)S(1)}, u32[]{:S(2)}, u32[]{:S(2)}) %collective-permute-start.3) | collective-permute-done | bytes 393248 | tf_op jit(solution)/shard_map/ppermute | solution.py:289
  36.1 0.7 copy-done.25
  36.8 0.7 copy-done.26
  37.5 0.7 copy-done.27
  38.1 0.7 copy.20.listed_ref
  38.8 0.7 copy-done.3
  39.5 1.2 %index.1 = (bf16[384,128]{1,0:T(8,128)(2,1)S(1)}, f32[384,8]{1,0:T(8,128)S(1)}, s32[8,384]{1,0:T(8,128)S(1)}) custom-call(s32[1,256]{1,0:T(1,128)S(1)} %bitcast.24, s32[1,256]{1,0:T(1,128)S(1)} %bitcast.25, s32[1,384]{1,0:T(1,128)S(1)} %reshape.55.src_ref, s32[1,384]{1,0:T(1,128)S(1)} %reshape.56.dst_ref, s32[1,384]{1,0:T(1,128)S(1)} %reshape.57.stamp_ref, ...), custom_call_target="tpu_custom_call" | custom-call | flops 4194304 | bytes 262144 | tf_op jit(solution)/shard_map/index/pallas_call | solution.py:340
  40.7 0.7 copy-done.6
  42.8 1.2 %collective-permute-done.6.refs_7_ = bf16[128,384]{1,0:T(8,128)(2,1)S(1)} collective-permute-done((bf16[128,384]{1,0:T(8,128)(2,1)S(1)}, bf16[128,384]{1,0:T(8,128)(2,1)S(1)}, u32[]{:S(2)}, u32[]{:S(2)}) %collective-permute-start.6) | collective-permute-done | bytes 98336 | tf_op jit(solution)/shard_map/ppermute | solution.py:289
  44.0 1.5 %collective-permute-start.13 = (bf16[512,256]{1,0:T(8,128)(2,1)S(1)}, bf16[512,256]{1,0:T(8,128)(2,1)S(1)}, u32[]{:S(2)}, u32[]{:S(2)}) collective-permute-start(bf16[512,256]{1,0:T(8,128)(2,1)S(1)} %copy-done.13), channel_id=1, source_target_pairs={{0,2},{1,3},{2,0},{3,1},{4,6},{5,7},{6,4},{7,5},{8,10},{9,11},{10,... | collective-permute-start | bytes 786440 | tf_op jit(solution)/shard_map/ppermute | solution.py:289
  46.4 0.8 copy-done.10
  47.1 7.7 %gru.1 = (bf16[32,72,128]{2,1,0:T(8,128)(2,1)}, f32[384,512]{1,0:T(8,128)}, bf16[384,512]{1,0:T(8,128)(2,1)}) custom-call(bf16[8,264,128]{2,1,0:T(8,128)(2,1)} %copy-done.10, bf16[384,128]{1,0:T(8,128)(2,1)} %copy-done.7, f32[384,8]{1,0:T(8,128)} %copy-done.6, s32[8,384]{1,0:T(8,128)} %copy-done.8, bf16[512,384]{1,0:T(8,128)(2,1)} %refs_0_.2, ...), custom_call_target="tpu_custom_call" | custom-call | flops 1207959552 | bytes 8388608 | tf_op jit(solution)/shard_map/gru/pallas_call | solution.py:371
  54.8 5.9 %all-to-all-start.2 = ((bf16[32,72,128]{2,1,0:T(8,128)(2,1)}), bf16[32,72,128]{2,1,0:T(8,128)(2,1)S(1)}, u32[]{:S(2)}, u32[]{:S(2)}) async-start(bf16[32,72,128]{2,1,0:T(8,128)(2,1)} %get-tuple-element.13), calls=%async_computation.2 | async-start | bytes 1179648 | tf_op jit(solution)/shard_map/all_to_all | solution.py:386
  61.4 1.6 %collective-permute-start.16 = (s32[8,128]{1,0:T(8,128)S(1)}, s32[8,128]{1,0:T(8,128)S(1)}, u32[]{:S(2)}, u32[]{:S(2)}) collective-permute-start(s32[8,128]{1,0:T(8,128)S(1)} %bitcast.31), channel_id=1, source_target_pairs={{0,2},{1,3},{2,0},{3,1},{4,6},{5,7},{6,4},{7,5},{8,10},{9,11},{10,... | collective-permute-start | bytes 12296 | tf_op jit(solution)/shard_map/ppermute | solution.py:289
  63.0 2.5 %collective-permute-done.16 = s32[8,128]{1,0:T(8,128)S(1)} collective-permute-done((s32[8,128]{1,0:T(8,128)S(1)}, s32[8,128]{1,0:T(8,128)S(1)}, u32[]{:S(2)}, u32[]{:S(2)}) %collective-permute-start.16) | collective-permute-done | bytes 4128 | tf_op jit(solution)/shard_map/ppermute | solution.py:289
  65.4 1.2 %collective-permute-done.15 = s32[8,128]{1,0:T(8,128)S(1)} collective-permute-done((s32[8,128]{1,0:T(8,128)S(1)}, s32[8,128]{1,0:T(8,128)S(1)}, u32[]{:S(2)}, u32[]{:S(2)}) %collective-permute-start.15) | collective-permute-done | bytes 4128 | tf_op jit(solution)/shard_map/ppermute | solution.py:289
  68.3 0.7 reshape.60.ids_ref
  70.0 5.9 %attend.1.after_ref = bf16[384,512]{1,0:T(8,128)(2,1)} custom-call(s32[3,2]{1,0:T(4,128)} %copy.20.listed_ref, f32[384,512]{1,0:T(8,128)} %get-tuple-element.11.hnew_ref, bf16[384,512]{1,0:T(8,128)(2,1)} %get-tuple-element.12.hdst_ref, bf16[512,128]{1,0:T(8,128)(2,1)} %refs_0_.3, bf16[512,128]{1,0:T(8,128)(2,1)} %copy-done.19, bf16[512,128]{1,0:T(8,128)(2,1)} %copy-done.18, ...), custom_call_target="tpu_custom_call" | custom-call | flops 603979776 | bytes 4194304 | tf_op jit(solution)/shard_map/attend/pallas_call | solution.py:388
  75.9 1.4 %all-to-all-done.2 = bf16[32,72,128]{2,1,0:T(8,128)(2,1)S(1)} async-done(((bf16[32,72,128]{2,1,0:T(8,128)(2,1)}), bf16[32,72,128]{2,1,0:T(8,128)(2,1)S(1)}, u32[]{:S(2)}, u32[]{:S(2)}) %all-to-all-start.2) | async-done | bytes 589856 | tf_op jit(solution)/shard_map/all_to_all | solution.py:386
  77.2 0.8 copy-done.9
  78.1 3.9 %apply.1.refs_0_ = bf16[1024,128]{1,0:T(8,128)(2,1)} custom-call(s32[1,2304]{1,0:T(1,128)} %reshape.60.ids_ref, bf16[2304,128]{1,0:T(8,128)(2,1)} %bitcast.28, bf16[1024,512]{1,0:T(8,128)(2,1)} %memory_ref.3, bf16[384,512]{1,0:T(8,128)(2,1)} %attend.1.after_ref), custom_call_target="tpu_custom_call" | custom-call | flops 1207959552 | bytes 4194304 | tf_op jit(solution)/shard_map/apply/pallas_call | solution.py:404
  81.9 1.2 %collective-permute-start.19 = (bf16[1024,128]{1,0:T(8,128)(2,1)}, bf16[1024,128]{1,0:T(8,128)(2,1)S(1)}, u32[]{:S(2)}, u32[]{:S(2)}) collective-permute-start(bf16[1024,128]{1,0:T(8,128)(2,1)} %apply.1.refs_0_), channel_id=1, source_target_pairs={{0,2},{1,3},{2,0},{3,1},{4,6},{5,7},{6,4},{7,5},{8,10},{9,11},{10,... | collective-permute-start | bytes 786440 | tf_op jit(solution)/shard_map/ppermute | solution.py:289
  83.2 7.2 %collective-permute-done.19.refs_2_ = bf16[1024,128]{1,0:T(8,128)(2,1)S(1)} collective-permute-done((bf16[1024,128]{1,0:T(8,128)(2,1)}, bf16[1024,128]{1,0:T(8,128)(2,1)S(1)}, u32[]{:S(2)}, u32[]{:S(2)}) %collective-permute-start.19) | collective-permute-done | bytes 262176 | tf_op jit(solution)/shard_map/ppermute | solution.py:289
  90.4 1.5 %collective-permute-done.20.refs_3_ = bf16[1024,128]{1,0:T(8,128)(2,1)S(1)} collective-permute-done((bf16[1024,128]{1,0:T(8,128)(2,1)S(1)}, bf16[1024,128]{1,0:T(8,128)(2,1)S(1)}, u32[]{:S(2)}, u32[]{:S(2)}) %collective-permute-start.20) | collective-permute-done | bytes 262176 | tf_op jit(solution)/shard_map/ppermute | solution.py:289
  91.9 0.9 %copy-done = bf16[1024,128]{1,0:T(8,128)(2,1)S(1)} copy-done((bf16[1024,128]{1,0:T(8,128)(2,1)S(1)}, bf16[1024,128]{1,0:T(8,128)(2,1)}, u32[]{:S(2)}) %copy-start) | copy-done | bytes 262168
  92.9 1.2 %join.1 = bf16[1024,512]{1,0:T(8,128)(2,1)} custom-call(bf16[1024,128]{1,0:T(8,128)(2,1)S(1)} %copy-done, bf16[1024,128]{1,0:T(8,128)(2,1)S(1)} %collective-permute-done.18.refs_1_, bf16[1024,128]{1,0:T(8,128)(2,1)S(1)} %collective-permute-done.19.refs_2_, bf16[1024,128]{1,0:T(8,128)(2,1)S(1)} %collective-permute-done.20.refs_3_), custom_call_target="tpu_custom_call" | custom-call | flops 1048576 | bytes 2097152 | tf_op jit(solution)/shard_map/join/pallas_call | solution.py:413
  (104 shorter events, 7.9 us)
Async XLA Ops:
  0.6 16.6 %collective-permute-start = (bf16[512,384]{1,0:T(8,128)(2,1)}, bf16[512,384]{1,0:T(8,128)(2,1)S(1)}, u32[]{:S(2)}, u32[]{:S(2)}) collective-permute-start(bf16[512,384]{1,0:T(8,128)(2,1)} %refs_8_.1), channel_id=1, source_target_pairs={{0,2},{1,3},{2,0},{3,1},{4,6},{5,7},{6,4},{7,5},{8,10},{9,11},{10,... | collective-permute-start | bytes 1179656 | tf_op jit(solution)/shard_map/ppermute | solution.py:289
  3.6 13.6 %collective-permute-start.1 = (bf16[128,384]{1,0:T(8,128)(2,1)}, bf16[128,384]{1,0:T(8,128)(2,1)S(1)}, u32[]{:S(2)}, u32[]{:S(2)}) collective-permute-start(bf16[128,384]{1,0:T(8,128)(2,1)} %refs_4_.2), channel_id=1, source_target_pairs={{0,2},{1,3},{2,0},{3,1},{4,6},{5,7},{6,4},{7,5},{8,10},{9,11},{10,... | collective-permute-start | bytes 294920 | tf_op jit(solution)/shard_map/ppermute | solution.py:289
  18.1 7.7 %copy-start.29 = (bf16[512,384]{1,0:T(8,128)(2,1)S(1)}, bf16[512,384]{1,0:T(8,128)(2,1)}, u32[]{:S(2)}) copy-start(bf16[512,384]{1,0:T(8,128)(2,1)} %refs_0_.2) | copy-start | bytes 1179652
  18.1 9.3 %copy-start.28 = (bf16[512,384]{1,0:T(8,128)(2,1)S(1)}, bf16[512,384]{1,0:T(8,128)(2,1)}, u32[]{:S(2)}) copy-start(bf16[512,384]{1,0:T(8,128)(2,1)} %refs_8_.1) | copy-start | bytes 1179652
  21.7 13.9 %copy-start.31 = (bf16[128,384]{1,0:T(8,128)(2,1)S(1)}, bf16[128,384]{1,0:T(8,128)(2,1)}, u32[]{:S(2)}) copy-start(bf16[128,384]{1,0:T(8,128)(2,1)} %refs_4_.2) | copy-start | bytes 294916
  21.7 14.4 %copy-start.24 = (s32[384]{0:T(512)S(1)}, s32[384]{0:T(512)}, u32[]{:S(2)}) copy-start(s32[384]{0:T(512)} %param.19) | copy-start | bytes 4612
  21.7 17.1 %copy-start.5 = (f32[128]{0:T(128)S(1)}, f32[128]{0:T(128)}, u32[]{:S(2)}) copy-start(f32[128]{0:T(128)} %param.24) | copy-start | bytes 1540
  21.7 20.9 %copy-start.22 = (bf16[128,384]{1,0:T(8,128)(2,1)S(1)}, bf16[128,384]{1,0:T(8,128)(2,1)}, u32[]{:S(2)}) copy-start(bf16[128,384]{1,0:T(8,128)(2,1)} %copy-done.21) | copy-start | bytes 294916
  21.7 22.2 %copy-start.13 = (bf16[512,256]{1,0:T(8,128)(2,1)S(1)}, bf16[512,256]{1,0:T(8,128)(2,1)}, u32[]{:S(2)}) copy-start(bf16[512,256]{1,0:T(8,128)(2,1)} %refs_4_.3) | copy-start | bytes 786436
  21.8 23.7 %copy-start.17 = (bf16[512,128]{1,0:T(8,128)(2,1)S(1)}, bf16[512,128]{1,0:T(8,128)(2,1)}, u32[]{:S(2)}) copy-start(bf16[512,128]{1,0:T(8,128)(2,1)} %refs_0_.3) | copy-start | bytes 393220
  21.8 24.6 %all-to-all-start.1 = ((bf16[8,264,128]{2,1,0:T(8,128)(2,1)}), bf16[8,264,128]{2,1,0:T(8,128)(2,1)S(1)}, u32[]{:S(2)}, u32[]{:S(2)}) async-start(bf16[8,264,128]{2,1,0:T(8,128)(2,1)} %serve.1), calls=%async_computation.1 | async-start | bytes 1081344 | tf_op jit(solution)/shard_map/all_to_all | solution.py:369
  25.8 9.8 %collective-permute-start.3 = (bf16[512,384]{1,0:T(8,128)(2,1)S(1)}, bf16[512,384]{1,0:T(8,128)(2,1)S(1)}, u32[]{:S(2)}, u32[]{:S(2)}) collective-permute-start(bf16[512,384]{1,0:T(8,128)(2,1)S(1)} %copy-done.29), channel_id=1, source_target_pairs={{0,2},{1,3},{2,0},{3,1},{4,6},{5,7},{6,4},{7,5},{8,10},{9,11},{10,... | collective-permute-start | bytes 1179656 | tf_op jit(solution)/shard_map/ppermute | solution.py:289
  27.4 18.1 %collective-permute-start.2 = (bf16[512,384]{1,0:T(8,128)(2,1)S(1)}, bf16[512,384]{1,0:T(8,128)(2,1)}, u32[]{:S(2)}, u32[]{:S(2)}) collective-permute-start(bf16[512,384]{1,0:T(8,128)(2,1)S(1)} %copy-done.29), channel_id=1, source_target_pairs={{0,1},{1,0},{2,3},{3,2},{4,5},{5,4},{6,7},{7,6},{8,9},{9,8},{10,11... | collective-permute-start | bytes 1179656 | tf_op jit(solution)/shard_map/ppermute | solution.py:289
  27.4 18.1 %collective-permute-start.7 = (bf16[512,384]{1,0:T(8,128)(2,1)S(1)}, bf16[512,384]{1,0:T(8,128)(2,1)}, u32[]{:S(2)}, u32[]{:S(2)}) collective-permute-start(bf16[512,384]{1,0:T(8,128)(2,1)S(1)} %copy-done.28), channel_id=1, source_target_pairs={{0,1},{1,0},{2,3},{3,2},{4,5},{5,4},{6,7},{7,6},{8,9},{9,8},{10,11... | collective-permute-start | bytes 1179656 | tf_op jit(solution)/shard_map/ppermute | solution.py:289
  27.9 18.2 %collective-permute-start.8 = (bf16[512,384]{1,0:T(8,128)(2,1)S(1)}, bf16[512,384]{1,0:T(8,128)(2,1)}, u32[]{:S(2)}, u32[]{:S(2)}) collective-permute-start(bf16[512,384]{1,0:T(8,128)(2,1)S(1)} %copy-done.12), channel_id=1, source_target_pairs={{0,1},{1,0},{2,3},{3,2},{4,5},{5,4},{6,7},{7,6},{8,9},{9,8},{10,11... | collective-permute-start | bytes 1179656 | tf_op jit(solution)/shard_map/ppermute | solution.py:289
  35.6 10.8 %copy-start.30 = (bf16[512,384]{1,0:T(8,128)(2,1)}, bf16[512,384]{1,0:T(8,128)(2,1)S(1)}, u32[]{:S(2)}) copy-start(bf16[512,384]{1,0:T(8,128)(2,1)S(1)} %collective-permute-done.3.refs_2_) | copy-start | bytes 1179652
  35.6 10.8 %collective-permute-start.4 = (bf16[512,384]{1,0:T(8,128)(2,1)S(1)}, bf16[512,384]{1,0:T(8,128)(2,1)}, u32[]{:S(2)}, u32[]{:S(2)}) collective-permute-start(bf16[512,384]{1,0:T(8,128)(2,1)S(1)} %collective-permute-done.3.refs_2_), channel_id=1, source_target_pairs={{0,1},{1,0},{2,3},{3,2},{4,5},{5,4},{6,7},{7,6},{8,9},{9,8},{10,11... | collective-permute-start | bytes 1179656 | tf_op jit(solution)/shard_map/ppermute | solution.py:289
  35.6 7.0 %collective-permute-start.5 = (bf16[128,384]{1,0:T(8,128)(2,1)S(1)}, bf16[128,384]{1,0:T(8,128)(2,1)S(1)}, u32[]{:S(2)}, u32[]{:S(2)}) collective-permute-start(bf16[128,384]{1,0:T(8,128)(2,1)S(1)} %copy-done.31), channel_id=1, source_target_pairs={{0,1},{1,0},{2,3},{3,2},{4,5},{5,4},{6,7},{7,6},{8,9},{9,8},{10,11... | collective-permute-start | bytes 294920 | tf_op jit(solution)/shard_map/ppermute | solution.py:289
  42.6 1.4 %collective-permute-start.6 = (bf16[128,384]{1,0:T(8,128)(2,1)S(1)}, bf16[128,384]{1,0:T(8,128)(2,1)S(1)}, u32[]{:S(2)}, u32[]{:S(2)}) collective-permute-start(bf16[128,384]{1,0:T(8,128)(2,1)S(1)} %copy-done.22), channel_id=1, source_target_pairs={{0,1},{1,0},{2,3},{3,2},{4,5},{5,4},{6,7},{7,6},{8,9},{9,8},{10,11... | collective-permute-start | bytes 294920 | tf_op jit(solution)/shard_map/ppermute | solution.py:289
  44.0 23.1 %collective-permute-start.13 = (bf16[512,256]{1,0:T(8,128)(2,1)S(1)}, bf16[512,256]{1,0:T(8,128)(2,1)S(1)}, u32[]{:S(2)}, u32[]{:S(2)}) collective-permute-start(bf16[512,256]{1,0:T(8,128)(2,1)S(1)} %copy-done.13), channel_id=1, source_target_pairs={{0,2},{1,3},{2,0},{3,1},{4,6},{5,7},{6,4},{7,5},{8,10},{9,11},{10,... | collective-permute-start | bytes 786440 | tf_op jit(solution)/shard_map/ppermute | solution.py:289
  45.5 23.6 %collective-permute-start.12 = (bf16[512,256]{1,0:T(8,128)(2,1)S(1)}, bf16[512,256]{1,0:T(8,128)(2,1)S(1)}, u32[]{:S(2)}, u32[]{:S(2)}) collective-permute-start(bf16[512,256]{1,0:T(8,128)(2,1)S(1)} %copy-done.13), channel_id=1, source_target_pairs={{0,1},{1,0},{2,3},{3,2},{4,5},{5,4},{6,7},{7,6},{8,9},{9,8},{10,11... | collective-permute-start | bytes 786440 | tf_op jit(solution)/shard_map/ppermute | solution.py:289
  45.5 21.3 %collective-permute-start.10 = (bf16[512,128]{1,0:T(8,128)(2,1)S(1)}, bf16[512,128]{1,0:T(8,128)(2,1)S(1)}, u32[]{:S(2)}, u32[]{:S(2)}) collective-permute-start(bf16[512,128]{1,0:T(8,128)(2,1)S(1)} %copy-done.17), channel_id=1, source_target_pairs={{0,2},{1,3},{2,0},{3,1},{4,6},{5,7},{6,4},{7,5},{8,10},{9,11},{10,... | collective-permute-start | bytes 393224 | tf_op jit(solution)/shard_map/ppermute | solution.py:289
  46.1 22.9 %collective-permute-start.9 = (bf16[512,128]{1,0:T(8,128)(2,1)S(1)}, bf16[512,128]{1,0:T(8,128)(2,1)S(1)}, u32[]{:S(2)}, u32[]{:S(2)}) collective-permute-start(bf16[512,128]{1,0:T(8,128)(2,1)S(1)} %copy-done.17), channel_id=1, source_target_pairs={{0,1},{1,0},{2,3},{3,2},{4,5},{5,4},{6,7},{7,6},{8,9},{9,8},{10,11... | collective-permute-start | bytes 393224 | tf_op jit(solution)/shard_map/ppermute | solution.py:289
  54.8 22.4 %all-to-all-start.2 = ((bf16[32,72,128]{2,1,0:T(8,128)(2,1)}), bf16[32,72,128]{2,1,0:T(8,128)(2,1)S(1)}, u32[]{:S(2)}, u32[]{:S(2)}) async-start(bf16[32,72,128]{2,1,0:T(8,128)(2,1)} %get-tuple-element.13), calls=%async_computation.2 | async-start | bytes 1179648 | tf_op jit(solution)/shard_map/all_to_all | solution.py:386
  61.4 4.1 %collective-permute-start.16 = (s32[8,128]{1,0:T(8,128)S(1)}, s32[8,128]{1,0:T(8,128)S(1)}, u32[]{:S(2)}, u32[]{:S(2)}) collective-permute-start(s32[8,128]{1,0:T(8,128)S(1)} %bitcast.31), channel_id=1, source_target_pairs={{0,2},{1,3},{2,0},{3,1},{4,6},{5,7},{6,4},{7,5},{8,10},{9,11},{10,... | collective-permute-start | bytes 12296 | tf_op jit(solution)/shard_map/ppermute | solution.py:289
  65.4 1.2 %collective-permute-start.15 = (s32[8,128]{1,0:T(8,128)S(1)}, s32[8,128]{1,0:T(8,128)S(1)}, u32[]{:S(2)}, u32[]{:S(2)}) collective-permute-start(s32[8,128]{1,0:T(8,128)S(1)} %bitcast.33), channel_id=1, source_target_pairs={{0,1},{1,0},{2,3},{3,2},{4,5},{5,4},{6,7},{7,6},{8,9},{9,8},{10,11... | collective-permute-start | bytes 12296 | tf_op jit(solution)/shard_map/ppermute | solution.py:289
  66.6 1.2 %collective-permute-start.17 = (s32[8,128]{1,0:T(8,128)S(1)}, s32[8,128]{1,0:T(8,128)S(1)}, u32[]{:S(2)}, u32[]{:S(2)}) collective-permute-start(s32[8,128]{1,0:T(8,128)S(1)} %collective-permute-done.16), channel_id=1, source_target_pairs={{0,1},{1,0},{2,3},{3,2},{4,5},{5,4},{6,7},{7,6},{8,9},{9,8},{10,11... | collective-permute-start | bytes 12296 | tf_op jit(solution)/shard_map/ppermute | solution.py:289
  66.8 2.3 %collective-permute-start.11 = (bf16[512,128]{1,0:T(8,128)(2,1)S(1)}, bf16[512,128]{1,0:T(8,128)(2,1)S(1)}, u32[]{:S(2)}, u32[]{:S(2)}) collective-permute-start(bf16[512,128]{1,0:T(8,128)(2,1)S(1)} %collective-permute-done.10.refs_2_), channel_id=1, source_target_pairs={{0,1},{1,0},{2,3},{3,2},{4,5},{5,4},{6,7},{7,6},{8,9},{9,8},{10,11... | collective-permute-start | bytes 393224 | tf_op jit(solution)/shard_map/ppermute | solution.py:289
  67.1 2.0 %collective-permute-start.14 = (bf16[512,256]{1,0:T(8,128)(2,1)S(1)}, bf16[512,256]{1,0:T(8,128)(2,1)S(1)}, u32[]{:S(2)}, u32[]{:S(2)}) collective-permute-start(bf16[512,256]{1,0:T(8,128)(2,1)S(1)} %collective-permute-done.13.refs_6_), channel_id=1, source_target_pairs={{0,1},{1,0},{2,3},{3,2},{4,5},{5,4},{6,7},{7,6},{8,9},{9,8},{10,11... | collective-permute-start | bytes 786440 | tf_op jit(solution)/shard_map/ppermute | solution.py:289
  81.9 8.5 %collective-permute-start.19 = (bf16[1024,128]{1,0:T(8,128)(2,1)}, bf16[1024,128]{1,0:T(8,128)(2,1)S(1)}, u32[]{:S(2)}, u32[]{:S(2)}) collective-permute-start(bf16[1024,128]{1,0:T(8,128)(2,1)} %apply.1.refs_0_), channel_id=1, source_target_pairs={{0,2},{1,3},{2,0},{3,1},{4,6},{5,7},{6,4},{7,5},{8,10},{9,11},{10,... | collective-permute-start | bytes 786440 | tf_op jit(solution)/shard_map/ppermute | solution.py:289
  83.1 7.3 %collective-permute-start.18 = (bf16[1024,128]{1,0:T(8,128)(2,1)}, bf16[1024,128]{1,0:T(8,128)(2,1)S(1)}, u32[]{:S(2)}, u32[]{:S(2)}) collective-permute-start(bf16[1024,128]{1,0:T(8,128)(2,1)} %apply.1.refs_0_), channel_id=1, source_target_pairs={{0,1},{1,0},{2,3},{3,2},{4,5},{5,4},{6,7},{7,6},{8,9},{9,8},{10,11... | collective-permute-start | bytes 786440 | tf_op jit(solution)/shard_map/ppermute | solution.py:289
  90.4 1.5 %collective-permute-start.20 = (bf16[1024,128]{1,0:T(8,128)(2,1)S(1)}, bf16[1024,128]{1,0:T(8,128)(2,1)S(1)}, u32[]{:S(2)}, u32[]{:S(2)}) collective-permute-start(bf16[1024,128]{1,0:T(8,128)(2,1)S(1)} %collective-permute-done.19.refs_2_), channel_id=1, source_target_pairs={{0,1},{1,0},{2,3},{3,2},{4,5},{5,4},{6,7},{7,6},{8,9},{9,8},{10,11... | collective-permute-start | bytes 786440 | tf_op jit(solution)/shard_map/ppermute | solution.py:289
  (25 other events, 30.1 us)

commit v4 on v1

--- a/solution.py
+++ b/solution.py
@@ -17,6 +17,7 @@
 I32 = jnp.int32
 VMEM = pl.BlockSpec(memory_space=pltpu.VMEM)
 SMEM = pl.BlockSpec(memory_space=pltpu.SMEM)
+ANY = pl.BlockSpec(memory_space=pl.ANY)
 
 
 def iota(shape, dim):
@@ -27,7 +28,7 @@
     return jnp.dot(a, b, preferred_element_type=F32)
 
 
-def call(body, outs, specs, flops, bytes_, name, scratch=(), limit=32):
+def call(body, outs, specs, flops, bytes_, name, scratch=(), limit=8):
     return pl.pallas_call(
         body,
         out_shape=outs,
@@ -77,19 +78,22 @@
     out_ref[...] = (dot(high, spot) * 32.0 + dot(low, spot)).astype(I32)
 
 
-def index_kernel(plan, owner_ref, tick_ref, src_ref, dst_ref, stamp_ref, freq_ref, phase_ref, enc_ref, col_ref, row_ref):
-    events = src_ref.shape[1]
+def index_kernel(plan, owner_ref, packed_ref, freq_ref, phase_ref, enc_ref, col_ref, row_ref):
+    events = enc_ref.shape[0]
+    ends = [plan.entries + i * events for i in range(4)]
+    tick_row = packed_ref[:, : ends[0]]
+    src_row, dst_row, stamp_row = (packed_ref[:, a : a + events] for a in ends[:3])
     own_row = owner_ref[...]
     own_col = to_col(own_row, plan.entries)
     _, place = rank_of(own_col, own_row, plan.entries)
-    tick = to_col(tick_ref[...], plan.entries)
+    tick = to_col(tick_row, plan.entries)
     spot = own_col * plan.main + place
     if plan.tail:
         spare = plan.owners * plan.main + (place - plan.main) * plan.owners + own_col
         spot = jnp.where(place < plan.main, spot, spare)
     back = own_col * plan.pad + place
-    isrc = iota((plan.entries, events), 0) == src_ref[...]
-    idst = iota((plan.entries, events), 0) == dst_ref[...]
+    isrc = iota((plan.entries, events), 0) == src_row
+    idst = iota((plan.entries, events), 0) == dst_row
 
     def pick(mask, values):
         return jnp.sum(jnp.where(mask, values, 0), axis=0, keepdims=True)
@@ -97,7 +101,7 @@
     src_spot = pick(isrc, spot)
     dst_spot = pick(idst, spot)
     src_back = pick(isrc, back)
-    span = stamp_ref[...] - pick(isrc, tick)
+    span = stamp_row - pick(isrc, tick)
     zero = jnp.zeros((8 - 3, events), I32)
     rows = jnp.concatenate([src_spot, dst_spot, span, zero], axis=0)
     row_ref[...] = jnp.concatenate([src_back, jnp.zeros((7, events), I32)], axis=0)
@@ -166,7 +170,7 @@
 
 def gru_kernel(plan, ret_ref, enc_ref, col_ref, row_ref, *refs):
     reps = plan.reps
-    w_in, w_time, w_hid = refs[:reps], refs[reps : 2 * reps], refs[2 * reps : 3 * reps]
+    w_in, w_hid, w_time = refs[:reps], refs[reps : 2 * reps], refs[2 * reps : 3 * reps]
     out_ref, hnew_ref, hdst_ref, gin, ghid, delta = refs[3 * reps :]
     me = lax.axis_index("rep")
     events, width = hnew_ref.shape
@@ -207,20 +211,22 @@
             out_ref[o * reps + q] = mean[o * plan.pad : (o + 1) * plan.pad, q * piece : (q + 1) * piece].astype(BF16)
 
 
-def attend_kernel(plan, listed_ref, hnew_ref, hdst_ref, *refs):
+def attend_kernel(plan, listed_ref, hnew_ref, hdst_ref, memory_ref, *refs):
     reps = plan.reps
     w_query, w_keyval = refs[:reps], refs[reps : 2 * reps]
-    out_ref, query, keyval = refs[2 * reps :]
+    out_ref, quarter_ref, query, keyval = refs[2 * reps :]
     me = lax.axis_index("rep")
     events, width = hnew_ref.shape
+    piece = quarter_ref.shape[1]
+    quarter_ref[...] = memory_ref[:, pl.ds(pl.multiple_of(me * piece, LANES), piece)]
     head = width // H
     hround = hnew_ref[...].astype(BF16)
     target = hdst_ref[...]
+    first = width // reps
     for k in range(reps):
-        part = w_query[k].shape[1]
-        query[:, pl.ds(pl.multiple_of((me ^ k) * part, LANES), part)] = dot(hround, w_query[k][...]).astype(BF16)
-        part = w_keyval[k].shape[1]
-        keyval[:, pl.ds(pl.multiple_of((me ^ k) * part, LANES), part)] = dot(target, w_keyval[k][...]).astype(BF16)
+        query[:, pl.ds(pl.multiple_of((me ^ k) * first, LANES), first)] = dot(hround, w_query[k][...]).astype(BF16)
+        at = pl.ds(pl.multiple_of((me ^ k) * 2 * first, LANES), 2 * first)
+        keyval[:, at] = dot(target, w_keyval[k][...]).astype(BF16)
     for i in range(events // BLK):
         spans = [pl.ds(pl.multiple_of(listed_ref[i, j] * BLK, BLK), BLK) for j in range(NB)]
         at = slice(i * BLK, (i + 1) * BLK)
@@ -237,19 +243,16 @@
             out_ref[at, lane] = (hnew_ref[at, lane] + dot(prob, values)).astype(BF16)
 
 
-def apply_kernel(plan, ids_ref, landed_ref, memory_ref, out_ref):
-    stored = memory_ref.shape[0]
-    piece = out_ref.shape[1]
+def apply_kernel(plan, ids_ref, landed_ref, part_ref, out_ref):
+    stored = part_ref.shape[0]
     count = landed_ref.shape[0]
-    me = lax.axis_index("rep")
     landed = landed_ref[...]
-    lane = pl.ds(pl.multiple_of(me * piece, LANES), piece)
     step = min(256, stored)
     ids = ids_ref[...]
     for i in range(0, stored, step):
         hot = jnp.where(iota((step, count), 0) + i == ids, 1.0, 0.0).astype(BF16)
         total = dot(hot, landed)
-        out_ref[i : i + step, :] = (memory_ref[i : i + step, lane].astype(F32) + total).astype(BF16)
+        out_ref[i : i + step, :] = (part_ref[i : i + step, :].astype(F32) + total).astype(BF16)
 
 
 def join_kernel(plan, *refs):
@@ -307,25 +310,22 @@
         run(request_kernel, plan), [sds((owners, LANES), I32)], [VMEM] * 2, 1 << 20, 1 << 14, "request", limit=8
     )(owner, touch_row.reshape(1, entries))[0]
 
-    full_hidden, full_input, full_time, full_keyval, full_query = spread(
-        [w_hidden, w_input, w_time, w_keyval, w_query], reps
+    full_time, full_hidden, full_input, full_keyval, full_query = spread(
+        [w_time, w_hidden, w_input, w_keyval, w_query], reps
     )
 
     asked = lax.all_to_all(request, "shard", split_axis=0, concat_axis=0, tiled=True)
     encode, cols, rows = call(
         run(index_kernel, plan),
         [sds((events, time_freq.shape[0]), BF16), sds((events, 8), F32), sds((8, events), I32)],
-        [VMEM] * 7,
-        1 << 22,
+        [VMEM] * 4,
+        8 << 30,
         1 << 18,
         "index",
         limit=8,
     )(
         owner,
-        touch_time.reshape(1, entries),
-        src_slot.reshape(1, events),
-        dst_slot.reshape(1, events),
-        event_time.reshape(1, events),
+        jnp.concatenate([touch_time, src_slot, dst_slot, event_time]).reshape(1, -1),
         time_freq.reshape(1, -1),
         time_phase.reshape(1, -1),
     )
@@ -339,7 +339,7 @@
         2 * plan.rows * stored * width,
         2 * stored * width + 2 * plan.rows * width,
         "serve",
-        limit=24,
+        limit=12,
     )(asked, memory)[0]
     returned = lax.all_to_all(served, "shard", split_axis=0, concat_axis=0, tiled=True)
 
@@ -355,20 +355,23 @@
             pltpu.VMEM((events, 3 * width), F32),
             pltpu.VMEM((events, width), F32),
         ],
-        limit=40,
-    )(returned, encode, cols, rows, *full_input, *full_time, *full_hidden)
+        limit=24,
+    )(returned, encode, cols, rows, *full_input, *full_hidden, *full_time)
     landed = lax.all_to_all(outgoing, ("shard", "rep"), split_axis=0, concat_axis=0, tiled=True)
 
-    embed = call(
+    embed, part = call(
         run(attend_kernel, plan),
-        [sds((events, width), BF16)],
-        [SMEM] + [VMEM] * (2 + 2 * reps),
+        [sds((events, width), BF16), sds((stored, piece), BF16)],
+        [SMEM] + [VMEM] * (3 + 2 * reps),
         2 * events * width * 3 * width,
         4 << 20,
         "attend",
-        scratch=[pltpu.VMEM((events, width), BF16), pltpu.VMEM((events, 2 * width), BF16)],
-        limit=24,
-    )(neighbour_blocks, hnew, hdst, *full_query, *full_keyval)[0]
+        scratch=[
+            pltpu.VMEM((events, width), BF16),
+            pltpu.VMEM((events, 2 * width), BF16),
+        ],
+        limit=12,
+    )(neighbour_blocks, hnew, hdst, memory, *full_query, *full_keyval)
 
     me = lax.axis_index("rep")
     stack = jnp.stack([x[:, : plan.pad] for x in everyone])
@@ -381,8 +384,8 @@
         2 * stored * owners * reps * plan.pad * piece * 2,
         4 << 20,
         "apply",
-        limit=32,
-    )(ids, landed.reshape(owners * reps * plan.pad, piece), memory)[0]
+        limit=16,
+    )(ids, landed.reshape(owners * reps * plan.pad, piece), part)[0]
     new_memory = call(
         run(join_kernel, plan), [sds((stored, width), BF16)], [VMEM] * reps, 1 << 20, 2 << 20, "join", limit=8
     )(*spread([quarter], reps)[0])[0]

time: 116 us -> 87 us (0.75)
  waiting for transfers between devices: 44.7 us -> 25.2 us
  blocking collectives: 13.5 us -> 0 us
  starting transfers between devices: 19 us -> 25.7 us
  local copies, waits for them, and re-layouts: 21.3 us -> 17.5 us
    ppermute x21, waiting for transfers between devices: 34.7 us -> 14.5 us  [swap(): return lax.ppermute(x, 'rep', [(i, i ^ bit) for i in range(reps)])]
    all_to_all x1 -> x0, blocking collectives: 13.5 us -> none  [shards(): lax.all_to_all(request, 'shard', split_axis=0, concat_axis=0, tiled=True)]
    all_to_all x1, waiting for transfers between devices: 9.96 us -> 3.66 us  [shards(): lax.all_to_all(outgoing, ('shard', 'rep'), split_axis=0, concat_axis=0, t...]
    all_to_all x0 -> x1, starting transfers between devices: none -> 6.29 us  [shards(): lax.all_to_all(request, 'shard', split_axis=0, concat_axis=0, tiled=True)]
    all_to_all x0 -> x1, waiting for transfers between devices: none -> 4.39 us  [shards(): lax.all_to_all(request, 'shard', split_axis=0, concat_axis=0, tiled=True)]
    unnamed x71, local copies, waits for them, and re-layouts: 20.6 us -> 16.8 us
    all_to_all x1, waiting for transfers between devices: 0.01 us -> 2.6 us  [shards(): lax.all_to_all(served, 'shard', split_axis=0, concat_axis=0, tiled=True)]
    ppermute x21, starting transfers between devices: 10.7 us -> 12.1 us  [swap(): return lax.ppermute(x, 'rep', [(i, i ^ bit) for i in range(reps)])]
  transfers between devices with their start and end apart: 23 -> 24, of which waited for: 9 -> 10; matrix products, arithmetic and copies ran while one was open for 1% -> 1% of each run, Pallas kernels for 11% -> 17%
where the time goes in v4:
time: 87 us; the launch traced here: 86.2 us
  starting transfers between devices  25.7 us (30%)
  waiting for transfers between devices  25.2 us (29%)
  local copies, waits for them, and re-layouts  17.5 us (20%)
  Pallas kernels  16.9 us (19%)
  between operations  0.91 us (1%)
    unnamed x71, local copies, waits for them, and re-layouts  16.8 us
    ppermute x21, waiting for transfers between devices, swap(): return lax.ppermute(x, 'rep', [(i, i ^ bit) for i in range(reps)])  14.5 us
    ppermute x21, starting transfers between devices, swap(): return lax.ppermute(x, 'rep', [(i, i ^ bit) for i in range(reps)])  12.1 us
    all_to_all x1, starting transfers between devices, shards(): lax.all_to_all(request, 'shard', split_axis=0, concat_axis=0, tiled=True)  6.29 us
    pallas_call x1, Pallas kernels, shards(): call(run(gru_kernel, plan), [sds((owners * reps, plan.pad, piece), BF16),...  6.16 us
    all_to_all x1, waiting for transfers between devices, shards(): lax.all_to_all(request, 'shard', split_axis=0, concat_axis=0, tiled=True)  4.39 us
    pallas_call x1, Pallas kernels, shards(): call(run(attend_kernel, plan), [sds((events, width), BF16), sds((stored,...  4.09 us
    all_to_all x1, starting transfers between devices, shards(): lax.all_to_all(served, 'shard', split_axis=0, concat_axis=0, tiled=True)  3.68 us
  transfers between devices with their start and end apart: 24, of which 10 were waited for; matrix products, arithmetic and copies ran while one was open for 1% of the time, Pallas kernels for 17%

profile of v4, /device:TPU:0, one launch (start us, length us, event | category | flops | bytes accessed | tf_op | source)
XLA Modules:
  0.0 86.2 jit_solution(13701906543435367220)
XLA Ops:
  0.6 3.0 %collective-permute-start.1 = (bf16[512,384]{1,0:T(8,128)(2,1)}, bf16[512,384]{1,0:T(8,128)(2,1)S(1)}, u32[]{:S(2)}, u32[]{:S(2)}) collective-permute-start(bf16[512,384]{1,0:T(8,128)(2,1)} %refs_0_.2), channel_id=1, source_target_pairs={{0,2},{1,3},{2,0},{3,1},{4,6},{5,7},{6,4},{7,5},{8,10},{9,11},{10,... | collective-permute-start | bytes 1179656 | tf_op jit(solution)/shard_map/ppermute | solution.py:267
  4.4 1.0 %request.1 = s32[8,128]{1,0:T(8,128)} custom-call(s32[1,256]{1,0:T(1,128)S(1)} %bitcast.26, s32[1,256]{1,0:T(1,128)S(1)} %bitcast.25), custom_call_target="tpu_custom_call" | custom-call | flops 1048576 | bytes 16384 | tf_op jit(solution)/shard_map/request/pallas_call | solution.py:309
  5.4 6.3 %all-to-all-start = ((s32[8,1,128]{2,1,0:T(1,128)}), s32[8,1,128]{2,1,0:T(1,128)S(1)}, u32[]{:S(2)}, u32[]{:S(2)}) async-start(s32[8,1,128]{2,1,0:T(1,128)} %bitcast.3), calls=%async_computation | async-start | bytes 8192 | tf_op jit(solution)/shard_map/all_to_all | solution.py:317
  12.2 1.5 %collective-permute-start.7 = (bf16[128,384]{1,0:T(8,128)(2,1)}, bf16[128,384]{1,0:T(8,128)(2,1)S(1)}, u32[]{:S(2)}, u32[]{:S(2)}) collective-permute-start(bf16[128,384]{1,0:T(8,128)(2,1)} %refs_8_.1), channel_id=1, source_target_pairs={{0,2},{1,3},{2,0},{3,1},{4,6},{5,7},{6,4},{7,5},{8,10},{9,11},{10,... | collective-permute-start | bytes 294920 | tf_op jit(solution)/shard_map/ppermute | solution.py:267
  13.7 4.4 %all-to-all-done = s32[8,1,128]{2,1,0:T(1,128)S(1)} async-done(((s32[8,1,128]{2,1,0:T(1,128)}), s32[8,1,128]{2,1,0:T(1,128)S(1)}, u32[]{:S(2)}, u32[]{:S(2)}) %all-to-all-start) | async-done | bytes 4128 | tf_op jit(solution)/shard_map/all_to_all | solution.py:317
  18.0 1.2 %copy-done = bf16[1024,512]{1,0:T(8,128)(2,1)S(1)} copy-done((bf16[1024,512]{1,0:T(8,128)(2,1)S(1)}, bf16[1024,512]{1,0:T(8,128)(2,1)}, u32[]{:S(2)}) %copy-start) | copy-done | bytes 1048600
  19.3 1.9 %serve.1 = bf16[8,264,128]{2,1,0:T(8,128)(2,1)} custom-call(s32[8,128]{1,0:T(8,128)S(1)} %bitcast.21, bf16[1024,512]{1,0:T(8,128)(2,1)S(1)} %copy-done), custom_call_target="tpu_custom_call" | custom-call | flops 553648128 | bytes 1589248 | tf_op jit(solution)/shard_map/serve/pallas_call | solution.py:335
  21.2 3.7 %all-to-all-start.1 = ((bf16[8,264,128]{2,1,0:T(8,128)(2,1)}), bf16[8,264,128]{2,1,0:T(8,128)(2,1)S(1)}, u32[]{:S(2)}, u32[]{:S(2)}) async-start(bf16[8,264,128]{2,1,0:T(8,128)(2,1)} %serve.1), calls=%async_computation.1 | async-start | bytes 1081344 | tf_op jit(solution)/shard_map/all_to_all | solution.py:344
  26.4 1.2 %index.1 = (bf16[384,128]{1,0:T(8,128)(2,1)S(1)}, f32[384,8]{1,0:T(8,128)S(1)}, s32[8,384]{1,0:T(8,128)S(1)}) custom-call(s32[1,256]{1,0:T(1,128)S(1)} %bitcast.27, s32[1,1408]{1,0:T(1,128)S(1)} %reshape.45.packed_ref, f32[1,128]{1,0:T(1,128)S(1)} %bitcast.28, f32[1,128]{1,0:T(1,128)S(1)} %bitcast.29), custom_call_target="tpu_custom_call" | custom-call | flops 8589934592 | bytes 262144 | tf_op jit(solution)/shard_map/index/pallas_call | solution.py:318
  30.7 0.9 %collective-permute-done.8.refs_11_ = bf16[128,384]{1,0:T(8,128)(2,1)S(1)} collective-permute-done((bf16[128,384]{1,0:T(8,128)(2,1)S(1)}, bf16[128,384]{1,0:T(8,128)(2,1)S(1)}, u32[]{:S(2)}, u32[]{:S(2)}) %collective-permute-start.8) | collective-permute-done | bytes 98336 | tf_op jit(solution)/shard_map/ppermute | solution.py:267
  32.3 1.5 %collective-permute-start.13 = (bf16[512,256]{1,0:T(8,128)(2,1)S(1)}, bf16[512,256]{1,0:T(8,128)(2,1)S(1)}, u32[]{:S(2)}, u32[]{:S(2)}) collective-permute-start(bf16[512,256]{1,0:T(8,128)(2,1)S(1)} %copy-done.2), channel_id=1, source_target_pairs={{0,2},{1,3},{2,0},{3,1},{4,6},{5,7},{6,4},{7,5},{8,10},{9,11},{10,... | collective-permute-start | bytes 786440 | tf_op jit(solution)/shard_map/ppermute | solution.py:267
  35.3 2.6 %all-to-all-done.1.ret_ref = bf16[8,264,128]{2,1,0:T(8,128)(2,1)S(1)} async-done(((bf16[8,264,128]{2,1,0:T(8,128)(2,1)}), bf16[8,264,128]{2,1,0:T(8,128)(2,1)S(1)}, u32[]{:S(2)}, u32[]{:S(2)}) %all-to-all-start.1) | async-done | bytes 540704 | tf_op jit(solution)/shard_map/all_to_all | solution.py:344
  38.0 1.0 %copy-done.9 = bf16[512,384]{1,0:T(8,128)(2,1)S(1)} copy-done((bf16[512,384]{1,0:T(8,128)(2,1)S(1)}, bf16[512,384]{1,0:T(8,128)(2,1)}, u32[]{:S(2)}) %copy-start.9) | copy-done | bytes 393240
  38.9 1.0 %copy-done.11 = bf16[512,384]{1,0:T(8,128)(2,1)S(1)} copy-done((bf16[512,384]{1,0:T(8,128)(2,1)S(1)}, bf16[512,384]{1,0:T(8,128)(2,1)}, u32[]{:S(2)}) %copy-start.11) | copy-done | bytes 393240
  39.9 1.0 %copy-done.13 = bf16[512,384]{1,0:T(8,128)(2,1)S(1)} copy-done((bf16[512,384]{1,0:T(8,128)(2,1)S(1)}, bf16[512,384]{1,0:T(8,128)(2,1)}, u32[]{:S(2)}) %copy-start.13) | copy-done | bytes 393240
  40.9 0.9 %copy-done.17 = bf16[128,384]{1,0:T(8,128)(2,1)S(1)} copy-done((bf16[128,384]{1,0:T(8,128)(2,1)S(1)}, bf16[128,384]{1,0:T(8,128)(2,1)}, u32[]{:S(2)}) %copy-start.17) | copy-done | bytes 98328
  41.8 0.9 %copy-done.19 = bf16[128,384]{1,0:T(8,128)(2,1)S(1)} copy-done((bf16[128,384]{1,0:T(8,128)(2,1)S(1)}, bf16[128,384]{1,0:T(8,128)(2,1)}, u32[]{:S(2)}) %copy-start.19) | copy-done | bytes 98328
  42.7 0.9 %copy-done.21 = bf16[128,384]{1,0:T(8,128)(2,1)S(1)} copy-done((bf16[128,384]{1,0:T(8,128)(2,1)S(1)}, bf16[128,384]{1,0:T(8,128)(2,1)}, u32[]{:S(2)}) %copy-start.21) | copy-done | bytes 98328
  44.5 0.9 %copy-done.27 = f32[384,8]{1,0:T(8,128)S(1)} copy-done((f32[384,8]{1,0:T(8,128)S(1)}, f32[384,8]{1,0:T(8,128)}, u32[]{:S(2)}) %copy-start.27) | copy-done | bytes 12312
  46.3 6.2 %gru.1 = (bf16[32,72,128]{2,1,0:T(8,128)(2,1)}, f32[384,512]{1,0:T(8,128)S(1)}, bf16[384,512]{1,0:T(8,128)(2,1)S(1)}) custom-call(bf16[8,264,128]{2,1,0:T(8,128)(2,1)S(1)} %all-to-all-done.1.ret_ref, bf16[384,128]{1,0:T(8,128)(2,1)S(1)} %copy-done.29, f32[384,8]{1,0:T(8,128)S(1)} %copy-done.27, s32[8,384]{1,0:T(8,128)S(1)} %get-tuple-element.12.row_ref, ...), custom_call_target="tpu_custom_call" | custom-call | flops 1207959552 | bytes 8388608 | tf_op jit(solution)/shard_map/gru/pallas_call | solution.py:346
  52.5 3.6 %all-to-all-start.2 = ((bf16[32,72,128]{2,1,0:T(8,128)(2,1)}), bf16[32,72,128]{2,1,0:T(8,128)(2,1)S(1)}, u32[]{:S(2)}, u32[]{:S(2)}) async-start(bf16[32,72,128]{2,1,0:T(8,128)(2,1)} %get-tuple-element.16), calls=%async_computation.2 | async-start | bytes 1179648 | tf_op jit(solution)/shard_map/all_to_all | solution.py:360
  56.1 1.8 %collective-permute-start.16 = (s32[8,128]{1,0:T(8,128)S(1)}, s32[8,128]{1,0:T(8,128)S(1)}, u32[]{:S(2)}, u32[]{:S(2)}) collective-permute-start(s32[8,128]{1,0:T(8,128)S(1)} %bitcast.22), channel_id=1, source_target_pairs={{0,2},{1,3},{2,0},{3,1},{4,6},{5,7},{6,4},{7,5},{8,10},{9,11},{10,... | collective-permute-start | bytes 12296 | tf_op jit(solution)/shard_map/ppermute | solution.py:267
  58.0 3.1 %collective-permute-done.16 = s32[8,128]{1,0:T(8,128)S(1)} collective-permute-done((s32[8,128]{1,0:T(8,128)S(1)}, s32[8,128]{1,0:T(8,128)S(1)}, u32[]{:S(2)}, u32[]{:S(2)}) %collective-permute-start.16) | collective-permute-done | bytes 4128 | tf_op jit(solution)/shard_map/ppermute | solution.py:267
  61.0 1.2 %collective-permute-done.15 = s32[8,128]{1,0:T(8,128)S(1)} collective-permute-done((s32[8,128]{1,0:T(8,128)S(1)}, s32[8,128]{1,0:T(8,128)S(1)}, u32[]{:S(2)}, u32[]{:S(2)}) %collective-permute-start.15) | collective-permute-done | bytes 4128 | tf_op jit(solution)/shard_map/ppermute | solution.py:267
  64.4 4.1 %attend.1 = (bf16[384,512]{1,0:T(8,128)(2,1)}, bf16[1024,128]{1,0:T(8,128)(2,1)S(1)}) custom-call(s32[3,2]{1,0:T(4,128)S(1)} %copy.20.listed_ref, f32[384,512]{1,0:T(8,128)S(1)} %get-tuple-element.13.hnew_ref, bf16[384,512]{1,0:T(8,128)(2,1)S(1)} %get-tuple-element.14.hdst_ref, bf16[1024,512]{1,0:T(8,128)(2,1)S(1)} %copy-done.1, ...), custom_call_target="tpu_custom_call" | custom-call | flops 603979776 | bytes 4194304 | tf_op jit(solution)/shard_map/attend/pallas_call | solution.py:362
  69.2 3.7 %all-to-all-done.2 = bf16[32,72,128]{2,1,0:T(8,128)(2,1)S(1)} async-done(((bf16[32,72,128]{2,1,0:T(8,128)(2,1)}), bf16[32,72,128]{2,1,0:T(8,128)(2,1)S(1)}, u32[]{:S(2)}, u32[]{:S(2)}) %all-to-all-start.2) | async-done | bytes 589856 | tf_op jit(solution)/shard_map/all_to_all | solution.py:360
  72.9 0.9 %copy-done.15 = bf16[1024,128]{1,0:T(8,128)(2,1)S(1)} copy-done((bf16[1024,128]{1,0:T(8,128)(2,1)S(1)}, bf16[1024,128]{1,0:T(8,128)(2,1)}, u32[]{:S(2)}) %copy-start.15) | copy-done | bytes 262168
  73.8 1.4 %apply.1.refs_0_ = bf16[1024,128]{1,0:T(8,128)(2,1)S(1)} custom-call(s32[1,2304]{1,0:T(1,128)S(1)} %reshape.48.ids_ref, bf16[2304,128]{1,0:T(8,128)(2,1)S(1)} %bitcast.20, bf16[1024,128]{1,0:T(8,128)(2,1)S(1)} %copy-done.15), custom_call_target="tpu_custom_call" | custom-call | flops 1207959552 | bytes 4194304 | tf_op jit(solution)/shard_map/apply/pallas_call | solution.py:380
  75.2 1.2 %collective-permute-start.19 = (bf16[1024,128]{1,0:T(8,128)(2,1)S(1)}, bf16[1024,128]{1,0:T(8,128)(2,1)S(1)}, u32[]{:S(2)}, u32[]{:S(2)}) collective-permute-start(bf16[1024,128]{1,0:T(8,128)(2,1)S(1)} %apply.1.refs_0_), channel_id=1, source_target_pairs={{0,2},{1,3},{2,0},{3,1},{4,6},{5,7},{6,4},{7,5},{8,10},{9,11},{10,... | collective-permute-start | bytes 786440 | tf_op jit(solution)/shard_map/ppermute | solution.py:267
  76.5 7.0 %collective-permute-done.19.refs_2_ = bf16[1024,128]{1,0:T(8,128)(2,1)S(1)} collective-permute-done((bf16[1024,128]{1,0:T(8,128)(2,1)S(1)}, bf16[1024,128]{1,0:T(8,128)(2,1)S(1)}, u32[]{:S(2)}, u32[]{:S(2)}) %collective-permute-start.19) | collective-permute-done | bytes 262176 | tf_op jit(solution)/shard_map/ppermute | solution.py:267
  83.5 1.5 %collective-permute-done.20.refs_3_ = bf16[1024,128]{1,0:T(8,128)(2,1)S(1)} collective-permute-done((bf16[1024,128]{1,0:T(8,128)(2,1)S(1)}, bf16[1024,128]{1,0:T(8,128)(2,1)S(1)}, u32[]{:S(2)}, u32[]{:S(2)}) %collective-permute-start.20) | collective-permute-done | bytes 262176 | tf_op jit(solution)/shard_map/ppermute | solution.py:267
  85.0 1.2 %join.1 = bf16[1024,512]{1,0:T(8,128)(2,1)} custom-call(bf16[1024,128]{1,0:T(8,128)(2,1)S(1)} %apply.1.refs_0_, bf16[1024,128]{1,0:T(8,128)(2,1)S(1)} %collective-permute-done.18.refs_1_, bf16[1024,128]{1,0:T(8,128)(2,1)S(1)} %collective-permute-done.19.refs_2_, bf16[1024,128]{1,0:T(8,128)(2,1)S(1)} %collective-permute-done.20.refs_3_), custom_call_target="tpu_custom_call" | custom-call | flops 1048576 | bytes 2097152 | tf_op jit(solution)/shard_map/join/pallas_call | solution.py:389
  (106 shorter events, 12.7 us)
Async XLA Ops:
  0.6 24.4 %collective-permute-start.1 = (bf16[512,384]{1,0:T(8,128)(2,1)}, bf16[512,384]{1,0:T(8,128)(2,1)S(1)}, u32[]{:S(2)}, u32[]{:S(2)}) collective-permute-start(bf16[512,384]{1,0:T(8,128)(2,1)} %refs_0_.2), channel_id=1, source_target_pairs={{0,2},{1,3},{2,0},{3,1},{4,6},{5,7},{6,4},{7,5},{8,10},{9,11},{10,... | collective-permute-start | bytes 1179656 | tf_op jit(solution)/shard_map/ppermute | solution.py:267
  3.6 21.9 %collective-permute-start.4 = (bf16[512,384]{1,0:T(8,128)(2,1)}, bf16[512,384]{1,0:T(8,128)(2,1)S(1)}, u32[]{:S(2)}, u32[]{:S(2)}) collective-permute-start(bf16[512,384]{1,0:T(8,128)(2,1)} %refs_4_.2), channel_id=1, source_target_pairs={{0,2},{1,3},{2,0},{3,1},{4,6},{5,7},{6,4},{7,5},{8,10},{9,11},{10,... | collective-permute-start | bytes 1179656 | tf_op jit(solution)/shard_map/ppermute | solution.py:267
  5.4 12.7 %all-to-all-start = ((s32[8,1,128]{2,1,0:T(1,128)}), s32[8,1,128]{2,1,0:T(1,128)S(1)}, u32[]{:S(2)}, u32[]{:S(2)}) async-start(s32[8,1,128]{2,1,0:T(1,128)} %bitcast.3), calls=%async_computation | async-start | bytes 8192 | tf_op jit(solution)/shard_map/all_to_all | solution.py:317
  11.7 22.2 %collective-permute-start = (bf16[512,384]{1,0:T(8,128)(2,1)}, bf16[512,384]{1,0:T(8,128)(2,1)S(1)}, u32[]{:S(2)}, u32[]{:S(2)}) collective-permute-start(bf16[512,384]{1,0:T(8,128)(2,1)} %refs_0_.2), channel_id=1, source_target_pairs={{0,1},{1,0},{2,3},{3,2},{4,5},{5,4},{6,7},{7,6},{8,9},{9,8},{10,11... | collective-permute-start | bytes 1179656 | tf_op jit(solution)/shard_map/ppermute | solution.py:267
  11.7 23.0 %collective-permute-start.3 = (bf16[512,384]{1,0:T(8,128)(2,1)}, bf16[512,384]{1,0:T(8,128)(2,1)}, u32[]{:S(2)}, u32[]{:S(2)}) collective-permute-start(bf16[512,384]{1,0:T(8,128)(2,1)} %refs_4_.2), channel_id=1, source_target_pairs={{0,1},{1,0},{2,3},{3,2},{4,5},{5,4},{6,7},{7,6},{8,9},{9,8},{10,11... | collective-permute-start | bytes 1179656 | tf_op jit(solution)/shard_map/ppermute | solution.py:267
  12.2 12.7 %collective-permute-start.7 = (bf16[128,384]{1,0:T(8,128)(2,1)}, bf16[128,384]{1,0:T(8,128)(2,1)S(1)}, u32[]{:S(2)}, u32[]{:S(2)}) collective-permute-start(bf16[128,384]{1,0:T(8,128)(2,1)} %refs_8_.1), channel_id=1, source_target_pairs={{0,2},{1,3},{2,0},{3,1},{4,6},{5,7},{6,4},{7,5},{8,10},{9,11},{10,... | collective-permute-start | bytes 294920 | tf_op jit(solution)/shard_map/ppermute | solution.py:267
  21.1 3.7 %copy-start.34 = (s32[256]{0:T(256)S(1)}, s32[256]{0:T(256)}, u32[]{:S(2)}) copy-start(s32[256]{0:T(256)} %param.18) | copy-start | bytes 3076
  21.1 3.8 %copy-start.16 = (bf16[128,384]{1,0:T(8,128)(2,1)S(1)}, bf16[128,384]{1,0:T(8,128)(2,1)}, u32[]{:S(2)}) copy-start(bf16[128,384]{1,0:T(8,128)(2,1)} %refs_8_.1) | copy-start | bytes 294916
  21.2 16.8 %all-to-all-start.1 = ((bf16[8,264,128]{2,1,0:T(8,128)(2,1)}), bf16[8,264,128]{2,1,0:T(8,128)(2,1)S(1)}, u32[]{:S(2)}, u32[]{:S(2)}) async-start(bf16[8,264,128]{2,1,0:T(8,128)(2,1)} %serve.1), calls=%async_computation.1 | async-start | bytes 1081344 | tf_op jit(solution)/shard_map/all_to_all | solution.py:344
  24.9 4.8 %copy-start.18 = (bf16[128,384]{1,0:T(8,128)(2,1)}, bf16[128,384]{1,0:T(8,128)(2,1)S(1)}, u32[]{:S(2)}) copy-start(bf16[128,384]{1,0:T(8,128)(2,1)S(1)} %collective-permute-done.7.refs_10_) | copy-start | bytes 294916
  24.9 4.8 %collective-permute-start.6 = (bf16[128,384]{1,0:T(8,128)(2,1)S(1)}, bf16[128,384]{1,0:T(8,128)(2,1)S(1)}, u32[]{:S(2)}, u32[]{:S(2)}) collective-permute-start(bf16[128,384]{1,0:T(8,128)(2,1)S(1)} %copy-done.16), channel_id=1, source_target_pairs={{0,1},{1,0},{2,3},{3,2},{4,5},{5,4},{6,7},{7,6},{8,9},{9,8},{10,11... | collective-permute-start | bytes 294920 | tf_op jit(solution)/shard_map/ppermute | solution.py:267
  25.0 10.1 %collective-permute-start.2 = (bf16[512,384]{1,0:T(8,128)(2,1)S(1)}, bf16[512,384]{1,0:T(8,128)(2,1)}, u32[]{:S(2)}, u32[]{:S(2)}) collective-permute-start(bf16[512,384]{1,0:T(8,128)(2,1)S(1)} %collective-permute-done.1.refs_2_), channel_id=1, source_target_pairs={{0,1},{1,0},{2,3},{3,2},{4,5},{5,4},{6,7},{7,6},{8,9},{9,8},{10,11... | collective-permute-start | bytes 1179656 | tf_op jit(solution)/shard_map/ppermute | solution.py:267
  25.5 9.8 %collective-permute-start.5 = (bf16[512,384]{1,0:T(8,128)(2,1)S(1)}, bf16[512,384]{1,0:T(8,128)(2,1)}, u32[]{:S(2)}, u32[]{:S(2)}) collective-permute-start(bf16[512,384]{1,0:T(8,128)(2,1)S(1)} %collective-permute-done.4.refs_6_), channel_id=1, source_target_pairs={{0,1},{1,0},{2,3},{3,2},{4,5},{5,4},{6,7},{7,6},{8,9},{9,8},{10,11... | collective-permute-start | bytes 1179656 | tf_op jit(solution)/shard_map/ppermute | solution.py:267
  26.4 6.0 %copy-start.2 = (bf16[512,256]{1,0:T(8,128)(2,1)S(1)}, bf16[512,256]{1,0:T(8,128)(2,1)}, u32[]{:S(2)}) copy-start(bf16[512,256]{1,0:T(8,128)(2,1)} %refs_4_.3) | copy-start | bytes 786436
  26.4 8.3 %copy-start.3 = (bf16[512,128]{1,0:T(8,128)(2,1)S(1)}, bf16[512,128]{1,0:T(8,128)(2,1)}, u32[]{:S(2)}) copy-start(bf16[512,128]{1,0:T(8,128)(2,1)} %refs_0_.3) | copy-start | bytes 393220
  26.4 11.6 %copy-start.6 = (bf16[512,384]{1,0:T(8,128)(2,1)S(1)}, bf16[512,384]{1,0:T(8,128)(2,1)}, u32[]{:S(2)}) copy-start(bf16[512,384]{1,0:T(8,128)(2,1)} %refs_0_.2) | copy-start | bytes 1179652
  26.4 11.6 %copy-start.7 = (bf16[512,384]{1,0:T(8,128)(2,1)S(1)}, bf16[512,384]{1,0:T(8,128)(2,1)}, u32[]{:S(2)}) copy-start(bf16[512,384]{1,0:T(8,128)(2,1)} %refs_4_.2) | copy-start | bytes 1179652
  30.4 1.3 %collective-permute-start.8 = (bf16[128,384]{1,0:T(8,128)(2,1)S(1)}, bf16[128,384]{1,0:T(8,128)(2,1)S(1)}, u32[]{:S(2)}, u32[]{:S(2)}) collective-permute-start(bf16[128,384]{1,0:T(8,128)(2,1)S(1)} %collective-permute-done.7.refs_10_), channel_id=1, source_target_pairs={{0,1},{1,0},{2,3},{3,2},{4,5},{5,4},{6,7},{7,6},{8,9},{9,8},{10,11... | collective-permute-start | bytes 294920 | tf_op jit(solution)/shard_map/ppermute | solution.py:267
  32.3 30.4 %collective-permute-start.13 = (bf16[512,256]{1,0:T(8,128)(2,1)S(1)}, bf16[512,256]{1,0:T(8,128)(2,1)S(1)}, u32[]{:S(2)}, u32[]{:S(2)}) collective-permute-start(bf16[512,256]{1,0:T(8,128)(2,1)S(1)} %copy-done.2), channel_id=1, source_target_pairs={{0,2},{1,3},{2,0},{3,1},{4,6},{5,7},{6,4},{7,5},{8,10},{9,11},{10,... | collective-permute-start | bytes 786440 | tf_op jit(solution)/shard_map/ppermute | solution.py:267
  34.6 29.5 %collective-permute-start.12 = (bf16[512,256]{1,0:T(8,128)(2,1)S(1)}, bf16[512,256]{1,0:T(8,128)(2,1)}, u32[]{:S(2)}, u32[]{:S(2)}) collective-permute-start(bf16[512,256]{1,0:T(8,128)(2,1)S(1)} %copy-done.2), channel_id=1, source_target_pairs={{0,1},{1,0},{2,3},{3,2},{4,5},{5,4},{6,7},{7,6},{8,9},{9,8},{10,11... | collective-permute-start | bytes 786440 | tf_op jit(solution)/shard_map/ppermute | solution.py:267
  34.6 27.8 %collective-permute-start.10 = (bf16[512,128]{1,0:T(8,128)(2,1)S(1)}, bf16[512,128]{1,0:T(8,128)(2,1)}, u32[]{:S(2)}, u32[]{:S(2)}) collective-permute-start(bf16[512,128]{1,0:T(8,128)(2,1)S(1)} %copy-done.3), channel_id=1, source_target_pairs={{0,2},{1,3},{2,0},{3,1},{4,6},{5,7},{6,4},{7,5},{8,10},{9,11},{10,... | collective-permute-start | bytes 393224 | tf_op jit(solution)/shard_map/ppermute | solution.py:267
  35.2 28.9 %collective-permute-start.9 = (bf16[512,128]{1,0:T(8,128)(2,1)S(1)}, bf16[512,128]{1,0:T(8,128)(2,1)}, u32[]{:S(2)}, u32[]{:S(2)}) collective-permute-start(bf16[512,128]{1,0:T(8,128)(2,1)S(1)} %copy-done.3), channel_id=1, source_target_pairs={{0,1},{1,0},{2,3},{3,2},{4,5},{5,4},{6,7},{7,6},{8,9},{9,8},{10,11... | collective-permute-start | bytes 393224 | tf_op jit(solution)/shard_map/ppermute | solution.py:267
  52.5 11.9 %copy-start.1 = (bf16[1024,512]{1,0:T(8,128)(2,1)S(1)}, bf16[1024,512]{1,0:T(8,128)(2,1)}, u32[]{:S(2)}) copy-start(bf16[1024,512]{1,0:T(8,128)(2,1)} %memory_ref.3) | copy-start | bytes 3145732
  52.5 20.4 %all-to-all-start.2 = ((bf16[32,72,128]{2,1,0:T(8,128)(2,1)}), bf16[32,72,128]{2,1,0:T(8,128)(2,1)S(1)}, u32[]{:S(2)}, u32[]{:S(2)}) async-start(bf16[32,72,128]{2,1,0:T(8,128)(2,1)} %get-tuple-element.16), calls=%async_computation.2 | async-start | bytes 1179648 | tf_op jit(solution)/shard_map/all_to_all | solution.py:360
  56.1 4.9 %collective-permute-start.16 = (s32[8,128]{1,0:T(8,128)S(1)}, s32[8,128]{1,0:T(8,128)S(1)}, u32[]{:S(2)}, u32[]{:S(2)}) collective-permute-start(s32[8,128]{1,0:T(8,128)S(1)} %bitcast.22), channel_id=1, source_target_pairs={{0,2},{1,3},{2,0},{3,1},{4,6},{5,7},{6,4},{7,5},{8,10},{9,11},{10,... | collective-permute-start | bytes 12296 | tf_op jit(solution)/shard_map/ppermute | solution.py:267
  61.0 1.2 %collective-permute-start.15 = (s32[8,128]{1,0:T(8,128)S(1)}, s32[8,128]{1,0:T(8,128)S(1)}, u32[]{:S(2)}, u32[]{:S(2)}) collective-permute-start(s32[8,128]{1,0:T(8,128)S(1)} %bitcast.24), channel_id=1, source_target_pairs={{0,1},{1,0},{2,3},{3,2},{4,5},{5,4},{6,7},{7,6},{8,9},{9,8},{10,11... | collective-permute-start | bytes 12296 | tf_op jit(solution)/shard_map/ppermute | solution.py:267
  62.2 1.2 %collective-permute-start.17 = (s32[8,128]{1,0:T(8,128)S(1)}, s32[8,128]{1,0:T(8,128)S(1)}, u32[]{:S(2)}, u32[]{:S(2)}) collective-permute-start(s32[8,128]{1,0:T(8,128)S(1)} %collective-permute-done.16), channel_id=1, source_target_pairs={{0,1},{1,0},{2,3},{3,2},{4,5},{5,4},{6,7},{7,6},{8,9},{9,8},{10,11... | collective-permute-start | bytes 12296 | tf_op jit(solution)/shard_map/ppermute | solution.py:267
  62.4 1.7 %collective-permute-start.11 = (bf16[512,128]{1,0:T(8,128)(2,1)}, bf16[512,128]{1,0:T(8,128)(2,1)}, u32[]{:S(2)}, u32[]{:S(2)}) collective-permute-start(bf16[512,128]{1,0:T(8,128)(2,1)} %collective-permute-done.10.refs_2_), channel_id=1, source_target_pairs={{0,1},{1,0},{2,3},{3,2},{4,5},{5,4},{6,7},{7,6},{8,9},{9,8},{10,11... | collective-permute-start | bytes 393224 | tf_op jit(solution)/shard_map/ppermute | solution.py:267
  62.7 1.7 %collective-permute-start.14 = (bf16[512,256]{1,0:T(8,128)(2,1)S(1)}, bf16[512,256]{1,0:T(8,128)(2,1)}, u32[]{:S(2)}, u32[]{:S(2)}) collective-permute-start(bf16[512,256]{1,0:T(8,128)(2,1)S(1)} %collective-permute-done.13.refs_6_), channel_id=1, source_target_pairs={{0,1},{1,0},{2,3},{3,2},{4,5},{5,4},{6,7},{7,6},{8,9},{9,8},{10,11... | collective-permute-start | bytes 786440 | tf_op jit(solution)/shard_map/ppermute | solution.py:267
  75.2 8.3 %collective-permute-start.19 = (bf16[1024,128]{1,0:T(8,128)(2,1)S(1)}, bf16[1024,128]{1,0:T(8,128)(2,1)S(1)}, u32[]{:S(2)}, u32[]{:S(2)}) collective-permute-start(bf16[1024,128]{1,0:T(8,128)(2,1)S(1)} %apply.1.refs_0_), channel_id=1, source_target_pairs={{0,2},{1,3},{2,0},{3,1},{4,6},{5,7},{6,4},{7,5},{8,10},{9,11},{10,... | collective-permute-start | bytes 786440 | tf_op jit(solution)/shard_map/ppermute | solution.py:267
  76.4 7.1 %collective-permute-start.18 = (bf16[1024,128]{1,0:T(8,128)(2,1)S(1)}, bf16[1024,128]{1,0:T(8,128)(2,1)S(1)}, u32[]{:S(2)}, u32[]{:S(2)}) collective-permute-start(bf16[1024,128]{1,0:T(8,128)(2,1)S(1)} %apply.1.refs_0_), channel_id=1, source_target_pairs={{0,1},{1,0},{2,3},{3,2},{4,5},{5,4},{6,7},{7,6},{8,9},{9,8},{10,11... | collective-permute-start | bytes 786440 | tf_op jit(solution)/shard_map/ppermute | solution.py:267
  83.5 1.5 %collective-permute-start.20 = (bf16[1024,128]{1,0:T(8,128)(2,1)S(1)}, bf16[1024,128]{1,0:T(8,128)(2,1)S(1)}, u32[]{:S(2)}, u32[]{:S(2)}) collective-permute-start(bf16[1024,128]{1,0:T(8,128)(2,1)S(1)} %collective-permute-done.19.refs_2_), channel_id=1, source_target_pairs={{0,1},{1,0},{2,3},{3,2},{4,5},{5,4},{6,7},{7,6},{8,9},{9,8},{10,11... | collective-permute-start | bytes 786440 | tf_op jit(solution)/shard_map/ppermute | solution.py:267
  (27 other events, 33.9 us)

commit v5 on v4

--- a/solution.py
+++ b/solution.py
@@ -51,6 +51,7 @@
         self.main = self.cap - self.tail if self.tail else -(-self.cap // 16) * 16
         self.rows = self.owners * (self.main + self.tail)
         self.pad = -(-self.cap // 8) * 8
+        self.pairs = owners <= 8 and owners & (owners - 1) == 0
 
 
 def rank_of(own_col, own_row, entries):
@@ -87,9 +88,10 @@
     own_col = to_col(own_row, plan.entries)
     _, place = rank_of(own_col, own_row, plan.entries)
     tick = to_col(tick_row, plan.entries)
-    spot = own_col * plan.main + place
+    slot = own_col ^ lax.axis_index("shard") if plan.pairs else own_col
+    spot = slot * plan.main + place
     if plan.tail:
-        spare = plan.owners * plan.main + (place - plan.main) * plan.owners + own_col
+        spare = plan.owners * plan.main + (place - plan.main) * plan.owners + slot
         spot = jnp.where(place < plan.main, spot, spare)
     back = own_col * plan.pad + place
     isrc = iota((plan.entries, events), 0) == src_row
@@ -120,24 +122,32 @@
     return jnp.where((inner * plan.owners + owner) == here, 1.0, 0.0).astype(BF16)
 
 
-def serve_kernel(plan, asked_ref, memory_ref, out_ref):
+def at_slot(refs, s):
+    return refs[s] if len(refs) > 1 else refs[0].at[s]
+
+
+def serve_kernel(plan, asked_ref, memory_ref, *out_refs):
     stored, width = memory_ref.shape
     piece = width // 4
-    asked = asked_ref[...].astype(F32)
-    turned = asked.T
+    if plan.pairs:
+        me = lax.axis_index("shard")
+        asked = jnp.concatenate([asked_ref[pl.ds(me ^ k, 1), :] for k in range(plan.owners)], axis=0)
+    else:
+        asked = asked_ref[...]
+    turned = asked.astype(F32).T
     blocks = [
         jnp.where(turned[: plan.main, s : s + 1].astype(I32) == iota((plan.main, stored), 1), 1.0, 0.0)
         for s in range(plan.owners)
     ]
     for i in range(plan.tail):
-        spare = asked_ref[:, plan.main + i : plan.main + i + 1]
+        spare = asked[:, plan.main + i : plan.main + i + 1]
         blocks.append(jnp.where(spare == iota((plan.owners, stored), 1), 1.0, 0.0))
     hot = jnp.concatenate(blocks, axis=0).astype(BF16)
     rows = dot(hot, memory_ref[...])
     main = plan.main
     for s in range(plan.owners):
         for c in range(4):
-            out_ref[s, c * main : (c + 1) * main, :] = rows[
+            at_slot(out_refs, s)[c * main : (c + 1) * main, :] = rows[
                 s * main : (s + 1) * main, c * piece : (c + 1) * piece
             ].astype(BF16)
     if plan.tail:
@@ -145,21 +155,21 @@
         stack = jnp.concatenate([spare[:, c * piece : (c + 1) * piece] for c in range(4)], axis=0)
         ordered = dot(tail_order(plan, True), stack.astype(BF16))
         for s in range(plan.owners):
-            out_ref[s, 4 * main : 4 * (main + plan.tail), :] = ordered[
+            at_slot(out_refs, s)[4 * main : 4 * (main + plan.tail), :] = ordered[
                 s * 4 * plan.tail : (s + 1) * 4 * plan.tail
             ].astype(BF16)
 
 
-def table_of(plan, ret_ref):
+def table_of(plan, refs):
     main = plan.main
     pieces = [
-        jnp.concatenate([ret_ref[s, c * main : (c + 1) * main, :] for s in range(plan.owners)], axis=0)
+        jnp.concatenate([at_slot(refs, s)[c * main : (c + 1) * main, :] for s in range(plan.owners)], axis=0)
         for c in range(4)
     ]
     table = jnp.concatenate(pieces, axis=1)
     if plan.tail:
         stack = jnp.concatenate(
-            [ret_ref[s, 4 * main : 4 * (main + plan.tail), :].astype(F32) for s in range(plan.owners)], axis=0
+            [at_slot(refs, s)[4 * main : 4 * (main + plan.tail), :].astype(F32) for s in range(plan.owners)], axis=0
         )
         ordered = dot(tail_order(plan, False), stack.astype(BF16))
         count = plan.tail * plan.owners
@@ -168,8 +178,10 @@
     return table
 
 
-def gru_kernel(plan, ret_ref, enc_ref, col_ref, row_ref, *refs):
+def gru_kernel(plan, enc_ref, col_ref, row_ref, *refs):
     reps = plan.reps
+    slots = plan.owners if plan.pairs else 1
+    rows, refs = refs[:slots], refs[slots:]
     w_in, w_hid, w_time = refs[:reps], refs[reps : 2 * reps], refs[2 * reps : 3 * reps]
     out_ref, hnew_ref, hdst_ref, gin, ghid, delta = refs[3 * reps :]
     me = lax.axis_index("rep")
@@ -177,17 +189,21 @@
     piece = width // reps
     cols = col_ref[...].astype(I32)
     spots = iota((events, plan.rows), 1)
-    table = table_of(plan, ret_ref)
+    table = table_of(plan, rows)
     hsrc = dot(jnp.where(cols[:, 0:1] == spots, 1.0, 0.0).astype(BF16), table)
     source = hsrc.astype(BF16)
     target = dot(jnp.where(cols[:, 1:2] == spots, 1.0, 0.0).astype(BF16), table).astype(BF16)
     hdst_ref[...] = target
     enc = enc_ref[...]
     part = w_in[0].shape[1]
-    for k in range(reps):
-        at = pl.ds(pl.multiple_of((me ^ k) * part, LANES), part)
-        gin[:, at] = dot(target, w_in[k][...]) + dot(enc, w_time[k][...])
-        ghid[:, at] = dot(source, w_hid[k][...])
+    for k in range(0, reps, 2):
+        both = [jnp.concatenate([w[k][...], w[k + 1][...]], axis=1) for w in (w_in, w_time, w_hid)]
+        into = dot(target, both[0]) + dot(enc, both[1])
+        hidden = dot(source, both[2])
+        for j in range(2):
+            at = pl.ds(pl.multiple_of((me ^ (k + j)) * part, LANES), part)
+            gin[:, at] = into[:, j * part : (j + 1) * part]
+            ghid[:, at] = hidden[:, j * part : (j + 1) * part]
     step = 64
     for i in range(0, events, step):
         at = slice(i, i + step)
@@ -197,15 +213,12 @@
         hold = hsrc[at]
         new = (1.0 - update) * fresh + update * hold
         hnew_ref[at, :] = new
-        delta[at, :] = new - hold
-    change = delta[...]
-    high = change.astype(BF16)
-    low = (change - high.astype(F32)).astype(BF16)
+        delta[at, :] = (new - hold).astype(BF16)
     slots = plan.owners * plan.pad
     hits = jnp.where(row_ref[0:1, :] == iota((slots, events), 0), 1.0, 0.0)
     counts = jnp.maximum(jnp.sum(hits, axis=1, keepdims=True), 1.0)
     hits = hits.astype(BF16)
-    mean = (dot(hits, high) + dot(hits, low)) / counts
+    mean = dot(hits, delta[...]) / counts
     for o in range(plan.owners):
         for q in range(reps):
             out_ref[o * reps + q] = mean[o * plan.pad : (o + 1) * plan.pad, q * piece : (q + 1) * piece].astype(BF16)
@@ -243,16 +256,21 @@
             out_ref[at, lane] = (hnew_ref[at, lane] + dot(prob, values)).astype(BF16)
 
 
-def apply_kernel(plan, ids_ref, landed_ref, part_ref, out_ref):
+def apply_kernel(plan, ids_ref, landed_ref, part_ref, out_ref, held, sem):
+    copy = pltpu.make_async_copy(part_ref, held, sem)
+    copy.start()
     stored = part_ref.shape[0]
     count = landed_ref.shape[0]
     landed = landed_ref[...]
     step = min(256, stored)
     ids = ids_ref[...]
+    totals = []
     for i in range(0, stored, step):
         hot = jnp.where(iota((step, count), 0) + i == ids, 1.0, 0.0).astype(BF16)
-        total = dot(hot, landed)
-        out_ref[i : i + step, :] = (part_ref[i : i + step, :].astype(F32) + total).astype(BF16)
+        totals.append(dot(hot, landed))
+    copy.wait()
+    for i, total in zip(range(0, stored, step), totals):
+        out_ref[i : i + step, :] = (held[i : i + step, :].astype(F32) + total).astype(BF16)
 
 
 def join_kernel(plan, *refs):
@@ -331,32 +349,38 @@
     )
     everyone = [x for x in spread([asked], reps)[0]]
 
-    chunk = 4 * (plan.main + plan.tail)
+    chunk = (4 * (plan.main + plan.tail), width // 4)
     served = call(
         run(serve_kernel, plan),
-        [sds((owners, chunk, width // 4), BF16)],
+        [sds(chunk, BF16)] * owners if plan.pairs else [sds((owners,) + chunk, BF16)],
         [VMEM] * 2,
         2 * plan.rows * stored * width,
         2 * stored * width + 2 * plan.rows * width,
         "serve",
         limit=12,
-    )(asked, memory)[0]
-    returned = lax.all_to_all(served, "shard", split_axis=0, concat_axis=0, tiled=True)
+    )(asked, memory)
+    if plan.pairs:
+        returned = [served[0]] * owners
+        far = sorted(range(1, owners), key=lambda k: (k < owners // 2, k < owners * 3 // 4, k))
+        for k in far:
+            returned[k] = lax.ppermute(served[k], "shard", [(i, i ^ k) for i in range(owners)])
+    else:
+        returned = [lax.all_to_all(served[0], "shard", split_axis=0, concat_axis=0, tiled=True)]
 
     outgoing, hnew, hdst = call(
         run(gru_kernel, plan),
         [sds((owners * reps, plan.pad, piece), BF16), sds((events, width), F32), sds((events, width), BF16)],
-        [VMEM] * (4 + 3 * reps),
+        [VMEM] * (3 + len(returned) + 3 * reps),
         2 * events * width * 3 * width * 2,
         8 << 20,
         "gru",
         scratch=[
             pltpu.VMEM((events, 3 * width), F32),
             pltpu.VMEM((events, 3 * width), F32),
-            pltpu.VMEM((events, width), F32),
+            pltpu.VMEM((events, width), BF16),
         ],
         limit=24,
-    )(returned, encode, cols, rows, *full_input, *full_hidden, *full_time)
+    )(encode, cols, rows, *returned, *full_input, *full_hidden, *full_time)
     landed = lax.all_to_all(outgoing, ("shard", "rep"), split_axis=0, concat_axis=0, tiled=True)
 
     embed, part = call(
@@ -380,11 +404,12 @@
     quarter = call(
         run(apply_kernel, plan),
         [sds((stored, piece), BF16)],
-        [VMEM] * 3,
+        [VMEM] * 2 + [ANY],
         2 * stored * owners * reps * plan.pad * piece * 2,
         4 << 20,
         "apply",
-        limit=16,
+        scratch=[pltpu.VMEM((stored, piece), BF16), pltpu.SemaphoreType.DMA],
+        limit=60,
     )(ids, landed.reshape(owners * reps * plan.pad, piece), part)[0]
     new_memory = call(
         run(join_kernel, plan), [sds((stored, width), BF16)], [VMEM] * reps, 1 << 20, 2 << 20, "join", limit=8

time: 87 us -> 108 us (1.24)
  blocking collectives: 0 us -> 12.5 us
  local copies, waits for them, and re-layouts: 17.5 us -> 27.9 us
  waiting for transfers between devices: 25.2 us -> 23.3 us
    all_to_all x0 -> x1, blocking collectives: none -> 12.5 us  [shards(): lax.all_to_all(request, 'shard', split_axis=0, concat_axis=0, tiled=True)]
    all_to_all x2 -> x0, starting transfers between devices: 9.97 us -> none  [the longest x1 6.29 us: shards(): lax.all_to_all(request, 'shard', split_axis=0, concat_axis=0, tiled=True)]
    ppermute x0 -> x7, starting transfers between devices: none -> 8.7 us  [shards(): lax.ppermute(served[k], 'shard', [(i, i ^ k) for i in range(owners)])]
    ppermute x0 -> x7, waiting for transfers between devices: none -> 8.33 us  [shards(): lax.ppermute(served[k], 'shard', [(i, i ^ k) for i in range(owners)])]
    all_to_all x2 -> x0, waiting for transfers between devices: 6.98 us -> none  [the longest x1 4.39 us: shards(): lax.all_to_all(request, 'shard', split_axis=0, concat_axis=0, tiled=True)]
    unnamed x71 -> x89, local copies, waits for them, and re-layouts: 16.8 us -> 23.3 us
    all_to_all x1, waiting for transfers between devices: 3.66 us -> 0.01 us  [shards(): lax.all_to_all(outgoing, ('shard', 'rep'), split_axis=0, concat_axis=0, t...]
    transpose x1, local copies, waits for them, and re-layouts: 0.01 us -> 1.33 us  [shards(): ids = jnp.swapaxes(stack[order], 0, 1).reshape(1, owners * reps * plan.pad)]
  transfers between devices with their start and end apart: 24 -> 29, of which waited for: 10 -> 11; matrix products, arithmetic and copies ran while one was open for 1% -> 5% of each run, Pallas kernels for 17% -> 11%
where the time goes in v5:
time: 108 us; the launch traced here: 106 us
  local copies, waits for them, and re-layouts  27.9 us (26%)
  starting transfers between devices  24.9 us (23%)
  waiting for transfers between devices  23.3 us (22%)
  Pallas kernels  16.4 us (15%)
  blocking collectives  12.5 us (12%)
    unnamed x89, local copies, waits for them, and re-layouts  23.3 us
    ppermute x21, waiting for transfers between devices, swap(): return lax.ppermute(x, 'rep', [(i, i ^ bit) for i in range(reps)])  15 us
    all_to_all x1, blocking collectives, shards(): lax.all_to_all(request, 'shard', split_axis=0, concat_axis=0, tiled=True)  12.5 us
    ppermute x21, starting transfers between devices, swap(): return lax.ppermute(x, 'rep', [(i, i ^ bit) for i in range(reps)])  11.6 us
    ppermute x7, starting transfers between devices, shards(): lax.ppermute(served[k], 'shard', [(i, i ^ k) for i in range(owners)])  8.7 us
    ppermute x7, waiting for transfers between devices, shards(): lax.ppermute(served[k], 'shard', [(i, i ^ k) for i in range(owners)])  8.33 us
    pallas_call x1, Pallas kernels, shards(): call(run(gru_kernel, plan), [sds((owners * reps, plan.pad, piece), BF16),...  5.42 us
    all_to_all x1, starting transfers between devices, shards(): lax.all_to_all(outgoing, ('shard', 'rep'), split_axis=0, concat_axis=0, t...  4.62 us
  transfers between devices with their start and end apart: 29, of which 11 were waited for; matrix products, arithmetic and copies ran while one was open for 5% of the time, Pallas kernels for 11%

profile of v5, /device:TPU:0, one launch (start us, length us, event | category | flops | bytes accessed | tf_op | source)
XLA Modules:
  0.0 106.5 jit_solution(7254943714704273386)
XLA Ops:
  0.6 3.0 %collective-permute-start.11 = (bf16[512,384]{1,0:T(8,128)(2,1)}, bf16[512,384]{1,0:T(8,128)(2,1)S(1)}, u32[]{:S(2)}, u32[]{:S(2)}) collective-permute-start(bf16[512,384]{1,0:T(8,128)(2,1)} %refs_12_.1), channel_id=1, source_target_pairs={{0,2},{1,3},{2,0},{3,1},{4,6},{5,7},{6,4},{7,5},{8,10},{9,11},{10,... | collective-permute-start | bytes 1179656 | tf_op jit(solution)/shard_map/ppermute | solution.py:285
  4.8 12.5 %all_to_all.16 = s32[8,1,128]{2,1,0:T(1,128)S(1)} all-to-all(s32[8,1,128]{2,1,0:T(1,128)S(1)} %bitcast.24), channel_id=1, replica_groups=mesh['shard'=8,'rep'=4] {'shard'}, dimensions={0} | all-to-all | bytes 8192 | tf_op jit(solution)/shard_map/all_to_all | solution.py:335
  17.3 1.2 %copy-done = bf16[1024,512]{1,0:T(8,128)(2,1)S(1)} copy-done((bf16[1024,512]{1,0:T(8,128)(2,1)S(1)}, bf16[1024,512]{1,0:T(8,128)(2,1)}, u32[]{:S(2)}) %copy-start) | copy-done | bytes 1048600
  18.5 1.1 serve.1
  21.4 2.4 %collective-permute-start.2 = (bf16[264,128]{1,0:T(8,128)(2,1)S(1)}, bf16[264,128]{1,0:T(8,128)(2,1)S(1)}, u32[]{:S(2)}, u32[]{:S(2)}) collective-permute-start(bf16[264,128]{1,0:T(8,128)(2,1)S(1)} %get-tuple-element.24), channel_id=1, source_target_pairs={{0,12},{4,8},{8,4},{12,0},{16,28},{20,24},{24,20},{28,16},{1,13},{... | collective-permute-start | bytes 202760 | tf_op jit(solution)/shard_map/ppermute | solution.py:366
  26.3 2.4 %collective-permute-start.4 = (bf16[264,128]{1,0:T(8,128)(2,1)S(1)}, bf16[264,128]{1,0:T(8,128)(2,1)S(1)}, u32[]{:S(2)}, u32[]{:S(2)}) collective-permute-start(bf16[264,128]{1,0:T(8,128)(2,1)S(1)} %get-tuple-element.26), channel_id=1, source_target_pairs={{0,20},{4,16},{8,28},{12,24},{16,4},{20,0},{24,12},{28,8},{1,21},{... | collective-permute-start | bytes 202760 | tf_op jit(solution)/shard_map/ppermute | solution.py:366
  28.7 1.5 %collective-permute-start.14 = (bf16[128,384]{1,0:T(8,128)(2,1)S(1)}, bf16[128,384]{1,0:T(8,128)(2,1)S(1)}, u32[]{:S(2)}, u32[]{:S(2)}) collective-permute-start(bf16[128,384]{1,0:T(8,128)(2,1)S(1)} %copy-done.16), channel_id=1, source_target_pairs={{0,2},{1,3},{2,0},{3,1},{4,6},{5,7},{6,4},{7,5},{8,10},{9,11},{10,... | collective-permute-start | bytes 294920 | tf_op jit(solution)/shard_map/ppermute | solution.py:285
  30.3 2.9 %collective-permute-done.3.refs_4_ = bf16[264,128]{1,0:T(8,128)(2,1)S(1)} collective-permute-done((bf16[264,128]{1,0:T(8,128)(2,1)S(1)}, bf16[264,128]{1,0:T(8,128)(2,1)S(1)}, u32[]{:S(2)}, u32[]{:S(2)}) %collective-permute-start.3) | collective-permute-done | bytes 67616 | tf_op jit(solution)/shard_map/ppermute | solution.py:366
  35.0 2.3 %collective-permute-start.6 = (bf16[264,128]{1,0:T(8,128)(2,1)S(1)}, bf16[264,128]{1,0:T(8,128)(2,1)S(1)}, u32[]{:S(2)}, u32[]{:S(2)}) collective-permute-start(bf16[264,128]{1,0:T(8,128)(2,1)S(1)} %get-tuple-element.28), channel_id=1, source_target_pairs={{0,28},{4,24},{8,20},{12,16},{16,12},{20,8},{24,4},{28,0},{1,29},{... | collective-permute-start | bytes 202760 | tf_op jit(solution)/shard_map/ppermute | solution.py:366
  37.4 2.5 %collective-permute-done.5.refs_6_ = bf16[264,128]{1,0:T(8,128)(2,1)S(1)} collective-permute-done((bf16[264,128]{1,0:T(8,128)(2,1)S(1)}, bf16[264,128]{1,0:T(8,128)(2,1)S(1)}, u32[]{:S(2)}, u32[]{:S(2)}) %collective-permute-start.5) | collective-permute-done | bytes 67616 | tf_op jit(solution)/shard_map/ppermute | solution.py:366
  40.5 1.5 %collective-permute-done.6.refs_7_ = bf16[264,128]{1,0:T(8,128)(2,1)S(1)} collective-permute-done((bf16[264,128]{1,0:T(8,128)(2,1)S(1)}, bf16[264,128]{1,0:T(8,128)(2,1)S(1)}, u32[]{:S(2)}, u32[]{:S(2)}) %collective-permute-start.6) | collective-permute-done | bytes 67616 | tf_op jit(solution)/shard_map/ppermute | solution.py:366
  44.4 1.2 %index.1 = (bf16[384,128]{1,0:T(8,128)(2,1)S(1)}, f32[384,8]{1,0:T(8,128)S(1)}, s32[8,384]{1,0:T(8,128)S(1)}) custom-call(s32[1,256]{1,0:T(1,128)S(1)} %bitcast.27, s32[1,1408]{1,0:T(1,128)S(1)} %reshape.44.packed_ref, f32[1,128]{1,0:T(1,128)S(1)} %bitcast.28, f32[1,128]{1,0:T(1,128)S(1)} %bitcast.29), custom_call_target="tpu_custom_call" | custom-call | flops 8589934592 | bytes 262144 | tf_op jit(solution)/shard_map/index/pallas_call | solution.py:336
  47.9 1.1 %collective-permute-done.15.refs_19_ = bf16[128,384]{1,0:T(8,128)(2,1)S(1)} collective-permute-done((bf16[128,384]{1,0:T(8,128)(2,1)S(1)}, bf16[128,384]{1,0:T(8,128)(2,1)S(1)}, u32[]{:S(2)}, u32[]{:S(2)}) %collective-permute-start.15) | collective-permute-done | bytes 98336 | tf_op jit(solution)/shard_map/ppermute | solution.py:285
  49.0 1.5 %collective-permute-start.20 = (bf16[512,256]{1,0:T(8,128)(2,1)S(1)}, bf16[512,256]{1,0:T(8,128)(2,1)S(1)}, u32[]{:S(2)}, u32[]{:S(2)}) collective-permute-start(bf16[512,256]{1,0:T(8,128)(2,1)S(1)} %copy-done.2), channel_id=1, source_target_pairs={{0,2},{1,3},{2,0},{3,1},{4,6},{5,7},{6,4},{7,5},{8,10},{9,11},{10,... | collective-permute-start | bytes 786440 | tf_op jit(solution)/shard_map/ppermute | solution.py:285
  52.0 1.0 copy-done.10
  53.0 1.0 copy-done.12
  54.0 1.0 copy-done.14
  63.9 5.4 %gru.1 = (bf16[32,72,128]{2,1,0:T(8,128)(2,1)}, f32[384,512]{1,0:T(8,128)S(1)}, bf16[384,512]{1,0:T(8,128)(2,1)S(1)}) custom-call(bf16[384,128]{1,0:T(8,128)(2,1)S(1)} %copy-done.36, f32[384,8]{1,0:T(8,128)S(1)} %copy-done.34, s32[8,384]{1,0:T(8,128)S(1)} %get-tuple-element.20.row_ref, bf16[264,128]{1,0:T(8,128)(2,1)S(1)} %copy-done.38, ...), custom_call_target="tpu_custom_call" | custom-call | flops 1207959552 | bytes 8388608 | tf_op jit(solution)/shard_map/gru/pallas_call | solution.py:370
  69.3 4.6 %all-to-all-start.1 = ((bf16[32,72,128]{2,1,0:T(8,128)(2,1)}), bf16[32,72,128]{2,1,0:T(8,128)(2,1)}, u32[]{:S(2)}, u32[]{:S(2)}) async-start(bf16[32,72,128]{2,1,0:T(8,128)(2,1)} %get-tuple-element.32), calls=%async_computation.1 | async-start | bytes 1179648 | tf_op jit(solution)/shard_map/all_to_all | solution.py:384
  74.0 1.8 %collective-permute-start.23 = (s32[8,128]{1,0:T(8,128)S(1)}, s32[8,128]{1,0:T(8,128)S(1)}, u32[]{:S(2)}, u32[]{:S(2)}) collective-permute-start(s32[8,128]{1,0:T(8,128)S(1)} %bitcast.21), channel_id=1, source_target_pairs={{0,2},{1,3},{2,0},{3,1},{4,6},{5,7},{6,4},{7,5},{8,10},{9,11},{10,... | collective-permute-start | bytes 12296 | tf_op jit(solution)/shard_map/ppermute | solution.py:285
  75.7 3.0 %collective-permute-done.23 = s32[8,128]{1,0:T(8,128)S(1)} collective-permute-done((s32[8,128]{1,0:T(8,128)S(1)}, s32[8,128]{1,0:T(8,128)S(1)}, u32[]{:S(2)}, u32[]{:S(2)}) %collective-permute-start.23) | collective-permute-done | bytes 4128 | tf_op jit(solution)/shard_map/ppermute | solution.py:285
  78.8 1.2 %collective-permute-done.22 = s32[8,128]{1,0:T(8,128)S(1)} collective-permute-done((s32[8,128]{1,0:T(8,128)S(1)}, s32[8,128]{1,0:T(8,128)S(1)}, u32[]{:S(2)}, u32[]{:S(2)}) %collective-permute-start.22) | collective-permute-done | bytes 4128 | tf_op jit(solution)/shard_map/ppermute | solution.py:285
  81.7 1.9 %gather_fusion = s32[4,8,72]{2,1,0:T(8,128)} fusion(s32[4,8,72]{2,1,0:T(8,128)} %pad_add_fusion, s32[1024]{0:T(1024)S(1)} %pad_clamp_fusion), kind=kCustom, calls=%fused_computation | custom fusion | bytes 18448 | tf_op jit(solution)/shard_map/gather | solution.py:403
  83.6 1.3 %copy.21 = s32[8,4,72]{2,1,0:T(4,128)} copy(s32[8,4,72]{2,0,1:T(8,128)} %bitcast.30) | data formatting | bytes 18432 | tf_op jit(solution)/shard_map/transpose | solution.py:403
  84.9 1.4 %reshape.48.ids_ref = s32[1,2304]{1,0:T(1,128)} reshape(s32[8,4,72]{2,1,0:T(4,128)} %copy.21) | data formatting | bytes 18432 | tf_op jit(solution)/shard_map/reshape | solution.py:403
  86.3 3.9 %attend.1 = (bf16[384,512]{1,0:T(8,128)(2,1)}, bf16[1024,128]{1,0:T(8,128)(2,1)S(1)}) custom-call(s32[3,2]{1,0:T(4,128)S(1)} %copy.20.listed_ref, f32[384,512]{1,0:T(8,128)S(1)} %get-tuple-element.29.hnew_ref, bf16[384,512]{1,0:T(8,128)(2,1)S(1)} %get-tuple-element.30.hdst_ref, bf16[1024,512]{1,0:T(8,128)(2,1)S(1)} %copy-done.1, ...), custom_call_target="tpu_custom_call" | custom-call | flops 603979776 | bytes 4194304 | tf_op jit(solution)/shard_map/attend/pallas_call | solution.py:386
  90.9 3.2 %apply.1.refs_0_ = bf16[1024,128]{1,0:T(8,128)(2,1)} custom-call(s32[1,2304]{1,0:T(1,128)} %reshape.48.ids_ref, bf16[2304,128]{1,0:T(8,128)(2,1)} %bitcast.13.landed_ref, bf16[1024,128]{1,0:T(8,128)(2,1)} %copy-done.15), custom_call_target="tpu_custom_call" | custom-call | flops 1207959552 | bytes 4194304 | tf_op jit(solution)/shard_map/apply/pallas_call | solution.py:404
  94.1 1.0 collective-permute-start.26
  95.2 7.6 %collective-permute-done.26.refs_2_ = bf16[1024,128]{1,0:T(8,128)(2,1)S(1)} collective-permute-done((bf16[1024,128]{1,0:T(8,128)(2,1)}, bf16[1024,128]{1,0:T(8,128)(2,1)S(1)}, u32[]{:S(2)}, u32[]{:S(2)}) %collective-permute-start.26) | collective-permute-done | bytes 262176 | tf_op jit(solution)/shard_map/ppermute | solution.py:285
  102.8 1.5 %collective-permute-done.27.refs_3_ = bf16[1024,128]{1,0:T(8,128)(2,1)S(1)} collective-permute-done((bf16[1024,128]{1,0:T(8,128)(2,1)S(1)}, bf16[1024,128]{1,0:T(8,128)(2,1)S(1)}, u32[]{:S(2)}, u32[]{:S(2)}) %collective-permute-start.27) | collective-permute-done | bytes 262176 | tf_op jit(solution)/shard_map/ppermute | solution.py:285
  104.3 0.9 copy-done.3
  105.3 1.2 %join.1 = bf16[1024,512]{1,0:T(8,128)(2,1)} custom-call(bf16[1024,128]{1,0:T(8,128)(2,1)S(1)} %copy-done.3, bf16[1024,128]{1,0:T(8,128)(2,1)S(1)} %collective-permute-done.25.refs_1_, bf16[1024,128]{1,0:T(8,128)(2,1)S(1)} %collective-permute-done.26.refs_2_, bf16[1024,128]{1,0:T(8,128)(2,1)S(1)} %collective-permute-done.27.refs_3_), custom_call_target="tpu_custom_call" | custom-call | flops 1048576 | bytes 2097152 | tf_op jit(solution)/shard_map/join/pallas_call | solution.py:414
  (135 shorter events, 25.6 us)
Async XLA Ops:
  0.6 42.5 %collective-permute-start.11 = (bf16[512,384]{1,0:T(8,128)(2,1)}, bf16[512,384]{1,0:T(8,128)(2,1)S(1)}, u32[]{:S(2)}, u32[]{:S(2)}) collective-permute-start(bf16[512,384]{1,0:T(8,128)(2,1)} %refs_12_.1), channel_id=1, source_target_pairs={{0,2},{1,3},{2,0},{3,1},{4,6},{5,7},{6,4},{7,5},{8,10},{9,11},{10,... | collective-permute-start | bytes 1179656 | tf_op jit(solution)/shard_map/ppermute | solution.py:285
  3.6 39.6 %collective-permute-start.8 = (bf16[512,384]{1,0:T(8,128)(2,1)}, bf16[512,384]{1,0:T(8,128)(2,1)S(1)}, u32[]{:S(2)}, u32[]{:S(2)}) collective-permute-start(bf16[512,384]{1,0:T(8,128)(2,1)} %refs_8_.1), channel_id=1, source_target_pairs={{0,2},{1,3},{2,0},{3,1},{4,6},{5,7},{6,4},{7,5},{8,10},{9,11},{10,... | collective-permute-start | bytes 1179656 | tf_op jit(solution)/shard_map/ppermute | solution.py:285
  18.5 22.0 %copy-start.8 = (bf16[512,384]{1,0:T(8,128)(2,1)S(1)}, bf16[512,384]{1,0:T(8,128)(2,1)}, u32[]{:S(2)}) copy-start(bf16[512,384]{1,0:T(8,128)(2,1)} %refs_12_.1) | copy-start | bytes 1179652
  18.5 24.1 %copy-start.7 = (bf16[512,384]{1,0:T(8,128)(2,1)S(1)}, bf16[512,384]{1,0:T(8,128)(2,1)}, u32[]{:S(2)}) copy-start(bf16[512,384]{1,0:T(8,128)(2,1)} %refs_8_.1) | copy-start | bytes 1179652
  20.2 4.3 %collective-permute-start = (bf16[264,128]{1,0:T(8,128)(2,1)S(1)}, bf16[264,128]{1,0:T(8,128)(2,1)S(1)}, u32[]{:S(2)}, u32[]{:S(2)}) collective-permute-start(bf16[264,128]{1,0:T(8,128)(2,1)S(1)} %get-tuple-element.22), channel_id=1, source_target_pairs={{0,4},{4,0},{8,12},{12,8},{16,20},{20,16},{24,28},{28,24},{1,5},{5... | collective-permute-start | bytes 202760 | tf_op jit(solution)/shard_map/ppermute | solution.py:366
  20.8 4.9 %collective-permute-start.1 = (bf16[264,128]{1,0:T(8,128)(2,1)S(1)}, bf16[264,128]{1,0:T(8,128)(2,1)S(1)}, u32[]{:S(2)}, u32[]{:S(2)}) collective-permute-start(bf16[264,128]{1,0:T(8,128)(2,1)S(1)} %get-tuple-element.23), channel_id=1, source_target_pairs={{0,8},{4,12},{8,0},{12,4},{16,24},{20,28},{24,16},{28,20},{1,9},{5... | collective-permute-start | bytes 202760 | tf_op jit(solution)/shard_map/ppermute | solution.py:366
  21.4 7.3 %collective-permute-start.2 = (bf16[264,128]{1,0:T(8,128)(2,1)S(1)}, bf16[264,128]{1,0:T(8,128)(2,1)S(1)}, u32[]{:S(2)}, u32[]{:S(2)}) collective-permute-start(bf16[264,128]{1,0:T(8,128)(2,1)S(1)} %get-tuple-element.24), channel_id=1, source_target_pairs={{0,12},{4,8},{8,4},{12,0},{16,28},{20,24},{24,20},{28,16},{1,13},{... | collective-permute-start | bytes 202760 | tf_op jit(solution)/shard_map/ppermute | solution.py:366
  25.2 8.0 %collective-permute-start.3 = (bf16[264,128]{1,0:T(8,128)(2,1)S(1)}, bf16[264,128]{1,0:T(8,128)(2,1)S(1)}, u32[]{:S(2)}, u32[]{:S(2)}) collective-permute-start(bf16[264,128]{1,0:T(8,128)(2,1)S(1)} %get-tuple-element.25), channel_id=1, source_target_pairs={{0,16},{4,20},{8,24},{12,28},{16,0},{20,4},{24,8},{28,12},{1,17},{... | collective-permute-start | bytes 202760 | tf_op jit(solution)/shard_map/ppermute | solution.py:366
  26.3 8.1 %collective-permute-start.4 = (bf16[264,128]{1,0:T(8,128)(2,1)S(1)}, bf16[264,128]{1,0:T(8,128)(2,1)S(1)}, u32[]{:S(2)}, u32[]{:S(2)}) collective-permute-start(bf16[264,128]{1,0:T(8,128)(2,1)S(1)} %get-tuple-element.26), channel_id=1, source_target_pairs={{0,20},{4,16},{8,28},{12,24},{16,4},{20,0},{24,12},{28,8},{1,21},{... | collective-permute-start | bytes 202760 | tf_op jit(solution)/shard_map/ppermute | solution.py:366
  28.7 13.9 %collective-permute-start.14 = (bf16[128,384]{1,0:T(8,128)(2,1)S(1)}, bf16[128,384]{1,0:T(8,128)(2,1)S(1)}, u32[]{:S(2)}, u32[]{:S(2)}) collective-permute-start(bf16[128,384]{1,0:T(8,128)(2,1)S(1)} %copy-done.16), channel_id=1, source_target_pairs={{0,2},{1,3},{2,0},{3,1},{4,6},{5,7},{6,4},{7,5},{8,10},{9,11},{10,... | collective-permute-start | bytes 294920 | tf_op jit(solution)/shard_map/ppermute | solution.py:285
  33.8 6.1 %collective-permute-start.5 = (bf16[264,128]{1,0:T(8,128)(2,1)S(1)}, bf16[264,128]{1,0:T(8,128)(2,1)S(1)}, u32[]{:S(2)}, u32[]{:S(2)}) collective-permute-start(bf16[264,128]{1,0:T(8,128)(2,1)S(1)} %get-tuple-element.27), channel_id=1, source_target_pairs={{0,24},{4,28},{8,16},{12,20},{16,8},{20,12},{24,0},{28,4},{1,25},{... | collective-permute-start | bytes 202760 | tf_op jit(solution)/shard_map/ppermute | solution.py:366
  35.0 7.0 %collective-permute-start.6 = (bf16[264,128]{1,0:T(8,128)(2,1)S(1)}, bf16[264,128]{1,0:T(8,128)(2,1)S(1)}, u32[]{:S(2)}, u32[]{:S(2)}) collective-permute-start(bf16[264,128]{1,0:T(8,128)(2,1)S(1)} %get-tuple-element.28), channel_id=1, source_target_pairs={{0,28},{4,24},{8,20},{12,16},{16,12},{20,8},{24,4},{28,0},{1,29},{... | collective-permute-start | bytes 202760 | tf_op jit(solution)/shard_map/ppermute | solution.py:366
  40.5 10.0 %collective-permute-start.10 = (bf16[512,384]{1,0:T(8,128)(2,1)S(1)}, bf16[512,384]{1,0:T(8,128)(2,1)S(1)}, u32[]{:S(2)}, u32[]{:S(2)}) collective-permute-start(bf16[512,384]{1,0:T(8,128)(2,1)S(1)} %copy-done.8), channel_id=1, source_target_pairs={{0,1},{1,0},{2,3},{3,2},{4,5},{5,4},{6,7},{7,6},{8,9},{9,8},{10,11... | collective-permute-start | bytes 1179656 | tf_op jit(solution)/shard_map/ppermute | solution.py:285
  42.6 8.6 %collective-permute-start.7 = (bf16[512,384]{1,0:T(8,128)(2,1)S(1)}, bf16[512,384]{1,0:T(8,128)(2,1)}, u32[]{:S(2)}, u32[]{:S(2)}) collective-permute-start(bf16[512,384]{1,0:T(8,128)(2,1)S(1)} %copy-done.7), channel_id=1, source_target_pairs={{0,1},{1,0},{2,3},{3,2},{4,5},{5,4},{6,7},{7,6},{8,9},{9,8},{10,11... | collective-permute-start | bytes 1179656 | tf_op jit(solution)/shard_map/ppermute | solution.py:285
  42.7 5.1 %collective-permute-start.13 = (bf16[128,384]{1,0:T(8,128)(2,1)S(1)}, bf16[128,384]{1,0:T(8,128)(2,1)S(1)}, u32[]{:S(2)}, u32[]{:S(2)}) collective-permute-start(bf16[128,384]{1,0:T(8,128)(2,1)S(1)} %copy-done.16), channel_id=1, source_target_pairs={{0,1},{1,0},{2,3},{3,2},{4,5},{5,4},{6,7},{7,6},{8,9},{9,8},{10,11... | collective-permute-start | bytes 294920 | tf_op jit(solution)/shard_map/ppermute | solution.py:285
  43.2 8.7 %collective-permute-start.12 = (bf16[512,384]{1,0:T(8,128)(2,1)S(1)}, bf16[512,384]{1,0:T(8,128)(2,1)}, u32[]{:S(2)}, u32[]{:S(2)}) collective-permute-start(bf16[512,384]{1,0:T(8,128)(2,1)S(1)} %collective-permute-done.11.refs_14_), channel_id=1, source_target_pairs={{0,1},{1,0},{2,3},{3,2},{4,5},{5,4},{6,7},{7,6},{8,9},{9,8},{10,11... | collective-permute-start | bytes 1179656 | tf_op jit(solution)/shard_map/ppermute | solution.py:285
  43.3 8.8 %collective-permute-start.9 = (bf16[512,384]{1,0:T(8,128)(2,1)S(1)}, bf16[512,384]{1,0:T(8,128)(2,1)}, u32[]{:S(2)}, u32[]{:S(2)}) collective-permute-start(bf16[512,384]{1,0:T(8,128)(2,1)S(1)} %collective-permute-done.8.refs_10_), channel_id=1, source_target_pairs={{0,1},{1,0},{2,3},{3,2},{4,5},{5,4},{6,7},{7,6},{8,9},{9,8},{10,11... | collective-permute-start | bytes 1179656 | tf_op jit(solution)/shard_map/ppermute | solution.py:285
  47.7 1.3 %collective-permute-start.15 = (bf16[128,384]{1,0:T(8,128)(2,1)S(1)}, bf16[128,384]{1,0:T(8,128)(2,1)S(1)}, u32[]{:S(2)}, u32[]{:S(2)}) collective-permute-start(bf16[128,384]{1,0:T(8,128)(2,1)S(1)} %collective-permute-done.14.refs_18_), channel_id=1, source_target_pairs={{0,1},{1,0},{2,3},{3,2},{4,5},{5,4},{6,7},{7,6},{8,9},{9,8},{10,11... | collective-permute-start | bytes 294920 | tf_op jit(solution)/shard_map/ppermute | solution.py:285
  49.0 31.4 %collective-permute-start.20 = (bf16[512,256]{1,0:T(8,128)(2,1)S(1)}, bf16[512,256]{1,0:T(8,128)(2,1)S(1)}, u32[]{:S(2)}, u32[]{:S(2)}) collective-permute-start(bf16[512,256]{1,0:T(8,128)(2,1)S(1)} %copy-done.2), channel_id=1, source_target_pairs={{0,2},{1,3},{2,0},{3,1},{4,6},{5,7},{6,4},{7,5},{8,10},{9,11},{10,... | collective-permute-start | bytes 786440 | tf_op jit(solution)/shard_map/ppermute | solution.py:285
  51.2 35.1 %collective-permute-start.19 = (bf16[512,256]{1,0:T(8,128)(2,1)S(1)}, bf16[512,256]{1,0:T(8,128)(2,1)S(1)}, u32[]{:S(2)}, u32[]{:S(2)}) collective-permute-start(bf16[512,256]{1,0:T(8,128)(2,1)S(1)} %copy-done.2), channel_id=1, source_target_pairs={{0,1},{1,0},{2,3},{3,2},{4,5},{5,4},{6,7},{7,6},{8,9},{9,8},{10,11... | collective-permute-start | bytes 786440 | tf_op jit(solution)/shard_map/ppermute | solution.py:285
  51.3 28.9 %collective-permute-start.17 = (bf16[512,128]{1,0:T(8,128)(2,1)S(1)}, bf16[512,128]{1,0:T(8,128)(2,1)S(1)}, u32[]{:S(2)}, u32[]{:S(2)}) collective-permute-start(bf16[512,128]{1,0:T(8,128)(2,1)S(1)} %copy-done.4), channel_id=1, source_target_pairs={{0,2},{1,3},{2,0},{3,1},{4,6},{5,7},{6,4},{7,5},{8,10},{9,11},{10,... | collective-permute-start | bytes 393224 | tf_op jit(solution)/shard_map/ppermute | solution.py:285
  51.9 34.4 %collective-permute-start.16 = (bf16[512,128]{1,0:T(8,128)(2,1)S(1)}, bf16[512,128]{1,0:T(8,128)(2,1)}, u32[]{:S(2)}, u32[]{:S(2)}) collective-permute-start(bf16[512,128]{1,0:T(8,128)(2,1)S(1)} %copy-done.4), channel_id=1, source_target_pairs={{0,1},{1,0},{2,3},{3,2},{4,5},{5,4},{6,7},{7,6},{8,9},{9,8},{10,11... | collective-permute-start | bytes 393224 | tf_op jit(solution)/shard_map/ppermute | solution.py:285
  69.3 17.0 %copy-start.1 = (bf16[1024,512]{1,0:T(8,128)(2,1)S(1)}, bf16[1024,512]{1,0:T(8,128)(2,1)}, u32[]{:S(2)}) copy-start(bf16[1024,512]{1,0:T(8,128)(2,1)} %memory_ref.3) | copy-start | bytes 3145732
  69.3 21.6 %all-to-all-start.1 = ((bf16[32,72,128]{2,1,0:T(8,128)(2,1)}), bf16[32,72,128]{2,1,0:T(8,128)(2,1)}, u32[]{:S(2)}, u32[]{:S(2)}) async-start(bf16[32,72,128]{2,1,0:T(8,128)(2,1)} %get-tuple-element.32), calls=%async_computation.1 | async-start | bytes 1179648 | tf_op jit(solution)/shard_map/all_to_all | solution.py:384
  74.0 4.8 %collective-permute-start.23 = (s32[8,128]{1,0:T(8,128)S(1)}, s32[8,128]{1,0:T(8,128)S(1)}, u32[]{:S(2)}, u32[]{:S(2)}) collective-permute-start(s32[8,128]{1,0:T(8,128)S(1)} %bitcast.21), channel_id=1, source_target_pairs={{0,2},{1,3},{2,0},{3,1},{4,6},{5,7},{6,4},{7,5},{8,10},{9,11},{10,... | collective-permute-start | bytes 12296 | tf_op jit(solution)/shard_map/ppermute | solution.py:285
  78.8 1.2 %collective-permute-start.22 = (s32[8,128]{1,0:T(8,128)S(1)}, s32[8,128]{1,0:T(8,128)S(1)}, u32[]{:S(2)}, u32[]{:S(2)}) collective-permute-start(s32[8,128]{1,0:T(8,128)S(1)} %bitcast.23), channel_id=1, source_target_pairs={{0,1},{1,0},{2,3},{3,2},{4,5},{5,4},{6,7},{7,6},{8,9},{9,8},{10,11... | collective-permute-start | bytes 12296 | tf_op jit(solution)/shard_map/ppermute | solution.py:285
  79.9 1.2 %collective-permute-start.24 = (s32[8,128]{1,0:T(8,128)S(1)}, s32[8,128]{1,0:T(8,128)S(1)}, u32[]{:S(2)}, u32[]{:S(2)}) collective-permute-start(s32[8,128]{1,0:T(8,128)S(1)} %collective-permute-done.23), channel_id=1, source_target_pairs={{0,1},{1,0},{2,3},{3,2},{4,5},{5,4},{6,7},{7,6},{8,9},{9,8},{10,11... | collective-permute-start | bytes 12296 | tf_op jit(solution)/shard_map/ppermute | solution.py:285
  80.1 6.2 %collective-permute-start.18 = (bf16[512,128]{1,0:T(8,128)(2,1)S(1)}, bf16[512,128]{1,0:T(8,128)(2,1)}, u32[]{:S(2)}, u32[]{:S(2)}) collective-permute-start(bf16[512,128]{1,0:T(8,128)(2,1)S(1)} %collective-permute-done.17.refs_2_), channel_id=1, source_target_pairs={{0,1},{1,0},{2,3},{3,2},{4,5},{5,4},{6,7},{7,6},{8,9},{9,8},{10,11... | collective-permute-start | bytes 393224 | tf_op jit(solution)/shard_map/ppermute | solution.py:285
  80.5 5.9 %collective-permute-start.21 = (bf16[512,256]{1,0:T(8,128)(2,1)S(1)}, bf16[512,256]{1,0:T(8,128)(2,1)S(1)}, u32[]{:S(2)}, u32[]{:S(2)}) collective-permute-start(bf16[512,256]{1,0:T(8,128)(2,1)S(1)} %collective-permute-done.20.refs_6_), channel_id=1, source_target_pairs={{0,1},{1,0},{2,3},{3,2},{4,5},{5,4},{6,7},{7,6},{8,9},{9,8},{10,11... | collective-permute-start | bytes 786440 | tf_op jit(solution)/shard_map/ppermute | solution.py:285
  94.1 8.7 %collective-permute-start.26 = (bf16[1024,128]{1,0:T(8,128)(2,1)}, bf16[1024,128]{1,0:T(8,128)(2,1)S(1)}, u32[]{:S(2)}, u32[]{:S(2)}) collective-permute-start(bf16[1024,128]{1,0:T(8,128)(2,1)} %apply.1.refs_0_), channel_id=1, source_target_pairs={{0,2},{1,3},{2,0},{3,1},{4,6},{5,7},{6,4},{7,5},{8,10},{9,11},{10,... | collective-permute-start | bytes 786440 | tf_op jit(solution)/shard_map/ppermute | solution.py:285
  95.1 7.7 %collective-permute-start.25 = (bf16[1024,128]{1,0:T(8,128)(2,1)}, bf16[1024,128]{1,0:T(8,128)(2,1)S(1)}, u32[]{:S(2)}, u32[]{:S(2)}) collective-permute-start(bf16[1024,128]{1,0:T(8,128)(2,1)} %apply.1.refs_0_), channel_id=1, source_target_pairs={{0,1},{1,0},{2,3},{3,2},{4,5},{5,4},{6,7},{7,6},{8,9},{9,8},{10,11... | collective-permute-start | bytes 786440 | tf_op jit(solution)/shard_map/ppermute | solution.py:285
  102.8 1.5 %collective-permute-start.27 = (bf16[1024,128]{1,0:T(8,128)(2,1)S(1)}, bf16[1024,128]{1,0:T(8,128)(2,1)S(1)}, u32[]{:S(2)}, u32[]{:S(2)}) collective-permute-start(bf16[1024,128]{1,0:T(8,128)(2,1)S(1)} %collective-permute-done.26.refs_2_), channel_id=1, source_target_pairs={{0,1},{1,0},{2,3},{3,2},{4,5},{5,4},{6,7},{7,6},{8,9},{9,8},{10,11... | collective-permute-start | bytes 786440 | tf_op jit(solution)/shard_map/ppermute | solution.py:285
  (41 other events, 105.7 us)

commit v6 on v4

--- a/solution.py
+++ b/solution.py
@@ -17,7 +17,7 @@
 I32 = jnp.int32
 VMEM = pl.BlockSpec(memory_space=pltpu.VMEM)
 SMEM = pl.BlockSpec(memory_space=pltpu.SMEM)
-ANY = pl.BlockSpec(memory_space=pl.ANY)
+HBM = pl.BlockSpec(memory_space=pltpu.HBM)
 
 
 def iota(shape, dim):
@@ -39,6 +39,10 @@
         cost_estimate=pl.CostEstimate(flops=flops, bytes_accessed=bytes_, transcendentals=0),
         name=name,
     )
+
+
+def far(arrays):
+    return [pltpu.with_memory_space_constraint(x, pltpu.HBM) for x in arrays]
 
 
 class Plan:
@@ -120,20 +124,29 @@
     return jnp.where((inner * plan.owners + owner) == here, 1.0, 0.0).astype(BF16)
 
 
-def serve_kernel(plan, asked_ref, memory_ref, out_ref):
+def serve_kernel(plan, asked_ref, memory_ref, out_ref, held, hot_ref, sems):
     stored, width = memory_ref.shape
     piece = width // 4
-    asked = asked_ref[...].astype(F32)
-    turned = asked.T
+    step = stored // 4
+    copies = [
+        pltpu.make_async_copy(memory_ref.at[pl.ds(i * step, step)], held.at[pl.ds(i * step, step)], sems.at[i])
+        for i in range(4)
+    ]
+    for copy in copies:
+        copy.start()
+    asked = asked_ref[...]
+    turned = asked.astype(F32).T
     blocks = [
         jnp.where(turned[: plan.main, s : s + 1].astype(I32) == iota((plan.main, stored), 1), 1.0, 0.0)
         for s in range(plan.owners)
     ]
     for i in range(plan.tail):
-        spare = asked_ref[:, plan.main + i : plan.main + i + 1]
+        spare = asked[:, plan.main + i : plan.main + i + 1]
         blocks.append(jnp.where(spare == iota((plan.owners, stored), 1), 1.0, 0.0))
-    hot = jnp.concatenate(blocks, axis=0).astype(BF16)
-    rows = dot(hot, memory_ref[...])
+    hot_ref[...] = jnp.concatenate(blocks, axis=0).astype(BF16)
+    for copy in copies:
+        copy.wait()
+    rows = dot(hot_ref[...], held[...])
     main = plan.main
     for s in range(plan.owners):
         for c in range(4):
@@ -168,44 +181,54 @@
     return table
 
 
-def gru_kernel(plan, ret_ref, enc_ref, col_ref, row_ref, *refs):
+def gru_kernel(plan, ret_ref, row_ref, col_ref, far_enc, *refs):
     reps = plan.reps
-    w_in, w_hid, w_time = refs[:reps], refs[reps : 2 * reps], refs[2 * reps : 3 * reps]
-    out_ref, hnew_ref, hdst_ref, gin, ghid, delta = refs[3 * reps :]
+    parts = refs[: 3 * reps]
+    out_ref, hnew_ref, hdst_ref, gin, ghid, delta, hsrc_ref, enc_ref, w_in, w_hid, w_time, sems = refs[3 * reps :]
+    copies = [pltpu.make_async_copy(far_enc, enc_ref, sems.at[0])]
+    for g, held in ((1, w_hid), (0, w_in), (2, w_time)):
+        for k in range(reps):
+            copies.append(pltpu.make_async_copy(parts[g * reps + k], held.at[k], sems.at[1 + g * reps + k]))
+    for copy in copies:
+        copy.start()
     me = lax.axis_index("rep")
     events, width = hnew_ref.shape
     piece = width // reps
     cols = col_ref[...].astype(I32)
     spots = iota((events, plan.rows), 1)
     table = table_of(plan, ret_ref)
-    hsrc = dot(jnp.where(cols[:, 0:1] == spots, 1.0, 0.0).astype(BF16), table)
-    source = hsrc.astype(BF16)
+    source = dot(jnp.where(cols[:, 0:1] == spots, 1.0, 0.0).astype(BF16), table).astype(BF16)
+    hsrc_ref[...] = source
     target = dot(jnp.where(cols[:, 1:2] == spots, 1.0, 0.0).astype(BF16), table).astype(BF16)
     hdst_ref[...] = target
+    for copy in copies:
+        copy.wait()
+    source, target = hsrc_ref[...], hdst_ref[...]
     enc = enc_ref[...]
-    part = w_in[0].shape[1]
-    for k in range(reps):
-        at = pl.ds(pl.multiple_of((me ^ k) * part, LANES), part)
-        gin[:, at] = dot(target, w_in[k][...]) + dot(enc, w_time[k][...])
-        ghid[:, at] = dot(source, w_hid[k][...])
+    part = w_in.shape[2]
+    for k in range(0, reps, 2):
+        both = [jnp.concatenate([w[k], w[k + 1]], axis=1) for w in (w_in, w_time, w_hid)]
+        into = dot(target, both[0]) + dot(enc, both[1])
+        hidden = dot(source, both[2])
+        for j in range(2):
+            at = pl.ds(pl.multiple_of((me ^ (k + j)) * part, LANES), part)
+            gin[:, at] = into[:, j * part : (j + 1) * part]
+            ghid[:, at] = hidden[:, j * part : (j + 1) * part]
     step = 64
     for i in range(0, events, step):
         at = slice(i, i + step)
         reset = 0.5 * jnp.tanh(0.5 * (gin[at, :width] + ghid[at, :width])) + 0.5
         update = 0.5 * jnp.tanh(0.5 * (gin[at, width : 2 * width] + ghid[at, width : 2 * width])) + 0.5
         fresh = jnp.tanh(gin[at, 2 * width :] + reset * ghid[at, 2 * width :])
-        hold = hsrc[at]
+        hold = hsrc_ref[at, :].astype(F32)
         new = (1.0 - update) * fresh + update * hold
         hnew_ref[at, :] = new
-        delta[at, :] = new - hold
-    change = delta[...]
-    high = change.astype(BF16)
-    low = (change - high.astype(F32)).astype(BF16)
+        delta[at, :] = (new - hold).astype(BF16)
     slots = plan.owners * plan.pad
     hits = jnp.where(row_ref[0:1, :] == iota((slots, events), 0), 1.0, 0.0)
     counts = jnp.maximum(jnp.sum(hits, axis=1, keepdims=True), 1.0)
     hits = hits.astype(BF16)
-    mean = (dot(hits, high) + dot(hits, low)) / counts
+    mean = dot(hits, delta[...]) / counts
     for o in range(plan.owners):
         for q in range(reps):
             out_ref[o * reps + q] = mean[o * plan.pad : (o + 1) * plan.pad, q * piece : (q + 1) * piece].astype(BF16)
@@ -243,16 +266,21 @@
             out_ref[at, lane] = (hnew_ref[at, lane] + dot(prob, values)).astype(BF16)
 
 
-def apply_kernel(plan, ids_ref, landed_ref, part_ref, out_ref):
+def apply_kernel(plan, ids_ref, landed_ref, part_ref, out_ref, held, sem):
+    copy = pltpu.make_async_copy(part_ref, held, sem)
+    copy.start()
     stored = part_ref.shape[0]
     count = landed_ref.shape[0]
     landed = landed_ref[...]
     step = min(256, stored)
     ids = ids_ref[...]
+    totals = []
     for i in range(0, stored, step):
         hot = jnp.where(iota((step, count), 0) + i == ids, 1.0, 0.0).astype(BF16)
-        total = dot(hot, landed)
-        out_ref[i : i + step, :] = (part_ref[i : i + step, :].astype(F32) + total).astype(BF16)
+        totals.append(dot(hot, landed))
+    copy.wait()
+    for i, total in zip(range(0, stored, step), totals):
+        out_ref[i : i + step, :] = (held[i : i + step, :].astype(F32) + total).astype(BF16)
 
 
 def join_kernel(plan, *refs):
@@ -310,6 +338,9 @@
         run(request_kernel, plan), [sds((owners, LANES), I32)], [VMEM] * 2, 1 << 20, 1 << 14, "request", limit=8
     )(owner, touch_row.reshape(1, entries))[0]
 
+    request, w_time, w_hidden, w_input, w_keyval, w_query = lax.optimization_barrier(
+        (request, w_time, w_hidden, w_input, w_keyval, w_query)
+    )
     full_time, full_hidden, full_input, full_keyval, full_query = spread(
         [w_time, w_hidden, w_input, w_keyval, w_query], reps
     )
@@ -331,32 +362,40 @@
     )
     everyone = [x for x in spread([asked], reps)[0]]
 
-    chunk = 4 * (plan.main + plan.tail)
     served = call(
         run(serve_kernel, plan),
-        [sds((owners, chunk, width // 4), BF16)],
-        [VMEM] * 2,
+        [sds((owners, 4 * (plan.main + plan.tail), width // 4), BF16)],
+        [VMEM, HBM],
         2 * plan.rows * stored * width,
         2 * stored * width + 2 * plan.rows * width,
         "serve",
-        limit=12,
-    )(asked, memory)[0]
+        scratch=[
+            pltpu.VMEM((stored, width), BF16),
+            pltpu.VMEM((plan.rows, stored), BF16),
+            pltpu.SemaphoreType.DMA((4,)),
+        ],
+        limit=16,
+    )(asked, *far([memory]))[0]
     returned = lax.all_to_all(served, "shard", split_axis=0, concat_axis=0, tiled=True)
 
     outgoing, hnew, hdst = call(
         run(gru_kernel, plan),
         [sds((owners * reps, plan.pad, piece), BF16), sds((events, width), F32), sds((events, width), BF16)],
-        [VMEM] * (4 + 3 * reps),
+        [VMEM] * 3 + [HBM] * (1 + 3 * reps),
         2 * events * width * 3 * width * 2,
         8 << 20,
         "gru",
         scratch=[
             pltpu.VMEM((events, 3 * width), F32),
             pltpu.VMEM((events, 3 * width), F32),
-            pltpu.VMEM((events, width), F32),
-        ],
+            pltpu.VMEM((events, width), BF16),
+            pltpu.VMEM((events, width), BF16),
+            pltpu.VMEM(encode.shape, BF16),
+        ]
+        + [pltpu.VMEM((reps,) + x.shape, BF16) for x in (w_input, w_hidden, w_time)]
+        + [pltpu.SemaphoreType.DMA((1 + 3 * reps,))],
         limit=24,
-    )(returned, encode, cols, rows, *full_input, *full_hidden, *full_time)
+    )(returned, rows, cols, *far([encode, *full_input, *full_hidden, *full_time]))
     landed = lax.all_to_all(outgoing, ("shard", "rep"), split_axis=0, concat_axis=0, tiled=True)
 
     embed, part = call(
@@ -380,12 +419,13 @@
     quarter = call(
         run(apply_kernel, plan),
         [sds((stored, piece), BF16)],
-        [VMEM] * 3,
+        [VMEM] * 2 + [HBM],
         2 * stored * owners * reps * plan.pad * piece * 2,
         4 << 20,
         "apply",
+        scratch=[pltpu.VMEM((stored, piece), BF16), pltpu.SemaphoreType.DMA],
         limit=16,
-    )(ids, landed.reshape(owners * reps * plan.pad, piece), part)[0]
+    )(ids, landed.reshape(owners * reps * plan.pad, piece), *far([part]))[0]
     new_memory = call(
         run(join_kernel, plan), [sds((stored, width), BF16)], [VMEM] * reps, 1 << 20, 2 << 20, "join", limit=8
     )(*spread([quarter], reps)[0])[0]

time: 87 us -> 77.6 us (0.89)
  local copies, waits for them, and re-layouts: 17.5 us -> 4.25 us
  waiting for transfers between devices: 25.2 us -> 27.8 us
  Pallas kernels: 16.9 us -> 18.4 us
    unnamed x71 -> x43, local copies, waits for them, and re-layouts: 16.8 us -> 3.58 us
    all_to_all x1, waiting for transfers between devices: 2.6 us -> 4.66 us  [shards(): lax.all_to_all(served, 'shard', split_axis=0, concat_axis=0, tiled=True)]
    pallas_call x2, Pallas kernels: 3.24 us -> 5.06 us  [the longest x1 2.86 us: shards(): call(run(serve_kernel, plan), [sds((owners, 4 * (plan.main + plan.tail),...]
  transfers between devices with their start and end apart: 24 -> 24, of which waited for: 10 -> 11; matrix products, arithmetic and copies ran while one was open for 1% -> 1% of each run, Pallas kernels for 17% -> 18%
where the time goes in v6:
time: 77.6 us; the launch traced here: 77.1 us
  waiting for transfers between devices  27.8 us (36%)
  starting transfers between devices  25.8 us (33%)
  Pallas kernels  18.4 us (24%)
  local copies, waits for them, and re-layouts  4.25 us (5%)
  between operations  0.93 us (1%)
    ppermute x21, waiting for transfers between devices, swap(): return lax.ppermute(x, 'rep', [(i, i ^ bit) for i in range(reps)])  15 us
    ppermute x21, starting transfers between devices, swap(): return lax.ppermute(x, 'rep', [(i, i ^ bit) for i in range(reps)])  12.2 us
    all_to_all x1, starting transfers between devices, shards(): lax.all_to_all(request, 'shard', split_axis=0, concat_axis=0, tiled=True)  6.34 us
    pallas_call x1, Pallas kernels, shards(): call(run(gru_kernel, plan), [sds((owners * reps, plan.pad, piece), BF16),...  5.83 us
    all_to_all x1, waiting for transfers between devices, shards(): lax.all_to_all(served, 'shard', split_axis=0, concat_axis=0, tiled=True)  4.66 us
    all_to_all x1, waiting for transfers between devices, shards(): lax.all_to_all(request, 'shard', split_axis=0, concat_axis=0, tiled=True)  4.39 us
    pallas_call x1, Pallas kernels, shards(): call(run(attend_kernel, plan), [sds((events, width), BF16), sds((stored,...  4.09 us
    all_to_all x1, starting transfers between devices, shards(): lax.all_to_all(served, 'shard', split_axis=0, concat_axis=0, tiled=True)  3.68 us
  transfers between devices with their start and end apart: 24, of which 11 were waited for; matrix products, arithmetic and copies ran while one was open for 1% of the time, Pallas kernels for 18%

profile of v6, /device:TPU:0, one launch (start us, length us, event | category | flops | bytes accessed | tf_op | source)
XLA Modules:
  0.0 77.1 jit_solution(13915552327400746221)
XLA Ops:
  0.6 0.7 copy-done.4
  1.3 1.0 %request.1 = s32[8,128]{1,0:T(8,128)} custom-call(s32[1,256]{1,0:T(1,128)S(1)} %bitcast.26, s32[1,256]{1,0:T(1,128)S(1)} %bitcast.25), custom_call_target="tpu_custom_call" | custom-call | flops 1048576 | bytes 16384 | tf_op jit(solution)/shard_map/request/pallas_call | solution.py:337
  2.3 2.9 %collective-permute-start.1 = (bf16[512,384]{1,0:T(8,128)(2,1)}, bf16[512,384]{1,0:T(8,128)(2,1)S(1)}, u32[]{:S(2)}, u32[]{:S(2)}) collective-permute-start(bf16[512,384]{1,0:T(8,128)(2,1)} %refs_0_), channel_id=1, source_target_pairs={{0,2},{1,3},{2,0},{3,1},{4,6},{5,7},{6,4},{7,5},{8,10},{9,11},{10,... | collective-permute-start | bytes 1179656 | tf_op jit(solution)/shard_map/ppermute | solution.py:295
  5.3 6.3 %all-to-all-start = ((s32[8,1,128]{2,1,0:T(1,128)}), s32[8,1,128]{2,1,0:T(1,128)S(1)}, u32[]{:S(2)}, u32[]{:S(2)}) async-start(s32[8,1,128]{2,1,0:T(1,128)} %bitcast.3), calls=%async_computation | async-start | bytes 8192 | tf_op jit(solution)/shard_map/all_to_all | solution.py:348
  11.6 0.5 collective-permute-start.3
  12.1 1.5 %collective-permute-start.7 = (bf16[128,384]{1,0:T(8,128)(2,1)}, bf16[128,384]{1,0:T(8,128)(2,1)S(1)}, u32[]{:S(2)}, u32[]{:S(2)}) collective-permute-start(bf16[128,384]{1,0:T(8,128)(2,1)} %refs_8_), channel_id=1, source_target_pairs={{0,2},{1,3},{2,0},{3,1},{4,6},{5,7},{6,4},{7,5},{8,10},{9,11},{10,... | collective-permute-start | bytes 294920 | tf_op jit(solution)/shard_map/ppermute | solution.py:295
  13.6 4.4 %all-to-all-done = s32[8,1,128]{2,1,0:T(1,128)S(1)} async-done(((s32[8,1,128]{2,1,0:T(1,128)}), s32[8,1,128]{2,1,0:T(1,128)S(1)}, u32[]{:S(2)}, u32[]{:S(2)}) %all-to-all-start) | async-done | bytes 4128 | tf_op jit(solution)/shard_map/all_to_all | solution.py:348
  18.0 2.9 %serve.1 = bf16[8,264,128]{2,1,0:T(8,128)(2,1)} custom-call(s32[8,128]{1,0:T(8,128)S(1)} %bitcast.21, bf16[1024,512]{1,0:T(8,128)(2,1)} %memory_ref.3), custom_call_target="tpu_custom_call" | custom-call | flops 553648128 | bytes 1589248 | tf_op jit(solution)/shard_map/serve/pallas_call | solution.py:365
  20.9 3.7 %all-to-all-start.1 = ((bf16[8,264,128]{2,1,0:T(8,128)(2,1)}), bf16[8,264,128]{2,1,0:T(8,128)(2,1)S(1)}, u32[]{:S(2)}, u32[]{:S(2)}) async-start(bf16[8,264,128]{2,1,0:T(8,128)(2,1)} %serve.1), calls=%async_computation.1 | async-start | bytes 1081344 | tf_op jit(solution)/shard_map/all_to_all | solution.py:379
  25.1 0.5 collective-permute-start.2
  25.7 0.7 copy-done.6
  26.4 1.2 %index.1 = (bf16[384,128]{1,0:T(8,128)(2,1)S(1)}, f32[384,8]{1,0:T(8,128)S(1)}, s32[8,384]{1,0:T(8,128)S(1)}) custom-call(s32[1,256]{1,0:T(1,128)S(1)} %bitcast.27, s32[1,1408]{1,0:T(1,128)S(1)} %reshape.45.packed_ref, f32[1,128]{1,0:T(1,128)S(1)} %bitcast.28, f32[1,128]{1,0:T(1,128)S(1)} %bitcast.29), custom_call_target="tpu_custom_call" | custom-call | flops 8589934592 | bytes 262144 | tf_op jit(solution)/shard_map/index/pallas_call | solution.py:349
  27.7 0.6 copy-done.8
  28.3 0.7 copy-done.12
  29.5 1.1 %collective-permute-done.8.refs_11_ = bf16[128,384]{1,0:T(8,128)(2,1)} collective-permute-done((bf16[128,384]{1,0:T(8,128)(2,1)S(1)}, bf16[128,384]{1,0:T(8,128)(2,1)}, u32[]{:S(2)}, u32[]{:S(2)}) %collective-permute-start.8) | collective-permute-done | bytes 98336 | tf_op jit(solution)/shard_map/ppermute | solution.py:295
  30.6 1.8 %collective-permute-start.13 = (bf16[512,256]{1,0:T(8,128)(2,1)S(1)}, bf16[512,256]{1,0:T(8,128)(2,1)S(1)}, u32[]{:S(2)}, u32[]{:S(2)}) collective-permute-start(bf16[512,256]{1,0:T(8,128)(2,1)S(1)} %copy-done.1), channel_id=1, source_target_pairs={{0,2},{1,3},{2,0},{3,1},{4,6},{5,7},{6,4},{7,5},{8,10},{9,11},{10,... | collective-permute-start | bytes 786440 | tf_op jit(solution)/shard_map/ppermute | solution.py:295
  33.1 4.7 %all-to-all-done.1.ret_ref = bf16[8,264,128]{2,1,0:T(8,128)(2,1)S(1)} async-done(((bf16[8,264,128]{2,1,0:T(8,128)(2,1)}), bf16[8,264,128]{2,1,0:T(8,128)(2,1)S(1)}, u32[]{:S(2)}, u32[]{:S(2)}) %all-to-all-start.1) | async-done | bytes 540704 | tf_op jit(solution)/shard_map/all_to_all | solution.py:379
  37.7 5.8 %gru.1 = (bf16[32,72,128]{2,1,0:T(8,128)(2,1)}, f32[384,512]{1,0:T(8,128)S(1)}, bf16[384,512]{1,0:T(8,128)(2,1)S(1)}) custom-call(bf16[8,264,128]{2,1,0:T(8,128)(2,1)S(1)} %all-to-all-done.1.ret_ref, s32[8,384]{1,0:T(8,128)S(1)} %get-tuple-element.17.row_ref, f32[384,8]{1,0:T(8,128)S(1)} %get-tuple-element.18.col_ref, bf16[384,128]{1,0:T(8,128)(2,1)} %copy-done.8, ...), custom_call_target="tpu_custom_call" | custom-call | flops 1207959552 | bytes 8388608 | tf_op jit(solution)/shard_map/gru/pallas_call | solution.py:381
  43.6 3.6 %all-to-all-start.2 = ((bf16[32,72,128]{2,1,0:T(8,128)(2,1)}), bf16[32,72,128]{2,1,0:T(8,128)(2,1)S(1)}, u32[]{:S(2)}, u32[]{:S(2)}) async-start(bf16[32,72,128]{2,1,0:T(8,128)(2,1)} %get-tuple-element.28), calls=%async_computation.2 | async-start | bytes 1179648 | tf_op jit(solution)/shard_map/all_to_all | solution.py:399
  47.2 1.8 %collective-permute-start.16 = (s32[8,128]{1,0:T(8,128)S(1)}, s32[8,128]{1,0:T(8,128)S(1)}, u32[]{:S(2)}, u32[]{:S(2)}) collective-permute-start(s32[8,128]{1,0:T(8,128)S(1)} %bitcast.22), channel_id=1, source_target_pairs={{0,2},{1,3},{2,0},{3,1},{4,6},{5,7},{6,4},{7,5},{8,10},{9,11},{10,... | collective-permute-start | bytes 12296 | tf_op jit(solution)/shard_map/ppermute | solution.py:295
  49.0 3.1 %collective-permute-done.16 = s32[8,128]{1,0:T(8,128)S(1)} collective-permute-done((s32[8,128]{1,0:T(8,128)S(1)}, s32[8,128]{1,0:T(8,128)S(1)}, u32[]{:S(2)}, u32[]{:S(2)}) %collective-permute-start.16) | collective-permute-done | bytes 4128 | tf_op jit(solution)/shard_map/ppermute | solution.py:295
  52.1 1.2 %collective-permute-done.15 = s32[8,128]{1,0:T(8,128)S(1)} collective-permute-done((s32[8,128]{1,0:T(8,128)S(1)}, s32[8,128]{1,0:T(8,128)S(1)}, u32[]{:S(2)}, u32[]{:S(2)}) %collective-permute-start.15) | collective-permute-done | bytes 4128 | tf_op jit(solution)/shard_map/ppermute | solution.py:295
  54.0 0.5 collective-permute-done.17
  54.5 0.5 gather_fusion
  55.5 4.1 %attend.1 = (bf16[384,512]{1,0:T(8,128)(2,1)}, bf16[1024,128]{1,0:T(8,128)(2,1)S(1)}) custom-call(s32[3,2]{1,0:T(4,128)S(1)} %copy.20.listed_ref, f32[384,512]{1,0:T(8,128)S(1)} %get-tuple-element.23.hnew_ref, bf16[384,512]{1,0:T(8,128)(2,1)S(1)} %get-tuple-element.24.hdst_ref, bf16[1024,512]{1,0:T(8,128)(2,1)S(1)} %copy-done, ...), custom_call_target="tpu_custom_call" | custom-call | flops 603979776 | bytes 4194304 | tf_op jit(solution)/shard_map/attend/pallas_call | solution.py:401
  59.6 0.7 copy-done.5
  60.3 3.7 %all-to-all-done.2 = bf16[32,72,128]{2,1,0:T(8,128)(2,1)S(1)} async-done(((bf16[32,72,128]{2,1,0:T(8,128)(2,1)}), bf16[32,72,128]{2,1,0:T(8,128)(2,1)S(1)}, u32[]{:S(2)}, u32[]{:S(2)}) %all-to-all-start.2) | async-done | bytes 589856 | tf_op jit(solution)/shard_map/all_to_all | solution.py:399
  63.9 2.2 %apply.1.refs_0_ = bf16[1024,128]{1,0:T(8,128)(2,1)S(1)} custom-call(s32[1,2304]{1,0:T(1,128)S(1)} %reshape.48.ids_ref, bf16[2304,128]{1,0:T(8,128)(2,1)S(1)} %bitcast.20, bf16[1024,128]{1,0:T(8,128)(2,1)} %copy-done.5), custom_call_target="tpu_custom_call" | custom-call | flops 1207959552 | bytes 4194304 | tf_op jit(solution)/shard_map/apply/pallas_call | solution.py:419
  66.1 1.2 %collective-permute-start.19 = (bf16[1024,128]{1,0:T(8,128)(2,1)S(1)}, bf16[1024,128]{1,0:T(8,128)(2,1)S(1)}, u32[]{:S(2)}, u32[]{:S(2)}) collective-permute-start(bf16[1024,128]{1,0:T(8,128)(2,1)S(1)} %apply.1.refs_0_), channel_id=1, source_target_pairs={{0,2},{1,3},{2,0},{3,1},{4,6},{5,7},{6,4},{7,5},{8,10},{9,11},{10,... | collective-permute-start | bytes 786440 | tf_op jit(solution)/shard_map/ppermute | solution.py:295
  67.4 7.0 %collective-permute-done.19.refs_2_ = bf16[1024,128]{1,0:T(8,128)(2,1)S(1)} collective-permute-done((bf16[1024,128]{1,0:T(8,128)(2,1)S(1)}, bf16[1024,128]{1,0:T(8,128)(2,1)S(1)}, u32[]{:S(2)}, u32[]{:S(2)}) %collective-permute-start.19) | collective-permute-done | bytes 262176 | tf_op jit(solution)/shard_map/ppermute | solution.py:295
  74.4 1.5 %collective-permute-done.20.refs_3_ = bf16[1024,128]{1,0:T(8,128)(2,1)S(1)} collective-permute-done((bf16[1024,128]{1,0:T(8,128)(2,1)S(1)}, bf16[1024,128]{1,0:T(8,128)(2,1)S(1)}, u32[]{:S(2)}, u32[]{:S(2)}) %collective-permute-start.20) | collective-permute-done | bytes 262176 | tf_op jit(solution)/shard_map/ppermute | solution.py:295
  75.9 1.2 %join.1 = bf16[1024,512]{1,0:T(8,128)(2,1)} custom-call(bf16[1024,128]{1,0:T(8,128)(2,1)S(1)} %apply.1.refs_0_, bf16[1024,128]{1,0:T(8,128)(2,1)S(1)} %collective-permute-done.18.refs_1_, bf16[1024,128]{1,0:T(8,128)(2,1)S(1)} %collective-permute-done.19.refs_2_, bf16[1024,128]{1,0:T(8,128)(2,1)S(1)} %collective-permute-done.20.refs_3_), custom_call_target="tpu_custom_call" | custom-call | flops 1048576 | bytes 2097152 | tf_op jit(solution)/shard_map/join/pallas_call | solution.py:429
  (78 shorter events, 3.1 us)
Async XLA Ops:
  2.3 22.8 %collective-permute-start.1 = (bf16[512,384]{1,0:T(8,128)(2,1)}, bf16[512,384]{1,0:T(8,128)(2,1)S(1)}, u32[]{:S(2)}, u32[]{:S(2)}) collective-permute-start(bf16[512,384]{1,0:T(8,128)(2,1)} %refs_0_), channel_id=1, source_target_pairs={{0,2},{1,3},{2,0},{3,1},{4,6},{5,7},{6,4},{7,5},{8,10},{9,11},{10,... | collective-permute-start | bytes 1179656 | tf_op jit(solution)/shard_map/ppermute | solution.py:295
  5.2 20.4 %collective-permute-start.4 = (bf16[512,384]{1,0:T(8,128)(2,1)}, bf16[512,384]{1,0:T(8,128)(2,1)S(1)}, u32[]{:S(2)}, u32[]{:S(2)}) collective-permute-start(bf16[512,384]{1,0:T(8,128)(2,1)} %refs_4_), channel_id=1, source_target_pairs={{0,2},{1,3},{2,0},{3,1},{4,6},{5,7},{6,4},{7,5},{8,10},{9,11},{10,... | collective-permute-start | bytes 1179656 | tf_op jit(solution)/shard_map/ppermute | solution.py:295
  5.3 12.7 %all-to-all-start = ((s32[8,1,128]{2,1,0:T(1,128)}), s32[8,1,128]{2,1,0:T(1,128)S(1)}, u32[]{:S(2)}, u32[]{:S(2)}) async-start(s32[8,1,128]{2,1,0:T(1,128)} %bitcast.3), calls=%async_computation | async-start | bytes 8192 | tf_op jit(solution)/shard_map/all_to_all | solution.py:348
  11.6 20.8 %collective-permute-start = (bf16[512,384]{1,0:T(8,128)(2,1)}, bf16[512,384]{1,0:T(8,128)(2,1)S(1)}, u32[]{:S(2)}, u32[]{:S(2)}) collective-permute-start(bf16[512,384]{1,0:T(8,128)(2,1)} %refs_0_), channel_id=1, source_target_pairs={{0,1},{1,0},{2,3},{3,2},{4,5},{5,4},{6,7},{7,6},{8,9},{9,8},{10,11... | collective-permute-start | bytes 1179656 | tf_op jit(solution)/shard_map/ppermute | solution.py:295
  11.6 20.8 %collective-permute-start.3 = (bf16[512,384]{1,0:T(8,128)(2,1)}, bf16[512,384]{1,0:T(8,128)(2,1)S(1)}, u32[]{:S(2)}, u32[]{:S(2)}) collective-permute-start(bf16[512,384]{1,0:T(8,128)(2,1)} %refs_4_), channel_id=1, source_target_pairs={{0,1},{1,0},{2,3},{3,2},{4,5},{5,4},{6,7},{7,6},{8,9},{9,8},{10,11... | collective-permute-start | bytes 1179656 | tf_op jit(solution)/shard_map/ppermute | solution.py:295
  12.1 13.0 %collective-permute-start.7 = (bf16[128,384]{1,0:T(8,128)(2,1)}, bf16[128,384]{1,0:T(8,128)(2,1)S(1)}, u32[]{:S(2)}, u32[]{:S(2)}) collective-permute-start(bf16[128,384]{1,0:T(8,128)(2,1)} %refs_8_), channel_id=1, source_target_pairs={{0,2},{1,3},{2,0},{3,1},{4,6},{5,7},{6,4},{7,5},{8,10},{9,11},{10,... | collective-permute-start | bytes 294920 | tf_op jit(solution)/shard_map/ppermute | solution.py:295
  20.9 4.2 %copy-start.18 = (bf16[128,384]{1,0:T(8,128)(2,1)S(1)}, bf16[128,384]{1,0:T(8,128)(2,1)}, u32[]{:S(2)}) copy-start(bf16[128,384]{1,0:T(8,128)(2,1)} %refs_8_) | copy-start | bytes 294916
  20.9 16.8 %all-to-all-start.1 = ((bf16[8,264,128]{2,1,0:T(8,128)(2,1)}), bf16[8,264,128]{2,1,0:T(8,128)(2,1)S(1)}, u32[]{:S(2)}, u32[]{:S(2)}) async-start(bf16[8,264,128]{2,1,0:T(8,128)(2,1)} %serve.1), calls=%async_computation.1 | async-start | bytes 1081344 | tf_op jit(solution)/shard_map/all_to_all | solution.py:379
  25.1 4.0 %copy-start.19 = (bf16[128,384]{1,0:T(8,128)(2,1)}, bf16[128,384]{1,0:T(8,128)(2,1)S(1)}, u32[]{:S(2)}) copy-start(bf16[128,384]{1,0:T(8,128)(2,1)S(1)} %collective-permute-done.7.refs_10_) | copy-start | bytes 294916
  25.1 4.0 %collective-permute-start.6 = (bf16[128,384]{1,0:T(8,128)(2,1)S(1)}, bf16[128,384]{1,0:T(8,128)(2,1)S(1)}, u32[]{:S(2)}, u32[]{:S(2)}) collective-permute-start(bf16[128,384]{1,0:T(8,128)(2,1)S(1)} %copy-done.18), channel_id=1, source_target_pairs={{0,1},{1,0},{2,3},{3,2},{4,5},{5,4},{6,7},{7,6},{8,9},{9,8},{10,11... | collective-permute-start | bytes 294920 | tf_op jit(solution)/shard_map/ppermute | solution.py:295
  25.1 7.8 %collective-permute-start.2 = (bf16[512,384]{1,0:T(8,128)(2,1)S(1)}, bf16[512,384]{1,0:T(8,128)(2,1)}, u32[]{:S(2)}, u32[]{:S(2)}) collective-permute-start(bf16[512,384]{1,0:T(8,128)(2,1)S(1)} %collective-permute-done.1.refs_2_), channel_id=1, source_target_pairs={{0,1},{1,0},{2,3},{3,2},{4,5},{5,4},{6,7},{7,6},{8,9},{9,8},{10,11... | collective-permute-start | bytes 1179656 | tf_op jit(solution)/shard_map/ppermute | solution.py:295
  25.6 7.4 %collective-permute-start.5 = (bf16[512,384]{1,0:T(8,128)(2,1)S(1)}, bf16[512,384]{1,0:T(8,128)(2,1)}, u32[]{:S(2)}, u32[]{:S(2)}) collective-permute-start(bf16[512,384]{1,0:T(8,128)(2,1)S(1)} %collective-permute-done.4.refs_6_), channel_id=1, source_target_pairs={{0,1},{1,0},{2,3},{3,2},{4,5},{5,4},{6,7},{7,6},{8,9},{9,8},{10,11... | collective-permute-start | bytes 1179656 | tf_op jit(solution)/shard_map/ppermute | solution.py:295
  26.4 4.2 %copy-start.1 = (bf16[512,256]{1,0:T(8,128)(2,1)S(1)}, bf16[512,256]{1,0:T(8,128)(2,1)}, u32[]{:S(2)}) copy-start(bf16[512,256]{1,0:T(8,128)(2,1)} %refs_4_.1) | copy-start | bytes 786436
  26.4 6.0 %copy-start.2 = (bf16[512,128]{1,0:T(8,128)(2,1)S(1)}, bf16[512,128]{1,0:T(8,128)(2,1)}, u32[]{:S(2)}) copy-start(bf16[512,128]{1,0:T(8,128)(2,1)} %refs_0_.1) | copy-start | bytes 393220
  29.1 8.6 %copy-start.20 = (bf16[128,384]{1,0:T(8,128)(2,1)}, bf16[128,384]{1,0:T(8,128)(2,1)S(1)}, u32[]{:S(2)}) copy-start(bf16[128,384]{1,0:T(8,128)(2,1)S(1)} %collective-permute-done.6.refs_9_) | copy-start | bytes 294916
  29.1 1.5 %collective-permute-start.8 = (bf16[128,384]{1,0:T(8,128)(2,1)S(1)}, bf16[128,384]{1,0:T(8,128)(2,1)}, u32[]{:S(2)}, u32[]{:S(2)}) collective-permute-start(bf16[128,384]{1,0:T(8,128)(2,1)S(1)} %collective-permute-done.7.refs_10_), channel_id=1, source_target_pairs={{0,1},{1,0},{2,3},{3,2},{4,5},{5,4},{6,7},{7,6},{8,9},{9,8},{10,11... | collective-permute-start | bytes 294920 | tf_op jit(solution)/shard_map/ppermute | solution.py:295
  30.6 23.2 %collective-permute-start.13 = (bf16[512,256]{1,0:T(8,128)(2,1)S(1)}, bf16[512,256]{1,0:T(8,128)(2,1)S(1)}, u32[]{:S(2)}, u32[]{:S(2)}) collective-permute-start(bf16[512,256]{1,0:T(8,128)(2,1)S(1)} %copy-done.1), channel_id=1, source_target_pairs={{0,2},{1,3},{2,0},{3,1},{4,6},{5,7},{6,4},{7,5},{8,10},{9,11},{10,... | collective-permute-start | bytes 786440 | tf_op jit(solution)/shard_map/ppermute | solution.py:295
  32.4 5.3 %copy-start.16 = (bf16[512,384]{1,0:T(8,128)(2,1)}, bf16[512,384]{1,0:T(8,128)(2,1)S(1)}, u32[]{:S(2)}) copy-start(bf16[512,384]{1,0:T(8,128)(2,1)S(1)} %collective-permute-done.refs_1_) | copy-start | bytes 1179652
  32.4 22.8 %collective-permute-start.12 = (bf16[512,256]{1,0:T(8,128)(2,1)S(1)}, bf16[512,256]{1,0:T(8,128)(2,1)}, u32[]{:S(2)}, u32[]{:S(2)}) collective-permute-start(bf16[512,256]{1,0:T(8,128)(2,1)S(1)} %copy-done.1), channel_id=1, source_target_pairs={{0,1},{1,0},{2,3},{3,2},{4,5},{5,4},{6,7},{7,6},{8,9},{9,8},{10,11... | collective-permute-start | bytes 786440 | tf_op jit(solution)/shard_map/ppermute | solution.py:295
  32.4 5.3 %copy-start.17 = (bf16[512,384]{1,0:T(8,128)(2,1)}, bf16[512,384]{1,0:T(8,128)(2,1)S(1)}, u32[]{:S(2)}) copy-start(bf16[512,384]{1,0:T(8,128)(2,1)S(1)} %collective-permute-done.3.refs_5_) | copy-start | bytes 1179652
  32.4 21.0 %collective-permute-start.10 = (bf16[512,128]{1,0:T(8,128)(2,1)S(1)}, bf16[512,128]{1,0:T(8,128)(2,1)}, u32[]{:S(2)}, u32[]{:S(2)}) collective-permute-start(bf16[512,128]{1,0:T(8,128)(2,1)S(1)} %copy-done.2), channel_id=1, source_target_pairs={{0,2},{1,3},{2,0},{3,1},{4,6},{5,7},{6,4},{7,5},{8,10},{9,11},{10,... | collective-permute-start | bytes 393224 | tf_op jit(solution)/shard_map/ppermute | solution.py:295
  32.9 22.3 %collective-permute-start.9 = (bf16[512,128]{1,0:T(8,128)(2,1)S(1)}, bf16[512,128]{1,0:T(8,128)(2,1)}, u32[]{:S(2)}, u32[]{:S(2)}) collective-permute-start(bf16[512,128]{1,0:T(8,128)(2,1)S(1)} %copy-done.2), channel_id=1, source_target_pairs={{0,1},{1,0},{2,3},{3,2},{4,5},{5,4},{6,7},{7,6},{8,9},{9,8},{10,11... | collective-permute-start | bytes 393224 | tf_op jit(solution)/shard_map/ppermute | solution.py:295
  43.6 11.9 %copy-start = (bf16[1024,512]{1,0:T(8,128)(2,1)S(1)}, bf16[1024,512]{1,0:T(8,128)(2,1)}, u32[]{:S(2)}) copy-start(bf16[1024,512]{1,0:T(8,128)(2,1)} %memory_ref.3) | copy-start | bytes 3145732
  43.6 20.4 %all-to-all-start.2 = ((bf16[32,72,128]{2,1,0:T(8,128)(2,1)}), bf16[32,72,128]{2,1,0:T(8,128)(2,1)S(1)}, u32[]{:S(2)}, u32[]{:S(2)}) async-start(bf16[32,72,128]{2,1,0:T(8,128)(2,1)} %get-tuple-element.28), calls=%async_computation.2 | async-start | bytes 1179648 | tf_op jit(solution)/shard_map/all_to_all | solution.py:399
  47.2 4.9 %collective-permute-start.16 = (s32[8,128]{1,0:T(8,128)S(1)}, s32[8,128]{1,0:T(8,128)S(1)}, u32[]{:S(2)}, u32[]{:S(2)}) collective-permute-start(s32[8,128]{1,0:T(8,128)S(1)} %bitcast.22), channel_id=1, source_target_pairs={{0,2},{1,3},{2,0},{3,1},{4,6},{5,7},{6,4},{7,5},{8,10},{9,11},{10,... | collective-permute-start | bytes 12296 | tf_op jit(solution)/shard_map/ppermute | solution.py:295
  52.1 1.2 %collective-permute-start.15 = (s32[8,128]{1,0:T(8,128)S(1)}, s32[8,128]{1,0:T(8,128)S(1)}, u32[]{:S(2)}, u32[]{:S(2)}) collective-permute-start(s32[8,128]{1,0:T(8,128)S(1)} %bitcast.24), channel_id=1, source_target_pairs={{0,1},{1,0},{2,3},{3,2},{4,5},{5,4},{6,7},{7,6},{8,9},{9,8},{10,11... | collective-permute-start | bytes 12296 | tf_op jit(solution)/shard_map/ppermute | solution.py:295
  53.3 1.2 %collective-permute-start.17 = (s32[8,128]{1,0:T(8,128)S(1)}, s32[8,128]{1,0:T(8,128)S(1)}, u32[]{:S(2)}, u32[]{:S(2)}) collective-permute-start(s32[8,128]{1,0:T(8,128)S(1)} %collective-permute-done.16), channel_id=1, source_target_pairs={{0,1},{1,0},{2,3},{3,2},{4,5},{5,4},{6,7},{7,6},{8,9},{9,8},{10,11... | collective-permute-start | bytes 12296 | tf_op jit(solution)/shard_map/ppermute | solution.py:295
  53.5 1.7 %collective-permute-start.11 = (bf16[512,128]{1,0:T(8,128)(2,1)}, bf16[512,128]{1,0:T(8,128)(2,1)}, u32[]{:S(2)}, u32[]{:S(2)}) collective-permute-start(bf16[512,128]{1,0:T(8,128)(2,1)} %collective-permute-done.10.refs_2_), channel_id=1, source_target_pairs={{0,1},{1,0},{2,3},{3,2},{4,5},{5,4},{6,7},{7,6},{8,9},{9,8},{10,11... | collective-permute-start | bytes 393224 | tf_op jit(solution)/shard_map/ppermute | solution.py:295
  53.8 1.7 %collective-permute-start.14 = (bf16[512,256]{1,0:T(8,128)(2,1)S(1)}, bf16[512,256]{1,0:T(8,128)(2,1)}, u32[]{:S(2)}, u32[]{:S(2)}) collective-permute-start(bf16[512,256]{1,0:T(8,128)(2,1)S(1)} %collective-permute-done.13.refs_6_), channel_id=1, source_target_pairs={{0,1},{1,0},{2,3},{3,2},{4,5},{5,4},{6,7},{7,6},{8,9},{9,8},{10,11... | collective-permute-start | bytes 786440 | tf_op jit(solution)/shard_map/ppermute | solution.py:295
  66.1 8.3 %collective-permute-start.19 = (bf16[1024,128]{1,0:T(8,128)(2,1)S(1)}, bf16[1024,128]{1,0:T(8,128)(2,1)S(1)}, u32[]{:S(2)}, u32[]{:S(2)}) collective-permute-start(bf16[1024,128]{1,0:T(8,128)(2,1)S(1)} %apply.1.refs_0_), channel_id=1, source_target_pairs={{0,2},{1,3},{2,0},{3,1},{4,6},{5,7},{6,4},{7,5},{8,10},{9,11},{10,... | collective-permute-start | bytes 786440 | tf_op jit(solution)/shard_map/ppermute | solution.py:295
  67.3 7.1 %collective-permute-start.18 = (bf16[1024,128]{1,0:T(8,128)(2,1)S(1)}, bf16[1024,128]{1,0:T(8,128)(2,1)S(1)}, u32[]{:S(2)}, u32[]{:S(2)}) collective-permute-start(bf16[1024,128]{1,0:T(8,128)(2,1)S(1)} %apply.1.refs_0_), channel_id=1, source_target_pairs={{0,1},{1,0},{2,3},{3,2},{4,5},{5,4},{6,7},{7,6},{8,9},{9,8},{10,11... | collective-permute-start | bytes 786440 | tf_op jit(solution)/shard_map/ppermute | solution.py:295
  74.4 1.5 %collective-permute-start.20 = (bf16[1024,128]{1,0:T(8,128)(2,1)S(1)}, bf16[1024,128]{1,0:T(8,128)(2,1)S(1)}, u32[]{:S(2)}, u32[]{:S(2)}) collective-permute-start(bf16[1024,128]{1,0:T(8,128)(2,1)S(1)} %collective-permute-done.19.refs_2_), channel_id=1, source_target_pairs={{0,1},{1,0},{2,3},{3,2},{4,5},{5,4},{6,7},{7,6},{8,9},{9,8},{10,11... | collective-permute-start | bytes 786440 | tf_op jit(solution)/shard_map/ppermute | solution.py:295
  (13 other events, 24.5 us)

commit v7 on v6

--- a/solution.py
+++ b/solution.py
@@ -28,12 +28,12 @@
     return jnp.dot(a, b, preferred_element_type=F32)
 
 
-def call(body, outs, specs, flops, bytes_, name, scratch=(), limit=8):
+def call(body, outs, specs, flops, bytes_, name, scratch=(), limit=8, out_specs=None):
     return pl.pallas_call(
         body,
         out_shape=outs,
         in_specs=specs,
-        out_specs=[VMEM] * len(outs),
+        out_specs=out_specs or [VMEM] * len(outs),
         scratch_shapes=list(scratch),
         compiler_params=pltpu.CompilerParams(vmem_limit_bytes=limit << 20),
         cost_estimate=pl.CostEstimate(flops=flops, bytes_accessed=bytes_, transcendentals=0),
@@ -144,9 +144,10 @@
         spare = asked[:, plan.main + i : plan.main + i + 1]
         blocks.append(jnp.where(spare == iota((plan.owners, stored), 1), 1.0, 0.0))
     hot_ref[...] = jnp.concatenate(blocks, axis=0).astype(BF16)
-    for copy in copies:
+    rows = 0.0
+    for i, copy in enumerate(copies):
         copy.wait()
-    rows = dot(hot_ref[...], held[...])
+        rows += dot(hot_ref[:, i * step : (i + 1) * step], held[i * step : (i + 1) * step, :])
     main = plan.main
     for s in range(plan.owners):
         for c in range(4):
@@ -266,7 +267,7 @@
             out_ref[at, lane] = (hnew_ref[at, lane] + dot(prob, values)).astype(BF16)
 
 
-def apply_kernel(plan, ids_ref, landed_ref, part_ref, out_ref, held, sem):
+def apply_kernel(plan, ids_ref, landed_ref, part_ref, out_ref, held, total, sem):
     copy = pltpu.make_async_copy(part_ref, held, sem)
     copy.start()
     stored = part_ref.shape[0]
@@ -274,21 +275,25 @@
     landed = landed_ref[...]
     step = min(256, stored)
     ids = ids_ref[...]
-    totals = []
     for i in range(0, stored, step):
         hot = jnp.where(iota((step, count), 0) + i == ids, 1.0, 0.0).astype(BF16)
-        totals.append(dot(hot, landed))
+        total[i : i + step, :] = dot(hot, landed)
     copy.wait()
-    for i, total in zip(range(0, stored, step), totals):
-        out_ref[i : i + step, :] = (held[i : i + step, :].astype(F32) + total).astype(BF16)
+    out_ref[...] = (held[...].astype(F32) + total[...]).astype(BF16)
 
 
 def join_kernel(plan, *refs):
     me = lax.axis_index("rep")
-    out_ref = refs[-1]
+    out_ref, sems = refs[plan.reps :]
+    copies = []
     for k in range(plan.reps):
         piece = refs[k].shape[1]
-        out_ref[:, pl.ds(pl.multiple_of((me ^ k) * piece, LANES), piece)] = refs[k][...]
+        at = pl.ds(pl.multiple_of((me ^ k) * piece, LANES), piece)
+        copies.append(pltpu.make_async_copy(refs[k], out_ref.at[:, at], sems.at[k]))
+    for copy in copies:
+        copy.start()
+    for copy in copies:
+        copy.wait()
 
 
 def swap(x, bit, reps):
@@ -338,14 +343,9 @@
         run(request_kernel, plan), [sds((owners, LANES), I32)], [VMEM] * 2, 1 << 20, 1 << 14, "request", limit=8
     )(owner, touch_row.reshape(1, entries))[0]
 
-    request, w_time, w_hidden, w_input, w_keyval, w_query = lax.optimization_barrier(
-        (request, w_time, w_hidden, w_input, w_keyval, w_query)
-    )
-    full_time, full_hidden, full_input, full_keyval, full_query = spread(
-        [w_time, w_hidden, w_input, w_keyval, w_query], reps
-    )
-
     asked = lax.all_to_all(request, "shard", split_axis=0, concat_axis=0, tiled=True)
+    packed = jnp.concatenate([touch_time, src_slot, dst_slot, event_time]).reshape(1, -1)
+    _, owner, packed = lax.optimization_barrier((request, owner, packed))
     encode, cols, rows = call(
         run(index_kernel, plan),
         [sds((events, time_freq.shape[0]), BF16), sds((events, 8), F32), sds((8, events), I32)],
@@ -353,12 +353,12 @@
         8 << 30,
         1 << 18,
         "index",
-        limit=8,
-    )(
-        owner,
-        jnp.concatenate([touch_time, src_slot, dst_slot, event_time]).reshape(1, -1),
-        time_freq.reshape(1, -1),
-        time_phase.reshape(1, -1),
+    )(owner, packed, time_freq.reshape(1, -1), time_phase.reshape(1, -1))
+    encode, w_time, w_hidden, w_input, w_keyval, w_query = lax.optimization_barrier(
+        (encode, w_time, w_hidden, w_input, w_keyval, w_query)
+    )
+    full_time, full_hidden, full_input, full_keyval, full_query = spread(
+        [w_time, w_hidden, w_input, w_keyval, w_query], reps
     )
     everyone = [x for x in spread([asked], reps)[0]]
 
@@ -423,11 +423,12 @@
         2 * stored * owners * reps * plan.pad * piece * 2,
         4 << 20,
         "apply",
-        scratch=[pltpu.VMEM((stored, piece), BF16), pltpu.SemaphoreType.DMA],
+        scratch=[pltpu.VMEM((stored, piece), BF16), pltpu.VMEM((stored, piece), F32), pltpu.SemaphoreType.DMA],
         limit=16,
     )(ids, landed.reshape(owners * reps * plan.pad, piece), *far([part]))[0]
     new_memory = call(
-        run(join_kernel, plan), [sds((stored, width), BF16)], [VMEM] * reps, 1 << 20, 2 << 20, "join", limit=8
+        run(join_kernel, plan), [sds((stored, width), BF16)], [VMEM] * reps, 1 << 20, 2 << 20, "join",
+        scratch=[pltpu.SemaphoreType.DMA((reps,))], out_specs=[HBM],
     )(*spread([quarter], reps)[0])[0]
     return (embed, new_memory)
 

time: 77.6 us -> 94.8 us (1.22)
  waiting for transfers between devices: 27.8 us -> 44.8 us
  starting transfers between devices: 25.8 us -> 27 us
    ppermute x21, waiting for transfers between devices: 15 us -> 34.9 us  [swap(): return lax.ppermute(x, 'rep', [(i, i ^ bit) for i in range(reps)])]
    all_to_all x1, waiting for transfers between devices: 4.66 us -> 0.01 us  [shards(): lax.all_to_all(served, 'shard', split_axis=0, concat_axis=0, tiled=True)]
    all_to_all x1, starting transfers between devices: 3.62 us -> 5.67 us  [shards(): lax.all_to_all(outgoing, ('shard', 'rep'), split_axis=0, concat_axis=0, t...]
    all_to_all x1, waiting for transfers between devices: 4.39 us -> 6.32 us  [shards(): lax.all_to_all(request, 'shard', split_axis=0, concat_axis=0, tiled=True)]
    ppermute x21, starting transfers between devices: 12.2 us -> 10.3 us  [swap(): return lax.ppermute(x, 'rep', [(i, i ^ bit) for i in range(reps)])]
    all_to_all x1, starting transfers between devices: 6.34 us -> 7.42 us  [shards(): lax.all_to_all(request, 'shard', split_axis=0, concat_axis=0, tiled=True)]
    unnamed x43 -> x45, local copies, waits for them, and re-layouts: 3.58 us -> 2.81 us
  transfers between devices with their start and end apart: 24 -> 24, of which waited for: 11 -> 13; matrix products, arithmetic and copies ran while one was open for 1% -> 1% of each run, Pallas kernels for 18% -> 12%
where the time goes in v7:
time: 94.8 us; the launch traced here: 94.3 us
  waiting for transfers between devices  44.8 us (47%)
  starting transfers between devices  27 us (28%)
  Pallas kernels  18.1 us (19%)
  local copies, waits for them, and re-layouts  3.48 us (4%)
    ppermute x21, waiting for transfers between devices, swap(): return lax.ppermute(x, 'rep', [(i, i ^ bit) for i in range(reps)])  34.9 us
    ppermute x21, starting transfers between devices, swap(): return lax.ppermute(x, 'rep', [(i, i ^ bit) for i in range(reps)])  10.3 us
    all_to_all x1, starting transfers between devices, shards(): lax.all_to_all(request, 'shard', split_axis=0, concat_axis=0, tiled=True)  7.42 us
    all_to_all x1, waiting for transfers between devices, shards(): lax.all_to_all(request, 'shard', split_axis=0, concat_axis=0, tiled=True)  6.32 us
    pallas_call x1, Pallas kernels, shards(): call(run(gru_kernel, plan), [sds((owners * reps, plan.pad, piece), BF16),...  5.83 us
    all_to_all x1, starting transfers between devices, shards(): lax.all_to_all(outgoing, ('shard', 'rep'), split_axis=0, concat_axis=0, t...  5.67 us
    pallas_call x1, Pallas kernels, shards(): call(run(attend_kernel, plan), [sds((events, width), BF16), sds((stored,...  4.09 us
    all_to_all x1, waiting for transfers between devices, shards(): lax.all_to_all(outgoing, ('shard', 'rep'), split_axis=0, concat_axis=0, t...  3.67 us
  transfers between devices with their start and end apart: 24, of which 13 were waited for; matrix products, arithmetic and copies ran while one was open for 1% of the time, Pallas kernels for 12%

profile of v7, /device:TPU:0, one launch (start us, length us, event | category | flops | bytes accessed | tf_op | source)
XLA Modules:
  0.0 94.3 jit_solution(3720931121279162431)
XLA Ops:
  0.6 0.7 copy-done.4
  1.3 1.0 %request.1 = s32[8,128]{1,0:T(8,128)} custom-call(s32[1,256]{1,0:T(1,128)S(1)} %bitcast.26, s32[1,256]{1,0:T(1,128)S(1)} %bitcast.25), custom_call_target="tpu_custom_call" | custom-call | flops 1048576 | bytes 16384 | tf_op jit(solution)/shard_map/request/pallas_call | solution.py:342
  2.3 7.4 %all-to-all-start = ((s32[8,1,128]{2,1,0:T(1,128)}), s32[8,1,128]{2,1,0:T(1,128)S(1)}, u32[]{:S(2)}, u32[]{:S(2)}) async-start(s32[8,1,128]{2,1,0:T(1,128)} %bitcast.3), calls=%async_computation | async-start | bytes 8192 | tf_op jit(solution)/shard_map/all_to_all | solution.py:346
  9.8 6.3 %all-to-all-done = s32[8,1,128]{2,1,0:T(1,128)S(1)} async-done(((s32[8,1,128]{2,1,0:T(1,128)}), s32[8,1,128]{2,1,0:T(1,128)S(1)}, u32[]{:S(2)}, u32[]{:S(2)}) %all-to-all-start) | async-done | bytes 4128 | tf_op jit(solution)/shard_map/all_to_all | solution.py:346
  16.1 2.8 %serve.1 = bf16[8,264,128]{2,1,0:T(8,128)(2,1)} custom-call(s32[8,128]{1,0:T(8,128)S(1)} %bitcast.21, bf16[1024,512]{1,0:T(8,128)(2,1)} %memory_ref.3), custom_call_target="tpu_custom_call" | custom-call | flops 553648128 | bytes 1589248 | tf_op jit(solution)/shard_map/serve/pallas_call | solution.py:365
  18.9 3.5 %all-to-all-start.1 = ((bf16[8,264,128]{2,1,0:T(8,128)(2,1)}), bf16[8,264,128]{2,1,0:T(8,128)(2,1)S(1)}, u32[]{:S(2)}, u32[]{:S(2)}) async-start(bf16[8,264,128]{2,1,0:T(8,128)(2,1)} %serve.1), calls=%async_computation.1 | async-start | bytes 1081344 | tf_op jit(solution)/shard_map/all_to_all | solution.py:379
  22.5 0.6 copy-done.6
  23.2 1.2 %index.1 = (bf16[384,128]{1,0:T(8,128)(2,1)S(1)}, f32[384,8]{1,0:T(8,128)S(1)}, s32[8,384]{1,0:T(8,128)S(1)}) custom-call(s32[1,256]{1,0:T(1,128)S(1)} %bitcast.27, s32[1,1408]{1,0:T(1,128)S(1)} %reshape.45.packed_ref, f32[1,128]{1,0:T(1,128)S(1)} %bitcast.28, f32[1,128]{1,0:T(1,128)S(1)} %bitcast.29), custom_call_target="tpu_custom_call" | custom-call | flops 8589934592 | bytes 262144 | tf_op jit(solution)/shard_map/index/pallas_call | solution.py:349
  24.4 0.6 copy-done.8
  25.1 1.5 %collective-permute-start.1 = (bf16[512,384]{1,0:T(8,128)(2,1)S(1)}, bf16[512,384]{1,0:T(8,128)(2,1)S(1)}, u32[]{:S(2)}, u32[]{:S(2)}) collective-permute-start(bf16[512,384]{1,0:T(8,128)(2,1)S(1)} %copy-done.14), channel_id=1, source_target_pairs={{0,2},{1,3},{2,0},{3,1},{4,6},{5,7},{6,4},{7,5},{8,10},{9,11},{10,... | collective-permute-start | bytes 1179656 | tf_op jit(solution)/shard_map/ppermute | solution.py:300
  27.6 9.5 %collective-permute-done.1.refs_2_ = bf16[512,384]{1,0:T(8,128)(2,1)S(1)} collective-permute-done((bf16[512,384]{1,0:T(8,128)(2,1)S(1)}, bf16[512,384]{1,0:T(8,128)(2,1)S(1)}, u32[]{:S(2)}, u32[]{:S(2)}) %collective-permute-start.1) | collective-permute-done | bytes 393248 | tf_op jit(solution)/shard_map/ppermute | solution.py:300
  37.1 5.8 %collective-permute-done.4.refs_6_ = bf16[512,384]{1,0:T(8,128)(2,1)S(1)} collective-permute-done((bf16[512,384]{1,0:T(8,128)(2,1)S(1)}, bf16[512,384]{1,0:T(8,128)(2,1)S(1)}, u32[]{:S(2)}, u32[]{:S(2)}) %collective-permute-start.4) | collective-permute-done | bytes 393248 | tf_op jit(solution)/shard_map/ppermute | solution.py:300
  42.9 1.6 %collective-permute-start.7 = (bf16[128,384]{1,0:T(8,128)(2,1)S(1)}, bf16[128,384]{1,0:T(8,128)(2,1)S(1)}, u32[]{:S(2)}, u32[]{:S(2)}) collective-permute-start(bf16[128,384]{1,0:T(8,128)(2,1)S(1)} %copy-done.18), channel_id=1, source_target_pairs={{0,2},{1,3},{2,0},{3,1},{4,6},{5,7},{6,4},{7,5},{8,10},{9,11},{10,... | collective-permute-start | bytes 294920 | tf_op jit(solution)/shard_map/ppermute | solution.py:300
  44.5 3.6 %collective-permute-done.7.refs_10_ = bf16[128,384]{1,0:T(8,128)(2,1)S(1)} collective-permute-done((bf16[128,384]{1,0:T(8,128)(2,1)S(1)}, bf16[128,384]{1,0:T(8,128)(2,1)S(1)}, u32[]{:S(2)}, u32[]{:S(2)}) %collective-permute-start.7) | collective-permute-done | bytes 98336 | tf_op jit(solution)/shard_map/ppermute | solution.py:300
  48.2 1.2 %collective-permute-done.6.refs_9_ = bf16[128,384]{1,0:T(8,128)(2,1)S(1)} collective-permute-done((bf16[128,384]{1,0:T(8,128)(2,1)S(1)}, bf16[128,384]{1,0:T(8,128)(2,1)S(1)}, u32[]{:S(2)}, u32[]{:S(2)}) %collective-permute-start.6) | collective-permute-done | bytes 98336 | tf_op jit(solution)/shard_map/ppermute | solution.py:300
  49.6 1.1 %collective-permute-done.8.refs_11_ = bf16[128,384]{1,0:T(8,128)(2,1)S(1)} collective-permute-done((bf16[128,384]{1,0:T(8,128)(2,1)S(1)}, bf16[128,384]{1,0:T(8,128)(2,1)S(1)}, u32[]{:S(2)}, u32[]{:S(2)}) %collective-permute-start.8) | collective-permute-done | bytes 98336 | tf_op jit(solution)/shard_map/ppermute | solution.py:300
  50.7 1.5 %collective-permute-start.13 = (bf16[512,256]{1,0:T(8,128)(2,1)S(1)}, bf16[512,256]{1,0:T(8,128)(2,1)S(1)}, u32[]{:S(2)}, u32[]{:S(2)}) collective-permute-start(bf16[512,256]{1,0:T(8,128)(2,1)S(1)} %copy-done.1), channel_id=1, source_target_pairs={{0,2},{1,3},{2,0},{3,1},{4,6},{5,7},{6,4},{7,5},{8,10},{9,11},{10,... | collective-permute-start | bytes 786440 | tf_op jit(solution)/shard_map/ppermute | solution.py:300
  52.3 0.6 collective-permute-start.10
  53.1 5.8 %gru.1 = (bf16[32,72,128]{2,1,0:T(8,128)(2,1)}, f32[384,512]{1,0:T(8,128)S(1)}, bf16[384,512]{1,0:T(8,128)(2,1)S(1)}) custom-call(bf16[8,264,128]{2,1,0:T(8,128)(2,1)S(1)} %all-to-all-done.1.ret_ref, s32[8,384]{1,0:T(8,128)S(1)} %get-tuple-element.20.row_ref, f32[384,8]{1,0:T(8,128)S(1)} %get-tuple-element.21.col_ref, bf16[384,128]{1,0:T(8,128)(2,1)} %copy-done.8, ...), custom_call_target="tpu_custom_call" | custom-call | flops 1207959552 | bytes 8388608 | tf_op jit(solution)/shard_map/gru/pallas_call | solution.py:381
  58.9 5.7 %all-to-all-start.2 = ((bf16[32,72,128]{2,1,0:T(8,128)(2,1)}), bf16[32,72,128]{2,1,0:T(8,128)(2,1)S(1)}, u32[]{:S(2)}, u32[]{:S(2)}) async-start(bf16[32,72,128]{2,1,0:T(8,128)(2,1)} %get-tuple-element.32), calls=%async_computation.2 | async-start | bytes 1179648 | tf_op jit(solution)/shard_map/all_to_all | solution.py:399
  64.6 1.8 %collective-permute-start.16 = (s32[8,128]{1,0:T(8,128)S(1)}, s32[8,128]{1,0:T(8,128)S(1)}, u32[]{:S(2)}, u32[]{:S(2)}) collective-permute-start(s32[8,128]{1,0:T(8,128)S(1)} %bitcast.22), channel_id=1, source_target_pairs={{0,2},{1,3},{2,0},{3,1},{4,6},{5,7},{6,4},{7,5},{8,10},{9,11},{10,... | collective-permute-start | bytes 12296 | tf_op jit(solution)/shard_map/ppermute | solution.py:300
  66.5 3.1 %collective-permute-done.16 = s32[8,128]{1,0:T(8,128)S(1)} collective-permute-done((s32[8,128]{1,0:T(8,128)S(1)}, s32[8,128]{1,0:T(8,128)S(1)}, u32[]{:S(2)}, u32[]{:S(2)}) %collective-permute-start.16) | collective-permute-done | bytes 4128 | tf_op jit(solution)/shard_map/ppermute | solution.py:300
  69.5 1.2 %collective-permute-done.15 = s32[8,128]{1,0:T(8,128)S(1)} collective-permute-done((s32[8,128]{1,0:T(8,128)S(1)}, s32[8,128]{1,0:T(8,128)S(1)}, u32[]{:S(2)}, u32[]{:S(2)}) %collective-permute-start.15) | collective-permute-done | bytes 4128 | tf_op jit(solution)/shard_map/ppermute | solution.py:300
  71.9 0.5 gather_fusion
  72.9 4.1 %attend.1 = (bf16[384,512]{1,0:T(8,128)(2,1)}, bf16[1024,128]{1,0:T(8,128)(2,1)S(1)}) custom-call(s32[3,2]{1,0:T(4,128)S(1)} %copy.20.listed_ref, f32[384,512]{1,0:T(8,128)S(1)} %get-tuple-element.27.hnew_ref, bf16[384,512]{1,0:T(8,128)(2,1)S(1)} %get-tuple-element.28.hdst_ref, bf16[1024,512]{1,0:T(8,128)(2,1)S(1)} %copy-done, ...), custom_call_target="tpu_custom_call" | custom-call | flops 603979776 | bytes 4194304 | tf_op jit(solution)/shard_map/attend/pallas_call | solution.py:401
  77.0 0.7 copy-done.5
  77.7 3.7 %all-to-all-done.2 = bf16[32,72,128]{2,1,0:T(8,128)(2,1)S(1)} async-done(((bf16[32,72,128]{2,1,0:T(8,128)(2,1)}), bf16[32,72,128]{2,1,0:T(8,128)(2,1)S(1)}, u32[]{:S(2)}, u32[]{:S(2)}) %all-to-all-start.2) | async-done | bytes 589856 | tf_op jit(solution)/shard_map/all_to_all | solution.py:399
  81.3 2.2 %apply.1.refs_0_ = bf16[1024,128]{1,0:T(8,128)(2,1)S(1)} custom-call(s32[1,2304]{1,0:T(1,128)S(1)} %reshape.48.ids_ref, bf16[2304,128]{1,0:T(8,128)(2,1)S(1)} %bitcast.20, bf16[1024,128]{1,0:T(8,128)(2,1)} %copy-done.5), custom_call_target="tpu_custom_call" | custom-call | flops 1207959552 | bytes 4194304 | tf_op jit(solution)/shard_map/apply/pallas_call | solution.py:419
  83.5 1.2 %collective-permute-start.19 = (bf16[1024,128]{1,0:T(8,128)(2,1)S(1)}, bf16[1024,128]{1,0:T(8,128)(2,1)S(1)}, u32[]{:S(2)}, u32[]{:S(2)}) collective-permute-start(bf16[1024,128]{1,0:T(8,128)(2,1)S(1)} %apply.1.refs_0_), channel_id=1, source_target_pairs={{0,2},{1,3},{2,0},{3,1},{4,6},{5,7},{6,4},{7,5},{8,10},{9,11},{10,... | collective-permute-start | bytes 786440 | tf_op jit(solution)/shard_map/ppermute | solution.py:300
  84.8 7.0 %collective-permute-done.19.refs_2_ = bf16[1024,128]{1,0:T(8,128)(2,1)S(1)} collective-permute-done((bf16[1024,128]{1,0:T(8,128)(2,1)S(1)}, bf16[1024,128]{1,0:T(8,128)(2,1)S(1)}, u32[]{:S(2)}, u32[]{:S(2)}) %collective-permute-start.19) | collective-permute-done | bytes 262176 | tf_op jit(solution)/shard_map/ppermute | solution.py:300
  91.8 1.5 %collective-permute-done.20.refs_3_ = bf16[1024,128]{1,0:T(8,128)(2,1)S(1)} collective-permute-done((bf16[1024,128]{1,0:T(8,128)(2,1)S(1)}, bf16[1024,128]{1,0:T(8,128)(2,1)S(1)}, u32[]{:S(2)}, u32[]{:S(2)}) %collective-permute-start.20) | collective-permute-done | bytes 262176 | tf_op jit(solution)/shard_map/ppermute | solution.py:300
  93.3 1.0 %join.1 = bf16[1024,512]{1,0:T(8,128)(2,1)} custom-call(bf16[1024,128]{1,0:T(8,128)(2,1)S(1)} %apply.1.refs_0_, bf16[1024,128]{1,0:T(8,128)(2,1)S(1)} %collective-permute-done.18.refs_1_, bf16[1024,128]{1,0:T(8,128)(2,1)S(1)} %collective-permute-done.19.refs_2_, bf16[1024,128]{1,0:T(8,128)(2,1)S(1)} %collective-permute-done.20.refs_3_), custom_call_target="tpu_custom_call" | custom-call | flops 1048576 | bytes 2097152 | tf_op jit(solution)/shard_map/join/pallas_call | solution.py:429
  (80 shorter events, 3.3 us)
Async XLA Ops:
  2.3 7.5 %copy-start.13 = (s32[256]{0:T(256)S(1)}, s32[256]{0:T(256)}, u32[]{:S(2)}) copy-start(s32[256]{0:T(256)} %param.18) | copy-start | bytes 3076
  2.3 13.8 %all-to-all-start = ((s32[8,1,128]{2,1,0:T(1,128)}), s32[8,1,128]{2,1,0:T(1,128)S(1)}, u32[]{:S(2)}, u32[]{:S(2)}) async-start(s32[8,1,128]{2,1,0:T(1,128)} %bitcast.3), calls=%async_computation | async-start | bytes 8192 | tf_op jit(solution)/shard_map/all_to_all | solution.py:346
  18.9 34.1 %all-to-all-start.1 = ((bf16[8,264,128]{2,1,0:T(8,128)(2,1)}), bf16[8,264,128]{2,1,0:T(8,128)(2,1)S(1)}, u32[]{:S(2)}, u32[]{:S(2)}) async-start(bf16[8,264,128]{2,1,0:T(8,128)(2,1)} %serve.1), calls=%async_computation.1 | async-start | bytes 1081344 | tf_op jit(solution)/shard_map/all_to_all | solution.py:379
  23.2 19.8 %copy-start.18 = (bf16[128,384]{1,0:T(8,128)(2,1)S(1)}, bf16[128,384]{1,0:T(8,128)(2,1)}, u32[]{:S(2)}) copy-start(bf16[128,384]{1,0:T(8,128)(2,1)} %refs_8_) | copy-start | bytes 294916
  23.2 27.6 %copy-start.1 = (bf16[512,256]{1,0:T(8,128)(2,1)S(1)}, bf16[512,256]{1,0:T(8,128)(2,1)}, u32[]{:S(2)}) copy-start(bf16[512,256]{1,0:T(8,128)(2,1)} %refs_4_.1) | copy-start | bytes 786436
  23.2 29.1 %copy-start.2 = (bf16[512,128]{1,0:T(8,128)(2,1)S(1)}, bf16[512,128]{1,0:T(8,128)(2,1)}, u32[]{:S(2)}) copy-start(bf16[512,128]{1,0:T(8,128)(2,1)} %refs_0_.1) | copy-start | bytes 393220
  25.1 23.1 %copy-start.12 = (s32[3,2]{0,1:T(2,128)S(1)}, s32[3,2]{0,1:T(2,128)}, u32[]{:S(2)}) copy-start(s32[3,2]{0,1:T(2,128)} %param.22) | copy-start | bytes 76
  25.1 12.1 %collective-permute-start.1 = (bf16[512,384]{1,0:T(8,128)(2,1)S(1)}, bf16[512,384]{1,0:T(8,128)(2,1)S(1)}, u32[]{:S(2)}, u32[]{:S(2)}) collective-permute-start(bf16[512,384]{1,0:T(8,128)(2,1)S(1)} %copy-done.14), channel_id=1, source_target_pairs={{0,2},{1,3},{2,0},{3,1},{4,6},{5,7},{6,4},{7,5},{8,10},{9,11},{10,... | collective-permute-start | bytes 1179656 | tf_op jit(solution)/shard_map/ppermute | solution.py:300
  26.6 16.4 %collective-permute-start.4 = (bf16[512,384]{1,0:T(8,128)(2,1)S(1)}, bf16[512,384]{1,0:T(8,128)(2,1)S(1)}, u32[]{:S(2)}, u32[]{:S(2)}) collective-permute-start(bf16[512,384]{1,0:T(8,128)(2,1)S(1)} %copy-done.15), channel_id=1, source_target_pairs={{0,2},{1,3},{2,0},{3,1},{4,6},{5,7},{6,4},{7,5},{8,10},{9,11},{10,... | collective-permute-start | bytes 1179656 | tf_op jit(solution)/shard_map/ppermute | solution.py:300
  27.1 25.2 %collective-permute-start = (bf16[512,384]{1,0:T(8,128)(2,1)S(1)}, bf16[512,384]{1,0:T(8,128)(2,1)}, u32[]{:S(2)}, u32[]{:S(2)}) collective-permute-start(bf16[512,384]{1,0:T(8,128)(2,1)S(1)} %copy-done.14), channel_id=1, source_target_pairs={{0,1},{1,0},{2,3},{3,2},{4,5},{5,4},{6,7},{7,6},{8,9},{9,8},{10,11... | collective-permute-start | bytes 1179656 | tf_op jit(solution)/shard_map/ppermute | solution.py:300
  27.1 25.2 %collective-permute-start.3 = (bf16[512,384]{1,0:T(8,128)(2,1)S(1)}, bf16[512,384]{1,0:T(8,128)(2,1)}, u32[]{:S(2)}, u32[]{:S(2)}) collective-permute-start(bf16[512,384]{1,0:T(8,128)(2,1)S(1)} %copy-done.15), channel_id=1, source_target_pairs={{0,1},{1,0},{2,3},{3,2},{4,5},{5,4},{6,7},{7,6},{8,9},{9,8},{10,11... | collective-permute-start | bytes 1179656 | tf_op jit(solution)/shard_map/ppermute | solution.py:300
  37.1 15.9 %copy-start.16 = (bf16[512,384]{1,0:T(8,128)(2,1)}, bf16[512,384]{1,0:T(8,128)(2,1)S(1)}, u32[]{:S(2)}) copy-start(bf16[512,384]{1,0:T(8,128)(2,1)S(1)} %collective-permute-done.1.refs_2_) | copy-start | bytes 1179652
  37.1 15.7 %collective-permute-start.2 = (bf16[512,384]{1,0:T(8,128)(2,1)S(1)}, bf16[512,384]{1,0:T(8,128)(2,1)}, u32[]{:S(2)}, u32[]{:S(2)}) collective-permute-start(bf16[512,384]{1,0:T(8,128)(2,1)S(1)} %collective-permute-done.1.refs_2_), channel_id=1, source_target_pairs={{0,1},{1,0},{2,3},{3,2},{4,5},{5,4},{6,7},{7,6},{8,9},{9,8},{10,11... | collective-permute-start | bytes 1179656 | tf_op jit(solution)/shard_map/ppermute | solution.py:300
  42.9 10.1 %copy-start.17 = (bf16[512,384]{1,0:T(8,128)(2,1)}, bf16[512,384]{1,0:T(8,128)(2,1)S(1)}, u32[]{:S(2)}) copy-start(bf16[512,384]{1,0:T(8,128)(2,1)S(1)} %collective-permute-done.4.refs_6_) | copy-start | bytes 1179652
  42.9 10.1 %collective-permute-start.5 = (bf16[512,384]{1,0:T(8,128)(2,1)S(1)}, bf16[512,384]{1,0:T(8,128)(2,1)}, u32[]{:S(2)}, u32[]{:S(2)}) collective-permute-start(bf16[512,384]{1,0:T(8,128)(2,1)S(1)} %collective-permute-done.4.refs_6_), channel_id=1, source_target_pairs={{0,1},{1,0},{2,3},{3,2},{4,5},{5,4},{6,7},{7,6},{8,9},{9,8},{10,11... | collective-permute-start | bytes 1179656 | tf_op jit(solution)/shard_map/ppermute | solution.py:300
  42.9 5.2 %collective-permute-start.7 = (bf16[128,384]{1,0:T(8,128)(2,1)S(1)}, bf16[128,384]{1,0:T(8,128)(2,1)S(1)}, u32[]{:S(2)}, u32[]{:S(2)}) collective-permute-start(bf16[128,384]{1,0:T(8,128)(2,1)S(1)} %copy-done.18), channel_id=1, source_target_pairs={{0,2},{1,3},{2,0},{3,1},{4,6},{5,7},{6,4},{7,5},{8,10},{9,11},{10,... | collective-permute-start | bytes 294920 | tf_op jit(solution)/shard_map/ppermute | solution.py:300
  48.1 1.3 %collective-permute-start.6 = (bf16[128,384]{1,0:T(8,128)(2,1)S(1)}, bf16[128,384]{1,0:T(8,128)(2,1)S(1)}, u32[]{:S(2)}, u32[]{:S(2)}) collective-permute-start(bf16[128,384]{1,0:T(8,128)(2,1)S(1)} %copy-done.18), channel_id=1, source_target_pairs={{0,1},{1,0},{2,3},{3,2},{4,5},{5,4},{6,7},{7,6},{8,9},{9,8},{10,11... | collective-permute-start | bytes 294920 | tf_op jit(solution)/shard_map/ppermute | solution.py:300
  49.4 1.3 %collective-permute-start.8 = (bf16[128,384]{1,0:T(8,128)(2,1)S(1)}, bf16[128,384]{1,0:T(8,128)(2,1)S(1)}, u32[]{:S(2)}, u32[]{:S(2)}) collective-permute-start(bf16[128,384]{1,0:T(8,128)(2,1)S(1)} %collective-permute-done.7.refs_10_), channel_id=1, source_target_pairs={{0,1},{1,0},{2,3},{3,2},{4,5},{5,4},{6,7},{7,6},{8,9},{9,8},{10,11... | collective-permute-start | bytes 294920 | tf_op jit(solution)/shard_map/ppermute | solution.py:300
  50.7 20.5 %collective-permute-start.13 = (bf16[512,256]{1,0:T(8,128)(2,1)S(1)}, bf16[512,256]{1,0:T(8,128)(2,1)S(1)}, u32[]{:S(2)}, u32[]{:S(2)}) collective-permute-start(bf16[512,256]{1,0:T(8,128)(2,1)S(1)} %copy-done.1), channel_id=1, source_target_pairs={{0,2},{1,3},{2,0},{3,1},{4,6},{5,7},{6,4},{7,5},{8,10},{9,11},{10,... | collective-permute-start | bytes 786440 | tf_op jit(solution)/shard_map/ppermute | solution.py:300
  52.2 20.3 %collective-permute-start.12 = (bf16[512,256]{1,0:T(8,128)(2,1)S(1)}, bf16[512,256]{1,0:T(8,128)(2,1)}, u32[]{:S(2)}, u32[]{:S(2)}) collective-permute-start(bf16[512,256]{1,0:T(8,128)(2,1)S(1)} %copy-done.1), channel_id=1, source_target_pairs={{0,1},{1,0},{2,3},{3,2},{4,5},{5,4},{6,7},{7,6},{8,9},{9,8},{10,11... | collective-permute-start | bytes 786440 | tf_op jit(solution)/shard_map/ppermute | solution.py:300
  52.3 18.6 %collective-permute-start.10 = (bf16[512,128]{1,0:T(8,128)(2,1)S(1)}, bf16[512,128]{1,0:T(8,128)(2,1)}, u32[]{:S(2)}, u32[]{:S(2)}) collective-permute-start(bf16[512,128]{1,0:T(8,128)(2,1)S(1)} %copy-done.2), channel_id=1, source_target_pairs={{0,2},{1,3},{2,0},{3,1},{4,6},{5,7},{6,4},{7,5},{8,10},{9,11},{10,... | collective-permute-start | bytes 393224 | tf_op jit(solution)/shard_map/ppermute | solution.py:300
  52.9 19.7 %collective-permute-start.9 = (bf16[512,128]{1,0:T(8,128)(2,1)S(1)}, bf16[512,128]{1,0:T(8,128)(2,1)}, u32[]{:S(2)}, u32[]{:S(2)}) collective-permute-start(bf16[512,128]{1,0:T(8,128)(2,1)S(1)} %copy-done.2), channel_id=1, source_target_pairs={{0,1},{1,0},{2,3},{3,2},{4,5},{5,4},{6,7},{7,6},{8,9},{9,8},{10,11... | collective-permute-start | bytes 393224 | tf_op jit(solution)/shard_map/ppermute | solution.py:300
  58.9 14.0 %copy-start = (bf16[1024,512]{1,0:T(8,128)(2,1)S(1)}, bf16[1024,512]{1,0:T(8,128)(2,1)}, u32[]{:S(2)}) copy-start(bf16[1024,512]{1,0:T(8,128)(2,1)} %memory_ref.3) | copy-start | bytes 3145732
  58.9 22.4 %all-to-all-start.2 = ((bf16[32,72,128]{2,1,0:T(8,128)(2,1)}), bf16[32,72,128]{2,1,0:T(8,128)(2,1)S(1)}, u32[]{:S(2)}, u32[]{:S(2)}) async-start(bf16[32,72,128]{2,1,0:T(8,128)(2,1)} %get-tuple-element.32), calls=%async_computation.2 | async-start | bytes 1179648 | tf_op jit(solution)/shard_map/all_to_all | solution.py:399
  64.6 4.9 %collective-permute-start.16 = (s32[8,128]{1,0:T(8,128)S(1)}, s32[8,128]{1,0:T(8,128)S(1)}, u32[]{:S(2)}, u32[]{:S(2)}) collective-permute-start(s32[8,128]{1,0:T(8,128)S(1)} %bitcast.22), channel_id=1, source_target_pairs={{0,2},{1,3},{2,0},{3,1},{4,6},{5,7},{6,4},{7,5},{8,10},{9,11},{10,... | collective-permute-start | bytes 12296 | tf_op jit(solution)/shard_map/ppermute | solution.py:300
  69.5 1.2 %collective-permute-start.15 = (s32[8,128]{1,0:T(8,128)S(1)}, s32[8,128]{1,0:T(8,128)S(1)}, u32[]{:S(2)}, u32[]{:S(2)}) collective-permute-start(s32[8,128]{1,0:T(8,128)S(1)} %bitcast.24), channel_id=1, source_target_pairs={{0,1},{1,0},{2,3},{3,2},{4,5},{5,4},{6,7},{7,6},{8,9},{9,8},{10,11... | collective-permute-start | bytes 12296 | tf_op jit(solution)/shard_map/ppermute | solution.py:300
  70.7 1.2 %collective-permute-start.17 = (s32[8,128]{1,0:T(8,128)S(1)}, s32[8,128]{1,0:T(8,128)S(1)}, u32[]{:S(2)}, u32[]{:S(2)}) collective-permute-start(s32[8,128]{1,0:T(8,128)S(1)} %collective-permute-done.16), channel_id=1, source_target_pairs={{0,1},{1,0},{2,3},{3,2},{4,5},{5,4},{6,7},{7,6},{8,9},{9,8},{10,11... | collective-permute-start | bytes 12296 | tf_op jit(solution)/shard_map/ppermute | solution.py:300
  70.9 1.7 %collective-permute-start.11 = (bf16[512,128]{1,0:T(8,128)(2,1)}, bf16[512,128]{1,0:T(8,128)(2,1)}, u32[]{:S(2)}, u32[]{:S(2)}) collective-permute-start(bf16[512,128]{1,0:T(8,128)(2,1)} %collective-permute-done.10.refs_2_), channel_id=1, source_target_pairs={{0,1},{1,0},{2,3},{3,2},{4,5},{5,4},{6,7},{7,6},{8,9},{9,8},{10,11... | collective-permute-start | bytes 393224 | tf_op jit(solution)/shard_map/ppermute | solution.py:300
  71.2 1.7 %collective-permute-start.14 = (bf16[512,256]{1,0:T(8,128)(2,1)S(1)}, bf16[512,256]{1,0:T(8,128)(2,1)}, u32[]{:S(2)}, u32[]{:S(2)}) collective-permute-start(bf16[512,256]{1,0:T(8,128)(2,1)S(1)} %collective-permute-done.13.refs_6_), channel_id=1, source_target_pairs={{0,1},{1,0},{2,3},{3,2},{4,5},{5,4},{6,7},{7,6},{8,9},{9,8},{10,11... | collective-permute-start | bytes 786440 | tf_op jit(solution)/shard_map/ppermute | solution.py:300
  83.5 8.3 %collective-permute-start.19 = (bf16[1024,128]{1,0:T(8,128)(2,1)S(1)}, bf16[1024,128]{1,0:T(8,128)(2,1)S(1)}, u32[]{:S(2)}, u32[]{:S(2)}) collective-permute-start(bf16[1024,128]{1,0:T(8,128)(2,1)S(1)} %apply.1.refs_0_), channel_id=1, source_target_pairs={{0,2},{1,3},{2,0},{3,1},{4,6},{5,7},{6,4},{7,5},{8,10},{9,11},{10,... | collective-permute-start | bytes 786440 | tf_op jit(solution)/shard_map/ppermute | solution.py:300
  84.7 7.1 %collective-permute-start.18 = (bf16[1024,128]{1,0:T(8,128)(2,1)S(1)}, bf16[1024,128]{1,0:T(8,128)(2,1)S(1)}, u32[]{:S(2)}, u32[]{:S(2)}) collective-permute-start(bf16[1024,128]{1,0:T(8,128)(2,1)S(1)} %apply.1.refs_0_), channel_id=1, source_target_pairs={{0,1},{1,0},{2,3},{3,2},{4,5},{5,4},{6,7},{7,6},{8,9},{9,8},{10,11... | collective-permute-start | bytes 786440 | tf_op jit(solution)/shard_map/ppermute | solution.py:300
  91.8 1.5 %collective-permute-start.20 = (bf16[1024,128]{1,0:T(8,128)(2,1)S(1)}, bf16[1024,128]{1,0:T(8,128)(2,1)S(1)}, u32[]{:S(2)}, u32[]{:S(2)}) collective-permute-start(bf16[1024,128]{1,0:T(8,128)(2,1)S(1)} %collective-permute-done.19.refs_2_), channel_id=1, source_target_pairs={{0,1},{1,0},{2,3},{3,2},{4,5},{5,4},{6,7},{7,6},{8,9},{9,8},{10,11... | collective-permute-start | bytes 786440 | tf_op jit(solution)/shard_map/ppermute | solution.py:300
  (14 other events, 39.1 us)

commit v8 on v7

--- a/solution.py
+++ b/solution.py
@@ -124,7 +124,7 @@
     return jnp.where((inner * plan.owners + owner) == here, 1.0, 0.0).astype(BF16)
 
 
-def serve_kernel(plan, asked_ref, memory_ref, out_ref, held, hot_ref, sems):
+def serve_kernel(plan, asked_ref, memory_ref, after_ref, out_ref, held, hot_ref, sems):
     stored, width = memory_ref.shape
     piece = width // 4
     step = stored // 4
@@ -365,7 +365,7 @@
     served = call(
         run(serve_kernel, plan),
         [sds((owners, 4 * (plan.main + plan.tail), width // 4), BF16)],
-        [VMEM, HBM],
+        [VMEM, HBM, HBM],
         2 * plan.rows * stored * width,
         2 * stored * width + 2 * plan.rows * width,
         "serve",
@@ -375,7 +375,7 @@
             pltpu.SemaphoreType.DMA((4,)),
         ],
         limit=16,
-    )(asked, *far([memory]))[0]
+    )(asked, *far([memory, encode]))[0]
     returned = lax.all_to_all(served, "shard", split_axis=0, concat_axis=0, tiled=True)
 
     outgoing, hnew, hdst = call(

time: 94.8 us -> 92.5 us (0.976)
  waiting for transfers between devices: 44.8 us -> 41.8 us
    all_to_all x1, waiting for transfers between devices: 6.32 us -> 3.78 us  [shards(): lax.all_to_all(request, 'shard', split_axis=0, concat_axis=0, tiled=True)]
where the time goes in v8:
time: 92.5 us; the launch traced here: 92.1 us
  waiting for transfers between devices  41.8 us (45%)
  starting transfers between devices  27.1 us (29%)
  Pallas kernels  18.2 us (20%)
  local copies, waits for them, and re-layouts  3.97 us (4%)
  between operations  0.95 us (1%)
    ppermute x21, waiting for transfers between devices, swap(): return lax.ppermute(x, 'rep', [(i, i ^ bit) for i in range(reps)])  34.4 us
    ppermute x21, starting transfers between devices, swap(): return lax.ppermute(x, 'rep', [(i, i ^ bit) for i in range(reps)])  10.4 us
    all_to_all x1, starting transfers between devices, shards(): lax.all_to_all(request, 'shard', split_axis=0, concat_axis=0, tiled=True)  7.42 us
    pallas_call x1, Pallas kernels, shards(): call(run(gru_kernel, plan), [sds((owners * reps, plan.pad, piece), BF16),...  5.83 us
    all_to_all x1, starting transfers between devices, shards(): lax.all_to_all(outgoing, ('shard', 'rep'), split_axis=0, concat_axis=0, t...  5.65 us
    pallas_call x1, Pallas kernels, shards(): call(run(attend_kernel, plan), [sds((events, width), BF16), sds((stored,...  4.09 us
    all_to_all x1, waiting for transfers between devices, shards(): lax.all_to_all(request, 'shard', split_axis=0, concat_axis=0, tiled=True)  3.78 us
    all_to_all x1, starting transfers between devices, shards(): lax.all_to_all(served, 'shard', split_axis=0, concat_axis=0, tiled=True)  3.68 us
  transfers between devices with their start and end apart: 24, of which 13 were waited for; matrix products, arithmetic and copies ran while one was open for 1% of the time, Pallas kernels for 12%

profile of v8, /device:TPU:0, one launch (start us, length us, event | category | flops | bytes accessed | tf_op | source)
XLA Modules:
  0.0 92.1 jit_solution(8280710843549652034)
XLA Ops:
  0.6 0.7 copy-done.4
  1.3 1.0 %request.1 = s32[8,128]{1,0:T(8,128)} custom-call(s32[1,256]{1,0:T(1,128)S(1)} %bitcast.26, s32[1,256]{1,0:T(1,128)S(1)} %bitcast.25), custom_call_target="tpu_custom_call" | custom-call | flops 1048576 | bytes 16384 | tf_op jit(solution)/shard_map/request/pallas_call | solution.py:342
  2.3 7.4 %all-to-all-start = ((s32[8,1,128]{2,1,0:T(1,128)}), s32[8,1,128]{2,1,0:T(1,128)S(1)}, u32[]{:S(2)}, u32[]{:S(2)}) async-start(s32[8,1,128]{2,1,0:T(1,128)} %bitcast.3), calls=%async_computation | async-start | bytes 8192 | tf_op jit(solution)/shard_map/all_to_all | solution.py:346
  9.8 0.6 copy-done.6
  10.5 1.2 %index.1 = (bf16[384,128]{1,0:T(8,128)(2,1)S(1)}, f32[384,8]{1,0:T(8,128)S(1)}, s32[8,384]{1,0:T(8,128)S(1)}) custom-call(s32[1,256]{1,0:T(1,128)S(1)} %bitcast.27, s32[1,1408]{1,0:T(1,128)S(1)} %reshape.45.packed_ref, f32[1,128]{1,0:T(1,128)S(1)} %bitcast.28, f32[1,128]{1,0:T(1,128)S(1)} %bitcast.29), custom_call_target="tpu_custom_call" | custom-call | flops 8589934592 | bytes 262144 | tf_op jit(solution)/shard_map/index/pallas_call | solution.py:349
  11.7 0.6 copy-done.8
  12.3 3.8 %all-to-all-done = s32[8,1,128]{2,1,0:T(1,128)S(1)} async-done(((s32[8,1,128]{2,1,0:T(1,128)}), s32[8,1,128]{2,1,0:T(1,128)S(1)}, u32[]{:S(2)}, u32[]{:S(2)}) %all-to-all-start) | async-done | bytes 4128 | tf_op jit(solution)/shard_map/all_to_all | solution.py:346
  16.1 2.9 %serve.1 = bf16[8,264,128]{2,1,0:T(8,128)(2,1)} custom-call(s32[8,128]{1,0:T(8,128)S(1)} %bitcast.21, bf16[1024,512]{1,0:T(8,128)(2,1)} %memory_ref.3, bf16[384,128]{1,0:T(8,128)(2,1)} %copy-done.8), custom_call_target="tpu_custom_call" | custom-call | flops 553648128 | bytes 1589248 | tf_op jit(solution)/shard_map/serve/pallas_call | solution.py:365
  19.0 3.7 %all-to-all-start.1 = ((bf16[8,264,128]{2,1,0:T(8,128)(2,1)}), bf16[8,264,128]{2,1,0:T(8,128)(2,1)S(1)}, u32[]{:S(2)}, u32[]{:S(2)}) async-start(bf16[8,264,128]{2,1,0:T(8,128)(2,1)} %serve.1), calls=%async_computation.1 | async-start | bytes 1081344 | tf_op jit(solution)/shard_map/all_to_all | solution.py:379
  22.7 1.6 %collective-permute-start.1 = (bf16[512,384]{1,0:T(8,128)(2,1)S(1)}, bf16[512,384]{1,0:T(8,128)(2,1)S(1)}, u32[]{:S(2)}, u32[]{:S(2)}) collective-permute-start(bf16[512,384]{1,0:T(8,128)(2,1)S(1)} %copy-done.14), channel_id=1, source_target_pairs={{0,2},{1,3},{2,0},{3,1},{4,6},{5,7},{6,4},{7,5},{8,10},{9,11},{10,... | collective-permute-start | bytes 1179656 | tf_op jit(solution)/shard_map/ppermute | solution.py:300
  25.3 9.5 %collective-permute-done.1.refs_2_ = bf16[512,384]{1,0:T(8,128)(2,1)S(1)} collective-permute-done((bf16[512,384]{1,0:T(8,128)(2,1)S(1)}, bf16[512,384]{1,0:T(8,128)(2,1)S(1)}, u32[]{:S(2)}, u32[]{:S(2)}) %collective-permute-start.1) | collective-permute-done | bytes 393248 | tf_op jit(solution)/shard_map/ppermute | solution.py:300
  34.9 5.8 %collective-permute-done.4.refs_6_ = bf16[512,384]{1,0:T(8,128)(2,1)S(1)} collective-permute-done((bf16[512,384]{1,0:T(8,128)(2,1)S(1)}, bf16[512,384]{1,0:T(8,128)(2,1)S(1)}, u32[]{:S(2)}, u32[]{:S(2)}) %collective-permute-start.4) | collective-permute-done | bytes 393248 | tf_op jit(solution)/shard_map/ppermute | solution.py:300
  40.7 1.6 %collective-permute-start.7 = (bf16[128,384]{1,0:T(8,128)(2,1)S(1)}, bf16[128,384]{1,0:T(8,128)(2,1)S(1)}, u32[]{:S(2)}, u32[]{:S(2)}) collective-permute-start(bf16[128,384]{1,0:T(8,128)(2,1)S(1)} %copy-done.18), channel_id=1, source_target_pairs={{0,2},{1,3},{2,0},{3,1},{4,6},{5,7},{6,4},{7,5},{8,10},{9,11},{10,... | collective-permute-start | bytes 294920 | tf_op jit(solution)/shard_map/ppermute | solution.py:300
  42.2 3.7 %collective-permute-done.7.refs_10_ = bf16[128,384]{1,0:T(8,128)(2,1)S(1)} collective-permute-done((bf16[128,384]{1,0:T(8,128)(2,1)S(1)}, bf16[128,384]{1,0:T(8,128)(2,1)S(1)}, u32[]{:S(2)}, u32[]{:S(2)}) %collective-permute-start.7) | collective-permute-done | bytes 98336 | tf_op jit(solution)/shard_map/ppermute | solution.py:300
  46.0 1.2 %collective-permute-done.6.refs_9_ = bf16[128,384]{1,0:T(8,128)(2,1)S(1)} collective-permute-done((bf16[128,384]{1,0:T(8,128)(2,1)S(1)}, bf16[128,384]{1,0:T(8,128)(2,1)S(1)}, u32[]{:S(2)}, u32[]{:S(2)}) %collective-permute-start.6) | collective-permute-done | bytes 98336 | tf_op jit(solution)/shard_map/ppermute | solution.py:300
  47.8 0.7 collective-permute-done.8.refs_11_
  48.5 1.5 %collective-permute-start.13 = (bf16[512,256]{1,0:T(8,128)(2,1)S(1)}, bf16[512,256]{1,0:T(8,128)(2,1)S(1)}, u32[]{:S(2)}, u32[]{:S(2)}) collective-permute-start(bf16[512,256]{1,0:T(8,128)(2,1)S(1)} %copy-done.1), channel_id=1, source_target_pairs={{0,2},{1,3},{2,0},{3,1},{4,6},{5,7},{6,4},{7,5},{8,10},{9,11},{10,... | collective-permute-start | bytes 786440 | tf_op jit(solution)/shard_map/ppermute | solution.py:300
  50.0 0.6 collective-permute-start.10
  50.8 5.8 %gru.1 = (bf16[32,72,128]{2,1,0:T(8,128)(2,1)}, f32[384,512]{1,0:T(8,128)S(1)}, bf16[384,512]{1,0:T(8,128)(2,1)S(1)}) custom-call(bf16[8,264,128]{2,1,0:T(8,128)(2,1)S(1)} %all-to-all-done.1.ret_ref, s32[8,384]{1,0:T(8,128)S(1)} %get-tuple-element.22.row_ref, f32[384,8]{1,0:T(8,128)S(1)} %get-tuple-element.23.col_ref, bf16[384,128]{1,0:T(8,128)(2,1)} %copy-done.8, ...), custom_call_target="tpu_custom_call" | custom-call | flops 1207959552 | bytes 8388608 | tf_op jit(solution)/shard_map/gru/pallas_call | solution.py:381
  56.7 5.6 %all-to-all-start.2 = ((bf16[32,72,128]{2,1,0:T(8,128)(2,1)}), bf16[32,72,128]{2,1,0:T(8,128)(2,1)S(1)}, u32[]{:S(2)}, u32[]{:S(2)}) async-start(bf16[32,72,128]{2,1,0:T(8,128)(2,1)} %get-tuple-element.32), calls=%async_computation.2 | async-start | bytes 1179648 | tf_op jit(solution)/shard_map/all_to_all | solution.py:399
  62.3 1.8 %collective-permute-start.16 = (s32[8,128]{1,0:T(8,128)S(1)}, s32[8,128]{1,0:T(8,128)S(1)}, u32[]{:S(2)}, u32[]{:S(2)}) collective-permute-start(s32[8,128]{1,0:T(8,128)S(1)} %bitcast.22), channel_id=1, source_target_pairs={{0,2},{1,3},{2,0},{3,1},{4,6},{5,7},{6,4},{7,5},{8,10},{9,11},{10,... | collective-permute-start | bytes 12296 | tf_op jit(solution)/shard_map/ppermute | solution.py:300
  64.2 3.1 %collective-permute-done.16 = s32[8,128]{1,0:T(8,128)S(1)} collective-permute-done((s32[8,128]{1,0:T(8,128)S(1)}, s32[8,128]{1,0:T(8,128)S(1)}, u32[]{:S(2)}, u32[]{:S(2)}) %collective-permute-start.16) | collective-permute-done | bytes 4128 | tf_op jit(solution)/shard_map/ppermute | solution.py:300
  67.2 1.2 %collective-permute-done.15 = s32[8,128]{1,0:T(8,128)S(1)} collective-permute-done((s32[8,128]{1,0:T(8,128)S(1)}, s32[8,128]{1,0:T(8,128)S(1)}, u32[]{:S(2)}, u32[]{:S(2)}) %collective-permute-start.15) | collective-permute-done | bytes 4128 | tf_op jit(solution)/shard_map/ppermute | solution.py:300
  69.6 0.5 gather_fusion
  70.6 4.1 %attend.1 = (bf16[384,512]{1,0:T(8,128)(2,1)}, bf16[1024,128]{1,0:T(8,128)(2,1)S(1)}) custom-call(s32[3,2]{1,0:T(4,128)S(1)} %copy.20.listed_ref, f32[384,512]{1,0:T(8,128)S(1)} %get-tuple-element.27.hnew_ref, bf16[384,512]{1,0:T(8,128)(2,1)S(1)} %get-tuple-element.28.hdst_ref, bf16[1024,512]{1,0:T(8,128)(2,1)S(1)} %copy-done, ...), custom_call_target="tpu_custom_call" | custom-call | flops 603979776 | bytes 4194304 | tf_op jit(solution)/shard_map/attend/pallas_call | solution.py:401
  74.7 0.7 copy-done.5
  75.4 3.7 %all-to-all-done.2 = bf16[32,72,128]{2,1,0:T(8,128)(2,1)S(1)} async-done(((bf16[32,72,128]{2,1,0:T(8,128)(2,1)}), bf16[32,72,128]{2,1,0:T(8,128)(2,1)S(1)}, u32[]{:S(2)}, u32[]{:S(2)}) %all-to-all-start.2) | async-done | bytes 589856 | tf_op jit(solution)/shard_map/all_to_all | solution.py:399
  79.1 2.2 %apply.1.refs_0_ = bf16[1024,128]{1,0:T(8,128)(2,1)S(1)} custom-call(s32[1,2304]{1,0:T(1,128)S(1)} %reshape.48.ids_ref, bf16[2304,128]{1,0:T(8,128)(2,1)S(1)} %bitcast.20, bf16[1024,128]{1,0:T(8,128)(2,1)} %copy-done.5), custom_call_target="tpu_custom_call" | custom-call | flops 1207959552 | bytes 4194304 | tf_op jit(solution)/shard_map/apply/pallas_call | solution.py:419
  81.3 1.2 %collective-permute-start.19 = (bf16[1024,128]{1,0:T(8,128)(2,1)S(1)}, bf16[1024,128]{1,0:T(8,128)(2,1)S(1)}, u32[]{:S(2)}, u32[]{:S(2)}) collective-permute-start(bf16[1024,128]{1,0:T(8,128)(2,1)S(1)} %apply.1.refs_0_), channel_id=1, source_target_pairs={{0,2},{1,3},{2,0},{3,1},{4,6},{5,7},{6,4},{7,5},{8,10},{9,11},{10,... | collective-permute-start | bytes 786440 | tf_op jit(solution)/shard_map/ppermute | solution.py:300
  82.5 7.0 %collective-permute-done.19.refs_2_ = bf16[1024,128]{1,0:T(8,128)(2,1)S(1)} collective-permute-done((bf16[1024,128]{1,0:T(8,128)(2,1)S(1)}, bf16[1024,128]{1,0:T(8,128)(2,1)S(1)}, u32[]{:S(2)}, u32[]{:S(2)}) %collective-permute-start.19) | collective-permute-done | bytes 262176 | tf_op jit(solution)/shard_map/ppermute | solution.py:300
  89.5 1.5 %collective-permute-done.20.refs_3_ = bf16[1024,128]{1,0:T(8,128)(2,1)S(1)} collective-permute-done((bf16[1024,128]{1,0:T(8,128)(2,1)S(1)}, bf16[1024,128]{1,0:T(8,128)(2,1)S(1)}, u32[]{:S(2)}, u32[]{:S(2)}) %collective-permute-start.20) | collective-permute-done | bytes 262176 | tf_op jit(solution)/shard_map/ppermute | solution.py:300
  91.1 1.0 %join.1 = bf16[1024,512]{1,0:T(8,128)(2,1)} custom-call(bf16[1024,128]{1,0:T(8,128)(2,1)S(1)} %apply.1.refs_0_, bf16[1024,128]{1,0:T(8,128)(2,1)S(1)} %collective-permute-done.18.refs_1_, bf16[1024,128]{1,0:T(8,128)(2,1)S(1)} %collective-permute-done.19.refs_2_, bf16[1024,128]{1,0:T(8,128)(2,1)S(1)} %collective-permute-done.20.refs_3_), custom_call_target="tpu_custom_call" | custom-call | flops 1048576 | bytes 2097152 | tf_op jit(solution)/shard_map/join/pallas_call | solution.py:429
  (80 shorter events, 3.8 us)
Async XLA Ops:
  2.3 13.8 %all-to-all-start = ((s32[8,1,128]{2,1,0:T(1,128)}), s32[8,1,128]{2,1,0:T(1,128)S(1)}, u32[]{:S(2)}, u32[]{:S(2)}) async-start(s32[8,1,128]{2,1,0:T(1,128)} %bitcast.3), calls=%async_computation | async-start | bytes 8192 | tf_op jit(solution)/shard_map/all_to_all | solution.py:346
  16.1 8.2 %copy-start.15 = (bf16[512,384]{1,0:T(8,128)(2,1)S(1)}, bf16[512,384]{1,0:T(8,128)(2,1)}, u32[]{:S(2)}) copy-start(bf16[512,384]{1,0:T(8,128)(2,1)} %refs_4_) | copy-start | bytes 1179652
  19.0 21.7 %copy-start.18 = (bf16[128,384]{1,0:T(8,128)(2,1)S(1)}, bf16[128,384]{1,0:T(8,128)(2,1)}, u32[]{:S(2)}) copy-start(bf16[128,384]{1,0:T(8,128)(2,1)} %refs_8_) | copy-start | bytes 294916
  19.0 29.5 %copy-start.1 = (bf16[512,256]{1,0:T(8,128)(2,1)S(1)}, bf16[512,256]{1,0:T(8,128)(2,1)}, u32[]{:S(2)}) copy-start(bf16[512,256]{1,0:T(8,128)(2,1)} %refs_4_.1) | copy-start | bytes 786436
  19.0 31.0 %copy-start.2 = (bf16[512,128]{1,0:T(8,128)(2,1)S(1)}, bf16[512,128]{1,0:T(8,128)(2,1)}, u32[]{:S(2)}) copy-start(bf16[512,128]{1,0:T(8,128)(2,1)} %refs_0_.1) | copy-start | bytes 393220
  19.0 31.7 %all-to-all-start.1 = ((bf16[8,264,128]{2,1,0:T(8,128)(2,1)}), bf16[8,264,128]{2,1,0:T(8,128)(2,1)S(1)}, u32[]{:S(2)}, u32[]{:S(2)}) async-start(bf16[8,264,128]{2,1,0:T(8,128)(2,1)} %serve.1), calls=%async_computation.1 | async-start | bytes 1081344 | tf_op jit(solution)/shard_map/all_to_all | solution.py:379
  22.7 23.2 %copy-start.12 = (s32[3,2]{0,1:T(2,128)S(1)}, s32[3,2]{0,1:T(2,128)}, u32[]{:S(2)}) copy-start(s32[3,2]{0,1:T(2,128)} %param.22) | copy-start | bytes 76
  22.7 12.1 %collective-permute-start.1 = (bf16[512,384]{1,0:T(8,128)(2,1)S(1)}, bf16[512,384]{1,0:T(8,128)(2,1)S(1)}, u32[]{:S(2)}, u32[]{:S(2)}) collective-permute-start(bf16[512,384]{1,0:T(8,128)(2,1)S(1)} %copy-done.14), channel_id=1, source_target_pairs={{0,2},{1,3},{2,0},{3,1},{4,6},{5,7},{6,4},{7,5},{8,10},{9,11},{10,... | collective-permute-start | bytes 1179656 | tf_op jit(solution)/shard_map/ppermute | solution.py:300
  24.3 16.4 %collective-permute-start.4 = (bf16[512,384]{1,0:T(8,128)(2,1)S(1)}, bf16[512,384]{1,0:T(8,128)(2,1)S(1)}, u32[]{:S(2)}, u32[]{:S(2)}) collective-permute-start(bf16[512,384]{1,0:T(8,128)(2,1)S(1)} %copy-done.15), channel_id=1, source_target_pairs={{0,2},{1,3},{2,0},{3,1},{4,6},{5,7},{6,4},{7,5},{8,10},{9,11},{10,... | collective-permute-start | bytes 1179656 | tf_op jit(solution)/shard_map/ppermute | solution.py:300
  24.8 25.1 %collective-permute-start = (bf16[512,384]{1,0:T(8,128)(2,1)S(1)}, bf16[512,384]{1,0:T(8,128)(2,1)}, u32[]{:S(2)}, u32[]{:S(2)}) collective-permute-start(bf16[512,384]{1,0:T(8,128)(2,1)S(1)} %copy-done.14), channel_id=1, source_target_pairs={{0,1},{1,0},{2,3},{3,2},{4,5},{5,4},{6,7},{7,6},{8,9},{9,8},{10,11... | collective-permute-start | bytes 1179656 | tf_op jit(solution)/shard_map/ppermute | solution.py:300
  24.8 25.1 %collective-permute-start.3 = (bf16[512,384]{1,0:T(8,128)(2,1)S(1)}, bf16[512,384]{1,0:T(8,128)(2,1)}, u32[]{:S(2)}, u32[]{:S(2)}) collective-permute-start(bf16[512,384]{1,0:T(8,128)(2,1)S(1)} %copy-done.15), channel_id=1, source_target_pairs={{0,1},{1,0},{2,3},{3,2},{4,5},{5,4},{6,7},{7,6},{8,9},{9,8},{10,11... | collective-permute-start | bytes 1179656 | tf_op jit(solution)/shard_map/ppermute | solution.py:300
  34.9 15.9 %copy-start.16 = (bf16[512,384]{1,0:T(8,128)(2,1)}, bf16[512,384]{1,0:T(8,128)(2,1)S(1)}, u32[]{:S(2)}) copy-start(bf16[512,384]{1,0:T(8,128)(2,1)S(1)} %collective-permute-done.1.refs_2_) | copy-start | bytes 1179652
  34.9 15.7 %collective-permute-start.2 = (bf16[512,384]{1,0:T(8,128)(2,1)S(1)}, bf16[512,384]{1,0:T(8,128)(2,1)}, u32[]{:S(2)}, u32[]{:S(2)}) collective-permute-start(bf16[512,384]{1,0:T(8,128)(2,1)S(1)} %collective-permute-done.1.refs_2_), channel_id=1, source_target_pairs={{0,1},{1,0},{2,3},{3,2},{4,5},{5,4},{6,7},{7,6},{8,9},{9,8},{10,11... | collective-permute-start | bytes 1179656 | tf_op jit(solution)/shard_map/ppermute | solution.py:300
  40.7 10.1 %copy-start.17 = (bf16[512,384]{1,0:T(8,128)(2,1)}, bf16[512,384]{1,0:T(8,128)(2,1)S(1)}, u32[]{:S(2)}) copy-start(bf16[512,384]{1,0:T(8,128)(2,1)S(1)} %collective-permute-done.4.refs_6_) | copy-start | bytes 1179652
  40.7 10.1 %collective-permute-start.5 = (bf16[512,384]{1,0:T(8,128)(2,1)S(1)}, bf16[512,384]{1,0:T(8,128)(2,1)}, u32[]{:S(2)}, u32[]{:S(2)}) collective-permute-start(bf16[512,384]{1,0:T(8,128)(2,1)S(1)} %collective-permute-done.4.refs_6_), channel_id=1, source_target_pairs={{0,1},{1,0},{2,3},{3,2},{4,5},{5,4},{6,7},{7,6},{8,9},{9,8},{10,11... | collective-permute-start | bytes 1179656 | tf_op jit(solution)/shard_map/ppermute | solution.py:300
  40.7 5.2 %collective-permute-start.7 = (bf16[128,384]{1,0:T(8,128)(2,1)S(1)}, bf16[128,384]{1,0:T(8,128)(2,1)S(1)}, u32[]{:S(2)}, u32[]{:S(2)}) collective-permute-start(bf16[128,384]{1,0:T(8,128)(2,1)S(1)} %copy-done.18), channel_id=1, source_target_pairs={{0,2},{1,3},{2,0},{3,1},{4,6},{5,7},{6,4},{7,5},{8,10},{9,11},{10,... | collective-permute-start | bytes 294920 | tf_op jit(solution)/shard_map/ppermute | solution.py:300
  45.9 1.3 %collective-permute-start.6 = (bf16[128,384]{1,0:T(8,128)(2,1)S(1)}, bf16[128,384]{1,0:T(8,128)(2,1)S(1)}, u32[]{:S(2)}, u32[]{:S(2)}) collective-permute-start(bf16[128,384]{1,0:T(8,128)(2,1)S(1)} %copy-done.18), channel_id=1, source_target_pairs={{0,1},{1,0},{2,3},{3,2},{4,5},{5,4},{6,7},{7,6},{8,9},{9,8},{10,11... | collective-permute-start | bytes 294920 | tf_op jit(solution)/shard_map/ppermute | solution.py:300
  47.2 1.3 %collective-permute-start.8 = (bf16[128,384]{1,0:T(8,128)(2,1)S(1)}, bf16[128,384]{1,0:T(8,128)(2,1)S(1)}, u32[]{:S(2)}, u32[]{:S(2)}) collective-permute-start(bf16[128,384]{1,0:T(8,128)(2,1)S(1)} %collective-permute-done.7.refs_10_), channel_id=1, source_target_pairs={{0,1},{1,0},{2,3},{3,2},{4,5},{5,4},{6,7},{7,6},{8,9},{9,8},{10,11... | collective-permute-start | bytes 294920 | tf_op jit(solution)/shard_map/ppermute | solution.py:300
  48.5 20.4 %collective-permute-start.13 = (bf16[512,256]{1,0:T(8,128)(2,1)S(1)}, bf16[512,256]{1,0:T(8,128)(2,1)S(1)}, u32[]{:S(2)}, u32[]{:S(2)}) collective-permute-start(bf16[512,256]{1,0:T(8,128)(2,1)S(1)} %copy-done.1), channel_id=1, source_target_pairs={{0,2},{1,3},{2,0},{3,1},{4,6},{5,7},{6,4},{7,5},{8,10},{9,11},{10,... | collective-permute-start | bytes 786440 | tf_op jit(solution)/shard_map/ppermute | solution.py:300
  50.0 20.3 %collective-permute-start.12 = (bf16[512,256]{1,0:T(8,128)(2,1)S(1)}, bf16[512,256]{1,0:T(8,128)(2,1)}, u32[]{:S(2)}, u32[]{:S(2)}) collective-permute-start(bf16[512,256]{1,0:T(8,128)(2,1)S(1)} %copy-done.1), channel_id=1, source_target_pairs={{0,1},{1,0},{2,3},{3,2},{4,5},{5,4},{6,7},{7,6},{8,9},{9,8},{10,11... | collective-permute-start | bytes 786440 | tf_op jit(solution)/shard_map/ppermute | solution.py:300
  50.0 18.6 %collective-permute-start.10 = (bf16[512,128]{1,0:T(8,128)(2,1)S(1)}, bf16[512,128]{1,0:T(8,128)(2,1)}, u32[]{:S(2)}, u32[]{:S(2)}) collective-permute-start(bf16[512,128]{1,0:T(8,128)(2,1)S(1)} %copy-done.2), channel_id=1, source_target_pairs={{0,2},{1,3},{2,0},{3,1},{4,6},{5,7},{6,4},{7,5},{8,10},{9,11},{10,... | collective-permute-start | bytes 393224 | tf_op jit(solution)/shard_map/ppermute | solution.py:300
  50.6 19.7 %collective-permute-start.9 = (bf16[512,128]{1,0:T(8,128)(2,1)S(1)}, bf16[512,128]{1,0:T(8,128)(2,1)}, u32[]{:S(2)}, u32[]{:S(2)}) collective-permute-start(bf16[512,128]{1,0:T(8,128)(2,1)S(1)} %copy-done.2), channel_id=1, source_target_pairs={{0,1},{1,0},{2,3},{3,2},{4,5},{5,4},{6,7},{7,6},{8,9},{9,8},{10,11... | collective-permute-start | bytes 393224 | tf_op jit(solution)/shard_map/ppermute | solution.py:300
  56.7 13.9 %copy-start = (bf16[1024,512]{1,0:T(8,128)(2,1)S(1)}, bf16[1024,512]{1,0:T(8,128)(2,1)}, u32[]{:S(2)}) copy-start(bf16[1024,512]{1,0:T(8,128)(2,1)} %memory_ref.3) | copy-start | bytes 3145732
  56.7 22.4 %all-to-all-start.2 = ((bf16[32,72,128]{2,1,0:T(8,128)(2,1)}), bf16[32,72,128]{2,1,0:T(8,128)(2,1)S(1)}, u32[]{:S(2)}, u32[]{:S(2)}) async-start(bf16[32,72,128]{2,1,0:T(8,128)(2,1)} %get-tuple-element.32), calls=%async_computation.2 | async-start | bytes 1179648 | tf_op jit(solution)/shard_map/all_to_all | solution.py:399
  62.3 4.9 %collective-permute-start.16 = (s32[8,128]{1,0:T(8,128)S(1)}, s32[8,128]{1,0:T(8,128)S(1)}, u32[]{:S(2)}, u32[]{:S(2)}) collective-permute-start(s32[8,128]{1,0:T(8,128)S(1)} %bitcast.22), channel_id=1, source_target_pairs={{0,2},{1,3},{2,0},{3,1},{4,6},{5,7},{6,4},{7,5},{8,10},{9,11},{10,... | collective-permute-start | bytes 12296 | tf_op jit(solution)/shard_map/ppermute | solution.py:300
  67.2 1.2 %collective-permute-start.15 = (s32[8,128]{1,0:T(8,128)S(1)}, s32[8,128]{1,0:T(8,128)S(1)}, u32[]{:S(2)}, u32[]{:S(2)}) collective-permute-start(s32[8,128]{1,0:T(8,128)S(1)} %bitcast.24), channel_id=1, source_target_pairs={{0,1},{1,0},{2,3},{3,2},{4,5},{5,4},{6,7},{7,6},{8,9},{9,8},{10,11... | collective-permute-start | bytes 12296 | tf_op jit(solution)/shard_map/ppermute | solution.py:300
  68.4 1.2 %collective-permute-start.17 = (s32[8,128]{1,0:T(8,128)S(1)}, s32[8,128]{1,0:T(8,128)S(1)}, u32[]{:S(2)}, u32[]{:S(2)}) collective-permute-start(s32[8,128]{1,0:T(8,128)S(1)} %collective-permute-done.16), channel_id=1, source_target_pairs={{0,1},{1,0},{2,3},{3,2},{4,5},{5,4},{6,7},{7,6},{8,9},{9,8},{10,11... | collective-permute-start | bytes 12296 | tf_op jit(solution)/shard_map/ppermute | solution.py:300
  68.6 1.7 %collective-permute-start.11 = (bf16[512,128]{1,0:T(8,128)(2,1)}, bf16[512,128]{1,0:T(8,128)(2,1)}, u32[]{:S(2)}, u32[]{:S(2)}) collective-permute-start(bf16[512,128]{1,0:T(8,128)(2,1)} %collective-permute-done.10.refs_2_), channel_id=1, source_target_pairs={{0,1},{1,0},{2,3},{3,2},{4,5},{5,4},{6,7},{7,6},{8,9},{9,8},{10,11... | collective-permute-start | bytes 393224 | tf_op jit(solution)/shard_map/ppermute | solution.py:300
  68.9 1.7 %collective-permute-start.14 = (bf16[512,256]{1,0:T(8,128)(2,1)S(1)}, bf16[512,256]{1,0:T(8,128)(2,1)}, u32[]{:S(2)}, u32[]{:S(2)}) collective-permute-start(bf16[512,256]{1,0:T(8,128)(2,1)S(1)} %collective-permute-done.13.refs_6_), channel_id=1, source_target_pairs={{0,1},{1,0},{2,3},{3,2},{4,5},{5,4},{6,7},{7,6},{8,9},{9,8},{10,11... | collective-permute-start | bytes 786440 | tf_op jit(solution)/shard_map/ppermute | solution.py:300
  81.3 8.3 %collective-permute-start.19 = (bf16[1024,128]{1,0:T(8,128)(2,1)S(1)}, bf16[1024,128]{1,0:T(8,128)(2,1)S(1)}, u32[]{:S(2)}, u32[]{:S(2)}) collective-permute-start(bf16[1024,128]{1,0:T(8,128)(2,1)S(1)} %apply.1.refs_0_), channel_id=1, source_target_pairs={{0,2},{1,3},{2,0},{3,1},{4,6},{5,7},{6,4},{7,5},{8,10},{9,11},{10,... | collective-permute-start | bytes 786440 | tf_op jit(solution)/shard_map/ppermute | solution.py:300
  82.5 7.1 %collective-permute-start.18 = (bf16[1024,128]{1,0:T(8,128)(2,1)S(1)}, bf16[1024,128]{1,0:T(8,128)(2,1)S(1)}, u32[]{:S(2)}, u32[]{:S(2)}) collective-permute-start(bf16[1024,128]{1,0:T(8,128)(2,1)S(1)} %apply.1.refs_0_), channel_id=1, source_target_pairs={{0,1},{1,0},{2,3},{3,2},{4,5},{5,4},{6,7},{7,6},{8,9},{9,8},{10,11... | collective-permute-start | bytes 786440 | tf_op jit(solution)/shard_map/ppermute | solution.py:300
  89.5 1.5 %collective-permute-start.20 = (bf16[1024,128]{1,0:T(8,128)(2,1)S(1)}, bf16[1024,128]{1,0:T(8,128)(2,1)S(1)}, u32[]{:S(2)}, u32[]{:S(2)}) collective-permute-start(bf16[1024,128]{1,0:T(8,128)(2,1)S(1)} %collective-permute-done.19.refs_2_), channel_id=1, source_target_pairs={{0,1},{1,0},{2,3},{3,2},{4,5},{5,4},{6,7},{7,6},{8,9},{9,8},{10,11... | collective-permute-start | bytes 786440 | tf_op jit(solution)/shard_map/ppermute | solution.py:300
  (14 other events, 45.4 us)

commit v9 on v8

--- a/solution.py
+++ b/solution.py
@@ -82,8 +82,8 @@
     out_ref[...] = (dot(high, spot) * 32.0 + dot(low, spot)).astype(I32)
 
 
-def index_kernel(plan, owner_ref, packed_ref, freq_ref, phase_ref, enc_ref, col_ref, row_ref):
-    events = enc_ref.shape[0]
+def index_kernel(plan, owner_ref, packed_ref, col_ref, row_ref):
+    events = col_ref.shape[0]
     ends = [plan.entries + i * events for i in range(4)]
     tick_row = packed_ref[:, : ends[0]]
     src_row, dst_row, stamp_row = (packed_ref[:, a : a + events] for a in ends[:3])
@@ -109,9 +109,11 @@
     zero = jnp.zeros((8 - 3, events), I32)
     rows = jnp.concatenate([src_spot, dst_spot, span, zero], axis=0)
     row_ref[...] = jnp.concatenate([src_back, jnp.zeros((7, events), I32)], axis=0)
-    cols = rows.astype(F32).T
-    col_ref[...] = cols
-    enc_ref[...] = jnp.cos(cols[:, 2:3] * freq_ref[...] + phase_ref[...]).astype(BF16)
+    col_ref[...] = rows.astype(F32).T
+
+
+def encode_kernel(col_ref, freq_ref, phase_ref, enc_ref):
+    enc_ref[...] = jnp.cos(col_ref[:, 2:3] * freq_ref[...] + phase_ref[...]).astype(BF16)
 
 
 def tail_order(plan, forward):
@@ -346,17 +348,20 @@
     asked = lax.all_to_all(request, "shard", split_axis=0, concat_axis=0, tiled=True)
     packed = jnp.concatenate([touch_time, src_slot, dst_slot, event_time]).reshape(1, -1)
     _, owner, packed = lax.optimization_barrier((request, owner, packed))
-    encode, cols, rows = call(
+    cols, rows = call(
         run(index_kernel, plan),
-        [sds((events, time_freq.shape[0]), BF16), sds((events, 8), F32), sds((8, events), I32)],
-        [VMEM] * 4,
+        [sds((events, 8), F32), sds((8, events), I32)],
+        [VMEM] * 2,
         8 << 30,
         1 << 18,
         "index",
-    )(owner, packed, time_freq.reshape(1, -1), time_phase.reshape(1, -1))
-    encode, w_time, w_hidden, w_input, w_keyval, w_query = lax.optimization_barrier(
-        (encode, w_time, w_hidden, w_input, w_keyval, w_query)
+    )(owner, packed)
+    cols, w_time, w_hidden, w_input, w_keyval, w_query = lax.optimization_barrier(
+        (cols, w_time, w_hidden, w_input, w_keyval, w_query)
     )
+    encode = call(
+        encode_kernel, [sds((events, time_freq.shape[0]), BF16)], [VMEM] * 3, 8 << 30, 1 << 18, "encode"
+    )(cols, time_freq.reshape(1, -1), time_phase.reshape(1, -1))[0]
     full_time, full_hidden, full_input, full_keyval, full_query = spread(
         [w_time, w_hidden, w_input, w_keyval, w_query], reps
     )
@@ -375,7 +380,7 @@
             pltpu.SemaphoreType.DMA((4,)),
         ],
         limit=16,
-    )(asked, *far([memory, encode]))[0]
+    )(asked, *far([memory, cols]))[0]
     returned = lax.all_to_all(served, "shard", split_axis=0, concat_axis=0, tiled=True)
 
     outgoing, hnew, hdst = call(

time: 92.5 us -> 78.9 us (0.85)
  waiting for transfers between devices: 41.8 us -> 23 us
  blocking collectives: 0 us -> 12.1 us
  starting transfers between devices: 27.1 us -> 19 us
  local copies, waits for them, and re-layouts: 3.97 us -> 5.11 us
    ppermute x21, waiting for transfers between devices: 34.4 us -> 14.3 us  [swap(): return lax.ppermute(x, 'rep', [(i, i ^ bit) for i in range(reps)])]
    all_to_all x0 -> x1, blocking collectives: none -> 12.1 us  [shards(): lax.all_to_all(request, 'shard', split_axis=0, concat_axis=0, tiled=True)]
    all_to_all x1 -> x0, starting transfers between devices: 7.42 us -> none  [shards(): lax.all_to_all(request, 'shard', split_axis=0, concat_axis=0, tiled=True)]
    all_to_all x1, waiting for transfers between devices: 0.01 us -> 5.05 us  [shards(): lax.all_to_all(served, 'shard', split_axis=0, concat_axis=0, tiled=True)]
    all_to_all x1 -> x0, waiting for transfers between devices: 3.78 us -> none  [shards(): lax.all_to_all(request, 'shard', split_axis=0, concat_axis=0, tiled=True)]
    all_to_all x1, starting transfers between devices: 5.65 us -> 2.76 us  [shards(): lax.all_to_all(outgoing, ('shard', 'rep'), split_axis=0, concat_axis=0, t...]
    ppermute x21, starting transfers between devices: 10.4 us -> 12.6 us  [swap(): return lax.ppermute(x, 'rep', [(i, i ^ bit) for i in range(reps)])]
    unnamed x45 -> x41, local copies, waits for them, and re-layouts: 3.31 us -> 4.44 us
  transfers between devices with their start and end apart: 24 -> 23, of which waited for: 13 -> 9; matrix products, arithmetic and copies ran while one was open for 1% -> 1% of each run, Pallas kernels for 12% -> 17%
where the time goes in v9:
time: 78.9 us; the launch traced here: 78.4 us
  waiting for transfers between devices  23 us (29%)
  starting transfers between devices  19 us (24%)
  Pallas kernels  17.5 us (22%)
  blocking collectives  12.1 us (15%)
  local copies, waits for them, and re-layouts  5.11 us (6%)
  between operations  0.86 us (1%)
    ppermute x21, waiting for transfers between devices, swap(): return lax.ppermute(x, 'rep', [(i, i ^ bit) for i in range(reps)])  14.3 us
    ppermute x21, starting transfers between devices, swap(): return lax.ppermute(x, 'rep', [(i, i ^ bit) for i in range(reps)])  12.6 us
    all_to_all x1, blocking collectives, shards(): lax.all_to_all(request, 'shard', split_axis=0, concat_axis=0, tiled=True)  12.1 us
    pallas_call x1, Pallas kernels, shards(): call(run(gru_kernel, plan), [sds((owners * reps, plan.pad, piece), BF16),...  5.82 us
    all_to_all x1, waiting for transfers between devices, shards(): lax.all_to_all(served, 'shard', split_axis=0, concat_axis=0, tiled=True)  5.05 us
    unnamed x41, local copies, waits for them, and re-layouts  4.44 us
    pallas_call x1, Pallas kernels, shards(): call(run(attend_kernel, plan), [sds((events, width), BF16), sds((stored,...  4.09 us
    all_to_all x1, waiting for transfers between devices, shards(): lax.all_to_all(outgoing, ('shard', 'rep'), split_axis=0, concat_axis=0, t...  3.69 us
  transfers between devices with their start and end apart: 23, of which 9 were waited for; matrix products, arithmetic and copies ran while one was open for 1% of the time, Pallas kernels for 17%

profile of v9, /device:TPU:0, one launch (start us, length us, event | category | flops | bytes accessed | tf_op | source)
XLA Modules:
  0.0 78.4 jit_solution(8326735720726736603)
XLA Ops:
  0.6 0.7 pad_add_fusion.1
  1.4 0.7 copy-done.4
  2.4 0.5 index.1
  3.0 0.7 copy-done.8
  3.7 2.9 %collective-permute-start.1 = (bf16[512,384]{1,0:T(8,128)(2,1)S(1)}, bf16[512,384]{1,0:T(8,128)(2,1)S(1)}, u32[]{:S(2)}, u32[]{:S(2)}) collective-permute-start(bf16[512,384]{1,0:T(8,128)(2,1)S(1)} %copy-done.12), channel_id=1, source_target_pairs={{0,2},{1,3},{2,0},{3,1},{4,6},{5,7},{6,4},{7,5},{8,10},{9,11},{10,... | collective-permute-start | bytes 1179656 | tf_op jit(solution)/shard_map/ppermute | solution.py:302
  6.7 2.0 %collective-permute-start.7 = (bf16[128,384]{1,0:T(8,128)(2,1)S(1)}, bf16[128,384]{1,0:T(8,128)(2,1)S(1)}, u32[]{:S(2)}, u32[]{:S(2)}) collective-permute-start(bf16[128,384]{1,0:T(8,128)(2,1)S(1)} %copy-done.16), channel_id=1, source_target_pairs={{0,2},{1,3},{2,0},{3,1},{4,6},{5,7},{6,4},{7,5},{8,10},{9,11},{10,... | collective-permute-start | bytes 294920 | tf_op jit(solution)/shard_map/ppermute | solution.py:302
  8.6 12.1 %all_to_all.21 = s32[8,1,128]{2,1,0:T(1,128)S(1)} all-to-all(s32[8,1,128]{2,1,0:T(1,128)S(1)} %bitcast.25), channel_id=1, replica_groups=mesh['shard'=8,'rep'=4] {'shard'}, dimensions={0} | all-to-all | bytes 8192 | tf_op jit(solution)/shard_map/all_to_all | solution.py:348
  20.7 2.8 %serve.1 = bf16[8,264,128]{2,1,0:T(8,128)(2,1)} custom-call(s32[8,128]{1,0:T(8,128)S(1)} %bitcast.21, bf16[1024,512]{1,0:T(8,128)(2,1)} %memory_ref.3, f32[384,8]{1,0:T(8,128)} %copy-done.8), custom_call_target="tpu_custom_call" | custom-call | flops 553648128 | bytes 1589248 | tf_op jit(solution)/shard_map/serve/pallas_call | solution.py:370
  23.6 3.7 %all-to-all-start.1 = ((bf16[8,264,128]{2,1,0:T(8,128)(2,1)}), bf16[8,264,128]{2,1,0:T(8,128)(2,1)S(1)}, u32[]{:S(2)}, u32[]{:S(2)}) async-start(bf16[8,264,128]{2,1,0:T(8,128)(2,1)} %serve.1), calls=%async_computation.1 | async-start | bytes 1081344 | tf_op jit(solution)/shard_map/all_to_all | solution.py:384
  27.3 0.5 collective-permute-start.3
  28.4 0.7 copy-done.6
  29.2 0.7 encode.1.far_enc
  29.9 0.6 copy-done.10
  30.5 0.7 copy-done.11
  32.0 0.7 collective-permute-done.8.refs_11_
  32.7 0.6 collective-permute-start.13
  33.3 1.5 %collective-permute-start.10 = (bf16[512,128]{1,0:T(8,128)(2,1)S(1)}, bf16[512,128]{1,0:T(8,128)(2,1)}, u32[]{:S(2)}, u32[]{:S(2)}) collective-permute-start(bf16[512,128]{1,0:T(8,128)(2,1)S(1)} %copy-done.2), channel_id=1, source_target_pairs={{0,2},{1,3},{2,0},{3,1},{4,6},{5,7},{6,4},{7,5},{8,10},{9,11},{10,... | collective-permute-start | bytes 393224 | tf_op jit(solution)/shard_map/ppermute | solution.py:302
  35.0 5.0 %all-to-all-done.1.ret_ref = bf16[8,264,128]{2,1,0:T(8,128)(2,1)S(1)} async-done(((bf16[8,264,128]{2,1,0:T(8,128)(2,1)}), bf16[8,264,128]{2,1,0:T(8,128)(2,1)S(1)}, u32[]{:S(2)}, u32[]{:S(2)}) %all-to-all-start.1) | async-done | bytes 540704 | tf_op jit(solution)/shard_map/all_to_all | solution.py:384
  40.1 5.8 %gru.1 = (bf16[32,72,128]{2,1,0:T(8,128)(2,1)}, f32[384,512]{1,0:T(8,128)S(1)}, bf16[384,512]{1,0:T(8,128)(2,1)S(1)}) custom-call(bf16[8,264,128]{2,1,0:T(8,128)(2,1)S(1)} %all-to-all-done.1.ret_ref, s32[8,384]{1,0:T(8,128)S(1)} %get-tuple-element.21.row_ref, f32[384,8]{1,0:T(8,128)S(1)} %copy-done.9, bf16[384,128]{1,0:T(8,128)(2,1)} %copy-done.10, ...), custom_call_target="tpu_custom_call" | custom-call | flops 1207959552 | bytes 8388608 | tf_op jit(solution)/shard_map/gru/pallas_call | solution.py:386
  45.9 2.8 %all-to-all-start.2 = ((bf16[32,72,128]{2,1,0:T(8,128)(2,1)}), bf16[32,72,128]{2,1,0:T(8,128)(2,1)S(1)}, u32[]{:S(2)}, u32[]{:S(2)}) async-start(bf16[32,72,128]{2,1,0:T(8,128)(2,1)} %get-tuple-element.30), calls=%async_computation.2 | async-start | bytes 1179648 | tf_op jit(solution)/shard_map/all_to_all | solution.py:404
  48.7 1.8 %collective-permute-start.16 = (s32[8,128]{1,0:T(8,128)S(1)}, s32[8,128]{1,0:T(8,128)S(1)}, u32[]{:S(2)}, u32[]{:S(2)}) collective-permute-start(s32[8,128]{1,0:T(8,128)S(1)} %bitcast.22), channel_id=1, source_target_pairs={{0,2},{1,3},{2,0},{3,1},{4,6},{5,7},{6,4},{7,5},{8,10},{9,11},{10,... | collective-permute-start | bytes 12296 | tf_op jit(solution)/shard_map/ppermute | solution.py:302
  50.5 3.1 %collective-permute-done.16 = s32[8,128]{1,0:T(8,128)S(1)} collective-permute-done((s32[8,128]{1,0:T(8,128)S(1)}, s32[8,128]{1,0:T(8,128)S(1)}, u32[]{:S(2)}, u32[]{:S(2)}) %collective-permute-start.16) | collective-permute-done | bytes 4128 | tf_op jit(solution)/shard_map/ppermute | solution.py:302
  53.5 1.2 %collective-permute-done.15 = s32[8,128]{1,0:T(8,128)S(1)} collective-permute-done((s32[8,128]{1,0:T(8,128)S(1)}, s32[8,128]{1,0:T(8,128)S(1)}, u32[]{:S(2)}, u32[]{:S(2)}) %collective-permute-start.15) | collective-permute-done | bytes 4128 | tf_op jit(solution)/shard_map/ppermute | solution.py:302
  55.9 0.5 gather_fusion
  56.9 4.1 %attend.1 = (bf16[384,512]{1,0:T(8,128)(2,1)}, bf16[1024,128]{1,0:T(8,128)(2,1)S(1)}) custom-call(s32[3,2]{1,0:T(4,128)S(1)} %copy.20.listed_ref, f32[384,512]{1,0:T(8,128)S(1)} %get-tuple-element.25.hnew_ref, bf16[384,512]{1,0:T(8,128)(2,1)S(1)} %get-tuple-element.26.hdst_ref, bf16[1024,512]{1,0:T(8,128)(2,1)S(1)} %copy-done, ...), custom_call_target="tpu_custom_call" | custom-call | flops 603979776 | bytes 4194304 | tf_op jit(solution)/shard_map/attend/pallas_call | solution.py:406
  61.0 0.7 copy-done.5
  61.7 3.7 %all-to-all-done.2 = bf16[32,72,128]{2,1,0:T(8,128)(2,1)S(1)} async-done(((bf16[32,72,128]{2,1,0:T(8,128)(2,1)}), bf16[32,72,128]{2,1,0:T(8,128)(2,1)S(1)}, u32[]{:S(2)}, u32[]{:S(2)}) %all-to-all-start.2) | async-done | bytes 589856 | tf_op jit(solution)/shard_map/all_to_all | solution.py:404
  65.4 2.2 %apply.1.refs_0_ = bf16[1024,128]{1,0:T(8,128)(2,1)S(1)} custom-call(s32[1,2304]{1,0:T(1,128)S(1)} %reshape.48.ids_ref, bf16[2304,128]{1,0:T(8,128)(2,1)S(1)} %bitcast.20, bf16[1024,128]{1,0:T(8,128)(2,1)} %copy-done.5), custom_call_target="tpu_custom_call" | custom-call | flops 1207959552 | bytes 4194304 | tf_op jit(solution)/shard_map/apply/pallas_call | solution.py:424
  67.6 1.2 %collective-permute-start.19 = (bf16[1024,128]{1,0:T(8,128)(2,1)S(1)}, bf16[1024,128]{1,0:T(8,128)(2,1)S(1)}, u32[]{:S(2)}, u32[]{:S(2)}) collective-permute-start(bf16[1024,128]{1,0:T(8,128)(2,1)S(1)} %apply.1.refs_0_), channel_id=1, source_target_pairs={{0,2},{1,3},{2,0},{3,1},{4,6},{5,7},{6,4},{7,5},{8,10},{9,11},{10,... | collective-permute-start | bytes 786440 | tf_op jit(solution)/shard_map/ppermute | solution.py:302
  68.9 7.0 %collective-permute-done.19.refs_2_ = bf16[1024,128]{1,0:T(8,128)(2,1)S(1)} collective-permute-done((bf16[1024,128]{1,0:T(8,128)(2,1)S(1)}, bf16[1024,128]{1,0:T(8,128)(2,1)S(1)}, u32[]{:S(2)}, u32[]{:S(2)}) %collective-permute-start.19) | collective-permute-done | bytes 262176 | tf_op jit(solution)/shard_map/ppermute | solution.py:302
  75.9 1.5 %collective-permute-done.20.refs_3_ = bf16[1024,128]{1,0:T(8,128)(2,1)S(1)} collective-permute-done((bf16[1024,128]{1,0:T(8,128)(2,1)S(1)}, bf16[1024,128]{1,0:T(8,128)(2,1)S(1)}, u32[]{:S(2)}, u32[]{:S(2)}) %collective-permute-start.20) | collective-permute-done | bytes 262176 | tf_op jit(solution)/shard_map/ppermute | solution.py:302
  77.4 1.0 %join.1 = bf16[1024,512]{1,0:T(8,128)(2,1)} custom-call(bf16[1024,128]{1,0:T(8,128)(2,1)S(1)} %apply.1.refs_0_, bf16[1024,128]{1,0:T(8,128)(2,1)S(1)} %collective-permute-done.18.refs_1_, bf16[1024,128]{1,0:T(8,128)(2,1)S(1)} %collective-permute-done.19.refs_2_, bf16[1024,128]{1,0:T(8,128)(2,1)S(1)} %collective-permute-done.20.refs_3_), custom_call_target="tpu_custom_call" | custom-call | flops 1048576 | bytes 2097152 | tf_op jit(solution)/shard_map/join/pallas_call | solution.py:434
  (76 shorter events, 3.9 us)
Async XLA Ops:
  2.4 4.2 %copy-start.13 = (bf16[512,384]{1,0:T(8,128)(2,1)S(1)}, bf16[512,384]{1,0:T(8,128)(2,1)}, u32[]{:S(2)}) copy-start(bf16[512,384]{1,0:T(8,128)(2,1)} %refs_4_) | copy-start | bytes 1179652
  2.4 4.3 %copy-start.16 = (bf16[128,384]{1,0:T(8,128)(2,1)S(1)}, bf16[128,384]{1,0:T(8,128)(2,1)}, u32[]{:S(2)}) copy-start(bf16[128,384]{1,0:T(8,128)(2,1)} %refs_8_) | copy-start | bytes 294916
  3.7 24.2 %collective-permute-start.1 = (bf16[512,384]{1,0:T(8,128)(2,1)S(1)}, bf16[512,384]{1,0:T(8,128)(2,1)S(1)}, u32[]{:S(2)}, u32[]{:S(2)}) collective-permute-start(bf16[512,384]{1,0:T(8,128)(2,1)S(1)} %copy-done.12), channel_id=1, source_target_pairs={{0,2},{1,3},{2,0},{3,1},{4,6},{5,7},{6,4},{7,5},{8,10},{9,11},{10,... | collective-permute-start | bytes 1179656 | tf_op jit(solution)/shard_map/ppermute | solution.py:302
  6.6 21.7 %collective-permute-start.4 = (bf16[512,384]{1,0:T(8,128)(2,1)S(1)}, bf16[512,384]{1,0:T(8,128)(2,1)S(1)}, u32[]{:S(2)}, u32[]{:S(2)}) collective-permute-start(bf16[512,384]{1,0:T(8,128)(2,1)S(1)} %copy-done.13), channel_id=1, source_target_pairs={{0,2},{1,3},{2,0},{3,1},{4,6},{5,7},{6,4},{7,5},{8,10},{9,11},{10,... | collective-permute-start | bytes 1179656 | tf_op jit(solution)/shard_map/ppermute | solution.py:302
  6.7 21.1 %collective-permute-start.7 = (bf16[128,384]{1,0:T(8,128)(2,1)S(1)}, bf16[128,384]{1,0:T(8,128)(2,1)S(1)}, u32[]{:S(2)}, u32[]{:S(2)}) collective-permute-start(bf16[128,384]{1,0:T(8,128)(2,1)S(1)} %copy-done.16), channel_id=1, source_target_pairs={{0,2},{1,3},{2,0},{3,1},{4,6},{5,7},{6,4},{7,5},{8,10},{9,11},{10,... | collective-permute-start | bytes 294920 | tf_op jit(solution)/shard_map/ppermute | solution.py:302
  23.5 4.9 %copy-start.9 = (f32[384,8]{1,0:T(8,128)S(1)}, f32[384,8]{1,0:T(8,128)}, u32[]{:S(2)}) copy-start(f32[384,8]{1,0:T(8,128)} %copy-done.8) | copy-start | bytes 36868
  23.6 16.5 %all-to-all-start.1 = ((bf16[8,264,128]{2,1,0:T(8,128)(2,1)}), bf16[8,264,128]{2,1,0:T(8,128)(2,1)S(1)}, u32[]{:S(2)}, u32[]{:S(2)}) async-start(bf16[8,264,128]{2,1,0:T(8,128)(2,1)} %serve.1), calls=%async_computation.1 | async-start | bytes 1081344 | tf_op jit(solution)/shard_map/all_to_all | solution.py:384
  27.2 6.0 %collective-permute-start = (bf16[512,384]{1,0:T(8,128)(2,1)S(1)}, bf16[512,384]{1,0:T(8,128)(2,1)}, u32[]{:S(2)}, u32[]{:S(2)}) collective-permute-start(bf16[512,384]{1,0:T(8,128)(2,1)S(1)} %copy-done.12), channel_id=1, source_target_pairs={{0,1},{1,0},{2,3},{3,2},{4,5},{5,4},{6,7},{7,6},{8,9},{9,8},{10,11... | collective-permute-start | bytes 1179656 | tf_op jit(solution)/shard_map/ppermute | solution.py:302
  27.3 6.0 %collective-permute-start.3 = (bf16[512,384]{1,0:T(8,128)(2,1)S(1)}, bf16[512,384]{1,0:T(8,128)(2,1)}, u32[]{:S(2)}, u32[]{:S(2)}) collective-permute-start(bf16[512,384]{1,0:T(8,128)(2,1)S(1)} %copy-done.13), channel_id=1, source_target_pairs={{0,1},{1,0},{2,3},{3,2},{4,5},{5,4},{6,7},{7,6},{8,9},{9,8},{10,11... | collective-permute-start | bytes 1179656 | tf_op jit(solution)/shard_map/ppermute | solution.py:302
  27.8 3.5 %copy-start.17 = (bf16[128,384]{1,0:T(8,128)(2,1)}, bf16[128,384]{1,0:T(8,128)(2,1)S(1)}, u32[]{:S(2)}) copy-start(bf16[128,384]{1,0:T(8,128)(2,1)S(1)} %collective-permute-done.7.refs_10_) | copy-start | bytes 294916
  27.8 3.5 %collective-permute-start.6 = (bf16[128,384]{1,0:T(8,128)(2,1)S(1)}, bf16[128,384]{1,0:T(8,128)(2,1)S(1)}, u32[]{:S(2)}, u32[]{:S(2)}) collective-permute-start(bf16[128,384]{1,0:T(8,128)(2,1)S(1)} %copy-done.16), channel_id=1, source_target_pairs={{0,1},{1,0},{2,3},{3,2},{4,5},{5,4},{6,7},{7,6},{8,9},{9,8},{10,11... | collective-permute-start | bytes 294920 | tf_op jit(solution)/shard_map/ppermute | solution.py:302
  27.9 2.0 %copy-start.14 = (bf16[512,384]{1,0:T(8,128)(2,1)}, bf16[512,384]{1,0:T(8,128)(2,1)S(1)}, u32[]{:S(2)}) copy-start(bf16[512,384]{1,0:T(8,128)(2,1)S(1)} %collective-permute-done.1.refs_2_) | copy-start | bytes 1179652
  27.9 6.9 %collective-permute-start.2 = (bf16[512,384]{1,0:T(8,128)(2,1)S(1)}, bf16[512,384]{1,0:T(8,128)(2,1)}, u32[]{:S(2)}, u32[]{:S(2)}) collective-permute-start(bf16[512,384]{1,0:T(8,128)(2,1)S(1)} %collective-permute-done.1.refs_2_), channel_id=1, source_target_pairs={{0,1},{1,0},{2,3},{3,2},{4,5},{5,4},{6,7},{7,6},{8,9},{9,8},{10,11... | collective-permute-start | bytes 1179656 | tf_op jit(solution)/shard_map/ppermute | solution.py:302
  28.3 6.7 %collective-permute-start.5 = (bf16[512,384]{1,0:T(8,128)(2,1)S(1)}, bf16[512,384]{1,0:T(8,128)(2,1)}, u32[]{:S(2)}, u32[]{:S(2)}) collective-permute-start(bf16[512,384]{1,0:T(8,128)(2,1)S(1)} %collective-permute-done.4.refs_6_), channel_id=1, source_target_pairs={{0,1},{1,0},{2,3},{3,2},{4,5},{5,4},{6,7},{7,6},{8,9},{9,8},{10,11... | collective-permute-start | bytes 1179656 | tf_op jit(solution)/shard_map/ppermute | solution.py:302
  29.2 3.5 %copy-start.1 = (bf16[512,256]{1,0:T(8,128)(2,1)S(1)}, bf16[512,256]{1,0:T(8,128)(2,1)}, u32[]{:S(2)}) copy-start(bf16[512,256]{1,0:T(8,128)(2,1)} %refs_4_.1) | copy-start | bytes 786436
  29.2 4.1 %copy-start.2 = (bf16[512,128]{1,0:T(8,128)(2,1)S(1)}, bf16[512,128]{1,0:T(8,128)(2,1)}, u32[]{:S(2)}) copy-start(bf16[512,128]{1,0:T(8,128)(2,1)} %refs_0_.1) | copy-start | bytes 393220
  31.3 1.4 %collective-permute-start.8 = (bf16[128,384]{1,0:T(8,128)(2,1)S(1)}, bf16[128,384]{1,0:T(8,128)(2,1)S(1)}, u32[]{:S(2)}, u32[]{:S(2)}) collective-permute-start(bf16[128,384]{1,0:T(8,128)(2,1)S(1)} %collective-permute-done.7.refs_10_), channel_id=1, source_target_pairs={{0,1},{1,0},{2,3},{3,2},{4,5},{5,4},{6,7},{7,6},{8,9},{9,8},{10,11... | collective-permute-start | bytes 294920 | tf_op jit(solution)/shard_map/ppermute | solution.py:302
  32.7 7.4 %copy-start.19 = (bf16[128,384]{1,0:T(8,128)(2,1)}, bf16[128,384]{1,0:T(8,128)(2,1)S(1)}, u32[]{:S(2)}) copy-start(bf16[128,384]{1,0:T(8,128)(2,1)S(1)} %collective-permute-done.8.refs_11_) | copy-start | bytes 294916
  32.7 22.5 %collective-permute-start.13 = (bf16[512,256]{1,0:T(8,128)(2,1)S(1)}, bf16[512,256]{1,0:T(8,128)(2,1)S(1)}, u32[]{:S(2)}, u32[]{:S(2)}) collective-permute-start(bf16[512,256]{1,0:T(8,128)(2,1)S(1)} %copy-done.1), channel_id=1, source_target_pairs={{0,2},{1,3},{2,0},{3,1},{4,6},{5,7},{6,4},{7,5},{8,10},{9,11},{10,... | collective-permute-start | bytes 786440 | tf_op jit(solution)/shard_map/ppermute | solution.py:302
  33.3 23.3 %collective-permute-start.12 = (bf16[512,256]{1,0:T(8,128)(2,1)S(1)}, bf16[512,256]{1,0:T(8,128)(2,1)}, u32[]{:S(2)}, u32[]{:S(2)}) collective-permute-start(bf16[512,256]{1,0:T(8,128)(2,1)S(1)} %copy-done.1), channel_id=1, source_target_pairs={{0,1},{1,0},{2,3},{3,2},{4,5},{5,4},{6,7},{7,6},{8,9},{9,8},{10,11... | collective-permute-start | bytes 786440 | tf_op jit(solution)/shard_map/ppermute | solution.py:302
  33.3 21.6 %collective-permute-start.10 = (bf16[512,128]{1,0:T(8,128)(2,1)S(1)}, bf16[512,128]{1,0:T(8,128)(2,1)}, u32[]{:S(2)}, u32[]{:S(2)}) collective-permute-start(bf16[512,128]{1,0:T(8,128)(2,1)S(1)} %copy-done.2), channel_id=1, source_target_pairs={{0,2},{1,3},{2,0},{3,1},{4,6},{5,7},{6,4},{7,5},{8,10},{9,11},{10,... | collective-permute-start | bytes 393224 | tf_op jit(solution)/shard_map/ppermute | solution.py:302
  34.8 21.7 %collective-permute-start.9 = (bf16[512,128]{1,0:T(8,128)(2,1)S(1)}, bf16[512,128]{1,0:T(8,128)(2,1)}, u32[]{:S(2)}, u32[]{:S(2)}) collective-permute-start(bf16[512,128]{1,0:T(8,128)(2,1)S(1)} %copy-done.2), channel_id=1, source_target_pairs={{0,1},{1,0},{2,3},{3,2},{4,5},{5,4},{6,7},{7,6},{8,9},{9,8},{10,11... | collective-permute-start | bytes 393224 | tf_op jit(solution)/shard_map/ppermute | solution.py:302
  45.9 11.0 %copy-start = (bf16[1024,512]{1,0:T(8,128)(2,1)S(1)}, bf16[1024,512]{1,0:T(8,128)(2,1)}, u32[]{:S(2)}) copy-start(bf16[1024,512]{1,0:T(8,128)(2,1)} %memory_ref.3) | copy-start | bytes 3145732
  45.9 19.5 %all-to-all-start.2 = ((bf16[32,72,128]{2,1,0:T(8,128)(2,1)}), bf16[32,72,128]{2,1,0:T(8,128)(2,1)S(1)}, u32[]{:S(2)}, u32[]{:S(2)}) async-start(bf16[32,72,128]{2,1,0:T(8,128)(2,1)} %get-tuple-element.30), calls=%async_computation.2 | async-start | bytes 1179648 | tf_op jit(solution)/shard_map/all_to_all | solution.py:404
  48.7 4.9 %collective-permute-start.16 = (s32[8,128]{1,0:T(8,128)S(1)}, s32[8,128]{1,0:T(8,128)S(1)}, u32[]{:S(2)}, u32[]{:S(2)}) collective-permute-start(s32[8,128]{1,0:T(8,128)S(1)} %bitcast.22), channel_id=1, source_target_pairs={{0,2},{1,3},{2,0},{3,1},{4,6},{5,7},{6,4},{7,5},{8,10},{9,11},{10,... | collective-permute-start | bytes 12296 | tf_op jit(solution)/shard_map/ppermute | solution.py:302
  53.5 1.2 %collective-permute-start.15 = (s32[8,128]{1,0:T(8,128)S(1)}, s32[8,128]{1,0:T(8,128)S(1)}, u32[]{:S(2)}, u32[]{:S(2)}) collective-permute-start(s32[8,128]{1,0:T(8,128)S(1)} %bitcast.24), channel_id=1, source_target_pairs={{0,1},{1,0},{2,3},{3,2},{4,5},{5,4},{6,7},{7,6},{8,9},{9,8},{10,11... | collective-permute-start | bytes 12296 | tf_op jit(solution)/shard_map/ppermute | solution.py:302
  54.7 1.2 %collective-permute-start.17 = (s32[8,128]{1,0:T(8,128)S(1)}, s32[8,128]{1,0:T(8,128)S(1)}, u32[]{:S(2)}, u32[]{:S(2)}) collective-permute-start(s32[8,128]{1,0:T(8,128)S(1)} %collective-permute-done.16), channel_id=1, source_target_pairs={{0,1},{1,0},{2,3},{3,2},{4,5},{5,4},{6,7},{7,6},{8,9},{9,8},{10,11... | collective-permute-start | bytes 12296 | tf_op jit(solution)/shard_map/ppermute | solution.py:302
  54.9 1.7 %collective-permute-start.11 = (bf16[512,128]{1,0:T(8,128)(2,1)}, bf16[512,128]{1,0:T(8,128)(2,1)}, u32[]{:S(2)}, u32[]{:S(2)}) collective-permute-start(bf16[512,128]{1,0:T(8,128)(2,1)} %collective-permute-done.10.refs_2_), channel_id=1, source_target_pairs={{0,1},{1,0},{2,3},{3,2},{4,5},{5,4},{6,7},{7,6},{8,9},{9,8},{10,11... | collective-permute-start | bytes 393224 | tf_op jit(solution)/shard_map/ppermute | solution.py:302
  55.2 1.7 %collective-permute-start.14 = (bf16[512,256]{1,0:T(8,128)(2,1)S(1)}, bf16[512,256]{1,0:T(8,128)(2,1)}, u32[]{:S(2)}, u32[]{:S(2)}) collective-permute-start(bf16[512,256]{1,0:T(8,128)(2,1)S(1)} %collective-permute-done.13.refs_6_), channel_id=1, source_target_pairs={{0,1},{1,0},{2,3},{3,2},{4,5},{5,4},{6,7},{7,6},{8,9},{9,8},{10,11... | collective-permute-start | bytes 786440 | tf_op jit(solution)/shard_map/ppermute | solution.py:302
  67.6 8.3 %collective-permute-start.19 = (bf16[1024,128]{1,0:T(8,128)(2,1)S(1)}, bf16[1024,128]{1,0:T(8,128)(2,1)S(1)}, u32[]{:S(2)}, u32[]{:S(2)}) collective-permute-start(bf16[1024,128]{1,0:T(8,128)(2,1)S(1)} %apply.1.refs_0_), channel_id=1, source_target_pairs={{0,2},{1,3},{2,0},{3,1},{4,6},{5,7},{6,4},{7,5},{8,10},{9,11},{10,... | collective-permute-start | bytes 786440 | tf_op jit(solution)/shard_map/ppermute | solution.py:302
  68.8 7.1 %collective-permute-start.18 = (bf16[1024,128]{1,0:T(8,128)(2,1)S(1)}, bf16[1024,128]{1,0:T(8,128)(2,1)S(1)}, u32[]{:S(2)}, u32[]{:S(2)}) collective-permute-start(bf16[1024,128]{1,0:T(8,128)(2,1)S(1)} %apply.1.refs_0_), channel_id=1, source_target_pairs={{0,1},{1,0},{2,3},{3,2},{4,5},{5,4},{6,7},{7,6},{8,9},{9,8},{10,11... | collective-permute-start | bytes 786440 | tf_op jit(solution)/shard_map/ppermute | solution.py:302
  75.9 1.5 %collective-permute-start.20 = (bf16[1024,128]{1,0:T(8,128)(2,1)S(1)}, bf16[1024,128]{1,0:T(8,128)(2,1)S(1)}, u32[]{:S(2)}, u32[]{:S(2)}) collective-permute-start(bf16[1024,128]{1,0:T(8,128)(2,1)S(1)} %collective-permute-done.19.refs_2_), channel_id=1, source_target_pairs={{0,1},{1,0},{2,3},{3,2},{4,5},{5,4},{6,7},{7,6},{8,9},{9,8},{10,11... | collective-permute-start | bytes 786440 | tf_op jit(solution)/shard_map/ppermute | solution.py:302
  (11 other events, 8.9 us)

commit v10 on v6

--- a/solution.py
+++ b/solution.py
@@ -28,12 +28,12 @@
     return jnp.dot(a, b, preferred_element_type=F32)
 
 
-def call(body, outs, specs, flops, bytes_, name, scratch=(), limit=8):
+def call(body, outs, specs, flops, bytes_, name, scratch=(), limit=8, out_specs=None):
     return pl.pallas_call(
         body,
         out_shape=outs,
         in_specs=specs,
-        out_specs=[VMEM] * len(outs),
+        out_specs=out_specs or [VMEM] * len(outs),
         scratch_shapes=list(scratch),
         compiler_params=pltpu.CompilerParams(vmem_limit_bytes=limit << 20),
         cost_estimate=pl.CostEstimate(flops=flops, bytes_accessed=bytes_, transcendentals=0),
@@ -237,11 +237,13 @@
 def attend_kernel(plan, listed_ref, hnew_ref, hdst_ref, memory_ref, *refs):
     reps = plan.reps
     w_query, w_keyval = refs[:reps], refs[reps : 2 * reps]
-    out_ref, quarter_ref, query, keyval = refs[2 * reps :]
+    out_ref, upper_ref, lower_ref, query, keyval = refs[2 * reps :]
     me = lax.axis_index("rep")
     events, width = hnew_ref.shape
-    piece = quarter_ref.shape[1]
-    quarter_ref[...] = memory_ref[:, pl.ds(pl.multiple_of(me * piece, LANES), piece)]
+    half, piece = upper_ref.shape
+    lane = pl.ds(pl.multiple_of(me * piece, LANES), piece)
+    upper_ref[...] = memory_ref[:half, lane]
+    lower_ref[...] = memory_ref[half:, lane]
     head = width // H
     hround = hnew_ref[...].astype(BF16)
     target = hdst_ref[...]
@@ -266,29 +268,36 @@
             out_ref[at, lane] = (hnew_ref[at, lane] + dot(prob, values)).astype(BF16)
 
 
-def apply_kernel(plan, ids_ref, landed_ref, part_ref, out_ref, held, sem):
+def apply_kernel(plan, first, ids_ref, landed_ref, part_ref, out_ref, held, total, sem):
     copy = pltpu.make_async_copy(part_ref, held, sem)
     copy.start()
-    stored = part_ref.shape[0]
+    rows = part_ref.shape[0]
     count = landed_ref.shape[0]
     landed = landed_ref[...]
-    step = min(256, stored)
-    ids = ids_ref[...]
-    totals = []
-    for i in range(0, stored, step):
-        hot = jnp.where(iota((step, count), 0) + i == ids, 1.0, 0.0).astype(BF16)
-        totals.append(dot(hot, landed))
+    step = min(256, rows)
+    ids = ids_ref[...].astype(jnp.int16)
+    for i in range(0, rows, step):
+        here = lax.broadcasted_iota(jnp.int16, (step, count), 0) + jnp.int16(first + i)
+        hot = jnp.where(here == ids, jnp.ones((), BF16), jnp.zeros((), BF16))
+        total[i : i + step, :] = dot(hot, landed)
     copy.wait()
-    for i, total in zip(range(0, stored, step), totals):
-        out_ref[i : i + step, :] = (held[i : i + step, :].astype(F32) + total).astype(BF16)
+    out_ref[...] = (held[...].astype(F32) + total[...]).astype(BF16)
 
 
 def join_kernel(plan, *refs):
     me = lax.axis_index("rep")
-    out_ref = refs[-1]
-    for k in range(plan.reps):
-        piece = refs[k].shape[1]
-        out_ref[:, pl.ds(pl.multiple_of((me ^ k) * piece, LANES), piece)] = refs[k][...]
+    out_ref, sems = refs[2 * plan.reps :]
+    copies = []
+    for h in range(2):
+        for k in range(plan.reps):
+            ref = refs[h * plan.reps + k]
+            rows, piece = ref.shape
+            at = pl.ds(pl.multiple_of((me ^ k) * piece, LANES), piece)
+            copies.append(pltpu.make_async_copy(ref, out_ref.at[pl.ds(h * rows, rows), at], sems.at[h, k]))
+    for copy in copies:
+        copy.start()
+    for copy in copies:
+        copy.wait()
 
 
 def swap(x, bit, reps):
@@ -398,9 +407,9 @@
     )(returned, rows, cols, *far([encode, *full_input, *full_hidden, *full_time]))
     landed = lax.all_to_all(outgoing, ("shard", "rep"), split_axis=0, concat_axis=0, tiled=True)
 
-    embed, part = call(
+    embed, *part = call(
         run(attend_kernel, plan),
-        [sds((events, width), BF16), sds((stored, piece), BF16)],
+        [sds((events, width), BF16)] + [sds((stored // 2, piece), BF16)] * 2,
         [SMEM] + [VMEM] * (3 + 2 * reps),
         2 * events * width * 3 * width,
         4 << 20,
@@ -416,19 +425,32 @@
     stack = jnp.stack([x[:, : plan.pad] for x in everyone])
     order = me ^ jnp.arange(reps, dtype=I32)
     ids = jnp.swapaxes(stack[order], 0, 1).reshape(1, owners * reps * plan.pad)
-    quarter = call(
-        run(apply_kernel, plan),
-        [sds((stored, piece), BF16)],
-        [VMEM] * 2 + [HBM],
-        2 * stored * owners * reps * plan.pad * piece * 2,
-        4 << 20,
-        "apply",
-        scratch=[pltpu.VMEM((stored, piece), BF16), pltpu.SemaphoreType.DMA],
-        limit=16,
-    )(ids, landed.reshape(owners * reps * plan.pad, piece), *far([part]))[0]
+    landed = landed.reshape(owners * reps * plan.pad, piece)
+    half = stored // 2
+    quarters = [
+        call(
+            run(apply_kernel, plan, h * half),
+            [sds((half, piece), BF16)],
+            [VMEM] * 2 + [HBM],
+            4 << 30,
+            1 << 20,
+            "apply",
+            scratch=[pltpu.VMEM((half, piece), BF16), pltpu.VMEM((half, piece), F32), pltpu.SemaphoreType.DMA],
+            limit=16,
+        )(ids, landed, *far([part[h]]))[0]
+        for h in range(2)
+    ]
+    upper, lower = spread(quarters, reps)
     new_memory = call(
-        run(join_kernel, plan), [sds((stored, width), BF16)], [VMEM] * reps, 1 << 20, 2 << 20, "join", limit=8
-    )(*spread([quarter], reps)[0])[0]
+        run(join_kernel, plan),
+        [sds((stored, width), BF16)],
+        [VMEM] * (2 * reps),
+        1 << 20,
+        2 << 20,
+        "join",
+        scratch=[pltpu.SemaphoreType.DMA((2, reps))],
+        out_specs=[HBM],
+    )(*upper, *lower)[0]
     return (embed, new_memory)
 
 

time: 77.6 us -> 76.5 us (0.986)
  waiting for transfers between devices: 27.8 us -> 24.1 us
  starting transfers between devices: 25.8 us -> 27.2 us
    ppermute x21 -> x24, waiting for transfers between devices: 15 us -> 12 us  [swap(): return lax.ppermute(x, 'rep', [(i, i ^ bit) for i in range(reps)])]
    ppermute x21 -> x24, starting transfers between devices: 12.2 us -> 13.6 us  [swap(): return lax.ppermute(x, 'rep', [(i, i ^ bit) for i in range(reps)])]
    unnamed x43 -> x45, local copies, waits for them, and re-layouts: 3.58 us -> 4.19 us
    pallas_call x3 -> x4, Pallas kernels: 7.49 us -> 8.04 us  [the longest x1 4.09 us: shards(): call(run(attend_kernel, plan), [sds((events, width), BF16)] + [sds((store...]
  transfers between devices with their start and end apart: 24 -> 27, of which waited for: 11 -> 12; matrix products, arithmetic and copies ran while one was open for 1% -> 1% of each run, Pallas kernels for 18% -> 20%
where the time goes in v10:
time: 76.5 us; the launch traced here: 76.1 us
  starting transfers between devices  27.2 us (36%)
  waiting for transfers between devices  24.1 us (32%)
  Pallas kernels  18.9 us (25%)
  local copies, waits for them, and re-layouts  4.85 us (6%)
  between operations  0.96 us (1%)
    ppermute x24, starting transfers between devices, swap(): return lax.ppermute(x, 'rep', [(i, i ^ bit) for i in range(reps)])  13.6 us
    ppermute x24, waiting for transfers between devices, swap(): return lax.ppermute(x, 'rep', [(i, i ^ bit) for i in range(reps)])  12 us
    all_to_all x1, starting transfers between devices, shards(): lax.all_to_all(request, 'shard', split_axis=0, concat_axis=0, tiled=True)  6.34 us
    pallas_call x1, Pallas kernels, shards(): call(run(gru_kernel, plan), [sds((owners * reps, plan.pad, piece), BF16),...  5.83 us
    all_to_all x1, waiting for transfers between devices, shards(): lax.all_to_all(served, 'shard', split_axis=0, concat_axis=0, tiled=True)  4.67 us
    all_to_all x1, waiting for transfers between devices, shards(): lax.all_to_all(request, 'shard', split_axis=0, concat_axis=0, tiled=True)  4.39 us
    unnamed x45, local copies, waits for them, and re-layouts  4.19 us
    pallas_call x1, Pallas kernels, shards(): call(run(attend_kernel, plan), [sds((events, width), BF16)] + [sds((store...  4.09 us
  transfers between devices with their start and end apart: 27, of which 12 were waited for; matrix products, arithmetic and copies ran while one was open for 1% of the time, Pallas kernels for 20%

profile of v10, /device:TPU:0, one launch (start us, length us, event | category | flops | bytes accessed | tf_op | source)
XLA Modules:
  0.0 76.1 jit_solution(17438538364160279654)
XLA Ops:
  0.6 0.7 copy-done.4
  1.3 1.0 %request.1 = s32[8,128]{1,0:T(8,128)} custom-call(s32[1,256]{1,0:T(1,128)S(1)} %bitcast.27, s32[1,256]{1,0:T(1,128)S(1)} %bitcast.26), custom_call_target="tpu_custom_call" | custom-call | flops 1048576 | bytes 16384 | tf_op jit(solution)/shard_map/request/pallas_call | solution.py:346
  2.3 2.9 %collective-permute-start.1 = (bf16[512,384]{1,0:T(8,128)(2,1)}, bf16[512,384]{1,0:T(8,128)(2,1)S(1)}, u32[]{:S(2)}, u32[]{:S(2)}) collective-permute-start(bf16[512,384]{1,0:T(8,128)(2,1)} %refs_0_), channel_id=1, source_target_pairs={{0,2},{1,3},{2,0},{3,1},{4,6},{5,7},{6,4},{7,5},{8,10},{9,11},{10,... | collective-permute-start | bytes 1179656 | tf_op jit(solution)/shard_map/ppermute | solution.py:304
  5.3 6.3 %all-to-all-start = ((s32[8,1,128]{2,1,0:T(1,128)}), s32[8,1,128]{2,1,0:T(1,128)S(1)}, u32[]{:S(2)}, u32[]{:S(2)}) async-start(s32[8,1,128]{2,1,0:T(1,128)} %bitcast.3), calls=%async_computation | async-start | bytes 8192 | tf_op jit(solution)/shard_map/all_to_all | solution.py:357
  12.1 1.5 %collective-permute-start.7 = (bf16[128,384]{1,0:T(8,128)(2,1)}, bf16[128,384]{1,0:T(8,128)(2,1)S(1)}, u32[]{:S(2)}, u32[]{:S(2)}) collective-permute-start(bf16[128,384]{1,0:T(8,128)(2,1)} %refs_8_), channel_id=1, source_target_pairs={{0,2},{1,3},{2,0},{3,1},{4,6},{5,7},{6,4},{7,5},{8,10},{9,11},{10,... | collective-permute-start | bytes 294920 | tf_op jit(solution)/shard_map/ppermute | solution.py:304
  13.6 4.4 %all-to-all-done = s32[8,1,128]{2,1,0:T(1,128)S(1)} async-done(((s32[8,1,128]{2,1,0:T(1,128)}), s32[8,1,128]{2,1,0:T(1,128)S(1)}, u32[]{:S(2)}, u32[]{:S(2)}) %all-to-all-start) | async-done | bytes 4128 | tf_op jit(solution)/shard_map/all_to_all | solution.py:357
  18.0 2.9 %serve.1 = bf16[8,264,128]{2,1,0:T(8,128)(2,1)} custom-call(s32[8,128]{1,0:T(8,128)S(1)} %bitcast.22, bf16[1024,512]{1,0:T(8,128)(2,1)} %memory_ref.3), custom_call_target="tpu_custom_call" | custom-call | flops 553648128 | bytes 1589248 | tf_op jit(solution)/shard_map/serve/pallas_call | solution.py:374
  20.9 3.7 %all-to-all-start.1 = ((bf16[8,264,128]{2,1,0:T(8,128)(2,1)}), bf16[8,264,128]{2,1,0:T(8,128)(2,1)S(1)}, u32[]{:S(2)}, u32[]{:S(2)}) async-start(bf16[8,264,128]{2,1,0:T(8,128)(2,1)} %serve.1), calls=%async_computation.1 | async-start | bytes 1081344 | tf_op jit(solution)/shard_map/all_to_all | solution.py:388
  25.7 0.7 copy-done.7
  26.4 1.2 %index.1 = (bf16[384,128]{1,0:T(8,128)(2,1)S(1)}, f32[384,8]{1,0:T(8,128)S(1)}, s32[8,384]{1,0:T(8,128)S(1)}) custom-call(s32[1,256]{1,0:T(1,128)S(1)} %bitcast.28, s32[1,1408]{1,0:T(1,128)S(1)} %reshape.45.packed_ref, f32[1,128]{1,0:T(1,128)S(1)} %bitcast.29, f32[1,128]{1,0:T(1,128)S(1)} %bitcast.30), custom_call_target="tpu_custom_call" | custom-call | flops 8589934592 | bytes 262144 | tf_op jit(solution)/shard_map/index/pallas_call | solution.py:358
  27.7 0.6 copy-done.9
  28.3 0.7 copy-done.13
  29.5 1.1 %collective-permute-done.8.refs_11_ = bf16[128,384]{1,0:T(8,128)(2,1)} collective-permute-done((bf16[128,384]{1,0:T(8,128)(2,1)S(1)}, bf16[128,384]{1,0:T(8,128)(2,1)}, u32[]{:S(2)}, u32[]{:S(2)}) %collective-permute-start.8) | collective-permute-done | bytes 98336 | tf_op jit(solution)/shard_map/ppermute | solution.py:304
  30.6 1.8 %collective-permute-start.13 = (bf16[512,256]{1,0:T(8,128)(2,1)S(1)}, bf16[512,256]{1,0:T(8,128)(2,1)S(1)}, u32[]{:S(2)}, u32[]{:S(2)}) collective-permute-start(bf16[512,256]{1,0:T(8,128)(2,1)S(1)} %copy-done.1), channel_id=1, source_target_pairs={{0,2},{1,3},{2,0},{3,1},{4,6},{5,7},{6,4},{7,5},{8,10},{9,11},{10,... | collective-permute-start | bytes 786440 | tf_op jit(solution)/shard_map/ppermute | solution.py:304
  33.1 4.7 %all-to-all-done.1.ret_ref = bf16[8,264,128]{2,1,0:T(8,128)(2,1)S(1)} async-done(((bf16[8,264,128]{2,1,0:T(8,128)(2,1)}), bf16[8,264,128]{2,1,0:T(8,128)(2,1)S(1)}, u32[]{:S(2)}, u32[]{:S(2)}) %all-to-all-start.1) | async-done | bytes 540704 | tf_op jit(solution)/shard_map/all_to_all | solution.py:388
  37.7 5.8 %gru.1 = (bf16[32,72,128]{2,1,0:T(8,128)(2,1)}, f32[384,512]{1,0:T(8,128)S(1)}, bf16[384,512]{1,0:T(8,128)(2,1)S(1)}) custom-call(bf16[8,264,128]{2,1,0:T(8,128)(2,1)S(1)} %all-to-all-done.1.ret_ref, s32[8,384]{1,0:T(8,128)S(1)} %get-tuple-element.18.row_ref, f32[384,8]{1,0:T(8,128)S(1)} %get-tuple-element.19.col_ref, bf16[384,128]{1,0:T(8,128)(2,1)} %copy-done.9, ...), custom_call_target="tpu_custom_call" | custom-call | flops 1207959552 | bytes 8388608 | tf_op jit(solution)/shard_map/gru/pallas_call | solution.py:390
  43.6 3.6 %all-to-all-start.2 = ((bf16[32,72,128]{2,1,0:T(8,128)(2,1)}), bf16[32,72,128]{2,1,0:T(8,128)(2,1)S(1)}, u32[]{:S(2)}, u32[]{:S(2)}) async-start(bf16[32,72,128]{2,1,0:T(8,128)(2,1)} %get-tuple-element.29), calls=%async_computation.2 | async-start | bytes 1179648 | tf_op jit(solution)/shard_map/all_to_all | solution.py:408
  47.2 1.8 %collective-permute-start.16 = (s32[8,128]{1,0:T(8,128)S(1)}, s32[8,128]{1,0:T(8,128)S(1)}, u32[]{:S(2)}, u32[]{:S(2)}) collective-permute-start(s32[8,128]{1,0:T(8,128)S(1)} %bitcast.23), channel_id=1, source_target_pairs={{0,2},{1,3},{2,0},{3,1},{4,6},{5,7},{6,4},{7,5},{8,10},{9,11},{10,... | collective-permute-start | bytes 12296 | tf_op jit(solution)/shard_map/ppermute | solution.py:304
  49.1 3.1 %collective-permute-done.16 = s32[8,128]{1,0:T(8,128)S(1)} collective-permute-done((s32[8,128]{1,0:T(8,128)S(1)}, s32[8,128]{1,0:T(8,128)S(1)}, u32[]{:S(2)}, u32[]{:S(2)}) %collective-permute-start.16) | collective-permute-done | bytes 4128 | tf_op jit(solution)/shard_map/ppermute | solution.py:304
  52.1 1.2 %collective-permute-done.15 = s32[8,128]{1,0:T(8,128)S(1)} collective-permute-done((s32[8,128]{1,0:T(8,128)S(1)}, s32[8,128]{1,0:T(8,128)S(1)}, u32[]{:S(2)}, u32[]{:S(2)}) %collective-permute-start.15) | collective-permute-done | bytes 4128 | tf_op jit(solution)/shard_map/ppermute | solution.py:304
  55.5 4.1 %attend.1 = (bf16[384,512]{1,0:T(8,128)(2,1)}, bf16[512,128]{1,0:T(8,128)(2,1)S(1)}, bf16[512,128]{1,0:T(8,128)(2,1)S(1)}) custom-call(s32[3,2]{1,0:T(4,128)S(1)} %copy.20.listed_ref, f32[384,512]{1,0:T(8,128)S(1)} %get-tuple-element.24.hnew_ref, bf16[384,512]{1,0:T(8,128)(2,1)S(1)} %get-tuple-element.25.hdst_ref, bf16[1024,512]{1,0:T(8,128)(2,1)S(1)} %copy-done, ...), custom_call_target="tpu_custom_call" | custom-call | flops 603979776 | bytes 4194304 | tf_op jit(solution)/shard_map/attend/pallas_call | solution.py:410
  59.6 0.7 copy-done.5
  60.2 0.6 copy-done.6
  60.9 3.1 %all-to-all-done.2 = bf16[32,72,128]{2,1,0:T(8,128)(2,1)S(1)} async-done(((bf16[32,72,128]{2,1,0:T(8,128)(2,1)}), bf16[32,72,128]{2,1,0:T(8,128)(2,1)S(1)}, u32[]{:S(2)}, u32[]{:S(2)}) %all-to-all-start.2) | async-done | bytes 589856 | tf_op jit(solution)/shard_map/all_to_all | solution.py:408
  63.9 1.5 %apply.3.refs_4_ = bf16[512,128]{1,0:T(8,128)(2,1)S(1)} custom-call(s32[1,2304]{1,0:T(1,128)S(1)} %reshape.48.ids_ref, bf16[2304,128]{1,0:T(8,128)(2,1)S(1)} %bitcast.20, bf16[512,128]{1,0:T(8,128)(2,1)} %copy-done.6), custom_call_target="tpu_custom_call" | custom-call | flops 4294967296 | bytes 1048576 | tf_op jit(solution)/shard_map/apply/pallas_call | solution.py:431
  65.4 1.2 %collective-permute-start.22 = (bf16[512,128]{1,0:T(8,128)(2,1)S(1)}, bf16[512,128]{1,0:T(8,128)(2,1)S(1)}, u32[]{:S(2)}, u32[]{:S(2)}) collective-permute-start(bf16[512,128]{1,0:T(8,128)(2,1)S(1)} %apply.3.refs_4_), channel_id=1, source_target_pairs={{0,2},{1,3},{2,0},{3,1},{4,6},{5,7},{6,4},{7,5},{8,10},{9,11},{10,... | collective-permute-start | bytes 393224 | tf_op jit(solution)/shard_map/ppermute | solution.py:304
  66.6 1.5 %apply.2.refs_0_ = bf16[512,128]{1,0:T(8,128)(2,1)S(1)} custom-call(s32[1,2304]{1,0:T(1,128)S(1)} %reshape.48.ids_ref, bf16[2304,128]{1,0:T(8,128)(2,1)S(1)} %bitcast.21, bf16[512,128]{1,0:T(8,128)(2,1)} %copy-done.5), custom_call_target="tpu_custom_call" | custom-call | flops 4294967296 | bytes 1048576 | tf_op jit(solution)/shard_map/apply/pallas_call | solution.py:431
  68.1 1.0 %collective-permute-start.19 = (bf16[512,128]{1,0:T(8,128)(2,1)S(1)}, bf16[512,128]{1,0:T(8,128)(2,1)S(1)}, u32[]{:S(2)}, u32[]{:S(2)}) collective-permute-start(bf16[512,128]{1,0:T(8,128)(2,1)S(1)} %apply.2.refs_0_), channel_id=1, source_target_pairs={{0,2},{1,3},{2,0},{3,1},{4,6},{5,7},{6,4},{7,5},{8,10},{9,11},{10,... | collective-permute-start | bytes 393224 | tf_op jit(solution)/shard_map/ppermute | solution.py:304
  69.6 1.3 %collective-permute-done.22.refs_6_ = bf16[512,128]{1,0:T(8,128)(2,1)S(1)} collective-permute-done((bf16[512,128]{1,0:T(8,128)(2,1)S(1)}, bf16[512,128]{1,0:T(8,128)(2,1)S(1)}, u32[]{:S(2)}, u32[]{:S(2)}) %collective-permute-start.22) | collective-permute-done | bytes 131104 | tf_op jit(solution)/shard_map/ppermute | solution.py:304
  70.9 2.8 %collective-permute-done.19.refs_2_ = bf16[512,128]{1,0:T(8,128)(2,1)S(1)} collective-permute-done((bf16[512,128]{1,0:T(8,128)(2,1)S(1)}, bf16[512,128]{1,0:T(8,128)(2,1)S(1)}, u32[]{:S(2)}, u32[]{:S(2)}) %collective-permute-start.19) | collective-permute-done | bytes 131104 | tf_op jit(solution)/shard_map/ppermute | solution.py:304
  73.7 1.3 %collective-permute-done.20.refs_3_ = bf16[512,128]{1,0:T(8,128)(2,1)S(1)} collective-permute-done((bf16[512,128]{1,0:T(8,128)(2,1)S(1)}, bf16[512,128]{1,0:T(8,128)(2,1)S(1)}, u32[]{:S(2)}, u32[]{:S(2)}) %collective-permute-start.20) | collective-permute-done | bytes 131104 | tf_op jit(solution)/shard_map/ppermute | solution.py:304
  75.0 1.0 %join.1 = bf16[1024,512]{1,0:T(8,128)(2,1)} custom-call(bf16[512,128]{1,0:T(8,128)(2,1)S(1)} %apply.2.refs_0_, bf16[512,128]{1,0:T(8,128)(2,1)S(1)} %collective-permute-done.18.refs_1_, bf16[512,128]{1,0:T(8,128)(2,1)S(1)} %collective-permute-done.19.refs_2_, bf16[512,128]{1,0:T(8,128)(2,1)S(1)} %collective-permute-done.20.refs_3_, ...), custom_call_target="tpu_custom_call" | custom-call | flops 1048576 | bytes 2097152 | tf_op jit(solution)/shard_map/join/pallas_call | solution.py:444
  (87 shorter events, 5.5 us)
Async XLA Ops:
  2.3 22.8 %collective-permute-start.1 = (bf16[512,384]{1,0:T(8,128)(2,1)}, bf16[512,384]{1,0:T(8,128)(2,1)S(1)}, u32[]{:S(2)}, u32[]{:S(2)}) collective-permute-start(bf16[512,384]{1,0:T(8,128)(2,1)} %refs_0_), channel_id=1, source_target_pairs={{0,2},{1,3},{2,0},{3,1},{4,6},{5,7},{6,4},{7,5},{8,10},{9,11},{10,... | collective-permute-start | bytes 1179656 | tf_op jit(solution)/shard_map/ppermute | solution.py:304
  5.2 20.4 %collective-permute-start.4 = (bf16[512,384]{1,0:T(8,128)(2,1)}, bf16[512,384]{1,0:T(8,128)(2,1)S(1)}, u32[]{:S(2)}, u32[]{:S(2)}) collective-permute-start(bf16[512,384]{1,0:T(8,128)(2,1)} %refs_4_), channel_id=1, source_target_pairs={{0,2},{1,3},{2,0},{3,1},{4,6},{5,7},{6,4},{7,5},{8,10},{9,11},{10,... | collective-permute-start | bytes 1179656 | tf_op jit(solution)/shard_map/ppermute | solution.py:304
  5.3 12.7 %all-to-all-start = ((s32[8,1,128]{2,1,0:T(1,128)}), s32[8,1,128]{2,1,0:T(1,128)S(1)}, u32[]{:S(2)}, u32[]{:S(2)}) async-start(s32[8,1,128]{2,1,0:T(1,128)} %bitcast.3), calls=%async_computation | async-start | bytes 8192 | tf_op jit(solution)/shard_map/all_to_all | solution.py:357
  11.6 20.8 %collective-permute-start = (bf16[512,384]{1,0:T(8,128)(2,1)}, bf16[512,384]{1,0:T(8,128)(2,1)S(1)}, u32[]{:S(2)}, u32[]{:S(2)}) collective-permute-start(bf16[512,384]{1,0:T(8,128)(2,1)} %refs_0_), channel_id=1, source_target_pairs={{0,1},{1,0},{2,3},{3,2},{4,5},{5,4},{6,7},{7,6},{8,9},{9,8},{10,11... | collective-permute-start | bytes 1179656 | tf_op jit(solution)/shard_map/ppermute | solution.py:304
  11.6 20.8 %collective-permute-start.3 = (bf16[512,384]{1,0:T(8,128)(2,1)}, bf16[512,384]{1,0:T(8,128)(2,1)S(1)}, u32[]{:S(2)}, u32[]{:S(2)}) collective-permute-start(bf16[512,384]{1,0:T(8,128)(2,1)} %refs_4_), channel_id=1, source_target_pairs={{0,1},{1,0},{2,3},{3,2},{4,5},{5,4},{6,7},{7,6},{8,9},{9,8},{10,11... | collective-permute-start | bytes 1179656 | tf_op jit(solution)/shard_map/ppermute | solution.py:304
  12.1 13.0 %collective-permute-start.7 = (bf16[128,384]{1,0:T(8,128)(2,1)}, bf16[128,384]{1,0:T(8,128)(2,1)S(1)}, u32[]{:S(2)}, u32[]{:S(2)}) collective-permute-start(bf16[128,384]{1,0:T(8,128)(2,1)} %refs_8_), channel_id=1, source_target_pairs={{0,2},{1,3},{2,0},{3,1},{4,6},{5,7},{6,4},{7,5},{8,10},{9,11},{10,... | collective-permute-start | bytes 294920 | tf_op jit(solution)/shard_map/ppermute | solution.py:304
  20.9 16.8 %all-to-all-start.1 = ((bf16[8,264,128]{2,1,0:T(8,128)(2,1)}), bf16[8,264,128]{2,1,0:T(8,128)(2,1)S(1)}, u32[]{:S(2)}, u32[]{:S(2)}) async-start(bf16[8,264,128]{2,1,0:T(8,128)(2,1)} %serve.1), calls=%async_computation.1 | async-start | bytes 1081344 | tf_op jit(solution)/shard_map/all_to_all | solution.py:388
  25.1 4.0 %collective-permute-start.6 = (bf16[128,384]{1,0:T(8,128)(2,1)S(1)}, bf16[128,384]{1,0:T(8,128)(2,1)S(1)}, u32[]{:S(2)}, u32[]{:S(2)}) collective-permute-start(bf16[128,384]{1,0:T(8,128)(2,1)S(1)} %copy-done.19), channel_id=1, source_target_pairs={{0,1},{1,0},{2,3},{3,2},{4,5},{5,4},{6,7},{7,6},{8,9},{9,8},{10,11... | collective-permute-start | bytes 294920 | tf_op jit(solution)/shard_map/ppermute | solution.py:304
  25.1 7.8 %collective-permute-start.2 = (bf16[512,384]{1,0:T(8,128)(2,1)S(1)}, bf16[512,384]{1,0:T(8,128)(2,1)}, u32[]{:S(2)}, u32[]{:S(2)}) collective-permute-start(bf16[512,384]{1,0:T(8,128)(2,1)S(1)} %collective-permute-done.1.refs_2_), channel_id=1, source_target_pairs={{0,1},{1,0},{2,3},{3,2},{4,5},{5,4},{6,7},{7,6},{8,9},{9,8},{10,11... | collective-permute-start | bytes 1179656 | tf_op jit(solution)/shard_map/ppermute | solution.py:304
  25.6 7.4 %collective-permute-start.5 = (bf16[512,384]{1,0:T(8,128)(2,1)S(1)}, bf16[512,384]{1,0:T(8,128)(2,1)}, u32[]{:S(2)}, u32[]{:S(2)}) collective-permute-start(bf16[512,384]{1,0:T(8,128)(2,1)S(1)} %collective-permute-done.4.refs_6_), channel_id=1, source_target_pairs={{0,1},{1,0},{2,3},{3,2},{4,5},{5,4},{6,7},{7,6},{8,9},{9,8},{10,11... | collective-permute-start | bytes 1179656 | tf_op jit(solution)/shard_map/ppermute | solution.py:304
  26.4 6.0 %copy-start.2 = (bf16[512,128]{1,0:T(8,128)(2,1)S(1)}, bf16[512,128]{1,0:T(8,128)(2,1)}, u32[]{:S(2)}) copy-start(bf16[512,128]{1,0:T(8,128)(2,1)} %refs_0_.1) | copy-start | bytes 393220
  29.1 8.6 %copy-start.21 = (bf16[128,384]{1,0:T(8,128)(2,1)}, bf16[128,384]{1,0:T(8,128)(2,1)S(1)}, u32[]{:S(2)}) copy-start(bf16[128,384]{1,0:T(8,128)(2,1)S(1)} %collective-permute-done.6.refs_9_) | copy-start | bytes 294916
  29.1 1.5 %collective-permute-start.8 = (bf16[128,384]{1,0:T(8,128)(2,1)S(1)}, bf16[128,384]{1,0:T(8,128)(2,1)}, u32[]{:S(2)}, u32[]{:S(2)}) collective-permute-start(bf16[128,384]{1,0:T(8,128)(2,1)S(1)} %collective-permute-done.7.refs_10_), channel_id=1, source_target_pairs={{0,1},{1,0},{2,3},{3,2},{4,5},{5,4},{6,7},{7,6},{8,9},{9,8},{10,11... | collective-permute-start | bytes 294920 | tf_op jit(solution)/shard_map/ppermute | solution.py:304
  30.6 23.2 %collective-permute-start.13 = (bf16[512,256]{1,0:T(8,128)(2,1)S(1)}, bf16[512,256]{1,0:T(8,128)(2,1)S(1)}, u32[]{:S(2)}, u32[]{:S(2)}) collective-permute-start(bf16[512,256]{1,0:T(8,128)(2,1)S(1)} %copy-done.1), channel_id=1, source_target_pairs={{0,2},{1,3},{2,0},{3,1},{4,6},{5,7},{6,4},{7,5},{8,10},{9,11},{10,... | collective-permute-start | bytes 786440 | tf_op jit(solution)/shard_map/ppermute | solution.py:304
  32.4 5.4 %copy-start.17 = (bf16[512,384]{1,0:T(8,128)(2,1)}, bf16[512,384]{1,0:T(8,128)(2,1)S(1)}, u32[]{:S(2)}) copy-start(bf16[512,384]{1,0:T(8,128)(2,1)S(1)} %collective-permute-done.refs_1_) | copy-start | bytes 1179652
  32.4 22.8 %collective-permute-start.12 = (bf16[512,256]{1,0:T(8,128)(2,1)S(1)}, bf16[512,256]{1,0:T(8,128)(2,1)}, u32[]{:S(2)}, u32[]{:S(2)}) collective-permute-start(bf16[512,256]{1,0:T(8,128)(2,1)S(1)} %copy-done.1), channel_id=1, source_target_pairs={{0,1},{1,0},{2,3},{3,2},{4,5},{5,4},{6,7},{7,6},{8,9},{9,8},{10,11... | collective-permute-start | bytes 786440 | tf_op jit(solution)/shard_map/ppermute | solution.py:304
  32.4 5.3 %copy-start.18 = (bf16[512,384]{1,0:T(8,128)(2,1)}, bf16[512,384]{1,0:T(8,128)(2,1)S(1)}, u32[]{:S(2)}) copy-start(bf16[512,384]{1,0:T(8,128)(2,1)S(1)} %collective-permute-done.3.refs_5_) | copy-start | bytes 1179652
  32.5 21.0 %collective-permute-start.10 = (bf16[512,128]{1,0:T(8,128)(2,1)S(1)}, bf16[512,128]{1,0:T(8,128)(2,1)}, u32[]{:S(2)}, u32[]{:S(2)}) collective-permute-start(bf16[512,128]{1,0:T(8,128)(2,1)S(1)} %copy-done.2), channel_id=1, source_target_pairs={{0,2},{1,3},{2,0},{3,1},{4,6},{5,7},{6,4},{7,5},{8,10},{9,11},{10,... | collective-permute-start | bytes 393224 | tf_op jit(solution)/shard_map/ppermute | solution.py:304
  32.9 22.3 %collective-permute-start.9 = (bf16[512,128]{1,0:T(8,128)(2,1)S(1)}, bf16[512,128]{1,0:T(8,128)(2,1)}, u32[]{:S(2)}, u32[]{:S(2)}) collective-permute-start(bf16[512,128]{1,0:T(8,128)(2,1)S(1)} %copy-done.2), channel_id=1, source_target_pairs={{0,1},{1,0},{2,3},{3,2},{4,5},{5,4},{6,7},{7,6},{8,9},{9,8},{10,11... | collective-permute-start | bytes 393224 | tf_op jit(solution)/shard_map/ppermute | solution.py:304
  43.6 11.9 %copy-start = (bf16[1024,512]{1,0:T(8,128)(2,1)S(1)}, bf16[1024,512]{1,0:T(8,128)(2,1)}, u32[]{:S(2)}) copy-start(bf16[1024,512]{1,0:T(8,128)(2,1)} %memory_ref.3) | copy-start | bytes 3145732
  43.6 20.4 %all-to-all-start.2 = ((bf16[32,72,128]{2,1,0:T(8,128)(2,1)}), bf16[32,72,128]{2,1,0:T(8,128)(2,1)S(1)}, u32[]{:S(2)}, u32[]{:S(2)}) async-start(bf16[32,72,128]{2,1,0:T(8,128)(2,1)} %get-tuple-element.29), calls=%async_computation.2 | async-start | bytes 1179648 | tf_op jit(solution)/shard_map/all_to_all | solution.py:408
  47.2 4.9 %collective-permute-start.16 = (s32[8,128]{1,0:T(8,128)S(1)}, s32[8,128]{1,0:T(8,128)S(1)}, u32[]{:S(2)}, u32[]{:S(2)}) collective-permute-start(s32[8,128]{1,0:T(8,128)S(1)} %bitcast.23), channel_id=1, source_target_pairs={{0,2},{1,3},{2,0},{3,1},{4,6},{5,7},{6,4},{7,5},{8,10},{9,11},{10,... | collective-permute-start | bytes 12296 | tf_op jit(solution)/shard_map/ppermute | solution.py:304
  52.1 1.2 %collective-permute-start.15 = (s32[8,128]{1,0:T(8,128)S(1)}, s32[8,128]{1,0:T(8,128)S(1)}, u32[]{:S(2)}, u32[]{:S(2)}) collective-permute-start(s32[8,128]{1,0:T(8,128)S(1)} %bitcast.25), channel_id=1, source_target_pairs={{0,1},{1,0},{2,3},{3,2},{4,5},{5,4},{6,7},{7,6},{8,9},{9,8},{10,11... | collective-permute-start | bytes 12296 | tf_op jit(solution)/shard_map/ppermute | solution.py:304
  53.3 1.2 %collective-permute-start.17 = (s32[8,128]{1,0:T(8,128)S(1)}, s32[8,128]{1,0:T(8,128)S(1)}, u32[]{:S(2)}, u32[]{:S(2)}) collective-permute-start(s32[8,128]{1,0:T(8,128)S(1)} %collective-permute-done.16), channel_id=1, source_target_pairs={{0,1},{1,0},{2,3},{3,2},{4,5},{5,4},{6,7},{7,6},{8,9},{9,8},{10,11... | collective-permute-start | bytes 12296 | tf_op jit(solution)/shard_map/ppermute | solution.py:304
  53.5 1.7 %collective-permute-start.11 = (bf16[512,128]{1,0:T(8,128)(2,1)}, bf16[512,128]{1,0:T(8,128)(2,1)}, u32[]{:S(2)}, u32[]{:S(2)}) collective-permute-start(bf16[512,128]{1,0:T(8,128)(2,1)} %collective-permute-done.10.refs_2_), channel_id=1, source_target_pairs={{0,1},{1,0},{2,3},{3,2},{4,5},{5,4},{6,7},{7,6},{8,9},{9,8},{10,11... | collective-permute-start | bytes 393224 | tf_op jit(solution)/shard_map/ppermute | solution.py:304
  53.8 1.7 %collective-permute-start.14 = (bf16[512,256]{1,0:T(8,128)(2,1)S(1)}, bf16[512,256]{1,0:T(8,128)(2,1)}, u32[]{:S(2)}, u32[]{:S(2)}) collective-permute-start(bf16[512,256]{1,0:T(8,128)(2,1)S(1)} %collective-permute-done.13.refs_6_), channel_id=1, source_target_pairs={{0,1},{1,0},{2,3},{3,2},{4,5},{5,4},{6,7},{7,6},{8,9},{9,8},{10,11... | collective-permute-start | bytes 786440 | tf_op jit(solution)/shard_map/ppermute | solution.py:304
  65.4 5.5 %collective-permute-start.22 = (bf16[512,128]{1,0:T(8,128)(2,1)S(1)}, bf16[512,128]{1,0:T(8,128)(2,1)S(1)}, u32[]{:S(2)}, u32[]{:S(2)}) collective-permute-start(bf16[512,128]{1,0:T(8,128)(2,1)S(1)} %apply.3.refs_4_), channel_id=1, source_target_pairs={{0,2},{1,3},{2,0},{3,1},{4,6},{5,7},{6,4},{7,5},{8,10},{9,11},{10,... | collective-permute-start | bytes 393224 | tf_op jit(solution)/shard_map/ppermute | solution.py:304
  68.1 5.6 %collective-permute-start.19 = (bf16[512,128]{1,0:T(8,128)(2,1)S(1)}, bf16[512,128]{1,0:T(8,128)(2,1)S(1)}, u32[]{:S(2)}, u32[]{:S(2)}) collective-permute-start(bf16[512,128]{1,0:T(8,128)(2,1)S(1)} %apply.2.refs_0_), channel_id=1, source_target_pairs={{0,2},{1,3},{2,0},{3,1},{4,6},{5,7},{6,4},{7,5},{8,10},{9,11},{10,... | collective-permute-start | bytes 393224 | tf_op jit(solution)/shard_map/ppermute | solution.py:304
  69.1 4.6 %collective-permute-start.21 = (bf16[512,128]{1,0:T(8,128)(2,1)S(1)}, bf16[512,128]{1,0:T(8,128)(2,1)S(1)}, u32[]{:S(2)}, u32[]{:S(2)}) collective-permute-start(bf16[512,128]{1,0:T(8,128)(2,1)S(1)} %apply.3.refs_4_), channel_id=1, source_target_pairs={{0,1},{1,0},{2,3},{3,2},{4,5},{5,4},{6,7},{7,6},{8,9},{9,8},{10,11... | collective-permute-start | bytes 393224 | tf_op jit(solution)/shard_map/ppermute | solution.py:304
  69.1 4.6 %collective-permute-start.18 = (bf16[512,128]{1,0:T(8,128)(2,1)S(1)}, bf16[512,128]{1,0:T(8,128)(2,1)S(1)}, u32[]{:S(2)}, u32[]{:S(2)}) collective-permute-start(bf16[512,128]{1,0:T(8,128)(2,1)S(1)} %apply.2.refs_0_), channel_id=1, source_target_pairs={{0,1},{1,0},{2,3},{3,2},{4,5},{5,4},{6,7},{7,6},{8,9},{9,8},{10,11... | collective-permute-start | bytes 393224 | tf_op jit(solution)/shard_map/ppermute | solution.py:304
  70.9 2.8 %collective-permute-start.23 = (bf16[512,128]{1,0:T(8,128)(2,1)S(1)}, bf16[512,128]{1,0:T(8,128)(2,1)S(1)}, u32[]{:S(2)}, u32[]{:S(2)}) collective-permute-start(bf16[512,128]{1,0:T(8,128)(2,1)S(1)} %collective-permute-done.22.refs_6_), channel_id=1, source_target_pairs={{0,1},{1,0},{2,3},{3,2},{4,5},{5,4},{6,7},{7,6},{8,9},{9,8},{10,11... | collective-permute-start | bytes 393224 | tf_op jit(solution)/shard_map/ppermute | solution.py:304
  73.7 1.3 %collective-permute-start.20 = (bf16[512,128]{1,0:T(8,128)(2,1)S(1)}, bf16[512,128]{1,0:T(8,128)(2,1)S(1)}, u32[]{:S(2)}, u32[]{:S(2)}) collective-permute-start(bf16[512,128]{1,0:T(8,128)(2,1)S(1)} %collective-permute-done.19.refs_2_), channel_id=1, source_target_pairs={{0,1},{1,0},{2,3},{3,2},{4,5},{5,4},{6,7},{7,6},{8,9},{9,8},{10,11... | collective-permute-start | bytes 393224 | tf_op jit(solution)/shard_map/ppermute | solution.py:304
  (17 other events, 37.5 us)

commit v11 on v10

--- a/solution.py
+++ b/solution.py
@@ -268,10 +268,7 @@
             out_ref[at, lane] = (hnew_ref[at, lane] + dot(prob, values)).astype(BF16)
 
 
-def apply_kernel(plan, first, ids_ref, landed_ref, part_ref, out_ref, held, total, sem):
-    copy = pltpu.make_async_copy(part_ref, held, sem)
-    copy.start()
-    rows = part_ref.shape[0]
+def total_of(first, rows, ids_ref, landed_ref, out):
     count = landed_ref.shape[0]
     landed = landed_ref[...]
     step = min(256, rows)
@@ -279,9 +276,23 @@
     for i in range(0, rows, step):
         here = lax.broadcasted_iota(jnp.int16, (step, count), 0) + jnp.int16(first + i)
         hot = jnp.where(here == ids, jnp.ones((), BF16), jnp.zeros((), BF16))
-        total[i : i + step, :] = dot(hot, landed)
-    copy.wait()
+        out[i : i + step, :] = dot(hot, landed)
+
+
+def upper_kernel(plan, ids_ref, landed_ref, part_ref, next_ref, out_ref, kept_ref, held, total, sems):
+    copies = [pltpu.make_async_copy(part_ref, held, sems.at[0]), pltpu.make_async_copy(next_ref, kept_ref, sems.at[1])]
+    for copy in copies:
+        copy.start()
+    total_of(0, part_ref.shape[0], ids_ref, landed_ref, total)
+    for copy in copies:
+        copy.wait()
     out_ref[...] = (held[...].astype(F32) + total[...]).astype(BF16)
+
+
+def lower_kernel(plan, ids_ref, landed_ref, part_ref, out_ref, total):
+    rows = part_ref.shape[0]
+    total_of(rows, rows, ids_ref, landed_ref, total)
+    out_ref[...] = (part_ref[...].astype(F32) + total[...]).astype(BF16)
 
 
 def join_kernel(plan, *refs):
@@ -375,7 +386,7 @@
         run(serve_kernel, plan),
         [sds((owners, 4 * (plan.main + plan.tail), width // 4), BF16)],
         [VMEM, HBM],
-        2 * plan.rows * stored * width,
+        8 << 30,
         2 * stored * width + 2 * plan.rows * width,
         "serve",
         scratch=[
@@ -427,20 +438,28 @@
     ids = jnp.swapaxes(stack[order], 0, 1).reshape(1, owners * reps * plan.pad)
     landed = landed.reshape(owners * reps * plan.pad, piece)
     half = stored // 2
-    quarters = [
-        call(
-            run(apply_kernel, plan, h * half),
-            [sds((half, piece), BF16)],
-            [VMEM] * 2 + [HBM],
-            4 << 30,
-            1 << 20,
-            "apply",
-            scratch=[pltpu.VMEM((half, piece), BF16), pltpu.VMEM((half, piece), F32), pltpu.SemaphoreType.DMA],
-            limit=16,
-        )(ids, landed, *far([part[h]]))[0]
-        for h in range(2)
-    ]
-    upper, lower = spread(quarters, reps)
+    sums = pltpu.VMEM((half, piece), F32)
+    first, kept = call(
+        run(upper_kernel, plan),
+        [sds((half, piece), BF16)] * 2,
+        [VMEM] * 2 + [HBM] * 2,
+        4 << 30,
+        1 << 20,
+        "upper",
+        scratch=[pltpu.VMEM((half, piece), BF16), sums, pltpu.SemaphoreType.DMA((2,))],
+        limit=16,
+    )(ids, landed, *far(part))
+    second = call(
+        run(lower_kernel, plan),
+        [sds((half, piece), BF16)],
+        [VMEM] * 3,
+        4 << 30,
+        1 << 20,
+        "lower",
+        scratch=[sums],
+        limit=16,
+    )(ids, landed, kept)[0]
+    upper, lower = spread([first, second], reps)
     new_memory = call(
         run(join_kernel, plan),
         [sds((stored, width), BF16)],

time: 76.5 us -> 80.5 us (1.052)
  waiting for transfers between devices: 24.1 us -> 27 us
  starting transfers between devices: 27.2 us -> 28.9 us
    ppermute x24, waiting for transfers between devices: 12 us -> 21.3 us  [swap(): return lax.ppermute(x, 'rep', [(i, i ^ bit) for i in range(reps)])]
    all_to_all x1, waiting for transfers between devices: 4.67 us -> 0.01 us  [shards(): lax.all_to_all(served, 'shard', split_axis=0, concat_axis=0, tiled=True)]
    all_to_all x1, starting transfers between devices: 3.62 us -> 5.74 us  [shards(): lax.all_to_all(outgoing, ('shard', 'rep'), split_axis=0, concat_axis=0, t...]
    all_to_all x1, waiting for transfers between devices: 4.39 us -> 2.64 us  [shards(): lax.all_to_all(request, 'shard', split_axis=0, concat_axis=0, tiled=True)]
    ppermute x24, starting transfers between devices: 13.6 us -> 12.2 us  [swap(): return lax.ppermute(x, 'rep', [(i, i ^ bit) for i in range(reps)])]
    all_to_all x1, starting transfers between devices: 6.34 us -> 7.28 us  [shards(): lax.all_to_all(request, 'shard', split_axis=0, concat_axis=0, tiled=True)]
  transfers between devices with their start and end apart: 27 -> 27, of which waited for: 12 -> 11; matrix products, arithmetic and copies ran while one was open for 1% -> 1% of each run, Pallas kernels for 20% -> 18%
where the time goes in v11:
time: 80.5 us; the launch traced here: 80.1 us
  starting transfers between devices  28.9 us (36%)
  waiting for transfers between devices  27 us (34%)
  Pallas kernels  18.3 us (23%)
  local copies, waits for them, and re-layouts  4.86 us (6%)
  between operations  0.95 us (1%)
    ppermute x24, waiting for transfers between devices, swap(): return lax.ppermute(x, 'rep', [(i, i ^ bit) for i in range(reps)])  21.3 us
    ppermute x24, starting transfers between devices, swap(): return lax.ppermute(x, 'rep', [(i, i ^ bit) for i in range(reps)])  12.2 us
    all_to_all x1, starting transfers between devices, shards(): lax.all_to_all(request, 'shard', split_axis=0, concat_axis=0, tiled=True)  7.28 us
    pallas_call x1, Pallas kernels, shards(): call(run(gru_kernel, plan), [sds((owners * reps, plan.pad, piece), BF16),...  5.83 us
    all_to_all x1, starting transfers between devices, shards(): lax.all_to_all(outgoing, ('shard', 'rep'), split_axis=0, concat_axis=0, t...  5.74 us
    unnamed x45, local copies, waits for them, and re-layouts  4.2 us
    pallas_call x1, Pallas kernels, shards(): call(run(attend_kernel, plan), [sds((events, width), BF16)] + [sds((store...  4.09 us
    all_to_all x1, starting transfers between devices, shards(): lax.all_to_all(served, 'shard', split_axis=0, concat_axis=0, tiled=True)  3.68 us
  transfers between devices with their start and end apart: 27, of which 11 were waited for; matrix products, arithmetic and copies ran while one was open for 1% of the time, Pallas kernels for 18%

profile of v11, /device:TPU:0, one launch (start us, length us, event | category | flops | bytes accessed | tf_op | source)
XLA Modules:
  0.0 80.1 jit_solution(16360252715226170975)
XLA Ops:
  0.6 0.7 copy-done.4
  1.3 1.0 %request.1 = s32[8,128]{1,0:T(8,128)} custom-call(s32[1,256]{1,0:T(1,128)S(1)} %bitcast.27, s32[1,256]{1,0:T(1,128)S(1)} %bitcast.26), custom_call_target="tpu_custom_call" | custom-call | flops 1048576 | bytes 16384 | tf_op jit(solution)/shard_map/request/pallas_call | solution.py:357
  2.3 7.3 %all-to-all-start = ((s32[8,1,128]{2,1,0:T(1,128)}), s32[8,1,128]{2,1,0:T(1,128)S(1)}, u32[]{:S(2)}, u32[]{:S(2)}) async-start(s32[8,1,128]{2,1,0:T(1,128)} %bitcast.3), calls=%async_computation | async-start | bytes 8192 | tf_op jit(solution)/shard_map/all_to_all | solution.py:368
  9.6 1.5 %collective-permute-start.1 = (bf16[512,384]{1,0:T(8,128)(2,1)}, bf16[512,384]{1,0:T(8,128)(2,1)S(1)}, u32[]{:S(2)}, u32[]{:S(2)}) collective-permute-start(bf16[512,384]{1,0:T(8,128)(2,1)} %refs_0_), channel_id=1, source_target_pairs={{0,2},{1,3},{2,0},{3,1},{4,6},{5,7},{6,4},{7,5},{8,10},{9,11},{10,... | collective-permute-start | bytes 1179656 | tf_op jit(solution)/shard_map/ppermute | solution.py:315
  11.8 1.5 %collective-permute-start.7 = (bf16[128,384]{1,0:T(8,128)(2,1)}, bf16[128,384]{1,0:T(8,128)(2,1)S(1)}, u32[]{:S(2)}, u32[]{:S(2)}) collective-permute-start(bf16[128,384]{1,0:T(8,128)(2,1)} %refs_8_), channel_id=1, source_target_pairs={{0,2},{1,3},{2,0},{3,1},{4,6},{5,7},{6,4},{7,5},{8,10},{9,11},{10,... | collective-permute-start | bytes 294920 | tf_op jit(solution)/shard_map/ppermute | solution.py:315
  13.3 2.6 %all-to-all-done = s32[8,1,128]{2,1,0:T(1,128)S(1)} async-done(((s32[8,1,128]{2,1,0:T(1,128)}), s32[8,1,128]{2,1,0:T(1,128)S(1)}, u32[]{:S(2)}, u32[]{:S(2)}) %all-to-all-start) | async-done | bytes 4128 | tf_op jit(solution)/shard_map/all_to_all | solution.py:368
  16.0 2.9 %serve.1 = bf16[8,264,128]{2,1,0:T(8,128)(2,1)} custom-call(s32[8,128]{1,0:T(8,128)S(1)} %bitcast.22, bf16[1024,512]{1,0:T(8,128)(2,1)} %memory_ref.3), custom_call_target="tpu_custom_call" | custom-call | flops 8589934592 | bytes 1589248 | tf_op jit(solution)/shard_map/serve/pallas_call | solution.py:385
  18.9 3.7 %all-to-all-start.1 = ((bf16[8,264,128]{2,1,0:T(8,128)(2,1)}), bf16[8,264,128]{2,1,0:T(8,128)(2,1)S(1)}, u32[]{:S(2)}, u32[]{:S(2)}) async-start(bf16[8,264,128]{2,1,0:T(8,128)(2,1)} %serve.1), calls=%async_computation.1 | async-start | bytes 1081344 | tf_op jit(solution)/shard_map/all_to_all | solution.py:399
  22.7 8.2 %collective-permute-done.7.refs_10_ = bf16[128,384]{1,0:T(8,128)(2,1)S(1)} collective-permute-done((bf16[128,384]{1,0:T(8,128)(2,1)}, bf16[128,384]{1,0:T(8,128)(2,1)S(1)}, u32[]{:S(2)}, u32[]{:S(2)}) %collective-permute-start.7) | collective-permute-done | bytes 98336 | tf_op jit(solution)/shard_map/ppermute | solution.py:315
  31.5 0.7 copy-done.7
  32.2 1.2 %index.1 = (bf16[384,128]{1,0:T(8,128)(2,1)S(1)}, f32[384,8]{1,0:T(8,128)S(1)}, s32[8,384]{1,0:T(8,128)S(1)}) custom-call(s32[1,256]{1,0:T(1,128)S(1)} %bitcast.28, s32[1,1408]{1,0:T(1,128)S(1)} %reshape.45.packed_ref, f32[1,128]{1,0:T(1,128)S(1)} %bitcast.29, f32[1,128]{1,0:T(1,128)S(1)} %bitcast.30), custom_call_target="tpu_custom_call" | custom-call | flops 8589934592 | bytes 262144 | tf_op jit(solution)/shard_map/index/pallas_call | solution.py:369
  33.5 0.6 copy-done.9
  34.1 0.7 copy-done.13
  35.3 1.1 %collective-permute-done.8.refs_11_ = bf16[128,384]{1,0:T(8,128)(2,1)} collective-permute-done((bf16[128,384]{1,0:T(8,128)(2,1)S(1)}, bf16[128,384]{1,0:T(8,128)(2,1)}, u32[]{:S(2)}, u32[]{:S(2)}) %collective-permute-start.8) | collective-permute-done | bytes 98336 | tf_op jit(solution)/shard_map/ppermute | solution.py:315
  36.4 1.5 %collective-permute-start.13 = (bf16[512,256]{1,0:T(8,128)(2,1)S(1)}, bf16[512,256]{1,0:T(8,128)(2,1)S(1)}, u32[]{:S(2)}, u32[]{:S(2)}) collective-permute-start(bf16[512,256]{1,0:T(8,128)(2,1)S(1)} %copy-done.1), channel_id=1, source_target_pairs={{0,2},{1,3},{2,0},{3,1},{4,6},{5,7},{6,4},{7,5},{8,10},{9,11},{10,... | collective-permute-start | bytes 786440 | tf_op jit(solution)/shard_map/ppermute | solution.py:315
  38.8 5.8 %gru.1 = (bf16[32,72,128]{2,1,0:T(8,128)(2,1)}, f32[384,512]{1,0:T(8,128)S(1)}, bf16[384,512]{1,0:T(8,128)(2,1)S(1)}) custom-call(bf16[8,264,128]{2,1,0:T(8,128)(2,1)S(1)} %all-to-all-done.1.ret_ref, s32[8,384]{1,0:T(8,128)S(1)} %get-tuple-element.20.row_ref, f32[384,8]{1,0:T(8,128)S(1)} %get-tuple-element.21.col_ref, bf16[384,128]{1,0:T(8,128)(2,1)} %copy-done.9, ...), custom_call_target="tpu_custom_call" | custom-call | flops 1207959552 | bytes 8388608 | tf_op jit(solution)/shard_map/gru/pallas_call | solution.py:401
  44.7 5.7 %all-to-all-start.2 = ((bf16[32,72,128]{2,1,0:T(8,128)(2,1)}), bf16[32,72,128]{2,1,0:T(8,128)(2,1)S(1)}, u32[]{:S(2)}, u32[]{:S(2)}) async-start(bf16[32,72,128]{2,1,0:T(8,128)(2,1)} %get-tuple-element.31), calls=%async_computation.2 | async-start | bytes 1179648 | tf_op jit(solution)/shard_map/all_to_all | solution.py:419
  50.4 1.8 %collective-permute-start.16 = (s32[8,128]{1,0:T(8,128)S(1)}, s32[8,128]{1,0:T(8,128)S(1)}, u32[]{:S(2)}, u32[]{:S(2)}) collective-permute-start(s32[8,128]{1,0:T(8,128)S(1)} %bitcast.23), channel_id=1, source_target_pairs={{0,2},{1,3},{2,0},{3,1},{4,6},{5,7},{6,4},{7,5},{8,10},{9,11},{10,... | collective-permute-start | bytes 12296 | tf_op jit(solution)/shard_map/ppermute | solution.py:315
  52.2 3.1 %collective-permute-done.16 = s32[8,128]{1,0:T(8,128)S(1)} collective-permute-done((s32[8,128]{1,0:T(8,128)S(1)}, s32[8,128]{1,0:T(8,128)S(1)}, u32[]{:S(2)}, u32[]{:S(2)}) %collective-permute-start.16) | collective-permute-done | bytes 4128 | tf_op jit(solution)/shard_map/ppermute | solution.py:315
  55.3 1.2 %collective-permute-done.15 = s32[8,128]{1,0:T(8,128)S(1)} collective-permute-done((s32[8,128]{1,0:T(8,128)S(1)}, s32[8,128]{1,0:T(8,128)S(1)}, u32[]{:S(2)}, u32[]{:S(2)}) %collective-permute-start.15) | collective-permute-done | bytes 4128 | tf_op jit(solution)/shard_map/ppermute | solution.py:315
  58.7 4.1 %attend.1 = (bf16[384,512]{1,0:T(8,128)(2,1)}, bf16[512,128]{1,0:T(8,128)(2,1)S(1)}, bf16[512,128]{1,0:T(8,128)(2,1)S(1)}) custom-call(s32[3,2]{1,0:T(4,128)S(1)} %copy.20.listed_ref, f32[384,512]{1,0:T(8,128)S(1)} %get-tuple-element.26.hnew_ref, bf16[384,512]{1,0:T(8,128)(2,1)S(1)} %get-tuple-element.27.hdst_ref, bf16[1024,512]{1,0:T(8,128)(2,1)S(1)} %copy-done, ...), custom_call_target="tpu_custom_call" | custom-call | flops 603979776 | bytes 4194304 | tf_op jit(solution)/shard_map/attend/pallas_call | solution.py:421
  62.8 0.7 copy-done.5
  63.4 0.6 copy-done.6
  64.1 3.1 %all-to-all-done.2 = bf16[32,72,128]{2,1,0:T(8,128)(2,1)S(1)} async-done(((bf16[32,72,128]{2,1,0:T(8,128)(2,1)}), bf16[32,72,128]{2,1,0:T(8,128)(2,1)S(1)}, u32[]{:S(2)}, u32[]{:S(2)}) %all-to-all-start.2) | async-done | bytes 589856 | tf_op jit(solution)/shard_map/all_to_all | solution.py:419
  67.1 1.5 %upper.1 = (bf16[512,128]{1,0:T(8,128)(2,1)S(1)}, bf16[512,128]{1,0:T(8,128)(2,1)S(1)}) custom-call(s32[1,2304]{1,0:T(1,128)S(1)} %reshape.48.ids_ref, bf16[2304,128]{1,0:T(8,128)(2,1)S(1)} %bitcast.20, bf16[512,128]{1,0:T(8,128)(2,1)} %copy-done.5, bf16[512,128]{1,0:T(8,128)(2,1)} %copy-done.6), custom_call_target="tpu_custom_call" | custom-call | flops 4294967296 | bytes 1048576 | tf_op jit(solution)/shard_map/upper/pallas_call | solution.py:442
  68.7 0.8 lower.1.refs_4_
  69.4 1.2 %collective-permute-start.22 = (bf16[512,128]{1,0:T(8,128)(2,1)S(1)}, bf16[512,128]{1,0:T(8,128)(2,1)S(1)}, u32[]{:S(2)}, u32[]{:S(2)}) collective-permute-start(bf16[512,128]{1,0:T(8,128)(2,1)S(1)} %lower.1.refs_4_), channel_id=1, source_target_pairs={{0,2},{1,3},{2,0},{3,1},{4,6},{5,7},{6,4},{7,5},{8,10},{9,11},{10,... | collective-permute-start | bytes 393224 | tf_op jit(solution)/shard_map/ppermute | solution.py:315
  70.7 0.9 %collective-permute-start.19 = (bf16[512,128]{1,0:T(8,128)(2,1)S(1)}, bf16[512,128]{1,0:T(8,128)(2,1)S(1)}, u32[]{:S(2)}, u32[]{:S(2)}) collective-permute-start(bf16[512,128]{1,0:T(8,128)(2,1)S(1)} %get-tuple-element.34.refs_0_), channel_id=1, source_target_pairs={{0,2},{1,3},{2,0},{3,1},{4,6},{5,7},{6,4},{7,5},{8,10},{9,11},{10,... | collective-permute-start | bytes 393224 | tf_op jit(solution)/shard_map/ppermute | solution.py:315
  72.0 3.8 %collective-permute-done.22.refs_6_ = bf16[512,128]{1,0:T(8,128)(2,1)S(1)} collective-permute-done((bf16[512,128]{1,0:T(8,128)(2,1)S(1)}, bf16[512,128]{1,0:T(8,128)(2,1)S(1)}, u32[]{:S(2)}, u32[]{:S(2)}) %collective-permute-start.22) | collective-permute-done | bytes 131104 | tf_op jit(solution)/shard_map/ppermute | solution.py:315
  75.9 1.8 %collective-permute-done.19.refs_2_ = bf16[512,128]{1,0:T(8,128)(2,1)S(1)} collective-permute-done((bf16[512,128]{1,0:T(8,128)(2,1)S(1)}, bf16[512,128]{1,0:T(8,128)(2,1)S(1)}, u32[]{:S(2)}, u32[]{:S(2)}) %collective-permute-start.19) | collective-permute-done | bytes 131104 | tf_op jit(solution)/shard_map/ppermute | solution.py:315
  77.7 1.3 %collective-permute-done.20.refs_3_ = bf16[512,128]{1,0:T(8,128)(2,1)S(1)} collective-permute-done((bf16[512,128]{1,0:T(8,128)(2,1)S(1)}, bf16[512,128]{1,0:T(8,128)(2,1)S(1)}, u32[]{:S(2)}, u32[]{:S(2)}) %collective-permute-start.20) | collective-permute-done | bytes 131104 | tf_op jit(solution)/shard_map/ppermute | solution.py:315
  79.1 1.0 %join.1 = bf16[1024,512]{1,0:T(8,128)(2,1)} custom-call(bf16[512,128]{1,0:T(8,128)(2,1)S(1)} %get-tuple-element.34.refs_0_, bf16[512,128]{1,0:T(8,128)(2,1)S(1)} %collective-permute-done.18.refs_1_, bf16[512,128]{1,0:T(8,128)(2,1)S(1)} %collective-permute-done.19.refs_2_, bf16[512,128]{1,0:T(8,128)(2,1)S(1)} %collective-permute-done.20.refs_3_, ...), custom_call_target="tpu_custom_call" | custom-call | flops 1048576 | bytes 2097152 | tf_op jit(solution)/shard_map/join/pallas_call | solution.py:463
  (87 shorter events, 5.5 us)
Async XLA Ops:
  2.3 13.7 %all-to-all-start = ((s32[8,1,128]{2,1,0:T(1,128)}), s32[8,1,128]{2,1,0:T(1,128)S(1)}, u32[]{:S(2)}, u32[]{:S(2)}) async-start(s32[8,1,128]{2,1,0:T(1,128)} %bitcast.3), calls=%async_computation | async-start | bytes 8192 | tf_op jit(solution)/shard_map/all_to_all | solution.py:368
  9.6 21.3 %collective-permute-start.1 = (bf16[512,384]{1,0:T(8,128)(2,1)}, bf16[512,384]{1,0:T(8,128)(2,1)S(1)}, u32[]{:S(2)}, u32[]{:S(2)}) collective-permute-start(bf16[512,384]{1,0:T(8,128)(2,1)} %refs_0_), channel_id=1, source_target_pairs={{0,2},{1,3},{2,0},{3,1},{4,6},{5,7},{6,4},{7,5},{8,10},{9,11},{10,... | collective-permute-start | bytes 1179656 | tf_op jit(solution)/shard_map/ppermute | solution.py:315
  11.1 26.9 %collective-permute-start = (bf16[512,384]{1,0:T(8,128)(2,1)}, bf16[512,384]{1,0:T(8,128)(2,1)S(1)}, u32[]{:S(2)}, u32[]{:S(2)}) collective-permute-start(bf16[512,384]{1,0:T(8,128)(2,1)} %refs_0_), channel_id=1, source_target_pairs={{0,1},{1,0},{2,3},{3,2},{4,5},{5,4},{6,7},{7,6},{8,9},{9,8},{10,11... | collective-permute-start | bytes 1179656 | tf_op jit(solution)/shard_map/ppermute | solution.py:315
  11.1 20.3 %collective-permute-start.4 = (bf16[512,384]{1,0:T(8,128)(2,1)}, bf16[512,384]{1,0:T(8,128)(2,1)S(1)}, u32[]{:S(2)}, u32[]{:S(2)}) collective-permute-start(bf16[512,384]{1,0:T(8,128)(2,1)} %refs_4_), channel_id=1, source_target_pairs={{0,2},{1,3},{2,0},{3,1},{4,6},{5,7},{6,4},{7,5},{8,10},{9,11},{10,... | collective-permute-start | bytes 1179656 | tf_op jit(solution)/shard_map/ppermute | solution.py:315
  11.6 26.4 %collective-permute-start.3 = (bf16[512,384]{1,0:T(8,128)(2,1)}, bf16[512,384]{1,0:T(8,128)(2,1)S(1)}, u32[]{:S(2)}, u32[]{:S(2)}) collective-permute-start(bf16[512,384]{1,0:T(8,128)(2,1)} %refs_4_), channel_id=1, source_target_pairs={{0,1},{1,0},{2,3},{3,2},{4,5},{5,4},{6,7},{7,6},{8,9},{9,8},{10,11... | collective-permute-start | bytes 1179656 | tf_op jit(solution)/shard_map/ppermute | solution.py:315
  11.8 19.1 %collective-permute-start.7 = (bf16[128,384]{1,0:T(8,128)(2,1)}, bf16[128,384]{1,0:T(8,128)(2,1)S(1)}, u32[]{:S(2)}, u32[]{:S(2)}) collective-permute-start(bf16[128,384]{1,0:T(8,128)(2,1)} %refs_8_), channel_id=1, source_target_pairs={{0,2},{1,3},{2,0},{3,1},{4,6},{5,7},{6,4},{7,5},{8,10},{9,11},{10,... | collective-permute-start | bytes 294920 | tf_op jit(solution)/shard_map/ppermute | solution.py:315
  18.9 12.0 %copy-start.19 = (bf16[128,384]{1,0:T(8,128)(2,1)S(1)}, bf16[128,384]{1,0:T(8,128)(2,1)}, u32[]{:S(2)}) copy-start(bf16[128,384]{1,0:T(8,128)(2,1)} %refs_8_) | copy-start | bytes 294916
  18.9 19.9 %all-to-all-start.1 = ((bf16[8,264,128]{2,1,0:T(8,128)(2,1)}), bf16[8,264,128]{2,1,0:T(8,128)(2,1)S(1)}, u32[]{:S(2)}, u32[]{:S(2)}) async-start(bf16[8,264,128]{2,1,0:T(8,128)(2,1)} %serve.1), calls=%async_computation.1 | async-start | bytes 1081344 | tf_op jit(solution)/shard_map/all_to_all | solution.py:399
  30.9 4.0 %copy-start.20 = (bf16[128,384]{1,0:T(8,128)(2,1)}, bf16[128,384]{1,0:T(8,128)(2,1)S(1)}, u32[]{:S(2)}) copy-start(bf16[128,384]{1,0:T(8,128)(2,1)S(1)} %collective-permute-done.7.refs_10_) | copy-start | bytes 294916
  30.9 4.0 %collective-permute-start.6 = (bf16[128,384]{1,0:T(8,128)(2,1)S(1)}, bf16[128,384]{1,0:T(8,128)(2,1)S(1)}, u32[]{:S(2)}, u32[]{:S(2)}) collective-permute-start(bf16[128,384]{1,0:T(8,128)(2,1)S(1)} %copy-done.19), channel_id=1, source_target_pairs={{0,1},{1,0},{2,3},{3,2},{4,5},{5,4},{6,7},{7,6},{8,9},{9,8},{10,11... | collective-permute-start | bytes 294920 | tf_op jit(solution)/shard_map/ppermute | solution.py:315
  30.9 7.7 %collective-permute-start.2 = (bf16[512,384]{1,0:T(8,128)(2,1)S(1)}, bf16[512,384]{1,0:T(8,128)(2,1)}, u32[]{:S(2)}, u32[]{:S(2)}) collective-permute-start(bf16[512,384]{1,0:T(8,128)(2,1)S(1)} %collective-permute-done.1.refs_2_), channel_id=1, source_target_pairs={{0,1},{1,0},{2,3},{3,2},{4,5},{5,4},{6,7},{7,6},{8,9},{9,8},{10,11... | collective-permute-start | bytes 1179656 | tf_op jit(solution)/shard_map/ppermute | solution.py:315
  31.4 7.4 %collective-permute-start.5 = (bf16[512,384]{1,0:T(8,128)(2,1)S(1)}, bf16[512,384]{1,0:T(8,128)(2,1)}, u32[]{:S(2)}, u32[]{:S(2)}) collective-permute-start(bf16[512,384]{1,0:T(8,128)(2,1)S(1)} %collective-permute-done.4.refs_6_), channel_id=1, source_target_pairs={{0,1},{1,0},{2,3},{3,2},{4,5},{5,4},{6,7},{7,6},{8,9},{9,8},{10,11... | collective-permute-start | bytes 1179656 | tf_op jit(solution)/shard_map/ppermute | solution.py:315
  32.2 4.2 %copy-start.1 = (bf16[512,256]{1,0:T(8,128)(2,1)S(1)}, bf16[512,256]{1,0:T(8,128)(2,1)}, u32[]{:S(2)}) copy-start(bf16[512,256]{1,0:T(8,128)(2,1)} %refs_4_.1) | copy-start | bytes 786436
  32.2 5.8 %copy-start.2 = (bf16[512,128]{1,0:T(8,128)(2,1)S(1)}, bf16[512,128]{1,0:T(8,128)(2,1)}, u32[]{:S(2)}) copy-start(bf16[512,128]{1,0:T(8,128)(2,1)} %refs_0_.1) | copy-start | bytes 393220
  34.9 1.5 %collective-permute-start.8 = (bf16[128,384]{1,0:T(8,128)(2,1)S(1)}, bf16[128,384]{1,0:T(8,128)(2,1)}, u32[]{:S(2)}, u32[]{:S(2)}) collective-permute-start(bf16[128,384]{1,0:T(8,128)(2,1)S(1)} %collective-permute-done.7.refs_10_), channel_id=1, source_target_pairs={{0,1},{1,0},{2,3},{3,2},{4,5},{5,4},{6,7},{7,6},{8,9},{9,8},{10,11... | collective-permute-start | bytes 294920 | tf_op jit(solution)/shard_map/ppermute | solution.py:315
  36.4 20.6 %collective-permute-start.13 = (bf16[512,256]{1,0:T(8,128)(2,1)S(1)}, bf16[512,256]{1,0:T(8,128)(2,1)S(1)}, u32[]{:S(2)}, u32[]{:S(2)}) collective-permute-start(bf16[512,256]{1,0:T(8,128)(2,1)S(1)} %copy-done.1), channel_id=1, source_target_pairs={{0,2},{1,3},{2,0},{3,1},{4,6},{5,7},{6,4},{7,5},{8,10},{9,11},{10,... | collective-permute-start | bytes 786440 | tf_op jit(solution)/shard_map/ppermute | solution.py:315
  37.9 20.4 %collective-permute-start.12 = (bf16[512,256]{1,0:T(8,128)(2,1)S(1)}, bf16[512,256]{1,0:T(8,128)(2,1)}, u32[]{:S(2)}, u32[]{:S(2)}) collective-permute-start(bf16[512,256]{1,0:T(8,128)(2,1)S(1)} %copy-done.1), channel_id=1, source_target_pairs={{0,1},{1,0},{2,3},{3,2},{4,5},{5,4},{6,7},{7,6},{8,9},{9,8},{10,11... | collective-permute-start | bytes 786440 | tf_op jit(solution)/shard_map/ppermute | solution.py:315
  38.0 18.7 %collective-permute-start.10 = (bf16[512,128]{1,0:T(8,128)(2,1)S(1)}, bf16[512,128]{1,0:T(8,128)(2,1)}, u32[]{:S(2)}, u32[]{:S(2)}) collective-permute-start(bf16[512,128]{1,0:T(8,128)(2,1)S(1)} %copy-done.2), channel_id=1, source_target_pairs={{0,2},{1,3},{2,0},{3,1},{4,6},{5,7},{6,4},{7,5},{8,10},{9,11},{10,... | collective-permute-start | bytes 393224 | tf_op jit(solution)/shard_map/ppermute | solution.py:315
  38.6 19.7 %collective-permute-start.9 = (bf16[512,128]{1,0:T(8,128)(2,1)S(1)}, bf16[512,128]{1,0:T(8,128)(2,1)}, u32[]{:S(2)}, u32[]{:S(2)}) collective-permute-start(bf16[512,128]{1,0:T(8,128)(2,1)S(1)} %copy-done.2), channel_id=1, source_target_pairs={{0,1},{1,0},{2,3},{3,2},{4,5},{5,4},{6,7},{7,6},{8,9},{9,8},{10,11... | collective-permute-start | bytes 393224 | tf_op jit(solution)/shard_map/ppermute | solution.py:315
  44.6 14.0 %copy-start = (bf16[1024,512]{1,0:T(8,128)(2,1)S(1)}, bf16[1024,512]{1,0:T(8,128)(2,1)}, u32[]{:S(2)}) copy-start(bf16[1024,512]{1,0:T(8,128)(2,1)} %memory_ref.3) | copy-start | bytes 3145732
  44.7 22.5 %all-to-all-start.2 = ((bf16[32,72,128]{2,1,0:T(8,128)(2,1)}), bf16[32,72,128]{2,1,0:T(8,128)(2,1)S(1)}, u32[]{:S(2)}, u32[]{:S(2)}) async-start(bf16[32,72,128]{2,1,0:T(8,128)(2,1)} %get-tuple-element.31), calls=%async_computation.2 | async-start | bytes 1179648 | tf_op jit(solution)/shard_map/all_to_all | solution.py:419
  50.4 4.9 %collective-permute-start.16 = (s32[8,128]{1,0:T(8,128)S(1)}, s32[8,128]{1,0:T(8,128)S(1)}, u32[]{:S(2)}, u32[]{:S(2)}) collective-permute-start(s32[8,128]{1,0:T(8,128)S(1)} %bitcast.23), channel_id=1, source_target_pairs={{0,2},{1,3},{2,0},{3,1},{4,6},{5,7},{6,4},{7,5},{8,10},{9,11},{10,... | collective-permute-start | bytes 12296 | tf_op jit(solution)/shard_map/ppermute | solution.py:315
  55.3 1.2 %collective-permute-start.15 = (s32[8,128]{1,0:T(8,128)S(1)}, s32[8,128]{1,0:T(8,128)S(1)}, u32[]{:S(2)}, u32[]{:S(2)}) collective-permute-start(s32[8,128]{1,0:T(8,128)S(1)} %bitcast.25), channel_id=1, source_target_pairs={{0,1},{1,0},{2,3},{3,2},{4,5},{5,4},{6,7},{7,6},{8,9},{9,8},{10,11... | collective-permute-start | bytes 12296 | tf_op jit(solution)/shard_map/ppermute | solution.py:315
  56.5 1.2 %collective-permute-start.17 = (s32[8,128]{1,0:T(8,128)S(1)}, s32[8,128]{1,0:T(8,128)S(1)}, u32[]{:S(2)}, u32[]{:S(2)}) collective-permute-start(s32[8,128]{1,0:T(8,128)S(1)} %collective-permute-done.16), channel_id=1, source_target_pairs={{0,1},{1,0},{2,3},{3,2},{4,5},{5,4},{6,7},{7,6},{8,9},{9,8},{10,11... | collective-permute-start | bytes 12296 | tf_op jit(solution)/shard_map/ppermute | solution.py:315
  56.7 1.7 %collective-permute-start.11 = (bf16[512,128]{1,0:T(8,128)(2,1)}, bf16[512,128]{1,0:T(8,128)(2,1)}, u32[]{:S(2)}, u32[]{:S(2)}) collective-permute-start(bf16[512,128]{1,0:T(8,128)(2,1)} %collective-permute-done.10.refs_2_), channel_id=1, source_target_pairs={{0,1},{1,0},{2,3},{3,2},{4,5},{5,4},{6,7},{7,6},{8,9},{9,8},{10,11... | collective-permute-start | bytes 393224 | tf_op jit(solution)/shard_map/ppermute | solution.py:315
  57.0 1.7 %collective-permute-start.14 = (bf16[512,256]{1,0:T(8,128)(2,1)S(1)}, bf16[512,256]{1,0:T(8,128)(2,1)}, u32[]{:S(2)}, u32[]{:S(2)}) collective-permute-start(bf16[512,256]{1,0:T(8,128)(2,1)S(1)} %collective-permute-done.13.refs_6_), channel_id=1, source_target_pairs={{0,1},{1,0},{2,3},{3,2},{4,5},{5,4},{6,7},{7,6},{8,9},{9,8},{10,11... | collective-permute-start | bytes 786440 | tf_op jit(solution)/shard_map/ppermute | solution.py:315
  69.4 6.4 %collective-permute-start.22 = (bf16[512,128]{1,0:T(8,128)(2,1)S(1)}, bf16[512,128]{1,0:T(8,128)(2,1)S(1)}, u32[]{:S(2)}, u32[]{:S(2)}) collective-permute-start(bf16[512,128]{1,0:T(8,128)(2,1)S(1)} %lower.1.refs_4_), channel_id=1, source_target_pairs={{0,2},{1,3},{2,0},{3,1},{4,6},{5,7},{6,4},{7,5},{8,10},{9,11},{10,... | collective-permute-start | bytes 393224 | tf_op jit(solution)/shard_map/ppermute | solution.py:315
  70.7 7.1 %collective-permute-start.19 = (bf16[512,128]{1,0:T(8,128)(2,1)S(1)}, bf16[512,128]{1,0:T(8,128)(2,1)S(1)}, u32[]{:S(2)}, u32[]{:S(2)}) collective-permute-start(bf16[512,128]{1,0:T(8,128)(2,1)S(1)} %get-tuple-element.34.refs_0_), channel_id=1, source_target_pairs={{0,2},{1,3},{2,0},{3,1},{4,6},{5,7},{6,4},{7,5},{8,10},{9,11},{10,... | collective-permute-start | bytes 393224 | tf_op jit(solution)/shard_map/ppermute | solution.py:315
  71.5 6.2 %collective-permute-start.21 = (bf16[512,128]{1,0:T(8,128)(2,1)S(1)}, bf16[512,128]{1,0:T(8,128)(2,1)S(1)}, u32[]{:S(2)}, u32[]{:S(2)}) collective-permute-start(bf16[512,128]{1,0:T(8,128)(2,1)S(1)} %lower.1.refs_4_), channel_id=1, source_target_pairs={{0,1},{1,0},{2,3},{3,2},{4,5},{5,4},{6,7},{7,6},{8,9},{9,8},{10,11... | collective-permute-start | bytes 393224 | tf_op jit(solution)/shard_map/ppermute | solution.py:315
  71.5 6.2 %collective-permute-start.18 = (bf16[512,128]{1,0:T(8,128)(2,1)S(1)}, bf16[512,128]{1,0:T(8,128)(2,1)S(1)}, u32[]{:S(2)}, u32[]{:S(2)}) collective-permute-start(bf16[512,128]{1,0:T(8,128)(2,1)S(1)} %get-tuple-element.34.refs_0_), channel_id=1, source_target_pairs={{0,1},{1,0},{2,3},{3,2},{4,5},{5,4},{6,7},{7,6},{8,9},{9,8},{10,11... | collective-permute-start | bytes 393224 | tf_op jit(solution)/shard_map/ppermute | solution.py:315
  75.9 1.9 %collective-permute-start.23 = (bf16[512,128]{1,0:T(8,128)(2,1)S(1)}, bf16[512,128]{1,0:T(8,128)(2,1)S(1)}, u32[]{:S(2)}, u32[]{:S(2)}) collective-permute-start(bf16[512,128]{1,0:T(8,128)(2,1)S(1)} %collective-permute-done.22.refs_6_), channel_id=1, source_target_pairs={{0,1},{1,0},{2,3},{3,2},{4,5},{5,4},{6,7},{7,6},{8,9},{9,8},{10,11... | collective-permute-start | bytes 393224 | tf_op jit(solution)/shard_map/ppermute | solution.py:315
  77.7 1.3 %collective-permute-start.20 = (bf16[512,128]{1,0:T(8,128)(2,1)S(1)}, bf16[512,128]{1,0:T(8,128)(2,1)S(1)}, u32[]{:S(2)}, u32[]{:S(2)}) collective-permute-start(bf16[512,128]{1,0:T(8,128)(2,1)S(1)} %collective-permute-done.19.refs_2_), channel_id=1, source_target_pairs={{0,1},{1,0},{2,3},{3,2},{4,5},{5,4},{6,7},{7,6},{8,9},{9,8},{10,11... | collective-permute-start | bytes 393224 | tf_op jit(solution)/shard_map/ppermute | solution.py:315
  (17 other events, 30.6 us)

commit v12 on v10

--- a/solution.py
+++ b/solution.py
@@ -82,8 +82,8 @@
     out_ref[...] = (dot(high, spot) * 32.0 + dot(low, spot)).astype(I32)
 
 
-def index_kernel(plan, owner_ref, packed_ref, freq_ref, phase_ref, enc_ref, col_ref, row_ref):
-    events = enc_ref.shape[0]
+def index_kernel(plan, owner_ref, packed_ref, col_ref, row_ref):
+    events = col_ref.shape[0]
     ends = [plan.entries + i * events for i in range(4)]
     tick_row = packed_ref[:, : ends[0]]
     src_row, dst_row, stamp_row = (packed_ref[:, a : a + events] for a in ends[:3])
@@ -109,9 +109,11 @@
     zero = jnp.zeros((8 - 3, events), I32)
     rows = jnp.concatenate([src_spot, dst_spot, span, zero], axis=0)
     row_ref[...] = jnp.concatenate([src_back, jnp.zeros((7, events), I32)], axis=0)
-    cols = rows.astype(F32).T
-    col_ref[...] = cols
-    enc_ref[...] = jnp.cos(cols[:, 2:3] * freq_ref[...] + phase_ref[...]).astype(BF16)
+    col_ref[...] = rows.astype(F32).T
+
+
+def encode_kernel(col_ref, freq_ref, phase_ref, enc_ref):
+    enc_ref[...] = jnp.cos(col_ref[:, 2:3] * freq_ref[...] + phase_ref[...]).astype(BF16)
 
 
 def tail_order(plan, forward):
@@ -124,7 +126,7 @@
     return jnp.where((inner * plan.owners + owner) == here, 1.0, 0.0).astype(BF16)
 
 
-def serve_kernel(plan, asked_ref, memory_ref, out_ref, held, hot_ref, sems):
+def serve_kernel(plan, asked_ref, memory_ref, after_ref, out_ref, held, hot_ref, sems):
     stored, width = memory_ref.shape
     piece = width // 4
     step = stored // 4
@@ -355,27 +357,26 @@
     )
 
     asked = lax.all_to_all(request, "shard", split_axis=0, concat_axis=0, tiled=True)
-    encode, cols, rows = call(
+    packed = jnp.concatenate([touch_time, src_slot, dst_slot, event_time]).reshape(1, -1)
+    _, owner, packed = lax.optimization_barrier((request, owner, packed))
+    cols, rows = call(
         run(index_kernel, plan),
-        [sds((events, time_freq.shape[0]), BF16), sds((events, 8), F32), sds((8, events), I32)],
-        [VMEM] * 4,
+        [sds((events, 8), F32), sds((8, events), I32)],
+        [VMEM] * 2,
         8 << 30,
         1 << 18,
         "index",
-        limit=8,
-    )(
-        owner,
-        jnp.concatenate([touch_time, src_slot, dst_slot, event_time]).reshape(1, -1),
-        time_freq.reshape(1, -1),
-        time_phase.reshape(1, -1),
-    )
+    )(owner, packed)
+    encode = call(
+        encode_kernel, [sds((events, time_freq.shape[0]), BF16)], [VMEM] * 3, 8 << 30, 1 << 18, "encode"
+    )(cols, time_freq.reshape(1, -1), time_phase.reshape(1, -1))[0]
     everyone = [x for x in spread([asked], reps)[0]]
 
     served = call(
         run(serve_kernel, plan),
         [sds((owners, 4 * (plan.main + plan.tail), width // 4), BF16)],
-        [VMEM, HBM],
-        2 * plan.rows * stored * width,
+        [VMEM, HBM, HBM],
+        8 << 30,
         2 * stored * width + 2 * plan.rows * width,
         "serve",
         scratch=[
@@ -384,7 +385,7 @@
             pltpu.SemaphoreType.DMA((4,)),
         ],
         limit=16,
-    )(asked, *far([memory]))[0]
+    )(asked, *far([memory, cols]))[0]
     returned = lax.all_to_all(served, "shard", split_axis=0, concat_axis=0, tiled=True)
 
     outgoing, hnew, hdst = call(

time: 76.5 us -> 79.1 us (1.034)
  starting transfers between devices: 27.2 us -> 30.3 us
  waiting for transfers between devices: 24.1 us -> 22.7 us
  local copies, waits for them, and re-layouts: 4.85 us -> 5.73 us
    ppermute x24, waiting for transfers between devices: 12 us -> 18.1 us  [swap(): return lax.ppermute(x, 'rep', [(i, i ^ bit) for i in range(reps)])]
    all_to_all x1, waiting for transfers between devices: 4.67 us -> 0.01 us  [shards(): lax.all_to_all(served, 'shard', split_axis=0, concat_axis=0, tiled=True)]
    all_to_all x1, waiting for transfers between devices: 4.39 us -> 1.59 us  [shards(): lax.all_to_all(request, 'shard', split_axis=0, concat_axis=0, tiled=True)]
    all_to_all x1, starting transfers between devices: 3.62 us -> 5.73 us  [shards(): lax.all_to_all(outgoing, ('shard', 'rep'), split_axis=0, concat_axis=0, t...]
    all_to_all x1, starting transfers between devices: 6.34 us -> 7.42 us  [shards(): lax.all_to_all(request, 'shard', split_axis=0, concat_axis=0, tiled=True)]
    ppermute x24, starting transfers between devices: 13.6 us -> 12.5 us  [swap(): return lax.ppermute(x, 'rep', [(i, i ^ bit) for i in range(reps)])]
    all_to_all x1, starting transfers between devices: 3.68 us -> 4.56 us  [shards(): lax.all_to_all(served, 'shard', split_axis=0, concat_axis=0, tiled=True)]
    unnamed x45 -> x51, local copies, waits for them, and re-layouts: 4.19 us -> 5.06 us
  transfers between devices with their start and end apart: 27 -> 27, of which waited for: 12 -> 11; matrix products, arithmetic and copies ran while one was open for 1% -> 1% of each run, Pallas kernels for 20% -> 20%
where the time goes in v12:
time: 79.1 us; the launch traced here: 78.7 us
  starting transfers between devices  30.3 us (38%)
  waiting for transfers between devices  22.7 us (29%)
  Pallas kernels  19 us (24%)
  local copies, waits for them, and re-layouts  5.73 us (7%)
  between operations  0.94 us (1%)
    ppermute x24, waiting for transfers between devices, swap(): return lax.ppermute(x, 'rep', [(i, i ^ bit) for i in range(reps)])  18.1 us
    ppermute x24, starting transfers between devices, swap(): return lax.ppermute(x, 'rep', [(i, i ^ bit) for i in range(reps)])  12.5 us
    all_to_all x1, starting transfers between devices, shards(): lax.all_to_all(request, 'shard', split_axis=0, concat_axis=0, tiled=True)  7.42 us
    pallas_call x1, Pallas kernels, shards(): call(run(gru_kernel, plan), [sds((owners * reps, plan.pad, piece), BF16),...  5.84 us
    all_to_all x1, starting transfers between devices, shards(): lax.all_to_all(outgoing, ('shard', 'rep'), split_axis=0, concat_axis=0, t...  5.73 us
    unnamed x51, local copies, waits for them, and re-layouts  5.06 us
    all_to_all x1, starting transfers between devices, shards(): lax.all_to_all(served, 'shard', split_axis=0, concat_axis=0, tiled=True)  4.56 us
    pallas_call x1, Pallas kernels, shards(): call(run(attend_kernel, plan), [sds((events, width), BF16)] + [sds((store...  4.09 us
  transfers between devices with their start and end apart: 27, of which 11 were waited for; matrix products, arithmetic and copies ran while one was open for 1% of the time, Pallas kernels for 20%

profile of v12, /device:TPU:0, one launch (start us, length us, event | category | flops | bytes accessed | tf_op | source)
XLA Modules:
  0.0 78.7 jit_solution(1208614729249720081)
XLA Ops:
  0.6 0.7 copy-done.4
  1.3 1.0 %request.1 = s32[8,128]{1,0:T(8,128)} custom-call(s32[1,256]{1,0:T(1,128)S(1)} %bitcast.27, s32[1,256]{1,0:T(1,128)S(1)} %bitcast.26), custom_call_target="tpu_custom_call" | custom-call | flops 1048576 | bytes 16384 | tf_op jit(solution)/shard_map/request/pallas_call | solution.py:348
  2.3 7.4 %all-to-all-start = ((s32[8,1,128]{2,1,0:T(1,128)}), s32[8,1,128]{2,1,0:T(1,128)S(1)}, u32[]{:S(2)}, u32[]{:S(2)}) async-start(s32[8,1,128]{2,1,0:T(1,128)} %bitcast.3), calls=%async_computation | async-start | bytes 8192 | tf_op jit(solution)/shard_map/all_to_all | solution.py:359
  9.7 1.5 %collective-permute-start.1 = (bf16[512,384]{1,0:T(8,128)(2,1)}, bf16[512,384]{1,0:T(8,128)(2,1)S(1)}, u32[]{:S(2)}, u32[]{:S(2)}) collective-permute-start(bf16[512,384]{1,0:T(8,128)(2,1)} %refs_0_), channel_id=1, source_target_pairs={{0,2},{1,3},{2,0},{3,1},{4,6},{5,7},{6,4},{7,5},{8,10},{9,11},{10,... | collective-permute-start | bytes 1179656 | tf_op jit(solution)/shard_map/ppermute | solution.py:306
  11.7 1.5 %collective-permute-start.7 = (bf16[128,384]{1,0:T(8,128)(2,1)}, bf16[128,384]{1,0:T(8,128)(2,1)S(1)}, u32[]{:S(2)}, u32[]{:S(2)}) collective-permute-start(bf16[128,384]{1,0:T(8,128)(2,1)} %refs_8_), channel_id=1, source_target_pairs={{0,2},{1,3},{2,0},{3,1},{4,6},{5,7},{6,4},{7,5},{8,10},{9,11},{10,... | collective-permute-start | bytes 294920 | tf_op jit(solution)/shard_map/ppermute | solution.py:306
  13.8 0.7 copy-done.9
  14.5 1.6 %all-to-all-done = s32[8,1,128]{2,1,0:T(1,128)S(1)} async-done(((s32[8,1,128]{2,1,0:T(1,128)}), s32[8,1,128]{2,1,0:T(1,128)S(1)}, u32[]{:S(2)}, u32[]{:S(2)}) %all-to-all-start) | async-done | bytes 4128 | tf_op jit(solution)/shard_map/all_to_all | solution.py:359
  16.1 2.9 %serve.1 = bf16[8,264,128]{2,1,0:T(8,128)(2,1)} custom-call(s32[8,128]{1,0:T(8,128)S(1)} %bitcast.22, bf16[1024,512]{1,0:T(8,128)(2,1)} %memory_ref.3, f32[384,8]{1,0:T(8,128)} %copy-done.9), custom_call_target="tpu_custom_call" | custom-call | flops 8589934592 | bytes 1589248 | tf_op jit(solution)/shard_map/serve/pallas_call | solution.py:375
  19.0 4.6 %all-to-all-start.1 = ((bf16[8,264,128]{2,1,0:T(8,128)(2,1)}), bf16[8,264,128]{2,1,0:T(8,128)(2,1)S(1)}, u32[]{:S(2)}, u32[]{:S(2)}) async-start(bf16[8,264,128]{2,1,0:T(8,128)(2,1)} %serve.1), calls=%async_computation.1 | async-start | bytes 1081344 | tf_op jit(solution)/shard_map/all_to_all | solution.py:389
  24.2 6.9 %collective-permute-done.7.refs_10_ = bf16[128,384]{1,0:T(8,128)(2,1)S(1)} collective-permute-done((bf16[128,384]{1,0:T(8,128)(2,1)}, bf16[128,384]{1,0:T(8,128)(2,1)S(1)}, u32[]{:S(2)}, u32[]{:S(2)}) %collective-permute-start.7) | collective-permute-done | bytes 98336 | tf_op jit(solution)/shard_map/ppermute | solution.py:306
  31.7 0.7 copy-done.7
  32.4 0.7 encode.1.far_enc
  33.8 0.7 copy-done.15
  35.2 0.7 collective-permute-done.8.refs_11_
  35.9 1.5 %collective-permute-start.13 = (bf16[512,256]{1,0:T(8,128)(2,1)S(1)}, bf16[512,256]{1,0:T(8,128)(2,1)S(1)}, u32[]{:S(2)}, u32[]{:S(2)}) collective-permute-start(bf16[512,256]{1,0:T(8,128)(2,1)S(1)} %copy-done.1), channel_id=1, source_target_pairs={{0,2},{1,3},{2,0},{3,1},{4,6},{5,7},{6,4},{7,5},{8,10},{9,11},{10,... | collective-permute-start | bytes 786440 | tf_op jit(solution)/shard_map/ppermute | solution.py:306
  38.2 5.8 %gru.1 = (bf16[32,72,128]{2,1,0:T(8,128)(2,1)}, f32[384,512]{1,0:T(8,128)S(1)}, bf16[384,512]{1,0:T(8,128)(2,1)S(1)}) custom-call(bf16[8,264,128]{2,1,0:T(8,128)(2,1)S(1)} %all-to-all-done.1.ret_ref, s32[8,384]{1,0:T(8,128)S(1)} %get-tuple-element.22.row_ref, f32[384,8]{1,0:T(8,128)S(1)} %copy-done.10, bf16[384,128]{1,0:T(8,128)(2,1)} %copy-done.11, ...), custom_call_target="tpu_custom_call" | custom-call | flops 1207959552 | bytes 8388608 | tf_op jit(solution)/shard_map/gru/pallas_call | solution.py:391
  44.1 5.7 %all-to-all-start.2 = ((bf16[32,72,128]{2,1,0:T(8,128)(2,1)}), bf16[32,72,128]{2,1,0:T(8,128)(2,1)S(1)}, u32[]{:S(2)}, u32[]{:S(2)}) async-start(bf16[32,72,128]{2,1,0:T(8,128)(2,1)} %get-tuple-element.31), calls=%async_computation.2 | async-start | bytes 1179648 | tf_op jit(solution)/shard_map/all_to_all | solution.py:409
  49.8 1.8 %collective-permute-start.16 = (s32[8,128]{1,0:T(8,128)S(1)}, s32[8,128]{1,0:T(8,128)S(1)}, u32[]{:S(2)}, u32[]{:S(2)}) collective-permute-start(s32[8,128]{1,0:T(8,128)S(1)} %bitcast.23), channel_id=1, source_target_pairs={{0,2},{1,3},{2,0},{3,1},{4,6},{5,7},{6,4},{7,5},{8,10},{9,11},{10,... | collective-permute-start | bytes 12296 | tf_op jit(solution)/shard_map/ppermute | solution.py:306
  51.7 3.1 %collective-permute-done.16 = s32[8,128]{1,0:T(8,128)S(1)} collective-permute-done((s32[8,128]{1,0:T(8,128)S(1)}, s32[8,128]{1,0:T(8,128)S(1)}, u32[]{:S(2)}, u32[]{:S(2)}) %collective-permute-start.16) | collective-permute-done | bytes 4128 | tf_op jit(solution)/shard_map/ppermute | solution.py:306
  54.8 1.2 %collective-permute-done.15 = s32[8,128]{1,0:T(8,128)S(1)} collective-permute-done((s32[8,128]{1,0:T(8,128)S(1)}, s32[8,128]{1,0:T(8,128)S(1)}, u32[]{:S(2)}, u32[]{:S(2)}) %collective-permute-start.15) | collective-permute-done | bytes 4128 | tf_op jit(solution)/shard_map/ppermute | solution.py:306
  58.1 4.1 %attend.1 = (bf16[384,512]{1,0:T(8,128)(2,1)}, bf16[512,128]{1,0:T(8,128)(2,1)S(1)}, bf16[512,128]{1,0:T(8,128)(2,1)S(1)}) custom-call(s32[3,2]{1,0:T(4,128)S(1)} %copy.20.listed_ref, f32[384,512]{1,0:T(8,128)S(1)} %get-tuple-element.26.hnew_ref, bf16[384,512]{1,0:T(8,128)(2,1)S(1)} %get-tuple-element.27.hdst_ref, bf16[1024,512]{1,0:T(8,128)(2,1)S(1)} %copy-done, ...), custom_call_target="tpu_custom_call" | custom-call | flops 603979776 | bytes 4194304 | tf_op jit(solution)/shard_map/attend/pallas_call | solution.py:411
  62.2 0.6 copy-done.5
  62.9 0.6 copy-done.6
  63.5 3.1 %all-to-all-done.2 = bf16[32,72,128]{2,1,0:T(8,128)(2,1)S(1)} async-done(((bf16[32,72,128]{2,1,0:T(8,128)(2,1)}), bf16[32,72,128]{2,1,0:T(8,128)(2,1)S(1)}, u32[]{:S(2)}, u32[]{:S(2)}) %all-to-all-start.2) | async-done | bytes 589856 | tf_op jit(solution)/shard_map/all_to_all | solution.py:409
  66.6 1.5 %apply.3.refs_4_ = bf16[512,128]{1,0:T(8,128)(2,1)S(1)} custom-call(s32[1,2304]{1,0:T(1,128)S(1)} %reshape.48.ids_ref, bf16[2304,128]{1,0:T(8,128)(2,1)S(1)} %bitcast.20, bf16[512,128]{1,0:T(8,128)(2,1)} %copy-done.6), custom_call_target="tpu_custom_call" | custom-call | flops 4294967296 | bytes 1048576 | tf_op jit(solution)/shard_map/apply/pallas_call | solution.py:432
  68.0 1.2 %collective-permute-start.22 = (bf16[512,128]{1,0:T(8,128)(2,1)S(1)}, bf16[512,128]{1,0:T(8,128)(2,1)S(1)}, u32[]{:S(2)}, u32[]{:S(2)}) collective-permute-start(bf16[512,128]{1,0:T(8,128)(2,1)S(1)} %apply.3.refs_4_), channel_id=1, source_target_pairs={{0,2},{1,3},{2,0},{3,1},{4,6},{5,7},{6,4},{7,5},{8,10},{9,11},{10,... | collective-permute-start | bytes 393224 | tf_op jit(solution)/shard_map/ppermute | solution.py:306
  69.2 1.5 %apply.2.refs_0_ = bf16[512,128]{1,0:T(8,128)(2,1)S(1)} custom-call(s32[1,2304]{1,0:T(1,128)S(1)} %reshape.48.ids_ref, bf16[2304,128]{1,0:T(8,128)(2,1)S(1)} %bitcast.21, bf16[512,128]{1,0:T(8,128)(2,1)} %copy-done.5), custom_call_target="tpu_custom_call" | custom-call | flops 4294967296 | bytes 1048576 | tf_op jit(solution)/shard_map/apply/pallas_call | solution.py:432
  70.7 1.0 %collective-permute-start.19 = (bf16[512,128]{1,0:T(8,128)(2,1)S(1)}, bf16[512,128]{1,0:T(8,128)(2,1)S(1)}, u32[]{:S(2)}, u32[]{:S(2)}) collective-permute-start(bf16[512,128]{1,0:T(8,128)(2,1)S(1)} %apply.2.refs_0_), channel_id=1, source_target_pairs={{0,2},{1,3},{2,0},{3,1},{4,6},{5,7},{6,4},{7,5},{8,10},{9,11},{10,... | collective-permute-start | bytes 393224 | tf_op jit(solution)/shard_map/ppermute | solution.py:306
  72.2 1.3 %collective-permute-done.22.refs_6_ = bf16[512,128]{1,0:T(8,128)(2,1)S(1)} collective-permute-done((bf16[512,128]{1,0:T(8,128)(2,1)S(1)}, bf16[512,128]{1,0:T(8,128)(2,1)S(1)}, u32[]{:S(2)}, u32[]{:S(2)}) %collective-permute-start.22) | collective-permute-done | bytes 131104 | tf_op jit(solution)/shard_map/ppermute | solution.py:306
  73.5 2.8 %collective-permute-done.19.refs_2_ = bf16[512,128]{1,0:T(8,128)(2,1)S(1)} collective-permute-done((bf16[512,128]{1,0:T(8,128)(2,1)S(1)}, bf16[512,128]{1,0:T(8,128)(2,1)S(1)}, u32[]{:S(2)}, u32[]{:S(2)}) %collective-permute-start.19) | collective-permute-done | bytes 131104 | tf_op jit(solution)/shard_map/ppermute | solution.py:306
  76.3 1.3 %collective-permute-done.20.refs_3_ = bf16[512,128]{1,0:T(8,128)(2,1)S(1)} collective-permute-done((bf16[512,128]{1,0:T(8,128)(2,1)S(1)}, bf16[512,128]{1,0:T(8,128)(2,1)S(1)}, u32[]{:S(2)}, u32[]{:S(2)}) %collective-permute-start.20) | collective-permute-done | bytes 131104 | tf_op jit(solution)/shard_map/ppermute | solution.py:306
  77.7 1.0 %join.1 = bf16[1024,512]{1,0:T(8,128)(2,1)} custom-call(bf16[512,128]{1,0:T(8,128)(2,1)S(1)} %apply.2.refs_0_, bf16[512,128]{1,0:T(8,128)(2,1)S(1)} %collective-permute-done.18.refs_1_, bf16[512,128]{1,0:T(8,128)(2,1)S(1)} %collective-permute-done.19.refs_2_, bf16[512,128]{1,0:T(8,128)(2,1)S(1)} %collective-permute-done.20.refs_3_, ...), custom_call_target="tpu_custom_call" | custom-call | flops 1048576 | bytes 2097152 | tf_op jit(solution)/shard_map/join/pallas_call | solution.py:445
  (94 shorter events, 7.2 us)
Async XLA Ops:
  2.3 11.0 %copy-start.14 = (s32[384]{0:T(512)S(1)}, s32[384]{0:T(512)}, u32[]{:S(2)}) copy-start(s32[384]{0:T(512)} %param.19) | copy-start | bytes 4612
  2.3 11.0 %copy-start.16 = (s32[256]{0:T(256)S(1)}, s32[256]{0:T(256)}, u32[]{:S(2)}) copy-start(s32[256]{0:T(256)} %param.18) | copy-start | bytes 3076
  2.3 13.8 %all-to-all-start = ((s32[8,1,128]{2,1,0:T(1,128)}), s32[8,1,128]{2,1,0:T(1,128)S(1)}, u32[]{:S(2)}, u32[]{:S(2)}) async-start(s32[8,1,128]{2,1,0:T(1,128)} %bitcast.3), calls=%async_computation | async-start | bytes 8192 | tf_op jit(solution)/shard_map/all_to_all | solution.py:359
  9.7 21.3 %collective-permute-start.1 = (bf16[512,384]{1,0:T(8,128)(2,1)}, bf16[512,384]{1,0:T(8,128)(2,1)S(1)}, u32[]{:S(2)}, u32[]{:S(2)}) collective-permute-start(bf16[512,384]{1,0:T(8,128)(2,1)} %refs_0_), channel_id=1, source_target_pairs={{0,2},{1,3},{2,0},{3,1},{4,6},{5,7},{6,4},{7,5},{8,10},{9,11},{10,... | collective-permute-start | bytes 1179656 | tf_op jit(solution)/shard_map/ppermute | solution.py:306
  11.2 20.4 %collective-permute-start.4 = (bf16[512,384]{1,0:T(8,128)(2,1)}, bf16[512,384]{1,0:T(8,128)(2,1)S(1)}, u32[]{:S(2)}, u32[]{:S(2)}) collective-permute-start(bf16[512,384]{1,0:T(8,128)(2,1)} %refs_4_), channel_id=1, source_target_pairs={{0,2},{1,3},{2,0},{3,1},{4,6},{5,7},{6,4},{7,5},{8,10},{9,11},{10,... | collective-permute-start | bytes 1179656 | tf_op jit(solution)/shard_map/ppermute | solution.py:306
  11.7 19.3 %collective-permute-start.7 = (bf16[128,384]{1,0:T(8,128)(2,1)}, bf16[128,384]{1,0:T(8,128)(2,1)S(1)}, u32[]{:S(2)}, u32[]{:S(2)}) collective-permute-start(bf16[128,384]{1,0:T(8,128)(2,1)} %refs_8_), channel_id=1, source_target_pairs={{0,2},{1,3},{2,0},{3,1},{4,6},{5,7},{6,4},{7,5},{8,10},{9,11},{10,... | collective-permute-start | bytes 294920 | tf_op jit(solution)/shard_map/ppermute | solution.py:306
  19.0 12.0 %copy-start.21 = (bf16[128,384]{1,0:T(8,128)(2,1)S(1)}, bf16[128,384]{1,0:T(8,128)(2,1)}, u32[]{:S(2)}) copy-start(bf16[128,384]{1,0:T(8,128)(2,1)} %refs_8_) | copy-start | bytes 294916
  19.0 12.6 %copy-start.10 = (f32[384,8]{1,0:T(8,128)S(1)}, f32[384,8]{1,0:T(8,128)}, u32[]{:S(2)}) copy-start(f32[384,8]{1,0:T(8,128)} %copy-done.9) | copy-start | bytes 36868
  19.0 19.2 %all-to-all-start.1 = ((bf16[8,264,128]{2,1,0:T(8,128)(2,1)}), bf16[8,264,128]{2,1,0:T(8,128)(2,1)S(1)}, u32[]{:S(2)}, u32[]{:S(2)}) async-start(bf16[8,264,128]{2,1,0:T(8,128)(2,1)} %serve.1), calls=%async_computation.1 | async-start | bytes 1081344 | tf_op jit(solution)/shard_map/all_to_all | solution.py:389
  23.6 13.8 %collective-permute-start = (bf16[512,384]{1,0:T(8,128)(2,1)S(1)}, bf16[512,384]{1,0:T(8,128)(2,1)}, u32[]{:S(2)}, u32[]{:S(2)}) collective-permute-start(bf16[512,384]{1,0:T(8,128)(2,1)S(1)} %copy-done.17), channel_id=1, source_target_pairs={{0,1},{1,0},{2,3},{3,2},{4,5},{5,4},{6,7},{7,6},{8,9},{9,8},{10,11... | collective-permute-start | bytes 1179656 | tf_op jit(solution)/shard_map/ppermute | solution.py:306
  23.7 13.8 %collective-permute-start.3 = (bf16[512,384]{1,0:T(8,128)(2,1)S(1)}, bf16[512,384]{1,0:T(8,128)(2,1)}, u32[]{:S(2)}, u32[]{:S(2)}) collective-permute-start(bf16[512,384]{1,0:T(8,128)(2,1)S(1)} %copy-done.18), channel_id=1, source_target_pairs={{0,1},{1,0},{2,3},{3,2},{4,5},{5,4},{6,7},{7,6},{8,9},{9,8},{10,11... | collective-permute-start | bytes 1179656 | tf_op jit(solution)/shard_map/ppermute | solution.py:306
  31.0 3.5 %collective-permute-start.6 = (bf16[128,384]{1,0:T(8,128)(2,1)S(1)}, bf16[128,384]{1,0:T(8,128)(2,1)S(1)}, u32[]{:S(2)}, u32[]{:S(2)}) collective-permute-start(bf16[128,384]{1,0:T(8,128)(2,1)S(1)} %copy-done.21), channel_id=1, source_target_pairs={{0,1},{1,0},{2,3},{3,2},{4,5},{5,4},{6,7},{7,6},{8,9},{9,8},{10,11... | collective-permute-start | bytes 294920 | tf_op jit(solution)/shard_map/ppermute | solution.py:306
  31.1 7.0 %collective-permute-start.2 = (bf16[512,384]{1,0:T(8,128)(2,1)S(1)}, bf16[512,384]{1,0:T(8,128)(2,1)}, u32[]{:S(2)}, u32[]{:S(2)}) collective-permute-start(bf16[512,384]{1,0:T(8,128)(2,1)S(1)} %collective-permute-done.1.refs_2_), channel_id=1, source_target_pairs={{0,1},{1,0},{2,3},{3,2},{4,5},{5,4},{6,7},{7,6},{8,9},{9,8},{10,11... | collective-permute-start | bytes 1179656 | tf_op jit(solution)/shard_map/ppermute | solution.py:306
  31.6 6.7 %collective-permute-start.5 = (bf16[512,384]{1,0:T(8,128)(2,1)S(1)}, bf16[512,384]{1,0:T(8,128)(2,1)}, u32[]{:S(2)}, u32[]{:S(2)}) collective-permute-start(bf16[512,384]{1,0:T(8,128)(2,1)S(1)} %collective-permute-done.4.refs_6_), channel_id=1, source_target_pairs={{0,1},{1,0},{2,3},{3,2},{4,5},{5,4},{6,7},{7,6},{8,9},{9,8},{10,11... | collective-permute-start | bytes 1179656 | tf_op jit(solution)/shard_map/ppermute | solution.py:306
  34.5 1.4 %collective-permute-start.8 = (bf16[128,384]{1,0:T(8,128)(2,1)S(1)}, bf16[128,384]{1,0:T(8,128)(2,1)S(1)}, u32[]{:S(2)}, u32[]{:S(2)}) collective-permute-start(bf16[128,384]{1,0:T(8,128)(2,1)S(1)} %collective-permute-done.7.refs_10_), channel_id=1, source_target_pairs={{0,1},{1,0},{2,3},{3,2},{4,5},{5,4},{6,7},{7,6},{8,9},{9,8},{10,11... | collective-permute-start | bytes 294920 | tf_op jit(solution)/shard_map/ppermute | solution.py:306
  35.9 20.5 %collective-permute-start.13 = (bf16[512,256]{1,0:T(8,128)(2,1)S(1)}, bf16[512,256]{1,0:T(8,128)(2,1)S(1)}, u32[]{:S(2)}, u32[]{:S(2)}) collective-permute-start(bf16[512,256]{1,0:T(8,128)(2,1)S(1)} %copy-done.1), channel_id=1, source_target_pairs={{0,2},{1,3},{2,0},{3,1},{4,6},{5,7},{6,4},{7,5},{8,10},{9,11},{10,... | collective-permute-start | bytes 786440 | tf_op jit(solution)/shard_map/ppermute | solution.py:306
  37.4 20.4 %collective-permute-start.12 = (bf16[512,256]{1,0:T(8,128)(2,1)S(1)}, bf16[512,256]{1,0:T(8,128)(2,1)}, u32[]{:S(2)}, u32[]{:S(2)}) collective-permute-start(bf16[512,256]{1,0:T(8,128)(2,1)S(1)} %copy-done.1), channel_id=1, source_target_pairs={{0,1},{1,0},{2,3},{3,2},{4,5},{5,4},{6,7},{7,6},{8,9},{9,8},{10,11... | collective-permute-start | bytes 786440 | tf_op jit(solution)/shard_map/ppermute | solution.py:306
  37.5 18.6 %collective-permute-start.10 = (bf16[512,128]{1,0:T(8,128)(2,1)S(1)}, bf16[512,128]{1,0:T(8,128)(2,1)}, u32[]{:S(2)}, u32[]{:S(2)}) collective-permute-start(bf16[512,128]{1,0:T(8,128)(2,1)S(1)} %copy-done.2), channel_id=1, source_target_pairs={{0,2},{1,3},{2,0},{3,1},{4,6},{5,7},{6,4},{7,5},{8,10},{9,11},{10,... | collective-permute-start | bytes 393224 | tf_op jit(solution)/shard_map/ppermute | solution.py:306
  38.0 19.7 %collective-permute-start.9 = (bf16[512,128]{1,0:T(8,128)(2,1)S(1)}, bf16[512,128]{1,0:T(8,128)(2,1)}, u32[]{:S(2)}, u32[]{:S(2)}) collective-permute-start(bf16[512,128]{1,0:T(8,128)(2,1)S(1)} %copy-done.2), channel_id=1, source_target_pairs={{0,1},{1,0},{2,3},{3,2},{4,5},{5,4},{6,7},{7,6},{8,9},{9,8},{10,11... | collective-permute-start | bytes 393224 | tf_op jit(solution)/shard_map/ppermute | solution.py:306
  44.1 14.0 %copy-start = (bf16[1024,512]{1,0:T(8,128)(2,1)S(1)}, bf16[1024,512]{1,0:T(8,128)(2,1)}, u32[]{:S(2)}) copy-start(bf16[1024,512]{1,0:T(8,128)(2,1)} %memory_ref.3) | copy-start | bytes 3145732
  44.1 22.5 %all-to-all-start.2 = ((bf16[32,72,128]{2,1,0:T(8,128)(2,1)}), bf16[32,72,128]{2,1,0:T(8,128)(2,1)S(1)}, u32[]{:S(2)}, u32[]{:S(2)}) async-start(bf16[32,72,128]{2,1,0:T(8,128)(2,1)} %get-tuple-element.31), calls=%async_computation.2 | async-start | bytes 1179648 | tf_op jit(solution)/shard_map/all_to_all | solution.py:409
  49.8 4.9 %collective-permute-start.16 = (s32[8,128]{1,0:T(8,128)S(1)}, s32[8,128]{1,0:T(8,128)S(1)}, u32[]{:S(2)}, u32[]{:S(2)}) collective-permute-start(s32[8,128]{1,0:T(8,128)S(1)} %bitcast.23), channel_id=1, source_target_pairs={{0,2},{1,3},{2,0},{3,1},{4,6},{5,7},{6,4},{7,5},{8,10},{9,11},{10,... | collective-permute-start | bytes 12296 | tf_op jit(solution)/shard_map/ppermute | solution.py:306
  54.8 1.2 %collective-permute-start.15 = (s32[8,128]{1,0:T(8,128)S(1)}, s32[8,128]{1,0:T(8,128)S(1)}, u32[]{:S(2)}, u32[]{:S(2)}) collective-permute-start(s32[8,128]{1,0:T(8,128)S(1)} %bitcast.25), channel_id=1, source_target_pairs={{0,1},{1,0},{2,3},{3,2},{4,5},{5,4},{6,7},{7,6},{8,9},{9,8},{10,11... | collective-permute-start | bytes 12296 | tf_op jit(solution)/shard_map/ppermute | solution.py:306
  55.9 1.2 %collective-permute-start.17 = (s32[8,128]{1,0:T(8,128)S(1)}, s32[8,128]{1,0:T(8,128)S(1)}, u32[]{:S(2)}, u32[]{:S(2)}) collective-permute-start(s32[8,128]{1,0:T(8,128)S(1)} %collective-permute-done.16), channel_id=1, source_target_pairs={{0,1},{1,0},{2,3},{3,2},{4,5},{5,4},{6,7},{7,6},{8,9},{9,8},{10,11... | collective-permute-start | bytes 12296 | tf_op jit(solution)/shard_map/ppermute | solution.py:306
  56.1 1.7 %collective-permute-start.11 = (bf16[512,128]{1,0:T(8,128)(2,1)}, bf16[512,128]{1,0:T(8,128)(2,1)}, u32[]{:S(2)}, u32[]{:S(2)}) collective-permute-start(bf16[512,128]{1,0:T(8,128)(2,1)} %collective-permute-done.10.refs_2_), channel_id=1, source_target_pairs={{0,1},{1,0},{2,3},{3,2},{4,5},{5,4},{6,7},{7,6},{8,9},{9,8},{10,11... | collective-permute-start | bytes 393224 | tf_op jit(solution)/shard_map/ppermute | solution.py:306
  56.4 1.7 %collective-permute-start.14 = (bf16[512,256]{1,0:T(8,128)(2,1)S(1)}, bf16[512,256]{1,0:T(8,128)(2,1)}, u32[]{:S(2)}, u32[]{:S(2)}) collective-permute-start(bf16[512,256]{1,0:T(8,128)(2,1)S(1)} %collective-permute-done.13.refs_6_), channel_id=1, source_target_pairs={{0,1},{1,0},{2,3},{3,2},{4,5},{5,4},{6,7},{7,6},{8,9},{9,8},{10,11... | collective-permute-start | bytes 786440 | tf_op jit(solution)/shard_map/ppermute | solution.py:306
  68.0 5.5 %collective-permute-start.22 = (bf16[512,128]{1,0:T(8,128)(2,1)S(1)}, bf16[512,128]{1,0:T(8,128)(2,1)S(1)}, u32[]{:S(2)}, u32[]{:S(2)}) collective-permute-start(bf16[512,128]{1,0:T(8,128)(2,1)S(1)} %apply.3.refs_4_), channel_id=1, source_target_pairs={{0,2},{1,3},{2,0},{3,1},{4,6},{5,7},{6,4},{7,5},{8,10},{9,11},{10,... | collective-permute-start | bytes 393224 | tf_op jit(solution)/shard_map/ppermute | solution.py:306
  70.7 5.6 %collective-permute-start.19 = (bf16[512,128]{1,0:T(8,128)(2,1)S(1)}, bf16[512,128]{1,0:T(8,128)(2,1)S(1)}, u32[]{:S(2)}, u32[]{:S(2)}) collective-permute-start(bf16[512,128]{1,0:T(8,128)(2,1)S(1)} %apply.2.refs_0_), channel_id=1, source_target_pairs={{0,2},{1,3},{2,0},{3,1},{4,6},{5,7},{6,4},{7,5},{8,10},{9,11},{10,... | collective-permute-start | bytes 393224 | tf_op jit(solution)/shard_map/ppermute | solution.py:306
  71.7 4.6 %collective-permute-start.21 = (bf16[512,128]{1,0:T(8,128)(2,1)S(1)}, bf16[512,128]{1,0:T(8,128)(2,1)S(1)}, u32[]{:S(2)}, u32[]{:S(2)}) collective-permute-start(bf16[512,128]{1,0:T(8,128)(2,1)S(1)} %apply.3.refs_4_), channel_id=1, source_target_pairs={{0,1},{1,0},{2,3},{3,2},{4,5},{5,4},{6,7},{7,6},{8,9},{9,8},{10,11... | collective-permute-start | bytes 393224 | tf_op jit(solution)/shard_map/ppermute | solution.py:306
  71.7 4.6 %collective-permute-start.18 = (bf16[512,128]{1,0:T(8,128)(2,1)S(1)}, bf16[512,128]{1,0:T(8,128)(2,1)S(1)}, u32[]{:S(2)}, u32[]{:S(2)}) collective-permute-start(bf16[512,128]{1,0:T(8,128)(2,1)S(1)} %apply.2.refs_0_), channel_id=1, source_target_pairs={{0,1},{1,0},{2,3},{3,2},{4,5},{5,4},{6,7},{7,6},{8,9},{9,8},{10,11... | collective-permute-start | bytes 393224 | tf_op jit(solution)/shard_map/ppermute | solution.py:306
  73.5 2.8 %collective-permute-start.23 = (bf16[512,128]{1,0:T(8,128)(2,1)S(1)}, bf16[512,128]{1,0:T(8,128)(2,1)S(1)}, u32[]{:S(2)}, u32[]{:S(2)}) collective-permute-start(bf16[512,128]{1,0:T(8,128)(2,1)S(1)} %collective-permute-done.22.refs_6_), channel_id=1, source_target_pairs={{0,1},{1,0},{2,3},{3,2},{4,5},{5,4},{6,7},{7,6},{8,9},{9,8},{10,11... | collective-permute-start | bytes 393224 | tf_op jit(solution)/shard_map/ppermute | solution.py:306
  76.3 1.3 %collective-permute-start.20 = (bf16[512,128]{1,0:T(8,128)(2,1)S(1)}, bf16[512,128]{1,0:T(8,128)(2,1)S(1)}, u32[]{:S(2)}, u32[]{:S(2)}) collective-permute-start(bf16[512,128]{1,0:T(8,128)(2,1)S(1)} %collective-permute-done.19.refs_2_), channel_id=1, source_target_pairs={{0,1},{1,0},{2,3},{3,2},{4,5},{5,4},{6,7},{7,6},{8,9},{9,8},{10,11... | collective-permute-start | bytes 393224 | tf_op jit(solution)/shard_map/ppermute | solution.py:306
  (20 other events, 56.0 us)

commit v13 on v10

--- a/solution.py
+++ b/solution.py
@@ -124,7 +124,7 @@
     return jnp.where((inner * plan.owners + owner) == here, 1.0, 0.0).astype(BF16)
 
 
-def serve_kernel(plan, asked_ref, memory_ref, out_ref, held, hot_ref, sems):
+def serve_kernel(plan, asked_ref, memory_ref, far_ref, out_ref, held, hot_ref, sems, out_sems):
     stored, width = memory_ref.shape
     piece = width // 4
     step = stored // 4
@@ -148,19 +148,24 @@
         copy.wait()
     rows = dot(hot_ref[...], held[...])
     main = plan.main
+    if plan.tail:
+        spare = rows[plan.owners * main :]
+        stack = jnp.concatenate([spare[:, c * piece : (c + 1) * piece] for c in range(4)], axis=0)
+        ordered = dot(tail_order(plan, True), stack.astype(BF16))
+    sends = []
     for s in range(plan.owners):
         for c in range(4):
             out_ref[s, c * main : (c + 1) * main, :] = rows[
                 s * main : (s + 1) * main, c * piece : (c + 1) * piece
             ].astype(BF16)
-    if plan.tail:
-        spare = rows[plan.owners * main :]
-        stack = jnp.concatenate([spare[:, c * piece : (c + 1) * piece] for c in range(4)], axis=0)
-        ordered = dot(tail_order(plan, True), stack.astype(BF16))
-        for s in range(plan.owners):
+        if plan.tail:
             out_ref[s, 4 * main : 4 * (main + plan.tail), :] = ordered[
                 s * 4 * plan.tail : (s + 1) * 4 * plan.tail
             ].astype(BF16)
+        sends.append(pltpu.make_async_copy(out_ref.at[s], far_ref.at[s], out_sems.at[s]))
+        sends[-1].start()
+    for send in sends:
+        send.wait()
 
 
 def table_of(plan, ret_ref):
@@ -184,7 +189,7 @@
 def gru_kernel(plan, ret_ref, row_ref, col_ref, far_enc, *refs):
     reps = plan.reps
     parts = refs[: 3 * reps]
-    out_ref, hnew_ref, hdst_ref, gin, ghid, delta, hsrc_ref, enc_ref, w_in, w_hid, w_time, sems = refs[3 * reps :]
+    far_ref, hnew_ref, hdst_ref, out_ref, gin, ghid, delta, hsrc_ref, enc_ref, w_in, w_hid, w_time, sems, out_sems = refs[3 * reps :]
     copies = [pltpu.make_async_copy(far_enc, enc_ref, sems.at[0])]
     for g, held in ((1, w_hid), (0, w_in), (2, w_time)):
         for k in range(reps):
@@ -229,9 +234,15 @@
     counts = jnp.maximum(jnp.sum(hits, axis=1, keepdims=True), 1.0)
     hits = hits.astype(BF16)
     mean = dot(hits, delta[...]) / counts
+    sends = []
     for o in range(plan.owners):
         for q in range(reps):
             out_ref[o * reps + q] = mean[o * plan.pad : (o + 1) * plan.pad, q * piece : (q + 1) * piece].astype(BF16)
+        at = pl.ds(o * reps, reps)
+        sends.append(pltpu.make_async_copy(out_ref.at[at], far_ref.at[at], out_sems.at[o]))
+        sends[-1].start()
+    for send in sends:
+        send.wait()
 
 
 def attend_kernel(plan, listed_ref, hnew_ref, hdst_ref, memory_ref, *refs):
@@ -379,10 +390,13 @@
         2 * stored * width + 2 * plan.rows * width,
         "serve",
         scratch=[
+            pltpu.VMEM((owners, 4 * (plan.main + plan.tail), width // 4), BF16),
             pltpu.VMEM((stored, width), BF16),
             pltpu.VMEM((plan.rows, stored), BF16),
             pltpu.SemaphoreType.DMA((4,)),
+            pltpu.SemaphoreType.DMA((owners,)),
         ],
+        out_specs=[HBM],
         limit=16,
     )(asked, *far([memory]))[0]
     returned = lax.all_to_all(served, "shard", split_axis=0, concat_axis=0, tiled=True)
@@ -394,7 +408,9 @@
         2 * events * width * 3 * width * 2,
         8 << 20,
         "gru",
+        out_specs=[HBM, VMEM, VMEM],
         scratch=[
+            pltpu.VMEM((owners * reps, plan.pad, piece), BF16),
             pltpu.VMEM((events, 3 * width), F32),
             pltpu.VMEM((events, 3 * width), F32),
             pltpu.VMEM((events, width), BF16),
@@ -402,7 +418,7 @@
             pltpu.VMEM(encode.shape, BF16),
         ]
         + [pltpu.VMEM((reps,) + x.shape, BF16) for x in (w_input, w_hidden, w_time)]
-        + [pltpu.SemaphoreType.DMA((1 + 3 * reps,))],
+        + [pltpu.SemaphoreType.DMA((1 + 3 * reps,)), pltpu.SemaphoreType.DMA((owners,))],
         limit=24,
     )(returned, rows, cols, *far([encode, *full_input, *full_hidden, *full_time]))
     landed = lax.all_to_all(outgoing, ("shard", "rep"), split_axis=0, concat_axis=0, tiled=True)

time: 76.5 us -> 76.8 us (level)
  transfers between devices with their start and end apart: 27 -> 27, of which waited for: 12 -> 12; matrix products, arithmetic and copies ran while one was open for 1% -> 1% of each run, Pallas kernels for 20% -> 21%
where the time goes in v13:
time: 76.8 us; the launch traced here: 76.3 us
  starting transfers between devices  27.2 us (35%)
  waiting for transfers between devices  24.1 us (31%)
  Pallas kernels  19.2 us (25%)
  local copies, waits for them, and re-layouts  4.85 us (6%)
  between operations  0.96 us (1%)
    ppermute x24, starting transfers between devices, swap(): return lax.ppermute(x, 'rep', [(i, i ^ bit) for i in range(reps)])  13.6 us
    ppermute x24, waiting for transfers between devices, swap(): return lax.ppermute(x, 'rep', [(i, i ^ bit) for i in range(reps)])  11.9 us
    all_to_all x1, starting transfers between devices, shards(): lax.all_to_all(request, 'shard', split_axis=0, concat_axis=0, tiled=True)  6.34 us
    pallas_call x1, Pallas kernels, shards(): call(run(gru_kernel, plan), [sds((owners * reps, plan.pad, piece), BF16),...  6.03 us
    all_to_all x1, waiting for transfers between devices, shards(): lax.all_to_all(served, 'shard', split_axis=0, concat_axis=0, tiled=True)  4.73 us
    all_to_all x1, waiting for transfers between devices, shards(): lax.all_to_all(request, 'shard', split_axis=0, concat_axis=0, tiled=True)  4.39 us
    unnamed x45, local copies, waits for them, and re-layouts  4.19 us
    pallas_call x1, Pallas kernels, shards(): call(run(attend_kernel, plan), [sds((events, width), BF16)] + [sds((store...  4.09 us
  transfers between devices with their start and end apart: 27, of which 12 were waited for; matrix products, arithmetic and copies ran while one was open for 1% of the time, Pallas kernels for 21%

profile of v13, /device:TPU:0, one launch (start us, length us, event | category | flops | bytes accessed | tf_op | source)
XLA Modules:
  0.0 76.3 jit_solution(5650092139362468069)
XLA Ops:
  0.6 0.7 copy-done.4
  1.3 1.0 %request.1 = s32[8,128]{1,0:T(8,128)} custom-call(s32[1,256]{1,0:T(1,128)S(1)} %bitcast.27, s32[1,256]{1,0:T(1,128)S(1)} %bitcast.26), custom_call_target="tpu_custom_call" | custom-call | flops 1048576 | bytes 16384 | tf_op jit(solution)/shard_map/request/pallas_call | solution.py:357
  2.3 2.9 %collective-permute-start.1 = (bf16[512,384]{1,0:T(8,128)(2,1)}, bf16[512,384]{1,0:T(8,128)(2,1)S(1)}, u32[]{:S(2)}, u32[]{:S(2)}) collective-permute-start(bf16[512,384]{1,0:T(8,128)(2,1)} %refs_0_), channel_id=1, source_target_pairs={{0,2},{1,3},{2,0},{3,1},{4,6},{5,7},{6,4},{7,5},{8,10},{9,11},{10,... | collective-permute-start | bytes 1179656 | tf_op jit(solution)/shard_map/ppermute | solution.py:315
  5.3 6.3 %all-to-all-start = ((s32[8,1,128]{2,1,0:T(1,128)}), s32[8,1,128]{2,1,0:T(1,128)S(1)}, u32[]{:S(2)}, u32[]{:S(2)}) async-start(s32[8,1,128]{2,1,0:T(1,128)} %bitcast.3), calls=%async_computation | async-start | bytes 8192 | tf_op jit(solution)/shard_map/all_to_all | solution.py:368
  12.1 1.5 %collective-permute-start.7 = (bf16[128,384]{1,0:T(8,128)(2,1)}, bf16[128,384]{1,0:T(8,128)(2,1)S(1)}, u32[]{:S(2)}, u32[]{:S(2)}) collective-permute-start(bf16[128,384]{1,0:T(8,128)(2,1)} %refs_8_), channel_id=1, source_target_pairs={{0,2},{1,3},{2,0},{3,1},{4,6},{5,7},{6,4},{7,5},{8,10},{9,11},{10,... | collective-permute-start | bytes 294920 | tf_op jit(solution)/shard_map/ppermute | solution.py:315
  13.6 4.4 %all-to-all-done = s32[8,1,128]{2,1,0:T(1,128)S(1)} async-done(((s32[8,1,128]{2,1,0:T(1,128)}), s32[8,1,128]{2,1,0:T(1,128)S(1)}, u32[]{:S(2)}, u32[]{:S(2)}) %all-to-all-start) | async-done | bytes 4128 | tf_op jit(solution)/shard_map/all_to_all | solution.py:368
  18.0 2.9 %serve.1 = bf16[8,264,128]{2,1,0:T(8,128)(2,1)} custom-call(s32[8,128]{1,0:T(8,128)S(1)} %bitcast.22, bf16[1024,512]{1,0:T(8,128)(2,1)} %memory_ref.3), custom_call_target="tpu_custom_call" | custom-call | flops 553648128 | bytes 1589248 | tf_op jit(solution)/shard_map/serve/pallas_call | solution.py:385
  21.0 3.7 %all-to-all-start.1 = ((bf16[8,264,128]{2,1,0:T(8,128)(2,1)}), bf16[8,264,128]{2,1,0:T(8,128)(2,1)S(1)}, u32[]{:S(2)}, u32[]{:S(2)}) async-start(bf16[8,264,128]{2,1,0:T(8,128)(2,1)} %serve.1), calls=%async_computation.1 | async-start | bytes 1081344 | tf_op jit(solution)/shard_map/all_to_all | solution.py:402
  25.7 0.7 copy-done.7
  26.4 1.2 %index.1 = (bf16[384,128]{1,0:T(8,128)(2,1)S(1)}, f32[384,8]{1,0:T(8,128)S(1)}, s32[8,384]{1,0:T(8,128)S(1)}) custom-call(s32[1,256]{1,0:T(1,128)S(1)} %bitcast.28, s32[1,1408]{1,0:T(1,128)S(1)} %reshape.45.packed_ref, f32[1,128]{1,0:T(1,128)S(1)} %bitcast.29, f32[1,128]{1,0:T(1,128)S(1)} %bitcast.30), custom_call_target="tpu_custom_call" | custom-call | flops 8589934592 | bytes 262144 | tf_op jit(solution)/shard_map/index/pallas_call | solution.py:369
  27.7 0.6 copy-done.9
  28.3 0.7 copy-done.13
  29.5 1.1 %collective-permute-done.8.refs_11_ = bf16[128,384]{1,0:T(8,128)(2,1)} collective-permute-done((bf16[128,384]{1,0:T(8,128)(2,1)S(1)}, bf16[128,384]{1,0:T(8,128)(2,1)}, u32[]{:S(2)}, u32[]{:S(2)}) %collective-permute-start.8) | collective-permute-done | bytes 98336 | tf_op jit(solution)/shard_map/ppermute | solution.py:315
  30.6 1.8 %collective-permute-start.13 = (bf16[512,256]{1,0:T(8,128)(2,1)S(1)}, bf16[512,256]{1,0:T(8,128)(2,1)S(1)}, u32[]{:S(2)}, u32[]{:S(2)}) collective-permute-start(bf16[512,256]{1,0:T(8,128)(2,1)S(1)} %copy-done.1), channel_id=1, source_target_pairs={{0,2},{1,3},{2,0},{3,1},{4,6},{5,7},{6,4},{7,5},{8,10},{9,11},{10,... | collective-permute-start | bytes 786440 | tf_op jit(solution)/shard_map/ppermute | solution.py:315
  33.1 4.7 %all-to-all-done.1.ret_ref = bf16[8,264,128]{2,1,0:T(8,128)(2,1)S(1)} async-done(((bf16[8,264,128]{2,1,0:T(8,128)(2,1)}), bf16[8,264,128]{2,1,0:T(8,128)(2,1)S(1)}, u32[]{:S(2)}, u32[]{:S(2)}) %all-to-all-start.1) | async-done | bytes 540704 | tf_op jit(solution)/shard_map/all_to_all | solution.py:402
  37.8 6.0 %gru.1 = (bf16[32,72,128]{2,1,0:T(8,128)(2,1)}, f32[384,512]{1,0:T(8,128)S(1)}, bf16[384,512]{1,0:T(8,128)(2,1)S(1)}) custom-call(bf16[8,264,128]{2,1,0:T(8,128)(2,1)S(1)} %all-to-all-done.1.ret_ref, s32[8,384]{1,0:T(8,128)S(1)} %get-tuple-element.18.row_ref, f32[384,8]{1,0:T(8,128)S(1)} %get-tuple-element.19.col_ref, bf16[384,128]{1,0:T(8,128)(2,1)} %copy-done.9, ...), custom_call_target="tpu_custom_call" | custom-call | flops 1207959552 | bytes 8388608 | tf_op jit(solution)/shard_map/gru/pallas_call | solution.py:404
  43.8 3.6 %all-to-all-start.2 = ((bf16[32,72,128]{2,1,0:T(8,128)(2,1)}), bf16[32,72,128]{2,1,0:T(8,128)(2,1)S(1)}, u32[]{:S(2)}, u32[]{:S(2)}) async-start(bf16[32,72,128]{2,1,0:T(8,128)(2,1)} %get-tuple-element.29), calls=%async_computation.2 | async-start | bytes 1179648 | tf_op jit(solution)/shard_map/all_to_all | solution.py:424
  47.5 1.8 %collective-permute-start.16 = (s32[8,128]{1,0:T(8,128)S(1)}, s32[8,128]{1,0:T(8,128)S(1)}, u32[]{:S(2)}, u32[]{:S(2)}) collective-permute-start(s32[8,128]{1,0:T(8,128)S(1)} %bitcast.23), channel_id=1, source_target_pairs={{0,2},{1,3},{2,0},{3,1},{4,6},{5,7},{6,4},{7,5},{8,10},{9,11},{10,... | collective-permute-start | bytes 12296 | tf_op jit(solution)/shard_map/ppermute | solution.py:315
  49.3 3.1 %collective-permute-done.16 = s32[8,128]{1,0:T(8,128)S(1)} collective-permute-done((s32[8,128]{1,0:T(8,128)S(1)}, s32[8,128]{1,0:T(8,128)S(1)}, u32[]{:S(2)}, u32[]{:S(2)}) %collective-permute-start.16) | collective-permute-done | bytes 4128 | tf_op jit(solution)/shard_map/ppermute | solution.py:315
  52.4 1.2 %collective-permute-done.15 = s32[8,128]{1,0:T(8,128)S(1)} collective-permute-done((s32[8,128]{1,0:T(8,128)S(1)}, s32[8,128]{1,0:T(8,128)S(1)}, u32[]{:S(2)}, u32[]{:S(2)}) %collective-permute-start.15) | collective-permute-done | bytes 4128 | tf_op jit(solution)/shard_map/ppermute | solution.py:315
  55.8 4.1 %attend.1 = (bf16[384,512]{1,0:T(8,128)(2,1)}, bf16[512,128]{1,0:T(8,128)(2,1)S(1)}, bf16[512,128]{1,0:T(8,128)(2,1)S(1)}) custom-call(s32[3,2]{1,0:T(4,128)S(1)} %copy.20.listed_ref, f32[384,512]{1,0:T(8,128)S(1)} %get-tuple-element.24.hnew_ref, bf16[384,512]{1,0:T(8,128)(2,1)S(1)} %get-tuple-element.25.hdst_ref, bf16[1024,512]{1,0:T(8,128)(2,1)S(1)} %copy-done, ...), custom_call_target="tpu_custom_call" | custom-call | flops 603979776 | bytes 4194304 | tf_op jit(solution)/shard_map/attend/pallas_call | solution.py:426
  59.8 0.7 copy-done.5
  60.5 0.6 copy-done.6
  61.1 3.1 %all-to-all-done.2 = bf16[32,72,128]{2,1,0:T(8,128)(2,1)S(1)} async-done(((bf16[32,72,128]{2,1,0:T(8,128)(2,1)}), bf16[32,72,128]{2,1,0:T(8,128)(2,1)S(1)}, u32[]{:S(2)}, u32[]{:S(2)}) %all-to-all-start.2) | async-done | bytes 589856 | tf_op jit(solution)/shard_map/all_to_all | solution.py:424
  64.2 1.5 %apply.3.refs_4_ = bf16[512,128]{1,0:T(8,128)(2,1)S(1)} custom-call(s32[1,2304]{1,0:T(1,128)S(1)} %reshape.48.ids_ref, bf16[2304,128]{1,0:T(8,128)(2,1)S(1)} %bitcast.20, bf16[512,128]{1,0:T(8,128)(2,1)} %copy-done.6), custom_call_target="tpu_custom_call" | custom-call | flops 4294967296 | bytes 1048576 | tf_op jit(solution)/shard_map/apply/pallas_call | solution.py:447
  65.7 1.2 %collective-permute-start.22 = (bf16[512,128]{1,0:T(8,128)(2,1)S(1)}, bf16[512,128]{1,0:T(8,128)(2,1)S(1)}, u32[]{:S(2)}, u32[]{:S(2)}) collective-permute-start(bf16[512,128]{1,0:T(8,128)(2,1)S(1)} %apply.3.refs_4_), channel_id=1, source_target_pairs={{0,2},{1,3},{2,0},{3,1},{4,6},{5,7},{6,4},{7,5},{8,10},{9,11},{10,... | collective-permute-start | bytes 393224 | tf_op jit(solution)/shard_map/ppermute | solution.py:315
  66.9 1.5 %apply.2.refs_0_ = bf16[512,128]{1,0:T(8,128)(2,1)S(1)} custom-call(s32[1,2304]{1,0:T(1,128)S(1)} %reshape.48.ids_ref, bf16[2304,128]{1,0:T(8,128)(2,1)S(1)} %bitcast.21, bf16[512,128]{1,0:T(8,128)(2,1)} %copy-done.5), custom_call_target="tpu_custom_call" | custom-call | flops 4294967296 | bytes 1048576 | tf_op jit(solution)/shard_map/apply/pallas_call | solution.py:447
  68.4 0.9 %collective-permute-start.19 = (bf16[512,128]{1,0:T(8,128)(2,1)S(1)}, bf16[512,128]{1,0:T(8,128)(2,1)S(1)}, u32[]{:S(2)}, u32[]{:S(2)}) collective-permute-start(bf16[512,128]{1,0:T(8,128)(2,1)S(1)} %apply.2.refs_0_), channel_id=1, source_target_pairs={{0,2},{1,3},{2,0},{3,1},{4,6},{5,7},{6,4},{7,5},{8,10},{9,11},{10,... | collective-permute-start | bytes 393224 | tf_op jit(solution)/shard_map/ppermute | solution.py:315
  69.8 1.3 %collective-permute-done.22.refs_6_ = bf16[512,128]{1,0:T(8,128)(2,1)S(1)} collective-permute-done((bf16[512,128]{1,0:T(8,128)(2,1)S(1)}, bf16[512,128]{1,0:T(8,128)(2,1)S(1)}, u32[]{:S(2)}, u32[]{:S(2)}) %collective-permute-start.22) | collective-permute-done | bytes 131104 | tf_op jit(solution)/shard_map/ppermute | solution.py:315
  71.1 2.8 %collective-permute-done.19.refs_2_ = bf16[512,128]{1,0:T(8,128)(2,1)S(1)} collective-permute-done((bf16[512,128]{1,0:T(8,128)(2,1)S(1)}, bf16[512,128]{1,0:T(8,128)(2,1)S(1)}, u32[]{:S(2)}, u32[]{:S(2)}) %collective-permute-start.19) | collective-permute-done | bytes 131104 | tf_op jit(solution)/shard_map/ppermute | solution.py:315
  74.0 1.3 %collective-permute-done.20.refs_3_ = bf16[512,128]{1,0:T(8,128)(2,1)S(1)} collective-permute-done((bf16[512,128]{1,0:T(8,128)(2,1)S(1)}, bf16[512,128]{1,0:T(8,128)(2,1)S(1)}, u32[]{:S(2)}, u32[]{:S(2)}) %collective-permute-start.20) | collective-permute-done | bytes 131104 | tf_op jit(solution)/shard_map/ppermute | solution.py:315
  75.3 1.0 %join.1 = bf16[1024,512]{1,0:T(8,128)(2,1)} custom-call(bf16[512,128]{1,0:T(8,128)(2,1)S(1)} %apply.2.refs_0_, bf16[512,128]{1,0:T(8,128)(2,1)S(1)} %collective-permute-done.18.refs_1_, bf16[512,128]{1,0:T(8,128)(2,1)S(1)} %collective-permute-done.19.refs_2_, bf16[512,128]{1,0:T(8,128)(2,1)S(1)} %collective-permute-done.20.refs_3_, ...), custom_call_target="tpu_custom_call" | custom-call | flops 1048576 | bytes 2097152 | tf_op jit(solution)/shard_map/join/pallas_call | solution.py:460
  (87 shorter events, 5.5 us)
Async XLA Ops:
  2.3 22.8 %collective-permute-start.1 = (bf16[512,384]{1,0:T(8,128)(2,1)}, bf16[512,384]{1,0:T(8,128)(2,1)S(1)}, u32[]{:S(2)}, u32[]{:S(2)}) collective-permute-start(bf16[512,384]{1,0:T(8,128)(2,1)} %refs_0_), channel_id=1, source_target_pairs={{0,2},{1,3},{2,0},{3,1},{4,6},{5,7},{6,4},{7,5},{8,10},{9,11},{10,... | collective-permute-start | bytes 1179656 | tf_op jit(solution)/shard_map/ppermute | solution.py:315
  5.2 20.4 %collective-permute-start.4 = (bf16[512,384]{1,0:T(8,128)(2,1)}, bf16[512,384]{1,0:T(8,128)(2,1)S(1)}, u32[]{:S(2)}, u32[]{:S(2)}) collective-permute-start(bf16[512,384]{1,0:T(8,128)(2,1)} %refs_4_), channel_id=1, source_target_pairs={{0,2},{1,3},{2,0},{3,1},{4,6},{5,7},{6,4},{7,5},{8,10},{9,11},{10,... | collective-permute-start | bytes 1179656 | tf_op jit(solution)/shard_map/ppermute | solution.py:315
  5.3 12.7 %all-to-all-start = ((s32[8,1,128]{2,1,0:T(1,128)}), s32[8,1,128]{2,1,0:T(1,128)S(1)}, u32[]{:S(2)}, u32[]{:S(2)}) async-start(s32[8,1,128]{2,1,0:T(1,128)} %bitcast.3), calls=%async_computation | async-start | bytes 8192 | tf_op jit(solution)/shard_map/all_to_all | solution.py:368
  11.6 20.8 %collective-permute-start = (bf16[512,384]{1,0:T(8,128)(2,1)}, bf16[512,384]{1,0:T(8,128)(2,1)S(1)}, u32[]{:S(2)}, u32[]{:S(2)}) collective-permute-start(bf16[512,384]{1,0:T(8,128)(2,1)} %refs_0_), channel_id=1, source_target_pairs={{0,1},{1,0},{2,3},{3,2},{4,5},{5,4},{6,7},{7,6},{8,9},{9,8},{10,11... | collective-permute-start | bytes 1179656 | tf_op jit(solution)/shard_map/ppermute | solution.py:315
  11.6 20.8 %collective-permute-start.3 = (bf16[512,384]{1,0:T(8,128)(2,1)}, bf16[512,384]{1,0:T(8,128)(2,1)S(1)}, u32[]{:S(2)}, u32[]{:S(2)}) collective-permute-start(bf16[512,384]{1,0:T(8,128)(2,1)} %refs_4_), channel_id=1, source_target_pairs={{0,1},{1,0},{2,3},{3,2},{4,5},{5,4},{6,7},{7,6},{8,9},{9,8},{10,11... | collective-permute-start | bytes 1179656 | tf_op jit(solution)/shard_map/ppermute | solution.py:315
  12.1 13.0 %collective-permute-start.7 = (bf16[128,384]{1,0:T(8,128)(2,1)}, bf16[128,384]{1,0:T(8,128)(2,1)S(1)}, u32[]{:S(2)}, u32[]{:S(2)}) collective-permute-start(bf16[128,384]{1,0:T(8,128)(2,1)} %refs_8_), channel_id=1, source_target_pairs={{0,2},{1,3},{2,0},{3,1},{4,6},{5,7},{6,4},{7,5},{8,10},{9,11},{10,... | collective-permute-start | bytes 294920 | tf_op jit(solution)/shard_map/ppermute | solution.py:315
  21.0 16.8 %all-to-all-start.1 = ((bf16[8,264,128]{2,1,0:T(8,128)(2,1)}), bf16[8,264,128]{2,1,0:T(8,128)(2,1)S(1)}, u32[]{:S(2)}, u32[]{:S(2)}) async-start(bf16[8,264,128]{2,1,0:T(8,128)(2,1)} %serve.1), calls=%async_computation.1 | async-start | bytes 1081344 | tf_op jit(solution)/shard_map/all_to_all | solution.py:402
  25.1 4.0 %collective-permute-start.6 = (bf16[128,384]{1,0:T(8,128)(2,1)S(1)}, bf16[128,384]{1,0:T(8,128)(2,1)S(1)}, u32[]{:S(2)}, u32[]{:S(2)}) collective-permute-start(bf16[128,384]{1,0:T(8,128)(2,1)S(1)} %copy-done.19), channel_id=1, source_target_pairs={{0,1},{1,0},{2,3},{3,2},{4,5},{5,4},{6,7},{7,6},{8,9},{9,8},{10,11... | collective-permute-start | bytes 294920 | tf_op jit(solution)/shard_map/ppermute | solution.py:315
  25.1 7.8 %collective-permute-start.2 = (bf16[512,384]{1,0:T(8,128)(2,1)S(1)}, bf16[512,384]{1,0:T(8,128)(2,1)}, u32[]{:S(2)}, u32[]{:S(2)}) collective-permute-start(bf16[512,384]{1,0:T(8,128)(2,1)S(1)} %collective-permute-done.1.refs_2_), channel_id=1, source_target_pairs={{0,1},{1,0},{2,3},{3,2},{4,5},{5,4},{6,7},{7,6},{8,9},{9,8},{10,11... | collective-permute-start | bytes 1179656 | tf_op jit(solution)/shard_map/ppermute | solution.py:315
  25.6 7.4 %collective-permute-start.5 = (bf16[512,384]{1,0:T(8,128)(2,1)S(1)}, bf16[512,384]{1,0:T(8,128)(2,1)}, u32[]{:S(2)}, u32[]{:S(2)}) collective-permute-start(bf16[512,384]{1,0:T(8,128)(2,1)S(1)} %collective-permute-done.4.refs_6_), channel_id=1, source_target_pairs={{0,1},{1,0},{2,3},{3,2},{4,5},{5,4},{6,7},{7,6},{8,9},{9,8},{10,11... | collective-permute-start | bytes 1179656 | tf_op jit(solution)/shard_map/ppermute | solution.py:315
  26.4 6.0 %copy-start.2 = (bf16[512,128]{1,0:T(8,128)(2,1)S(1)}, bf16[512,128]{1,0:T(8,128)(2,1)}, u32[]{:S(2)}) copy-start(bf16[512,128]{1,0:T(8,128)(2,1)} %refs_0_.1) | copy-start | bytes 393220
  29.1 8.7 %copy-start.21 = (bf16[128,384]{1,0:T(8,128)(2,1)}, bf16[128,384]{1,0:T(8,128)(2,1)S(1)}, u32[]{:S(2)}) copy-start(bf16[128,384]{1,0:T(8,128)(2,1)S(1)} %collective-permute-done.6.refs_9_) | copy-start | bytes 294916
  29.1 1.5 %collective-permute-start.8 = (bf16[128,384]{1,0:T(8,128)(2,1)S(1)}, bf16[128,384]{1,0:T(8,128)(2,1)}, u32[]{:S(2)}, u32[]{:S(2)}) collective-permute-start(bf16[128,384]{1,0:T(8,128)(2,1)S(1)} %collective-permute-done.7.refs_10_), channel_id=1, source_target_pairs={{0,1},{1,0},{2,3},{3,2},{4,5},{5,4},{6,7},{7,6},{8,9},{9,8},{10,11... | collective-permute-start | bytes 294920 | tf_op jit(solution)/shard_map/ppermute | solution.py:315
  30.6 23.5 %collective-permute-start.13 = (bf16[512,256]{1,0:T(8,128)(2,1)S(1)}, bf16[512,256]{1,0:T(8,128)(2,1)S(1)}, u32[]{:S(2)}, u32[]{:S(2)}) collective-permute-start(bf16[512,256]{1,0:T(8,128)(2,1)S(1)} %copy-done.1), channel_id=1, source_target_pairs={{0,2},{1,3},{2,0},{3,1},{4,6},{5,7},{6,4},{7,5},{8,10},{9,11},{10,... | collective-permute-start | bytes 786440 | tf_op jit(solution)/shard_map/ppermute | solution.py:315
  32.4 5.4 %copy-start.17 = (bf16[512,384]{1,0:T(8,128)(2,1)}, bf16[512,384]{1,0:T(8,128)(2,1)S(1)}, u32[]{:S(2)}) copy-start(bf16[512,384]{1,0:T(8,128)(2,1)S(1)} %collective-permute-done.refs_1_) | copy-start | bytes 1179652
  32.4 23.1 %collective-permute-start.12 = (bf16[512,256]{1,0:T(8,128)(2,1)S(1)}, bf16[512,256]{1,0:T(8,128)(2,1)}, u32[]{:S(2)}, u32[]{:S(2)}) collective-permute-start(bf16[512,256]{1,0:T(8,128)(2,1)S(1)} %copy-done.1), channel_id=1, source_target_pairs={{0,1},{1,0},{2,3},{3,2},{4,5},{5,4},{6,7},{7,6},{8,9},{9,8},{10,11... | collective-permute-start | bytes 786440 | tf_op jit(solution)/shard_map/ppermute | solution.py:315
  32.4 5.3 %copy-start.18 = (bf16[512,384]{1,0:T(8,128)(2,1)}, bf16[512,384]{1,0:T(8,128)(2,1)S(1)}, u32[]{:S(2)}) copy-start(bf16[512,384]{1,0:T(8,128)(2,1)S(1)} %collective-permute-done.3.refs_5_) | copy-start | bytes 1179652
  32.5 21.3 %collective-permute-start.10 = (bf16[512,128]{1,0:T(8,128)(2,1)S(1)}, bf16[512,128]{1,0:T(8,128)(2,1)}, u32[]{:S(2)}, u32[]{:S(2)}) collective-permute-start(bf16[512,128]{1,0:T(8,128)(2,1)S(1)} %copy-done.2), channel_id=1, source_target_pairs={{0,2},{1,3},{2,0},{3,1},{4,6},{5,7},{6,4},{7,5},{8,10},{9,11},{10,... | collective-permute-start | bytes 393224 | tf_op jit(solution)/shard_map/ppermute | solution.py:315
  32.9 22.5 %collective-permute-start.9 = (bf16[512,128]{1,0:T(8,128)(2,1)S(1)}, bf16[512,128]{1,0:T(8,128)(2,1)}, u32[]{:S(2)}, u32[]{:S(2)}) collective-permute-start(bf16[512,128]{1,0:T(8,128)(2,1)S(1)} %copy-done.2), channel_id=1, source_target_pairs={{0,1},{1,0},{2,3},{3,2},{4,5},{5,4},{6,7},{7,6},{8,9},{9,8},{10,11... | collective-permute-start | bytes 393224 | tf_op jit(solution)/shard_map/ppermute | solution.py:315
  43.8 11.9 %copy-start = (bf16[1024,512]{1,0:T(8,128)(2,1)S(1)}, bf16[1024,512]{1,0:T(8,128)(2,1)}, u32[]{:S(2)}) copy-start(bf16[1024,512]{1,0:T(8,128)(2,1)} %memory_ref.3) | copy-start | bytes 3145732
  43.8 20.4 %all-to-all-start.2 = ((bf16[32,72,128]{2,1,0:T(8,128)(2,1)}), bf16[32,72,128]{2,1,0:T(8,128)(2,1)S(1)}, u32[]{:S(2)}, u32[]{:S(2)}) async-start(bf16[32,72,128]{2,1,0:T(8,128)(2,1)} %get-tuple-element.29), calls=%async_computation.2 | async-start | bytes 1179648 | tf_op jit(solution)/shard_map/all_to_all | solution.py:424
  47.5 4.9 %collective-permute-start.16 = (s32[8,128]{1,0:T(8,128)S(1)}, s32[8,128]{1,0:T(8,128)S(1)}, u32[]{:S(2)}, u32[]{:S(2)}) collective-permute-start(s32[8,128]{1,0:T(8,128)S(1)} %bitcast.23), channel_id=1, source_target_pairs={{0,2},{1,3},{2,0},{3,1},{4,6},{5,7},{6,4},{7,5},{8,10},{9,11},{10,... | collective-permute-start | bytes 12296 | tf_op jit(solution)/shard_map/ppermute | solution.py:315
  52.4 1.2 %collective-permute-start.15 = (s32[8,128]{1,0:T(8,128)S(1)}, s32[8,128]{1,0:T(8,128)S(1)}, u32[]{:S(2)}, u32[]{:S(2)}) collective-permute-start(s32[8,128]{1,0:T(8,128)S(1)} %bitcast.25), channel_id=1, source_target_pairs={{0,1},{1,0},{2,3},{3,2},{4,5},{5,4},{6,7},{7,6},{8,9},{9,8},{10,11... | collective-permute-start | bytes 12296 | tf_op jit(solution)/shard_map/ppermute | solution.py:315
  53.6 1.2 %collective-permute-start.17 = (s32[8,128]{1,0:T(8,128)S(1)}, s32[8,128]{1,0:T(8,128)S(1)}, u32[]{:S(2)}, u32[]{:S(2)}) collective-permute-start(s32[8,128]{1,0:T(8,128)S(1)} %collective-permute-done.16), channel_id=1, source_target_pairs={{0,1},{1,0},{2,3},{3,2},{4,5},{5,4},{6,7},{7,6},{8,9},{9,8},{10,11... | collective-permute-start | bytes 12296 | tf_op jit(solution)/shard_map/ppermute | solution.py:315
  53.7 1.7 %collective-permute-start.11 = (bf16[512,128]{1,0:T(8,128)(2,1)}, bf16[512,128]{1,0:T(8,128)(2,1)}, u32[]{:S(2)}, u32[]{:S(2)}) collective-permute-start(bf16[512,128]{1,0:T(8,128)(2,1)} %collective-permute-done.10.refs_2_), channel_id=1, source_target_pairs={{0,1},{1,0},{2,3},{3,2},{4,5},{5,4},{6,7},{7,6},{8,9},{9,8},{10,11... | collective-permute-start | bytes 393224 | tf_op jit(solution)/shard_map/ppermute | solution.py:315
  54.1 1.7 %collective-permute-start.14 = (bf16[512,256]{1,0:T(8,128)(2,1)S(1)}, bf16[512,256]{1,0:T(8,128)(2,1)}, u32[]{:S(2)}, u32[]{:S(2)}) collective-permute-start(bf16[512,256]{1,0:T(8,128)(2,1)S(1)} %collective-permute-done.13.refs_6_), channel_id=1, source_target_pairs={{0,1},{1,0},{2,3},{3,2},{4,5},{5,4},{6,7},{7,6},{8,9},{9,8},{10,11... | collective-permute-start | bytes 786440 | tf_op jit(solution)/shard_map/ppermute | solution.py:315
  65.7 5.5 %collective-permute-start.22 = (bf16[512,128]{1,0:T(8,128)(2,1)S(1)}, bf16[512,128]{1,0:T(8,128)(2,1)S(1)}, u32[]{:S(2)}, u32[]{:S(2)}) collective-permute-start(bf16[512,128]{1,0:T(8,128)(2,1)S(1)} %apply.3.refs_4_), channel_id=1, source_target_pairs={{0,2},{1,3},{2,0},{3,1},{4,6},{5,7},{6,4},{7,5},{8,10},{9,11},{10,... | collective-permute-start | bytes 393224 | tf_op jit(solution)/shard_map/ppermute | solution.py:315
  68.4 5.6 %collective-permute-start.19 = (bf16[512,128]{1,0:T(8,128)(2,1)S(1)}, bf16[512,128]{1,0:T(8,128)(2,1)S(1)}, u32[]{:S(2)}, u32[]{:S(2)}) collective-permute-start(bf16[512,128]{1,0:T(8,128)(2,1)S(1)} %apply.2.refs_0_), channel_id=1, source_target_pairs={{0,2},{1,3},{2,0},{3,1},{4,6},{5,7},{6,4},{7,5},{8,10},{9,11},{10,... | collective-permute-start | bytes 393224 | tf_op jit(solution)/shard_map/ppermute | solution.py:315
  69.3 4.6 %collective-permute-start.21 = (bf16[512,128]{1,0:T(8,128)(2,1)S(1)}, bf16[512,128]{1,0:T(8,128)(2,1)S(1)}, u32[]{:S(2)}, u32[]{:S(2)}) collective-permute-start(bf16[512,128]{1,0:T(8,128)(2,1)S(1)} %apply.3.refs_4_), channel_id=1, source_target_pairs={{0,1},{1,0},{2,3},{3,2},{4,5},{5,4},{6,7},{7,6},{8,9},{9,8},{10,11... | collective-permute-start | bytes 393224 | tf_op jit(solution)/shard_map/ppermute | solution.py:315
  69.3 4.6 %collective-permute-start.18 = (bf16[512,128]{1,0:T(8,128)(2,1)S(1)}, bf16[512,128]{1,0:T(8,128)(2,1)S(1)}, u32[]{:S(2)}, u32[]{:S(2)}) collective-permute-start(bf16[512,128]{1,0:T(8,128)(2,1)S(1)} %apply.2.refs_0_), channel_id=1, source_target_pairs={{0,1},{1,0},{2,3},{3,2},{4,5},{5,4},{6,7},{7,6},{8,9},{9,8},{10,11... | collective-permute-start | bytes 393224 | tf_op jit(solution)/shard_map/ppermute | solution.py:315
  71.1 2.8 %collective-permute-start.23 = (bf16[512,128]{1,0:T(8,128)(2,1)S(1)}, bf16[512,128]{1,0:T(8,128)(2,1)S(1)}, u32[]{:S(2)}, u32[]{:S(2)}) collective-permute-start(bf16[512,128]{1,0:T(8,128)(2,1)S(1)} %collective-permute-done.22.refs_6_), channel_id=1, source_target_pairs={{0,1},{1,0},{2,3},{3,2},{4,5},{5,4},{6,7},{7,6},{8,9},{9,8},{10,11... | collective-permute-start | bytes 393224 | tf_op jit(solution)/shard_map/ppermute | solution.py:315
  73.9 1.3 %collective-permute-start.20 = (bf16[512,128]{1,0:T(8,128)(2,1)S(1)}, bf16[512,128]{1,0:T(8,128)(2,1)S(1)}, u32[]{:S(2)}, u32[]{:S(2)}) collective-permute-start(bf16[512,128]{1,0:T(8,128)(2,1)S(1)} %collective-permute-done.19.refs_2_), channel_id=1, source_target_pairs={{0,1},{1,0},{2,3},{3,2},{4,5},{5,4},{6,7},{7,6},{8,9},{9,8},{10,11... | collective-permute-start | bytes 393224 | tf_op jit(solution)/shard_map/ppermute | solution.py:315
  (17 other events, 37.4 us)
